TPU v7x, 128 devices: a whole 4x4x4 slice. The times are simulated.
128 devices in a mesh: seq: 32 (over z, x, y_lo), wshard: 4 (over y_hi, core).
Axes of the slice: x: 4, y: 4 (y_hi: 2, y_lo: 2; y = y_hi * 2 + y_lo), z: 4, core: 2. Of those that a mesh axis runs over, the one named last changes fastest.
Arguments:
- layer_in: bfloat16 [8, 4096, 1024], P('wshard', 'seq'), may hold values from -6 to 6
- gain_in: float32 [1024], replicated, may hold values from 0.25 to 1.75
- w_z: bfloat16 [1024, 2048], P('wshard'), may hold values from -0.1875 to 0.1875
- w_x: bfloat16 [1024, 2048], P('wshard'), may hold values from -0.1875 to 0.1875
- w_bc: bfloat16 [1024, 256], P('wshard'), may hold values from -0.1875 to 0.1875
- w_dt: bfloat16 [1024, 32], P('wshard'), may hold values from -0.1875 to 0.1875
- conv_x_weight: float32 [4, 2048], P(None, 'seq'), may hold values from -3 to 3
- conv_x_bias: float32 [2048], P('seq'), may hold values from -3 to 3
- conv_bc_weight: float32 [4, 256], replicated, may hold values from -3 to 3
- conv_bc_bias: float32 [256], replicated, may hold values from -3 to 3
- dt_bias: float32 [32], P('seq'), may hold values from -6 to -2
- a_log: float32 [32], P('seq'), may hold values from -1 to 2
- d_skip: float32 [32], P('seq'), may hold values from -3 to 3
- gain_norm: float32 [2048], replicated, may hold values from 0.25 to 1.75
- w_out: bfloat16 [2048, 1024], P('wshard'), may hold values from -0.125 to 0.125
- cotangent: bfloat16 [8, 4096, 1024], P('wshard', 'seq'), may hold values from -6 to 6
Outputs:
- layer_out: bfloat16 [8, 4096, 1024], P('wshard', 'seq')
- input_grad: float32 [8, 4096, 1024], P('wshard', 'seq')
- grad_gain_in: float32 [1024], replicated
- grad_w_z: float32 [1024, 2048], P('wshard')
- grad_w_x: float32 [1024, 2048], P('wshard')
- grad_w_bc: float32 [1024, 256], P('wshard')
- grad_w_dt: float32 [1024, 32], P('wshard')
- grad_conv_x_weight: float32 [4, 2048], P(None, 'seq')
- grad_conv_x_bias: float32 [2048], P('seq')
- grad_conv_bc_weight: float32 [4, 256], replicated
- grad_conv_bc_bias: float32 [256], replicated
- grad_dt_bias: float32 [32], P('seq')
- grad_a_log: float32 [32], P('seq')
- grad_d_skip: float32 [32], P('seq')
- grad_gain_norm: float32 [2048], replicated
- grad_w_out: float32 [2048, 1024], P('wshard')
All inputs are finite; a program needn't handle non-finite values.
Results may differ from a plain program's by a relative error of at most 0.035.
Values may be sent and summed in bfloat16 or wider, within the bound.
A program may use at most 192 MiB of HBM per device.

v0:
```python
import jax
import jax.numpy as jnp
from jax import lax
from jax.sharding import PartitionSpec as P

GROUP = 256


epsilon = 1e-05
highest = lax.Precision.HIGHEST


def side_by_side(arrays, axis, dim, along):
    ends, at = ([], 0)
    for a in arrays[:-1]:
        at += a.shape[along]
        ends.append(at)
    both = jnp.concatenate(arrays, axis=along)
    return tuple(jnp.split(lax.all_gather(both, axis, axis=dim, tiled=True), ends, axis=along))


def copy_for_each(shard, axis):
    size = lax.axis_size(axis)
    return lax.all_to_all(
        jnp.broadcast_to(shard[None], (size, *shard.shape)), axis, 0, 0, tiled=True
    )


def of_everyone(shard, axis):
    return copy_for_each(shard, axis).sum(axis=0)


def in_one(arrays, axis):
    ravelled, at, finished = (jnp.concatenate([a.reshape(-1) for a in arrays]), 0, [])
    running = of_everyone(ravelled, axis)
    for a in arrays:
        finished.append(running[at : at + a.size].reshape(a.shape))
        at += a.size
    return tuple(finished)


def in_one_piece(arrays, axis, dim, along):
    ends, at = ([], 0)
    for a in arrays[:-1]:
        at += a.shape[along]
        ends.append(at)
    both = jnp.concatenate(arrays, axis=along)
    return tuple(
        jnp.split(lax.psum_scatter(both, axis, scatter_dimension=dim, tiled=True), ends, axis=along)
    )


def conv_silu(values, kernel_taps, bias_vec):
    seq_rows = values.shape[0]
    taps_count = kernel_taps.shape[0]
    padded = jnp.pad(values, ((taps_count - 1, 0), (0, 0)))
    summed_in = bias_vec[None, :] + kernel_taps[0][None, :] * padded[0:seq_rows]
    for offset in range(1, taps_count):
        summed_in = summed_in + kernel_taps[offset][None, :] * padded[offset : offset + seq_rows]
    return jax.nn.silu(summed_in)


def group_step(carry_state, inputs, b_block, c_block, dt_block, dt_bias, a_log, d_skip):
    steps_dt = jax.nn.softplus(dt_block + dt_bias[None, :])
    log_decay = steps_dt * (-jnp.exp(a_log))[None, :]
    running = jnp.cumsum(log_decay, axis=0)
    length = inputs.shape[0]
    causal = (jnp.arange(length)[:, None] >= jnp.arange(length)[None, :])[:, :, None]
    spread = running[:, None, :] - running[None, :, :]
    decays = jnp.where(causal, jnp.exp(jnp.where(causal, spread, 0.0)), 0.0)
    intersection = jnp.dot(c_block, b_block.T, precision=highest)
    mixing = intersection[:, :, None] * decays * steps_dt[None, :, :]
    output = jnp.einsum("ijh,jhp->ihp", mixing, inputs, precision=highest)
    carried = jnp.einsum("in,hpn->ihp", c_block, carry_state, precision=highest)
    output = output + jnp.exp(running)[:, :, None] * carried + d_skip[None, :, None] * inputs
    to_end = jnp.exp(running[-1][None, :] - running) * steps_dt
    update = jnp.einsum("jhp,jn->hpn", inputs * to_end[:, :, None], b_block, precision=highest)
    new_state = jnp.exp(running[-1])[:, None, None] * carry_state + update
    return (new_state, output)


def rms_gain(values, gain_vec):
    return (
        values
        * lax.rsqrt(jnp.mean(values * values, axis=-1, keepdims=True) + epsilon)
        * gain_vec[None, :]
    )


def gated_norm(mixer_out, gate_lin, gain_vec):
    gated = mixer_out * jax.nn.silu(gate_lin)
    return rms_gain(gated, gain_vec)


def contract_rows(left_rows, right_rows):
    return lax.dot_general(
        left_rows, right_rows, (((0,), (0,)), ((), ())), preferred_element_type=jnp.float32
    )


def times_transpose(grad_rows, weight):
    return lax.dot_general(
        grad_rows, weight, (((1,), (1,)), ((), ())), preferred_element_type=jnp.float32
    )


def conv_piece(x_values, bc_values, taps_x, bias_x, taps_bc, bias_bc):
    return (conv_silu(x_values, taps_x, bias_x), conv_silu(bc_values, taps_bc, bias_bc))


def shards(
    layer_in,
    gain_in,
    w_z,
    w_x,
    w_bc,
    w_dt,
    conv_x_weight,
    conv_x_bias,
    conv_bc_weight,
    conv_bc_bias,
    dt_bias,
    a_log,
    d_skip,
    gain_norm,
    w_out,
    cotangent,
):
    seq_count = layer_in.shape[0]
    tok_count = layer_in.shape[1]
    width = layer_in.shape[2]
    hidden = layer_in.astype(jnp.float32).reshape(seq_count * tok_count, width)
    upstream = cotangent.reshape(seq_count * tok_count, width)
    full_z, full_x, full_bc, full_dt, full_out = (
        *side_by_side((w_z, w_x, w_bc, w_dt), "wshard", 0, 1),
        lax.all_gather(w_out, "wshard", axis=0, tiled=True),
    )
    normed, pull_in = jax.vjp(rms_gain, hidden, gain_in)
    normed_low = normed.astype(jnp.bfloat16)
    gate_lin = jnp.dot(normed_low, full_z, preferred_element_type=jnp.float32)
    x_raw = jnp.dot(normed_low, full_x, preferred_element_type=jnp.float32).astype(jnp.bfloat16)
    bc_raw = jnp.dot(normed_low, full_bc, preferred_element_type=jnp.float32).astype(jnp.bfloat16)
    dt_raw = jnp.dot(normed_low, full_dt, preferred_element_type=jnp.float32).astype(jnp.bfloat16)
    x_raw = x_raw.reshape(seq_count, tok_count, -1)
    bc_raw = bc_raw.reshape(seq_count, tok_count, -1)
    dt_raw = dt_raw.reshape(seq_count, tok_count, -1)
    bc_whole = lax.all_gather(bc_raw, "seq", axis=1, tiled=True)
    x_heads, dt_heads = (
        lax.all_to_all(x_raw, "seq", split_axis=2, concat_axis=1, tiled=True),
        lax.all_to_all(dt_raw, "seq", split_axis=2, concat_axis=1, tiled=True),
    )
    seq_len = x_heads.shape[1]
    head_dev = dt_heads.shape[2]
    head_size = x_heads.shape[2] // head_dev
    state_size = bc_whole.shape[2] // 2
    blocks_count = seq_len // GROUP
    conv_batch = jax.vmap(conv_piece, in_axes=(0, 0, None, None, None, None))
    (conv_x, conv_bc), pull_conv = jax.vjp(
        conv_batch,
        x_heads.astype(jnp.float32),
        bc_whole.astype(jnp.float32),
        conv_x_weight,
        conv_x_bias,
        conv_bc_weight,
        conv_bc_bias,
    )
    conv_x_low = conv_x.astype(jnp.bfloat16)
    conv_bc_low = conv_bc.astype(jnp.bfloat16)
    x_blocks = conv_x_low.reshape(seq_count, blocks_count, GROUP, head_dev, head_size).swapaxes(
        0, 1
    )
    b_blocks = (
        conv_bc_low[:, :, :state_size]
        .reshape(seq_count, blocks_count, GROUP, state_size)
        .swapaxes(0, 1)
    )
    c_blocks = (
        conv_bc_low[:, :, state_size:]
        .reshape(seq_count, blocks_count, GROUP, state_size)
        .swapaxes(0, 1)
    )
    t_blocks = dt_heads.reshape(seq_count, blocks_count, GROUP, head_dev).swapaxes(0, 1)
    batched_step = jax.vmap(group_step, in_axes=(0, 0, 0, 0, 0, None, None, None))

    def forward_step(carry_state, block):
        x_block, b_block, c_block, t_block = block
        new_state, output = batched_step(
            carry_state,
            x_block.astype(jnp.float32),
            b_block.astype(jnp.float32),
            c_block.astype(jnp.float32),
            t_block.astype(jnp.float32),
            dt_bias,
            a_log,
            d_skip,
        )
        return (new_state, (output.astype(jnp.bfloat16), carry_state))

    zero_state = jnp.zeros((seq_count, head_dev, head_size, state_size), jnp.float32)
    last_state, (y_blocks, start_states) = lax.scan(
        forward_step, zero_state, (x_blocks, b_blocks, c_blocks, t_blocks)
    )
    y_heads = y_blocks.swapaxes(0, 1).reshape(seq_count, seq_len, head_dev * head_size)
    y_tokens = lax.all_to_all(y_heads, "seq", split_axis=1, concat_axis=2, tiled=True)
    y_flat = y_tokens.reshape(seq_count * tok_count, -1)
    mixed, pull_gate = jax.vjp(gated_norm, y_flat.astype(jnp.float32), gate_lin, gain_norm)
    mixed_low = mixed.astype(jnp.bfloat16)
    result = hidden + jnp.dot(mixed_low, full_out, preferred_element_type=jnp.float32)
    layer_out = result.astype(jnp.bfloat16).reshape(seq_count, tok_count, width)
    d_mixed = times_transpose(upstream, full_out)
    d_y, d_gate, grad_gain_norm = pull_gate(d_mixed)
    d_gate_low = d_gate.astype(jnp.bfloat16)
    d_y_seq = d_y.astype(jnp.bfloat16).reshape(seq_count, tok_count, -1)
    d_y_heads = lax.all_to_all(d_y_seq, "seq", split_axis=2, concat_axis=1, tiled=True)
    dy_blocks = d_y_heads.reshape(seq_count, blocks_count, GROUP, head_dev, head_size).swapaxes(
        0, 1
    )

    def backward_step(carry, block):
        grad_state, sum_bias, sum_alog, sum_skip = carry
        x_block, b_block, c_block, t_block, start_state, dy_block = block
        unused, pullback = jax.vjp(
            batched_step,
            start_state,
            x_block.astype(jnp.float32),
            b_block.astype(jnp.float32),
            c_block.astype(jnp.float32),
            t_block.astype(jnp.float32),
            dt_bias,
            a_log,
            d_skip,
        )
        (
            grad_start,
            grad_inputs,
            grad_bmat,
            grad_cmat,
            grad_steps,
            grad_bias,
            grad_alog,
            grad_skip,
        ) = pullback((grad_state, dy_block.astype(jnp.float32)))
        new_carry = (grad_start, sum_bias + grad_bias, sum_alog + grad_alog, sum_skip + grad_skip)
        return (new_carry, (grad_inputs, grad_bmat, grad_cmat, grad_steps))

    zero_carry = (
        zero_state,
        jnp.zeros_like(dt_bias),
        jnp.zeros_like(a_log),
        jnp.zeros_like(d_skip),
    )
    (grad_first, grad_dt_bias, grad_a_log, grad_d_skip), (
        grad_inputs,
        grad_bmat,
        grad_cmat,
        grad_steps,
    ) = lax.scan(
        backward_step,
        zero_carry,
        (x_blocks, b_blocks, c_blocks, t_blocks, start_states, dy_blocks),
        reverse=True,
    )
    d_conv_x = grad_inputs.swapaxes(0, 1).reshape(seq_count, seq_len, head_dev * head_size)
    d_conv_bc = jnp.concatenate(
        [
            grad_bmat.swapaxes(0, 1).reshape(seq_count, seq_len, state_size),
            grad_cmat.swapaxes(0, 1).reshape(seq_count, seq_len, state_size),
        ],
        axis=2,
    )
    d_dt_heads = grad_steps.swapaxes(0, 1).reshape(seq_count, seq_len, head_dev)
    d_x_raw, d_bc_raw, grad_taps_x, grad_bias_x, grad_taps_bc, grad_bias_bc = pull_conv(
        (d_conv_x, d_conv_bc)
    )
    d_x_tokens, d_dt_tokens = (
        lax.all_to_all(
            d_x_raw.astype(jnp.bfloat16), "seq", split_axis=1, concat_axis=2, tiled=True
        ),
        lax.all_to_all(
            d_dt_heads.astype(jnp.bfloat16), "seq", split_axis=1, concat_axis=2, tiled=True
        ),
    )
    d_bc_tokens = lax.psum_scatter(
        d_bc_raw.astype(jnp.bfloat16), "seq", scatter_dimension=1, tiled=True
    )
    d_x_tokens = d_x_tokens.reshape(seq_count * tok_count, -1)
    d_dt_tokens = d_dt_tokens.reshape(seq_count * tok_count, -1)
    d_bc_tokens = d_bc_tokens.reshape(seq_count * tok_count, -1)
    d_normed = (
        times_transpose(d_gate_low, full_z)
        + times_transpose(d_x_tokens, full_x)
        + times_transpose(d_bc_tokens, full_bc)
        + times_transpose(d_dt_tokens, full_dt)
    )
    d_hidden, grad_gain_in = pull_in(d_normed)
    input_grad = (upstream.astype(jnp.float32) + d_hidden).reshape(seq_count, tok_count, width)
    term_z = contract_rows(normed_low, d_gate_low)
    term_x = contract_rows(normed_low, d_x_tokens)
    term_bc = contract_rows(normed_low, d_bc_tokens)
    term_dt = contract_rows(normed_low, d_dt_tokens)
    term_out = contract_rows(mixed_low, upstream)
    (
        sum_taps_x,
        sum_bias_x,
        sum_dt_bias,
        sum_a_log,
        sum_d_skip,
        part_taps_bc,
        part_bias_bc,
        part_gain_in,
        part_gain_norm,
    ) = in_one(
        (
            grad_taps_x,
            grad_bias_x,
            grad_dt_bias,
            grad_a_log,
            grad_d_skip,
            grad_taps_bc,
            grad_bias_bc,
            grad_gain_in,
            grad_gain_norm,
        ),
        "wshard",
    )
    shard_rows = (
        *tuple(
            (
                part.astype(jnp.float32)
                for part in in_one_piece(
                    (
                        term_z.astype(jnp.bfloat16),
                        term_x.astype(jnp.bfloat16),
                        term_bc.astype(jnp.bfloat16),
                        term_dt.astype(jnp.bfloat16),
                    ),
                    "wshard",
                    0,
                    1,
                )
            )
        ),
        lax.psum_scatter(
            term_out.astype(jnp.bfloat16), "wshard", scatter_dimension=0, tiled=True
        ).astype(jnp.float32),
    )
    (
        grad_w_z,
        grad_w_x,
        grad_w_bc,
        grad_w_dt,
        grad_w_out,
        sum_taps_bc,
        sum_bias_bc,
        sum_gain_in,
        sum_gain_norm,
    ) = (
        lax.psum(shard_rows[0].astype(jnp.bfloat16), "seq").astype(jnp.float32),
        lax.psum(shard_rows[1].astype(jnp.bfloat16), "seq").astype(jnp.float32),
        lax.psum(shard_rows[2].astype(jnp.bfloat16), "seq").astype(jnp.float32),
        lax.psum(shard_rows[3].astype(jnp.bfloat16), "seq").astype(jnp.float32),
        lax.psum(shard_rows[4].astype(jnp.bfloat16), "seq").astype(jnp.float32),
        lax.psum(part_taps_bc.astype(jnp.bfloat16), "seq").astype(jnp.float32),
        lax.psum(part_bias_bc.astype(jnp.bfloat16), "seq").astype(jnp.float32),
        lax.psum(part_gain_in.astype(jnp.bfloat16), "seq").astype(jnp.float32),
        lax.psum(part_gain_norm.astype(jnp.bfloat16), "seq").astype(jnp.float32),
    )
    return (
        layer_out,
        input_grad,
        sum_gain_in,
        grad_w_z,
        grad_w_x,
        grad_w_bc,
        grad_w_dt,
        sum_taps_x,
        sum_bias_x,
        sum_taps_bc,
        sum_bias_bc,
        sum_dt_bias,
        sum_a_log,
        sum_d_skip,
        sum_gain_norm,
        grad_w_out,
    )


def solution(mesh):
    return jax.shard_map(
        shards,
        mesh=mesh,
        in_specs=(
            P("wshard", "seq", None),
            P(),
            P("wshard", None),
            P("wshard", None),
            P("wshard", None),
            P("wshard", None),
            P(None, "seq"),
            P("seq"),
            P(),
            P(),
            P("seq"),
            P("seq"),
            P("seq"),
            P(),
            P("wshard", None),
            P("wshard", "seq", None),
        ),
        out_specs=(
            P("wshard", "seq", None),
            P("wshard", "seq", None),
            P(),
            P("wshard", None),
            P("wshard", None),
            P("wshard", None),
            P("wshard", None),
            P(None, "seq"),
            P("seq"),
            P(),
            P(),
            P("seq"),
            P("seq"),
            P("seq"),
            P(),
            P("wshard", None),
        ),
        check_vma=False,
    )
```

profile of v0, /device:TPU:0, one launch (start us, length us, event | category | flops | bytes accessed | tf_op | source)
XLA Modules:
  0.0 1998.3 jit_solution(10169368731815535252)
XLA Ops:
  8.1 3.2 pad_maximum_fusion.2
  12.7 68.0 %all-gather.4.cloned.1.call-done = bf16[1024,4384]{1,0:T(8,128)(2,1)} async-done(((bf16[256,4384]{1,0:T(8,128)(2,1)}), bf16[1024,4384]{1,0:T(8,128)(2,1)}) %all-gather.4.cloned.1.call-update) | async-done | bytes 8978448 | tf_op jit(solution)/shard_map/all_gather | solution.py:19
  82.7 3.4 fusion.181
  88.2 7.4 all-to-all-start.1
  99.0 17.7 all-to-all-done.1
  117.7 6.8 all-to-all-start
  130.2 119.4 %all-gather.6.cloned.1.call-done = bf16[2,4096,256]{2,1,0:T(8,128)(2,1)} async-done(((bf16[2,128,256]{2,1,0:T(8,128)(2,1)}), bf16[2,4096,256]{2,1,0:T(8,128)(2,1)}) %all-gather.6.cloned.1.call-update) | async-done | bytes 4194320 | tf_op jit(solution)/shard_map/all_gather | solution.py:147
  252.5 7.2 multiply_convert_fusion
  263.4 158.7 %while.46 = (s32[]{:T(128)}, f32[2,1,64,128]{3,2,0,1:T(8,128)S(1)}, bf16[16,2,256,1,64]{2,4,1,3,0:T(8,128)(2,1)}, f32[16,2,1,64,128]{4,3,1,2,0:T(8,128)}, bf16[1...) while((s32[]{:T(128)}, f32[2,1,64,128]{3,2,0,1:T(8,128)S(1)}, ...), condition=%wide.region_4.5_spmd.clone, body=%wide.region_1.4_spmd.clone.sunk | while | flops 236021248 | bytes 2610060 | solution.py:200
  422.0 6.1 copy.425
  428.1 5.8 reshape.1908
  433.9 19.3 all_to_all.84
  453.2 5.0 reshape.1909
  458.2 3.8 copy.398
  463.9 4.5 copy.429
  468.4 5.0 reshape.1903
  473.4 5.8 multiply_reduce_fusion.13
  479.2 4.8 multiply_reduce_fusion.7
  486.9 3.7 copy.402
  490.5 4.7 all-to-all-start.3
  495.7 13.1 all-to-all-done.3
  523.9 780.9 %while.47 = (s32[]{:T(128)}, f32[2,1,64,128]{3,2,0,1:T(8,128)S(1)}, f32[1]{0:T(128)}, f32[1]{0:T(128)}, f32[1]{0:T(128)}, /*index=5*/f32[16,2,256,1,64]{2,4,1,3,...) while((s32[]{:T(128)}, f32[2,1,64,128]{3,2,0,1:T(8,128)S(1)}, ...), condition=%wide.region_22.23_spmd.clone, body=%wide.region_7.0_spmd.clone.sunk | while | flops 810133504 | bytes 7804036 | solution.py:257
  543.2 3.2 reduce-window.74
  592.0 3.2 reduce-window.74
  640.8 3.2 reduce-window.74
  689.6 3.2 reduce-window.74
  738.4 3.2 reduce-window.74
  787.1 3.2 reduce-window.74
  836.0 3.2 reduce-window.74
  884.9 3.2 reduce-window.74
  933.7 3.2 reduce-window.74
  982.5 3.2 reduce-window.74
  1031.4 3.2 reduce-window.74
  1080.1 3.2 reduce-window.74
  1129.0 3.2 reduce-window.74
  1304.7 16.9 multiply_reduce_fusion.5
  1321.6 11.3 broadcast_multiply_fusion
  1332.9 14.2 fusion.172
  1347.8 3.8 copy.414
  1352.1 24.4 %reduce.88 = bf16[4096,2]{1,0:T(8,128)(2,1)} reduce(bf16[4096,1,2]{2,1,0:T(2,128)(2,1)} %bitcast.711, bf16[]{:T(256)} %broadcast.932), dimensions={1}, to_apply=%bitcast.498.reduce_sub_computation | reduce | bytes 32770
  1376.5 3.3 reshape.1910
  1379.8 4.0 all-to-all-start.5
  1383.9 4.1 copy.409
  1390.8 5.6 multiply_reduce_fusion.10
  1400.2 5.5 copy.410
  1405.7 5.8 reshape.1912
  1411.5 8.5 all-to-all-start.4
  1420.3 4.7 convolution_convert_fusion.2
  1425.0 4.6 reshape.1911
  1429.6 4.5 copy.415
  1436.3 5.7 reshape.1913
  1441.9 6.2 copy.411
  1448.1 4.6 convolution_convert_fusion.1
  1452.6 63.1 %reduce-scatter.4.cloned.1.call-done = bf16[2,128,256]{2,1,0:T(8,128)(2,1)} async-done(((bf16[2,4096,256]{2,1,0:T(8,128)(2,1)}), bf16[2,128,256]{2,1,0:T(8,128)(2,1)}) %reduce-scatter.4.cloned.1.call-update) | async-done | bytes 131088 | tf_op jit(solution)/shard_map/reduce_scatter | solution.py:283
  1517.0 9.0 pad_maximum_fusion
  1527.0 3.4 convolution_convert_fusion
  1530.4 77.6 %reduce-scatter.6.cloned.1.call-done = bf16[256,4384]{1,0:T(8,128)(2,1)} async-done(((bf16[1024,4384]{1,0:T(8,128)(2,1)}), bf16[256,4384]{1,0:T(8,128)(2,1)}) %reduce-scatter.6.cloned.1.call-update) | async-done | bytes 2244624 | tf_op jit(solution)/shard_map/reduce_scatter | solution.py:49
  1612.7 48.7 %reduce-scatter.8.cloned.1.call-done = bf16[512,1024]{1,0:T(8,128)(2,1)} async-done(((bf16[2048,1024]{1,0:T(8,128)(2,1)}), bf16[512,1024]{1,0:T(8,128)(2,1)}) %reduce-scatter.8.cloned.1.call-update) | async-done | bytes 1048592 | tf_op jit(solution)/shard_map/reduce_scatter | solution.py:343
  1661.4 4.9 fusion.173
  1669.9 4.1 fusion.192
  1676.5 3.3 all-to-all-start.6
  1681.1 5.3 all-to-all-done.6
  1688.5 158.3 %all-reduce.20 = (bf16[256,32]{1,0:T(8,128)(2,1)S(1)}, bf16[1024]{0:T(1024)(128)(2,1)S(1)}, bf16[4,256]{1,0:T(4,128)(2,1)S(1)}, bf16[256]{0:T(256)(128)(2,1)S(1)}, bf16[2048]{0:T(1024)(128)(2,1)S(1)}) all-reduce(bf16[256,32]{1,0:T(8,128)(2,1)S(1)} %slice-done, ...), channel_id=1, replica_groups=mesh['seq'=32,'wshard'=4] {'seq'}, use_global_device_ids=true, to_apply=%region_43.44 | all-reduce | flops 12544 | bytes 50176 | tf_op jit(solution)/shard_map/psum | solution.py:361
  1849.8 134.6 %all-reduce.24.cloned.1.call-done = (bf16[256,2048]{1,0:T(8,128)(2,1)}, bf16[256,2048]{1,0:T(8,128)(2,1)}, bf16[256,256]{1,0:T(8,128)(2,1)}, bf16[512,1024]{1,0:T(8,128)(2,1)}) async-done(((bf16[256,2048]{1,0:T(8,128)(2,1)}, bf16[256,2048]{1,0:T(8,128)(2,1)}, bf16[256,256]{1,0:T(8,128)(2,1)}, bf16[512,1024]{1,0:T(8,128)(2,1)}), (bf16[256,2048]{1,0:T(8,128)(2,1)}, bf16[256,2048]{1,0:T(8,128)(2,1)}, ...) | async-done | bytes 3276816 | tf_op jit(solution)/shard_map/psum | solution.py:358
  (1572 shorter events, 942.0 us)
Async XLA Ops:
  7.2 73.5 %all-gather.4.cloned.1.call-start = ((), (), s32[]{:S(2)}) async-start(), calls=%async_computation.10 | async-start | bytes 11468800 | tf_op jit(solution)/shard_map/all_gather | solution.py:19
  11.3 238.3 %all-gather.6.cloned.1.call-start = ((), (), s32[]{:S(2)}) async-start(), calls=%async_computation.11 | async-start | bytes 4325376 | tf_op jit(solution)/shard_map/all_gather | solution.py:147
  12.5 73.7 %copy-start.33 = (f32[2,128]{1,0:T(2,128)}, f32[2,128]{1,0:T(2,128)S(1)}, u32[]{:S(2)}) copy-start(f32[2,128]{1,0:T(2,128)S(1)} %fusion.204) | copy-start | bytes 3076
  12.5 73.7 %copy-start.35 = (f32[256]{0:T(256)}, f32[256]{0:T(256)S(1)}, u32[]{:S(2)}) copy-start(f32[256]{0:T(256)S(1)} %bitcast_rsqrt_fusion) | copy-start | bytes 3076
  12.7 460.6 %copy-start.6 = (bf16[256,1024]{1,0:T(8,128)(2,1)}, bf16[256,1024]{1,0:T(8,128)(2,1)S(1)}, u32[]{:S(2)}) copy-start(bf16[256,1024]{1,0:T(8,128)(2,1)S(1)} %fusion.202) | copy-start | bytes 1572868
  88.2 28.5 %all-to-all-start.1 = ((bf16[2,128,2048]{1,0,2:T(2,128)(2,1)}), bf16[2,128,2048]{1,0,2:T(2,128)(2,1)S(1)}, u32[]{:S(2)}, u32[]{:S(2)}) async-start(bf16[2,128,2048]{1,0,2:T(2,128)(2,1)} %copy.390), calls=%async_computation.1 | async-start | bytes 2097152 | tf_op jit(solution)/shard_map/all_to_all | solution.py:149
  95.6 383.6 %all-gather.8.cloned.1.call-start = ((), (), s32[]{:S(2)}) async-start(), calls=%async_computation.12 | async-start | bytes 5242880 | tf_op jit(solution)/shard_map/all_gather | solution.py:136
  97.1 29.0 %copy-start.45 = (f32[64]{0:T(128)}, f32[64]{0:T(128)S(1)}, u32[]{:S(2)}) copy-start(f32[64]{0:T(128)S(1)} %get-tuple-element.1103) | copy-start | bytes 772
  97.1 29.0 %copy-start.47 = (f32[64]{0:T(128)}, f32[64]{0:T(128)S(1)}, u32[]{:S(2)}) copy-start(f32[64]{0:T(128)S(1)} %get-tuple-element.1104) | copy-start | bytes 772
  97.1 29.0 %copy-start.49 = (f32[64]{0:T(128)}, f32[64]{0:T(128)S(1)}, u32[]{:S(2)}) copy-start(f32[64]{0:T(128)S(1)} %get-tuple-element.1105) | copy-start | bytes 772
  97.1 29.0 %copy-start.51 = (f32[64]{0:T(128)}, f32[64]{0:T(128)S(1)}, u32[]{:S(2)}) copy-start(f32[64]{0:T(128)S(1)} %get-tuple-element.1106) | copy-start | bytes 772
  97.2 155.3 %copy-start.37 = (f32[1,256]{1,0:T(1,128)}, f32[1,256]{1,0:T(1,128)S(1)}, u32[]{:S(2)}) copy-start(f32[1,256]{1,0:T(1,128)S(1)} %get-tuple-element.1099) | copy-start | bytes 3076
  97.2 155.3 %copy-start.39 = (f32[1,256]{1,0:T(1,128)}, f32[1,256]{1,0:T(1,128)S(1)}, u32[]{:S(2)}) copy-start(f32[1,256]{1,0:T(1,128)S(1)} %get-tuple-element.1100) | copy-start | bytes 3076
  97.2 155.3 %copy-start.41 = (f32[1,256]{1,0:T(1,128)}, f32[1,256]{1,0:T(1,128)S(1)}, u32[]{:S(2)}) copy-start(f32[1,256]{1,0:T(1,128)S(1)} %get-tuple-element.1101) | copy-start | bytes 3076
  97.2 155.3 %copy-start.43 = (f32[1,256]{1,0:T(1,128)}, f32[1,256]{1,0:T(1,128)S(1)}, u32[]{:S(2)}) copy-start(f32[1,256]{1,0:T(1,128)S(1)} %get-tuple-element.1102) | copy-start | bytes 3076
  117.7 145.7 %all-to-all-start = ((bf16[2,128,32]{1,0,2:T(2,128)(2,1)}), bf16[2,128,32]{1,0,2:T(2,128)(2,1)}, u32[]{:S(2)}, u32[]{:S(2)}) async-start(bf16[2,128,32]{1,0,2:T(2,128)(2,1)} %reshape.1843), calls=%async_computation | async-start | bytes 32768 | tf_op jit(solution)/shard_map/all_to_all | solution.py:150
  130.2 122.3 %copy-start.55 = (f32[256]{0:T(256)S(1)}, f32[256]{0:T(256)}, u32[]{:S(2)}) copy-start(f32[256]{0:T(256)} %param.29) | copy-start | bytes 3076
  422.0 11.9 copy-start.4
  490.5 18.3 all-to-all-start.3
  495.2 1020.5 %reduce-scatter.4.cloned.1.call-start = ((), (), s32[]{:S(2)}) async-start(), calls=%async_computation.13 | async-start | bytes 4325376 | tf_op jit(solution)/shard_map/reduce_scatter | solution.py:283
  529.4 9.7 copy-start.14
  529.4 9.7 copy-start.16
  578.2 9.7 copy-start.14
  578.2 9.7 copy-start.16
  627.0 9.7 copy-start.14
  627.0 9.7 copy-start.16
  675.8 9.7 copy-start.14
  675.8 9.7 copy-start.16
  724.6 9.7 copy-start.14
  724.6 9.7 copy-start.16
  773.3 9.7 copy-start.14
  773.3 9.7 copy-start.16
  822.2 9.7 copy-start.14
  822.2 9.7 copy-start.16
  871.1 9.7 copy-start.14
  871.1 9.7 copy-start.16
  919.9 9.7 copy-start.14
  919.9 9.7 copy-start.16
  968.7 9.7 copy-start.14
  968.8 9.7 copy-start.16
  1017.6 9.7 copy-start.14
  1017.6 9.7 copy-start.16
  1066.3 9.7 copy-start.14
  1066.3 9.7 copy-start.16
  1115.2 9.7 copy-start.14
  1115.2 9.7 copy-start.16
  1164.1 9.7 copy-start.14
  1164.1 9.7 copy-start.16
  1212.8 9.7 copy-start.14
  1261.6 9.7 copy-start.14
  1261.6 9.7 copy-start.16
  1304.7 16.9 copy-start.38
  1304.7 16.9 copy-start.40
  1304.7 16.9 copy-start.42
  1304.7 16.9 copy-start.44
  1379.8 31.7 %all-to-all-start.5 = ((bf16[32,2,128]{2,1,0:T(2,128)(2,1)}), bf16[32,2,128]{2,1,0:T(2,128)(2,1)S(1)}, u32[]{:S(2)}, u32[]{:S(2)}) async-start(bf16[32,2,128]{2,1,0:T(2,128)(2,1)} %reshape.1910), calls=%async_computation.6 | async-start | bytes 32768 | tf_op jit(solution)/shard_map/all_to_all | solution.py:279
  1405.7 14.4 copy-start.34
  1405.7 14.4 copy-start.31
  1411.5 24.7 %all-to-all-start.4 = ((bf16[32,2,8192]{2,1,0:T(2,128)(2,1)}), bf16[32,2,8192]{2,1,0:T(2,128)(2,1)}, u32[]{:S(2)}, u32[]{:S(2)}) async-start(bf16[32,2,8192]{2,1,0:T(2,128)(2,1)} %reshape.1912), calls=%async_computation.4 | async-start | bytes 2097152 | tf_op jit(solution)/shard_map/all_to_all | solution.py:276
  1420.0 188.0 %reduce-scatter.6.cloned.1.call-start = ((), (), s32[]{:S(2)}) async-start(), calls=%async_computation.14 | async-start | bytes 11468800 | tf_op jit(solution)/shard_map/reduce_scatter | solution.py:49
  1526.0 135.4 %reduce-scatter.8.cloned.1.call-start = ((), (), s32[]{:S(2)}) async-start(), calls=%async_computation.15 | async-start | bytes 5242880 | tf_op jit(solution)/shard_map/reduce_scatter | solution.py:343
  1530.4 454.1 %all-reduce.24.cloned.1.call-start = ((), (), s32[]{:S(2)}) async-start(), calls=%async_computation.16 | async-start | bytes 6553600 | tf_op jit(solution)/shard_map/psum | solution.py:358
  1675.7 12.8 slice-start
  1676.5 9.9 all-to-all-start.6
  (157 other events, 549.2 us)
Sparse Core Ops, SparseCore 0:
  11.4 69.2 all-gather.3
  82.9 166.5 all-gather.5
  251.3 35.4 all-gather.7
  1347.2 168.4 reduce-scatter.3
  1526.1 81.8 reduce-scatter.5
  1610.5 50.7 reduce-scatter.7
  1664.9 319.5 all-reduce.23
where the time goes:
time: 2020 us; the launch traced here: 2000 us
  waiting for transfers between devices  550 us (27%)
  other arithmetic  472 us (23%)
  matrix products  445 us (22%)
  local copies, waits for them, and re-layouts  269 us (13%)
  blocking collectives  178 us (9%)
  starting transfers between devices  35.4 us (2%)
  loops' own time  34.5 us (2%)
    psum x1, blocking collectives, shards(): lax.psum(shard_rows[3].astype(jnp.bfloat16), 'seq').astype(jnp.float32)  158 us
    dot_general x64, matrix products, group_step(): intersection = jnp.dot(c_block, b_block.T, precision=highest)  137 us
    psum x1, waiting for transfers between devices, shards(): lax.psum(shard_rows[0].astype(jnp.bfloat16), 'seq').astype(jnp.float32)  135 us
    another operation x306, local copies, waits for them, and re-layouts  120 us
    all_gather x1, waiting for transfers between devices, shards(): bc_whole = lax.all_gather(bc_raw, 'seq', axis=1, tiled=True)  119 us
    another operation x115, other arithmetic  116 us
    dot_general x48, matrix products, group_step(): output = jnp.einsum('ijh,jhp->ihp', mixing, inputs, precision=highest)  92 us
    dot_general x64, matrix products, group_step(): carried = jnp.einsum('in,hpn->ihp', c_block, carry_state, precision=highest)  89.8 us
  transfers between devices with their start and end apart: 13, of which 10 were waited for; matrix products, arithmetic and copies ran while one was open for 17% of the time, Pallas kernels for 0%

commit v1 on v0

v1 whole, which is shorter than its diff:
```python
import functools

import jax
import jax.numpy as jnp
from jax import lax
from jax.experimental import pallas as pl
from jax.experimental.pallas import tpu as pltpu
from jax.sharding import PartitionSpec as P

F32 = jnp.float32
BF16 = jnp.bfloat16
EPS = 1e-05
HIGHEST = lax.Precision.HIGHEST
HEADS = 32
HEAD = 64
STATE = 128
TOK = 128
SEQS = 2
ROWS = SEQS * TOK
HALO = 8
ALL = ROWS + SEQS * HALO
PAIRS = HEADS // 2
INNER = HEADS * HEAD
TAPS = 4


def mm(a, b, dims, precision=None):
    return lax.dot_general(a, b, ((dims[0], dims[1]), ((), ())), precision=precision, preferred_element_type=F32)


NN = ((1,), (0,))
NT = ((1,), (1,))
TN = ((0,), (0,))


def iota(shape, dim):
    return lax.broadcasted_iota(jnp.int32, shape, dim)


def pair_matrix(pair):
    upper = (iota((HEADS, 128), 1) >= HEAD).astype(jnp.int32)
    return (iota((HEADS, 128), 0) == 2 * pair + upper).astype(F32)


def pair_rows(pair):
    return (iota((8, HEADS), 1) == 2 * pair + iota((8, HEADS), 0)).astype(F32)


def causal_mask():
    return iota((TOK, TOK), 0) >= iota((TOK, TOK), 1)


def shifted(padded, k):
    back = TAPS - 1 - k
    if back:
        padded = pltpu.roll(padded, back, 0)
    return padded[HALO:, :]


def padded_of(rows, b):
    return jnp.concatenate(
        [rows[ROWS + HALO * b : ROWS + HALO * (b + 1), :], rows[TOK * b : TOK * (b + 1), :]], axis=0
    )


def conv_pre(padded, taps, bias):
    total = bias
    for k in range(TAPS):
        total = total + taps[k : k + 1, :] * shifted(padded, k)
    return total


def conv_back(padded, taps, bias, grad):
    pre = conv_pre(padded, taps, bias)
    sig = jax.nn.sigmoid(pre)
    d_pre = grad * (sig * (1.0 + pre * (1.0 - sig)))
    low = jnp.concatenate([jnp.zeros((HALO, d_pre.shape[1]), F32), d_pre], axis=0)
    d_pad = taps[TAPS - 1 : TAPS, :] * low
    for k in range(TAPS - 1):
        d_pad = d_pad + taps[k : k + 1, :] * pltpu.roll(low, HALO + TOK - (TAPS - 1 - k), 0)
    d_taps = [jnp.sum(d_pre * shifted(padded, k), axis=0, keepdims=True) for k in range(TAPS)]
    return d_pad, d_taps, jnp.sum(d_pre, axis=0, keepdims=True)


def block_diagonal(pair_values):
    first = iota(pair_values.shape, 1) < HEAD
    zero = jnp.zeros_like(pair_values)
    return jnp.concatenate(
        [jnp.where(first, pair_values, zero), jnp.where(first, zero, pair_values)], axis=0
    )


def decay_pair(r_lanes, r_rows):
    mask = causal_mask()
    out = []
    for q in range(2):
        spread = r_lanes[:, HEAD * q : HEAD * q + 1] - r_rows[q : q + 1, :]
        out.append(jnp.exp(jnp.where(mask, spread, -1e30)))
    return out


def front_kernel(x_raw, bc_raw, dt_raw, taps_x, bias_x, taps_bc, bias_bc, dt_bias, a_log, xc, bcc, dt, r, u):
    pair = pl.program_id(0)

    @pl.when(pair == 0)
    def _():
        raw = bc_raw[...].astype(F32)
        steps = dt_raw[0:ROWS, :].astype(F32) + dt_bias[...]
        dt[...] = jax.nn.softplus(steps)
        tri = causal_mask().astype(F32)
        decay = dt[...] * (-jnp.exp(a_log[...]))
        for b in range(SEQS):
            pre = conv_pre(padded_of(raw, b), taps_bc[...], bias_bc[...])
            bcc[TOK * b : TOK * (b + 1), :] = (pre * jax.nn.sigmoid(pre)).astype(BF16)
            r[TOK * b : TOK * (b + 1), :] = mm(tri, decay[TOK * b : TOK * (b + 1), :], NN, HIGHEST)

    raw = x_raw[...].astype(F32)
    ex = pair_matrix(pair)
    for b in range(SEQS):
        span = slice(TOK * b, TOK * (b + 1))
        pre = conv_pre(padded_of(raw, b), taps_x[...], bias_x[...])
        low = (pre * jax.nn.sigmoid(pre)).astype(BF16)
        xc[span, :] = low
        r_lanes = mm(r[span, :], ex, NN, HIGHEST)
        dt_lanes = mm(dt[span, :], ex, NN, HIGHEST)
        to_end = jnp.exp(r_lanes[TOK - 1 : TOK, :] - r_lanes)
        scaled = (to_end * (dt_lanes * low.astype(F32))).astype(BF16)
        state = mm(scaled, bcc[span, 0:STATE], TN).astype(BF16)
        u[0, b] = state[0:HEAD, :]
        u[1, b] = state[HEAD:, :]


def whole(shape):
    return pl.BlockSpec(shape, lambda *_: (0,) * len(shape))


def lanes(rows):
    return pl.BlockSpec((rows, 128), lambda j: (0, j))


STATES = pl.BlockSpec((2, SEQS, HEAD, STATE), lambda j: (j, 0, 0, 0))
STATES_SHAPE = (HEADS, SEQS, HEAD, STATE)
VMEM_LIMIT = 48 * 1024 * 1024


def call(kernel, outs, out_specs, in_specs, grid=(PAIRS,), scratch=(), cost=None):
    return pl.pallas_call(
        kernel,
        grid=grid,
        out_shape=[jax.ShapeDtypeStruct(s, d) for s, d in outs],
        in_specs=in_specs,
        out_specs=out_specs,
        scratch_shapes=scratch,
        compiler_params=pltpu.CompilerParams(
            vmem_limit_bytes=VMEM_LIMIT, dimension_semantics=("arbitrary",) * len(grid)
        ),
        cost_estimate=cost or pl.CostEstimate(flops=int(1e9), bytes_accessed=int(1e7), transcendentals=0),
    )


def front(x_raw, bc_raw, dt_raw, taps_x, bias_x, taps_bc, bias_bc, dt_bias, a_log):
    return call(
        front_kernel,
        [((ROWS, INNER), BF16), ((ROWS, 2 * STATE), BF16), ((ROWS, HEADS), F32), ((ROWS, HEADS), F32), (STATES_SHAPE, BF16)],
        [lanes(ROWS), whole((ROWS, 2 * STATE)), whole((ROWS, HEADS)), whole((ROWS, HEADS)), STATES],
        [
            lanes(ALL), whole((ALL, 2 * STATE)), whole((ALL, HEADS)), lanes(TAPS), lanes(1),
            whole((TAPS, 2 * STATE)), whole((1, 2 * STATE)), whole((1, HEADS)), whole((1, HEADS)),
        ],
    )(x_raw, bc_raw, dt_raw, taps_x, bias_x, taps_bc, bias_bc, dt_bias, a_log)


def states_kernel(reverse, decay, own, before):
    chunks = own.shape[0]

    def step(i, carry):
        c = chunks - 1 - i if reverse else i
        after = []
        for b in range(SEQS):
            before[c, b] = carry[b].astype(BF16)
            after.append(decay[c, b] * carry[b] + own[c, b].astype(F32))
        return tuple(after)

    lax.fori_loop(0, chunks, step, tuple(jnp.zeros((HEAD, STATE), F32) for _ in range(SEQS)))


def states(decay, own, reverse):
    return pl.pallas_call(
        functools.partial(states_kernel, reverse),
        out_shape=jax.ShapeDtypeStruct(own.shape, BF16),
        in_specs=[pl.BlockSpec(memory_space=pltpu.SMEM), pl.BlockSpec(memory_space=pltpu.VMEM)],
        out_specs=pl.BlockSpec(memory_space=pltpu.VMEM),
        compiler_params=pltpu.CompilerParams(vmem_limit_bytes=VMEM_LIMIT),
        cost_estimate=pl.CostEstimate(flops=int(1e6), bytes_accessed=int(2e6), transcendentals=0),
    )(decay, own)


def inside_kernel(xc, bcc, dt, r, y, scores):
    pair = pl.program_id(0)

    @pl.when(pair == 0)
    def _():
        for b in range(SEQS):
            span = slice(TOK * b, TOK * (b + 1))
            scores[b] = mm(bcc[span, STATE:], bcc[span, 0:STATE], NT)

    ex = pair_matrix(pair)
    rows = pair_rows(pair)
    for b in range(SEQS):
        span = slice(TOK * b, TOK * (b + 1))
        r_lanes = mm(r[span, :], ex, NN, HIGHEST)
        dt_lanes = mm(dt[span, :], ex, NN, HIGHEST)
        r_rows = mm(rows, r[span, :], NT, HIGHEST)
        first, second = decay_pair(r_lanes, r_rows)
        both = jnp.concatenate([scores[b] * first, scores[b] * second], axis=1).astype(BF16)
        stepped = (dt_lanes * xc[span, :].astype(F32)).astype(BF16)
        y[span, :] = mm(both, block_diagonal(stepped), NN)


def inside(xc, bcc, dt, r):
    return call(
        inside_kernel,
        [((ROWS, INNER), F32)],
        [lanes(ROWS)],
        [lanes(ROWS), whole((ROWS, 2 * STATE)), whole((ROWS, HEADS)), whole((ROWS, HEADS))],
        scratch=[pltpu.VMEM((SEQS, TOK, TOK), F32)],
    )(xc, bcc, dt, r)[0]


def middle_kernel(
    y_in, xc, bcc, r, start, d_skip, gate, d_mixed, gain,
    mixed, d_y, d_gate, own, d_gain, row_dot,
    y_all, square, cross, scale, slope,
):
    phase = pl.program_id(0)
    pair = pl.program_id(1)
    ex = pair_matrix(pair)
    skip = mm(jnp.broadcast_to(d_skip[...], (8, HEADS)), ex, NN, HIGHEST)[0:1, :]
    z = gate[...]
    sig = jax.nn.sigmoid(z)
    pulled = d_mixed[...] * gain[...]

    @pl.when(phase == 0)
    def _():
        @pl.when(pair == 0)
        def _():
            square[...] = jnp.zeros_like(square)
            cross[...] = jnp.zeros_like(cross)

        for b in range(SEQS):
            span = slice(TOK * b, TOK * (b + 1))
            before = jnp.concatenate([start[0, b], start[1, b]], axis=0)
            grown = jnp.exp(mm(r[span, :], ex, NN, HIGHEST))
            y_all[pair, span, :] = y_in[span, :] + grown * mm(bcc[span, STATE:], before, NT)
        y = (y_all[pair] + skip * xc[...].astype(F32)).astype(BF16).astype(F32)
        gated = y * (z * sig)
        square[...] += gated * gated
        cross[...] += pulled * gated

    @pl.when(phase == 1)
    def _():
        @pl.when(pair == 0)
        def _():
            inv = lax.rsqrt(jnp.sum(square[...], axis=1, keepdims=True) * (1.0 / INNER) + EPS)
            mean = jnp.sum(cross[...], axis=1, keepdims=True) * (1.0 / INNER)
            scale[...] = jnp.broadcast_to(inv, scale.shape)
            slope[...] = jnp.broadcast_to(inv * inv * inv * mean, slope.shape)
            row_dot[...] = jnp.zeros_like(row_dot)

        y = (y_all[pair] + skip * xc[...].astype(F32)).astype(BF16).astype(F32)
        silu = z * sig
        gated = y * silu
        unit = gated * scale[...]
        mixed[...] = (unit * gain[...]).astype(BF16)
        d_gain[...] = jnp.sum(d_mixed[...] * unit, axis=0, keepdims=True)
        d_gated = scale[...] * pulled - gated * slope[...]
        low = (d_gated * silu).astype(BF16)
        d_y[...] = low
        d_gate[...] = (d_gated * y * (sig * (1.0 + z * (1.0 - sig)))).astype(BF16)
        row_dot[...] += mm(low.astype(F32) * y_all[pair], ex, NT, HIGHEST)
        for b in range(SEQS):
            span = slice(TOK * b, TOK * (b + 1))
            grown = jnp.exp(mm(r[span, :], ex, NN, HIGHEST))
            state = mm((grown * low[span, :].astype(F32)).astype(BF16), bcc[span, STATE:], TN).astype(BF16)
            own[0, b] = state[0:HEAD, :]
            own[1, b] = state[HEAD:, :]


def middle(y_in, xc, bcc, r, start, d_skip, gate, d_mixed, gain):
    def cols(rows):
        return pl.BlockSpec((rows, 128), lambda p, j: (0, j))

    def first(rows):
        return pl.BlockSpec((rows, 128), lambda p, j: (0, jnp.where(p == 0, j, PAIRS - 1)))

    def second(rows):
        return pl.BlockSpec((rows, 128), lambda p, j: (0, jnp.where(p == 1, j, 0)))

    states_in = pl.BlockSpec((2, SEQS, HEAD, STATE), lambda p, j: (jnp.where(p == 0, j, PAIRS - 1), 0, 0, 0))
    states_out = pl.BlockSpec((2, SEQS, HEAD, STATE), lambda p, j: (jnp.where(p == 1, j, 0), 0, 0, 0))
    return call(
        middle_kernel,
        [((ROWS, INNER), BF16), ((ROWS, INNER), BF16), ((ROWS, INNER), BF16), (STATES_SHAPE, BF16), ((1, INNER), F32), ((ROWS, HEADS), F32)],
        [second(ROWS), second(ROWS), second(ROWS), states_out, second(1), whole((ROWS, HEADS))],
        [first(ROWS), cols(ROWS), whole((ROWS, 2 * STATE)), whole((ROWS, HEADS)), states_in, whole((1, HEADS)), cols(ROWS), cols(ROWS), cols(1)],
        grid=(2, PAIRS),
        scratch=[pltpu.VMEM((PAIRS, ROWS, 128), F32)] + [pltpu.VMEM((ROWS, 128), F32)] * 4,
    )(y_in, xc, bcc, r, start, d_skip, gate, d_mixed, gain)


def inside_back_kernel(xc, d_y, bcc, dt, r, d_stepped, d_bc, scores, d_scores):
    pair = pl.program_id(0)

    @pl.when(pair == 0)
    def _():
        d_scores[...] = jnp.zeros_like(d_scores)
        for b in range(SEQS):
            span = slice(TOK * b, TOK * (b + 1))
            scores[b] = mm(bcc[span, STATE:], bcc[span, 0:STATE], NT)

    ex = pair_matrix(pair)
    rows = pair_rows(pair)
    for b in range(SEQS):
        span = slice(TOK * b, TOK * (b + 1))
        r_lanes = mm(r[span, :], ex, NN, HIGHEST)
        dt_lanes = mm(dt[span, :], ex, NN, HIGHEST)
        r_rows = mm(rows, r[span, :], NT, HIGHEST)
        first, second = decay_pair(r_lanes, r_rows)
        both = jnp.concatenate([scores[b] * first, scores[b] * second], axis=0).astype(BF16)
        stepped = (dt_lanes * xc[span, :].astype(F32)).astype(BF16)
        wide = block_diagonal(d_y[span, :])
        d_stepped[span, :] = mm(both, wide, TN)
        d_both = mm(wide, stepped, NT)
        d_scores[b] += d_both[0:TOK, :] * first + d_both[TOK:, :] * second

    @pl.when(pair == PAIRS - 1)
    def _():
        for b in range(SEQS):
            span = slice(TOK * b, TOK * (b + 1))
            low = d_scores[b].astype(BF16)
            d_bc[span, 0:STATE] = mm(low, bcc[span, STATE:], TN)
            d_bc[span, STATE:] = mm(low, bcc[span, 0:STATE], NN)


def inside_back(xc, d_y, bcc, dt, r):
    return call(
        inside_back_kernel,
        [((ROWS, INNER), F32), ((ROWS, 2 * STATE), F32)],
        [lanes(ROWS), whole((ROWS, 2 * STATE))],
        [lanes(ROWS), lanes(ROWS), whole((ROWS, 2 * STATE)), whole((ROWS, HEADS)), whole((ROWS, HEADS))],
        scratch=[pltpu.VMEM((SEQS, TOK, TOK), F32)] * 2,
    )(xc, d_y, bcc, dt, r)


def back_kernel(
    d_stepped, xc, d_y, x_raw, start, end, bcc, dt, r, bc_raw, dt_raw, d_bc_in, row_dot,
    taps_x, bias_x, taps_bc, bias_bc, dt_bias, a_log, d_skip,
    d_x_raw, d_bc_raw, d_dt_raw, g_x, g_bc, g_heads,
    d_bc, d_dt, col_dot, ends, skips,
):
    pair = pl.program_id(0)

    @pl.when(pair == 0)
    def _():
        d_bc[...] = d_bc_in[...]
        d_dt[...] = jnp.zeros_like(d_dt)
        col_dot[...] = jnp.zeros_like(col_dot)
        ends[...] = jnp.zeros_like(ends)
        skips[...] = jnp.zeros_like(skips)

    ex = pair_matrix(pair)
    skip = mm(jnp.broadcast_to(d_skip[...], (8, HEADS)), ex, NN, HIGHEST)[0:1, :]
    raw = x_raw[...].astype(F32)
    ones = jnp.ones((8, STATE), F32)
    halos, grads = [], None
    skip_sum = jnp.zeros((1, 128), F32)
    for b in range(SEQS):
        span = slice(TOK * b, TOK * (b + 1))
        r_lanes = mm(r[span, :], ex, NN, HIGHEST)
        dt_lanes = mm(dt[span, :], ex, NN, HIGHEST)
        last = r_lanes[TOK - 1 : TOK, :]
        grown = jnp.exp(r_lanes)
        to_end = jnp.exp(last - r_lanes)
        before = jnp.concatenate([start[0, b], start[1, b]], axis=0)
        after = jnp.concatenate([end[0, b], end[1, b]], axis=0)
        x = xc[span, :].astype(F32)
        dy = d_y[span, :].astype(F32)
        stepped = (dt_lanes * x).astype(BF16).astype(F32)
        carried = to_end * mm(bcc[span, 0:STATE], after, NT)
        d_step = d_stepped[span, :] + carried
        col_dot[span, :] += mm(stepped * d_step, ex, NT, HIGHEST)
        d_x = dt_lanes * d_step + skip * dy
        d_dt[span, :] += mm(x * d_step, ex, NT, HIGHEST)
        inner = mm(ones, before.astype(F32) * after.astype(F32), NT, HIGHEST)[0:1, :]
        end_row = jnp.sum(stepped * carried, axis=0, keepdims=True) + jnp.exp(last) * inner
        ends[b] += mm(jnp.broadcast_to(end_row, (8, 128)), ex, NT, HIGHEST)
        d_bc[span, STATE:] += mm((grown * dy).astype(BF16), before, NN)
        d_bc[span, 0:STATE] += mm((to_end * stepped).astype(BF16), after, NN)
        skip_sum = skip_sum + jnp.sum(dy * x, axis=0, keepdims=True)
        d_pad, d_taps, d_bias = conv_back(padded_of(raw, b), taps_x[...], bias_x[...], d_x)
        d_x_raw[span, :] = d_pad[HALO:, :].astype(BF16)
        halos.append(d_pad[0:HALO, :])
        parts = [*d_taps, d_bias]
        grads = parts if grads is None else [g + p for g, p in zip(grads, parts)]
    d_x_raw[ROWS:, :] = jnp.concatenate(halos, axis=0).astype(BF16)
    g_x[...] = jnp.concatenate([*grads, jnp.zeros((8 - TAPS - 1, 128), F32)], axis=0)
    skips[...] += mm(jnp.broadcast_to(skip_sum, (8, 128)), ex, NT, HIGHEST)

    @pl.when(pair == PAIRS - 1)
    def _():
        raw = bc_raw[...].astype(F32)
        halos, grads = [], None
        for b in range(SEQS):
            span = slice(TOK * b, TOK * (b + 1))
            d_pad, d_taps, d_bias = conv_back(padded_of(raw, b), taps_bc[...], bias_bc[...], d_bc[span, :])
            d_bc_raw[span, :] = d_pad[HALO:, :].astype(BF16)
            halos.append(d_pad[0:HALO, :])
            parts = [*d_taps, d_bias]
            grads = parts if grads is None else [g + p for g, p in zip(grads, parts)]
        d_bc_raw[ROWS:, :] = jnp.concatenate(halos, axis=0).astype(BF16)
        g_bc[...] = jnp.concatenate([*grads, jnp.zeros((8 - TAPS - 1, 2 * STATE), F32)], axis=0)
        rate = -jnp.exp(a_log[...])
        tri = causal_mask().astype(F32)
        is_last = iota((TOK, HEADS), 0) == TOK - 1
        bias_sum = jnp.zeros((1, HEADS), F32)
        log_sum = jnp.zeros((1, HEADS), F32)
        for b in range(SEQS):
            span = slice(TOK * b, TOK * (b + 1))
            step = dt[span, :]
            d_r = row_dot[span, :] - col_dot[span, :] + jnp.where(is_last, ends[b][0:1, :], 0.0)
            d_log = mm(tri, d_r, TN, HIGHEST)
            d_pre = (d_dt[span, :] + rate * d_log) * jax.nn.sigmoid(dt_raw[span, :].astype(F32) + dt_bias[...])
            d_dt_raw[span, :] = d_pre.astype(BF16)
            bias_sum = bias_sum + jnp.sum(d_pre, axis=0, keepdims=True)
            log_sum = log_sum + jnp.sum(d_log * step, axis=0, keepdims=True) * rate
        d_dt_raw[ROWS:, :] = jnp.zeros((ALL - ROWS, HEADS), BF16)
        g_heads[...] = jnp.concatenate([bias_sum, log_sum, skips[0:1, :], jnp.zeros((5, HEADS), F32)], axis=0)


def back(d_stepped, xc, d_y, x_raw, start, end, bcc, dt, r, bc_raw, dt_raw, d_bc_in, row_dot, taps_x, bias_x, taps_bc, bias_bc, dt_bias, a_log, d_skip):
    return call(
        back_kernel,
        [((ALL, INNER), BF16), ((ALL, 2 * STATE), BF16), ((ALL, HEADS), BF16), ((8, INNER), F32), ((8, 2 * STATE), F32), ((8, HEADS), F32)],
        [lanes(ALL), whole((ALL, 2 * STATE)), whole((ALL, HEADS)), lanes(8), whole((8, 2 * STATE)), whole((8, HEADS))],
        [
            lanes(ROWS), lanes(ROWS), lanes(ROWS), lanes(ALL), STATES, STATES,
            whole((ROWS, 2 * STATE)), whole((ROWS, HEADS)), whole((ROWS, HEADS)), whole((ALL, 2 * STATE)),
            whole((ALL, HEADS)), whole((ROWS, 2 * STATE)), whole((ROWS, HEADS)),
            lanes(TAPS), lanes(1), whole((TAPS, 2 * STATE)), whole((1, 2 * STATE)),
            whole((1, HEADS)), whole((1, HEADS)), whole((1, HEADS)),
        ],
        scratch=[
            pltpu.VMEM((ROWS, 2 * STATE), F32), pltpu.VMEM((ROWS, HEADS), F32), pltpu.VMEM((ROWS, HEADS), F32),
            pltpu.VMEM((SEQS, 8, HEADS), F32), pltpu.VMEM((8, HEADS), F32),
        ],
    )(d_stepped, xc, d_y, x_raw, start, end, bcc, dt, r, bc_raw, dt_raw, d_bc_in, row_dot, taps_x, bias_x, taps_bc, bias_bc, dt_bias, a_log, d_skip)


def swap(values):
    return lax.all_to_all(values, "seq", split_axis=0, concat_axis=0, tiled=True)


def gather_rows(shard):
    return lax.all_gather(shard, "wshard", axis=0, tiled=True)


def reduce_rows(term):
    part = lax.psum_scatter(term.astype(BF16), "wshard", scatter_dimension=0, tiled=True)
    return lax.psum(part, "seq").astype(F32)


def shards(
    layer_in, gain_in, w_z, w_x, w_bc, w_dt, conv_x_weight, conv_x_bias, conv_bc_weight, conv_bc_bias,
    dt_bias, a_log, d_skip, gain_norm, w_out, cotangent,
):
    width = layer_in.shape[2]
    chunks = lax.axis_size("seq")
    place = lax.axis_index("seq")
    tail = lax.ppermute(layer_in[:, TOK - (TAPS - 1) :, :], "seq", [(i, i + 1) for i in range(chunks - 1)])
    full_x = gather_rows(w_x)
    full_small = gather_rows(jnp.concatenate([w_bc, w_dt], axis=1))
    full_bc, full_dt = full_small[:, : 2 * STATE], full_small[:, 2 * STATE :]
    full_z = gather_rows(w_z)
    full_out = gather_rows(w_out)
    own = jnp.concatenate([conv_x_weight.reshape(-1), conv_x_bias, dt_bias, a_log, d_skip, jnp.zeros((61,), F32)])
    params = lax.all_gather(own, "seq", axis=0, tiled=False)
    taps_x = params[:, : TAPS * HEAD].reshape(HEADS, TAPS, HEAD).swapaxes(0, 1).reshape(TAPS, INNER)
    bias_x = params[:, TAPS * HEAD : (TAPS + 1) * HEAD].reshape(1, INNER)
    bias_dt, log_a, skip = (params[:, (TAPS + 1) * HEAD + i].reshape(1, HEADS) for i in range(3))
    bias_bc = conv_bc_bias.reshape(1, -1)

    hidden = layer_in.astype(F32).reshape(ROWS, width)
    upstream = cotangent.reshape(ROWS, width)
    halo = jnp.pad(tail, ((0, 0), (HALO - (TAPS - 1), 0), (0, 0))).reshape(SEQS * HALO, width).astype(F32)
    tokens = jnp.concatenate([hidden, halo], axis=0)
    inv = lax.rsqrt(jnp.mean(tokens * tokens, axis=-1, keepdims=True) + EPS)
    normed = (tokens * inv * gain_in[None, :]).astype(BF16)
    inv = inv[:ROWS]

    x_raw = mm(normed, full_x, NN).astype(BF16)
    bc_raw = mm(normed, full_bc, NN).astype(BF16)
    dt_raw = mm(normed, full_dt, NN).astype(BF16)
    xc, bcc, dt, r, u = front(x_raw, bc_raw, dt_raw, taps_x, bias_x, conv_bc_weight, bias_bc, bias_dt, log_a)
    decay = jnp.exp(swap(r[TOK - 1 :: TOK].T))
    u_all = swap(u)
    y_in = inside(xc, bcc, dt, r)
    gate = mm(normed[:ROWS], full_z, NN)
    d_mixed = mm(upstream, full_out, NT)
    start = swap(states(decay, u_all, False))
    mixed, d_y, d_gate, v, g_norm, row_dot = middle(
        y_in, xc, bcc, r, start, skip, gate, d_mixed, gain_norm.reshape(1, INNER)
    )
    v_all = swap(v)
    layer_out = (hidden + mm(mixed, full_out, NN)).astype(BF16).reshape(SEQS, TOK, width)
    grad_w_out = reduce_rows(mm(mixed, upstream, TN))
    grad_w_z = reduce_rows(mm(normed[:ROWS], d_gate, TN))
    d_stepped, d_bc_in = inside_back(xc, d_y, bcc, dt, r)
    d_normed_z = mm(d_gate, full_z, NT)
    end = swap(states(decay, v_all, True))
    d_x_raw, d_bc_raw, d_dt_raw, g_x, g_bc, g_heads = back(
        d_stepped, xc, d_y, x_raw, start, end, bcc, dt, r, bc_raw, dt_raw, d_bc_in, row_dot,
        taps_x, bias_x, conv_bc_weight, bias_bc, bias_dt, log_a, skip,
    )
    grad_w_x = reduce_rows(mm(normed, d_x_raw, TN))
    grad_small = reduce_rows(jnp.concatenate([mm(normed, d_bc_raw, TN), mm(normed, d_dt_raw, TN)], axis=1))
    d_normed = mm(d_x_raw, full_x, NT) + mm(d_bc_raw, full_bc, NT) + mm(d_dt_raw, full_dt, NT)
    back_tail = d_normed[ROWS:].reshape(SEQS, HALO, width)[:, HALO - (TAPS - 1) :]
    back_tail = lax.ppermute(back_tail, "seq", [(i + 1, i) for i in range(chunks - 1)])
    d_normed = d_normed[:ROWS] + d_normed_z
    d_normed = d_normed + jnp.pad(back_tail, ((0, 0), (TOK - (TAPS - 1), 0), (0, 0))).reshape(ROWS, width)
    unit = hidden * inv
    g_in = jnp.sum(d_normed * unit, axis=0)
    pulled = d_normed * gain_in[None, :]
    d_hidden = inv * (pulled - unit * jnp.mean(pulled * unit, axis=-1, keepdims=True))
    input_grad = (upstream.astype(F32) + d_hidden).reshape(SEQS, TOK, width)

    pieces = (g_x[: TAPS + 1], g_bc[: TAPS + 1], g_heads[:3], g_in, g_norm)
    sizes = [p.size for p in pieces]
    total = lax.psum(jnp.concatenate([p.reshape(-1) for p in pieces]), ("seq", "wshard"))
    ends = [sum(sizes[: i + 1]) for i in range(len(sizes) - 1)]
    s_x, s_bc, s_heads, s_in, s_norm = jnp.split(total, ends)
    s_x = lax.dynamic_slice(s_x.reshape(TAPS + 1, INNER), (0, place * HEAD), (TAPS + 1, HEAD))
    s_bc = s_bc.reshape(TAPS + 1, 2 * STATE)
    s_heads = lax.dynamic_slice(s_heads.reshape(3, HEADS), (0, place), (3, 1))
    return (
        layer_out, input_grad, s_in, grad_w_z, grad_w_x, grad_small[:, : 2 * STATE], grad_small[:, 2 * STATE :],
        s_x[:TAPS], s_x[TAPS], s_bc[:TAPS], s_bc[TAPS], s_heads[0], s_heads[1], s_heads[2], s_norm, grad_w_out,
    )


def solution(mesh):
    rows, heads = P("wshard", None), P("seq")
    tokens = P("wshard", "seq", None)
    return jax.shard_map(
        shards,
        mesh=mesh,
        in_specs=(
            tokens, P(), rows, rows, rows, rows, P(None, "seq"), heads, P(), P(), heads, heads, heads, P(), rows, tokens,
        ),
        out_specs=(
            tokens, tokens, P(), rows, rows, rows, rows, P(None, "seq"), heads, P(), P(), heads, heads, heads, P(), rows,
        ),
        check_vma=False,
    )
```

time: 2020 us -> 852 us (0.42)
  other arithmetic: 472 us -> 9.97 us
  matrix products: 445 us -> 41.8 us
  local copies, waits for them, and re-layouts: 269 us -> 31.4 us
  waiting for transfers between devices: 550 us -> 424 us
  Pallas kernels: 0 us -> 113 us
  loops' own time: 34.5 us -> 0 us
    dot_general x239 -> x15, matrix products: 445 us -> 41.8 us  [mm(): lax.dot_general(a, b, ((dims[0], dims[1]), ((), ())), precision=precision...]
    all_gather x3, waiting for transfers between devices: 187 us -> 0.02 us  [gather_rows(): return lax.all_gather(shard, 'wshard', axis=0, tiled=True)]
    another operation x306 -> x0, local copies, waits for them, and re-layouts: 120 us -> none
    another operation x115 -> x0, other arithmetic: 116 us -> none
    reduce_sum x68 -> x1, other arithmetic: 114 us -> 0.17 us  [shards(): inv = lax.rsqrt(jnp.mean(tokens * tokens, axis=-1, keepdims=True) + EPS)]
    pallas_call x0 -> x7, Pallas kernels: none -> 113 us  [the longest x1 33.1 us: back(): call(back_kernel, [((ALL, INNER), BF16), ((ALL, 2 * STATE), BF16), ((ALL,...]
    psum x1, waiting for transfers between devices: 135 us -> 230 us  [reduce_rows(): return lax.psum(part, 'seq').astype(F32)]
    all_gather x0 -> x2, blocking collectives: none -> 91.6 us  [the longest x1 81.5 us: shards(): params = lax.all_gather(own, 'seq', axis=0, tiled=False)]
  transfers between devices with their start and end apart: 13 -> 13, of which waited for: 10 -> 7; matrix products, arithmetic and copies ran while one was open for 17% -> 6% of each run, Pallas kernels for 0% -> 6%
where the time goes in v1:
time: 852 us; the launch traced here: 850 us
  waiting for transfers between devices  424 us (50%)
  blocking collectives  195 us (23%)
  Pallas kernels  113 us (13%)
  matrix products  41.8 us (5%)
  local copies, waits for them, and re-layouts  31.4 us (4%)
  starting transfers between devices  17.5 us (2%)
  between operations  16.8 us (2%)
  other arithmetic  9.97 us (1%)
    psum x1, waiting for transfers between devices, reduce_rows(): return lax.psum(part, 'seq').astype(F32)  230 us
    reduce_scatter x4, waiting for transfers between devices, reduce_rows(): lax.psum_scatter(term.astype(BF16), 'wshard', scatter_dimension=0, tiled=...  173 us
    all_gather x1, blocking collectives, shards(): params = lax.all_gather(own, 'seq', axis=0, tiled=False)  81.5 us
    psum x1, blocking collectives, shards(): lax.psum(jnp.concatenate([p.reshape(-1) for p in pieces]), ('seq', 'wshar...  68.2 us
    dot_general x15, matrix products, mm(): lax.dot_general(a, b, ((dims[0], dims[1]), ((), ())), precision=precision...  41.8 us
    all_to_all x2, blocking collectives, swap(): lax.all_to_all(values, 'seq', split_axis=0, concat_axis=0, tiled=True)  35.3 us
    pallas_call x1, Pallas kernels, back(): call(back_kernel, [((ALL, INNER), BF16), ((ALL, 2 * STATE), BF16), ((ALL,...  33.1 us
    pallas_call x1, Pallas kernels, middle(): call(middle_kernel, [((ROWS, INNER), BF16), ((ROWS, INNER), BF16), ((ROWS...  29 us
  transfers between devices with their start and end apart: 13, of which 7 were waited for; matrix products, arithmetic and copies ran while one was open for 6% of the time, Pallas kernels for 6%

profile of v1, /device:TPU:0, one launch (start us, length us, event | category | flops | bytes accessed | tf_op | source)
XLA Modules:
  0.0 849.6 jit_solution(10186774362155490850)
XLA Ops:
  7.3 0.7 all-gather.6.cloned.1.call-update
  8.0 0.7 all-gather.8.cloned.1.call-update
  8.8 0.7 all-gather.10.cloned.1.call-update
  9.5 3.6 collective-permute-start
  15.2 81.5 %all-gather.1 = f32[32,1,384]{2,1,0:T(1,128)S(1)} all-gather(f32[1,1,384]{2,1,0:T(1,128)S(1)} %reshape.160), channel_id=2, replica_groups=mesh['seq'=32,'wshard'=4] {'seq'}, dimensions={0}, use_global_device_ids=true | all-gather | bytes 50688 | tf_op jit(solution)/shard_map/all_gather | solution.py:486
  96.9 10.1 %all_gather.19 = bf16[1024,288]{1,0:T(8,128)(2,1)S(1)} all-gather(bf16[256,288]{1,0:T(8,128)(2,1)S(1)} %pad_maximum_fusion.2), channel_id=1, replica_groups=mesh['seq'=32,'wshard'=4] {'wshard'}, dimensions={0}, use_global_device_ids=true | all-gather | bytes 737280 | tf_op jit(solution)/shard_map/all_gather | solution.py:464
  108.8 3.5 convolution_convert_fusion.3.x_raw
  112.5 13.6 %shard_map.279 = (bf16[256,2048]{1,0:T(8,128)(2,1)S(1)}, bf16[256,256]{1,0:T(8,128)(2,1)S(1)}, f32[256,32]{1,0:T(8,128)S(1)}, f32[256,32]{1,0:T(8,128)S(1)}, bf16[32,2,64,128]{3,2,1,0:T(8,128)(2,1)}) custom-call(bf16[272,2048]{1,0:T(8,128)(2,1)S(1)} %convolution_convert_fusion.3.x_raw, bf16[272,256]{1,0:T(8,128)(2,1)S(1)} %convolution_convert_fusion.5.bc_raw, ...), custom_call_target="tpu_custom_call" | custom-call | flops 1000000000 | bytes 10000000 | tf_op jit(solution)/shard_map/pallas_call | solution.py:162
  126.1 1.0 copy-done.6
  127.2 11.2 %all_to_all.29 = f32[32,1,2]{2,1,0:T(1,128)S(1)} all-to-all(f32[32,1,2]{2,1,0:T(1,128)S(1)} %copy.62), channel_id=1, replica_groups=mesh['seq'=32,'wshard'=4] {'seq'}, dimensions={0} | all-to-all | bytes 512 | tf_op jit(solution)/shard_map/all_to_all | solution.py:460
  138.4 3.9 all-to-all-start.1
  142.5 17.3 %all-to-all-done.1.own = bf16[32,2,64,128]{3,2,1,0:T(8,128)(2,1)S(1)} async-done(((bf16[32,2,64,128]{3,2,1,0:T(8,128)(2,1)}), bf16[32,2,64,128]{3,2,1,0:T(8,128)(2,1)S(1)}, u32[]{:S(2)}, u32[]{:S(2)}) %all-to-all-start.1) | async-done | bytes 1048608 | tf_op jit(solution)/shard_map/all_to_all | solution.py:460
  159.8 2.1 shard_map.281
  161.9 3.9 all-to-all-start.2
  165.8 14.6 %shard_map.280.y_in = f32[256,2048]{1,0:T(8,128)S(1)} custom-call(bf16[256,2048]{1,0:T(8,128)(2,1)S(1)} %get-tuple-element.35.xc, bf16[256,256]{1,0:T(8,128)(2,1)S(1)} %get-tuple-element.36.bcc, f32[256,32]{1,0:T(8,128)S(1)} %get-tuple-element.37.dt, f32[256,32]{1,0:T(8,128)S(1)} %get-tuple-element.38.r), custom_call_target="tpu_custom_call" | custom-call | flops 1000000000 | bytes 10000000 | tf_op jit(solution)/shard_map/pallas_call | solution.py:221
  180.4 1.3 copy-done.4
  181.8 4.8 fusion.3.gate
  186.5 5.0 fusion.12.d_mixed
  191.5 1.0 copy-done
  192.5 29.0 %shard_map.282 = (bf16[256,2048]{1,0:T(8,128)(2,1)S(1)}, bf16[256,2048]{1,0:T(8,128)(2,1)S(1)}, bf16[256,2048]{1,0:T(8,128)(2,1)S(1)}, bf16[32,2,64,128]{3,2,1,0...) custom-call(f32[256,2048]{1,0:T(8,128)} %copy-done.4, bf16[256,2048]{1,0:T(8,128)(2,1)S(1)} %get-tuple-element.35.xc, ...), custom_call_target="tpu_custom_call" | custom-call | flops 1000000000 | bytes 10000000 | tf_op jit(solution)/shard_map/pallas_call | solution.py:301
  221.5 1.0 copy-done.2
  223.7 24.1 %all_to_all.30.own = bf16[32,2,64,128]{3,2,1,0:T(8,128)(2,1)S(1)} all-to-all(bf16[32,2,64,128]{3,2,1,0:T(8,128)(2,1)S(1)} %get-tuple-element.43), channel_id=1, replica_groups=mesh['seq'=32,'wshard'=4] {'seq'}, dimensions={0} | all-to-all | bytes 2097152 | tf_op jit(solution)/shard_map/all_to_all | solution.py:460
  247.8 2.1 shard_map.284
  249.9 3.9 all-to-all-start.4
  254.1 1.3 copy-done.10
  255.4 18.4 %shard_map.283 = (f32[256,2048]{1,0:T(8,128)S(1)}, f32[256,256]{1,0:T(8,128)S(1)}) custom-call(bf16[256,2048]{1,0:T(8,128)(2,1)S(1)} %get-tuple-element.35.xc, bf16[256,2048]{1,0:T(8,128)(2,1)S(1)} %copy-done.10, bf16[256,256]{1,0:T(8,128)(2,1)S(1)} %get-tuple-element.36.bcc, f32[256,32]{1,0:T(8,128)S(1)} %get-tuple-element.37.dt, ...), custom_call_target="tpu_custom_call" | custom-call | flops 1000000000 | bytes 10000000 | tf_op jit(solution)/shard_map/pallas_call | solution.py:346
  273.8 1.3 copy-done.5
  275.1 0.7 copy-done.14
  275.8 1.2 copy-done.11
  277.0 0.9 copy-done.15
  278.0 0.9 copy-done.17
  278.9 0.9 copy-done.19
  279.8 0.9 copy-done.21
  280.7 0.8 copy-done.23
  281.5 0.9 copy-done.25
  283.0 0.7 copy-done.36
  285.0 0.7 copy-done.42
  285.7 33.1 %shard_map.285 = (bf16[272,2048]{1,0:T(8,128)(2,1)}, bf16[272,256]{1,0:T(8,128)(2,1)S(1)}, bf16[272,32]{1,0:T(8,128)(2,1)S(1)}, f32[8,2048]{1,0:T(8,128)S(1)}, f...) custom-call(f32[256,2048]{1,0:T(8,128)} %copy-done.5, bf16[256,2048]{1,0:T(8,128)(2,1)S(1)} %get-tuple-element.35.xc, ...), custom_call_target="tpu_custom_call" | custom-call | flops 1000000000 | bytes 10000000 | tf_op jit(solution)/shard_map/pallas_call | solution.py:441
  320.2 0.9 pad_maximum_fusion.1
  321.1 3.2 convolution_convert_fusion.2
  324.5 1.1 copy-done.3
  325.6 4.3 convolution_convert_fusion
  330.0 5.7 convolution_convert_fusion.1
  336.9 1.3 fusion.7
  338.2 12.1 %reduce-scatter.9.cloned.1.call-done = bf16[256,288]{0,1:T(8,128)(2,1)} async-done(((bf16[1024,288]{0,1:T(8,128)(2,1)}), bf16[256,288]{0,1:T(8,128)(2,1)}) %reduce-scatter.9.cloned.1.call-update) | async-done | bytes 147472 | tf_op jit(solution)/shard_map/reduce_scatter | solution.py:468
  350.3 53.3 %reduce-scatter.5.cloned.1.call-done = bf16[256,2048]{1,0:T(8,128)(2,1)} async-done(((bf16[1024,2048]{1,0:T(8,128)(2,1)}), bf16[256,2048]{1,0:T(8,128)(2,1)}) %reduce-scatter.5.cloned.1.call-update) | async-done | bytes 1048592 | tf_op jit(solution)/shard_map/reduce_scatter | solution.py:468
  403.7 53.5 %reduce-scatter.11.cloned.1.call-done = bf16[512,1024]{1,0:T(8,128)(2,1)} async-done(((bf16[2048,1024]{1,0:T(8,128)(2,1)}), bf16[512,1024]{1,0:T(8,128)(2,1)}) %reduce-scatter.11.cloned.1.call-update) | async-done | bytes 1048592 | tf_op jit(solution)/shard_map/reduce_scatter | solution.py:468
  457.2 53.5 %reduce-scatter.7.cloned.1.call-done = bf16[256,2048]{1,0:T(8,128)(2,1)} async-done(((bf16[1024,2048]{1,0:T(8,128)(2,1)}), bf16[256,2048]{1,0:T(8,128)(2,1)}) %reduce-scatter.7.cloned.1.call-update) | async-done | bytes 1048592 | tf_op jit(solution)/shard_map/reduce_scatter | solution.py:468
  510.8 4.0 fusion.13
  514.8 1.3 fusion
  516.2 0.8 slice_bitcast_fusion
  517.1 1.6 collective-permute-start.1
  518.7 2.1 fusion.1
  521.0 2.0 collective-permute-done.1
  523.1 5.2 multiply_reduce_fusion.1
  528.4 68.2 %psum.35 = f32[14688]{0:T(1024)S(1)} all-reduce(f32[14688]{0:T(1024)S(1)} %concatenate.19), channel_id=1, replica_groups=mesh['seq'=32,'wshard'=4] {'seq','wshard'}, use_global_device_ids=true, to_apply=%region_3.4 | all-reduce | flops 14688 | bytes 117504 | tf_op jit(solution)/shard_map/psum | solution.py:539
  600.9 2.7 multiply_add_fusion
  603.6 230.0 %all-reduce.5.cloned.1.call-done = (bf16[256,288]{0,1:T(8,128)(2,1)}, bf16[256,2048]{1,0:T(8,128)(2,1)}, bf16[256,2048]{1,0:T(8,128)(2,1)}, bf16[512,1024]{1,0:T(8,128)(2,1)}) async-done(((bf16[256,288]{0,1:T(8,128)(2,1)}, bf16[256,2048]{1,0:T(8,128)(2,1)}, bf16[256,2048]{1,0:T(8,128)(2,1)}, bf16[512,1024]{1,0:T(8,128)(2,1)}), (bf16[256,288]{0,1:T(8,128)(2,1)}, bf16[256,2048]{1,0:T(8,128)(2,1)}, ...) | async-done | bytes 3293200 | tf_op jit(solution)/shard_map/psum | solution.py:469
  833.7 1.3 slice.135
  835.0 1.0 slice.134
  836.0 0.8 copy.66
  836.9 2.8 convert_element_type.60
  839.7 1.6 convert_element_type.62
  841.2 1.6 convert_element_type.65
  (183 shorter events, 13.4 us)
Async XLA Ops:
  7.2 2.3 copy-start.51
  7.2 7.8 copy-start.62
  7.2 7.9 copy-start.63
  7.2 89.5 %copy-start.59 = (bf16[256,32]{0,1:T(8,128)(2,1)S(1)}, bf16[256,32]{0,1:T(8,128)(2,1)}, u32[]{:S(2)}) copy-start(bf16[256,32]{0,1:T(8,128)(2,1)} %param.21) | copy-start | bytes 49156
  7.2 89.6 %copy-start.56 = (bf16[256,256]{1,0:T(8,128)(2,1)S(1)}, bf16[256,256]{1,0:T(8,128)(2,1)}, u32[]{:S(2)}) copy-start(bf16[256,256]{1,0:T(8,128)(2,1)} %param.20) | copy-start | bytes 393220
  7.2 101.6 %all-gather.6.cloned.1.call-start = ((), (), s32[]{:S(2)}) async-start(), calls=%async_computation.9 | async-start | bytes 5242880 | tf_op jit(solution)/shard_map/all_gather | solution.py:464
  8.0 173.8 %all-gather.8.cloned.1.call-start = ((), (), s32[]{:S(2)}) async-start(), calls=%async_computation.10 | async-start | bytes 5242880 | tf_op jit(solution)/shard_map/all_gather | solution.py:464
  8.7 177.8 %all-gather.10.cloned.1.call-start = ((), (), s32[]{:S(2)}) async-start(), calls=%async_computation.11 | async-start | bytes 5242880 | tf_op jit(solution)/shard_map/all_gather | solution.py:464
  9.5 98.2 %collective-permute-start = (bf16[2,3,1024]{2,1,0:T(4,128)(2,1)S(1)}, bf16[2,3,1024]{2,1,0:T(4,128)(2,1)S(1)}, u32[]{:S(2)}, u32[]{:S(2)}) collective-permute-start(bf16[2,3,1024]{2,1,0:T(4,128)(2,1)S(1)} %slice.96), channel_id=1, source_target_pairs={{0,4},{4,8},{8,12},{12,16},{16,20},{20,24},{24,28},{28,32},{32,36}... | collective-permute-start | bytes 36872 | tf_op jit(solution)/shard_map/ppermute | solution.py:479
  96.9 11.0 %copy-start.57 = (f32[1024]{0:T(1024)S(1)}, f32[1024]{0:T(1024)}, u32[]{:S(2)}) copy-start(f32[1024]{0:T(1024)} %param.17) | copy-start | bytes 12292
  107.0 1.4 copy-start.49
  107.2 5.2 copy-start.37
  107.2 5.2 copy-start.39
  107.2 84.3 %copy-start.33 = (f32[32]{0:T(128)}, f32[32]{0:T(128)S(1)}, u32[]{:S(2)}) copy-start(f32[32]{0:T(128)S(1)} %get-tuple-element.136) | copy-start | bytes 388
  107.6 4.9 copy-start.22
  107.9 4.5 copy-start.60
  108.1 73.7 %copy-start.45 = (bf16[272,1024]{1,0:T(8,128)(2,1)}, bf16[272,1024]{1,0:T(8,128)(2,1)S(1)}, u32[]{:S(2)}) copy-start(bf16[272,1024]{1,0:T(8,128)(2,1)S(1)} %multiply_convert_fusion) | copy-start | bytes 1671172
  108.4 4.0 copy-start.24
  108.8 3.7 copy-start.16
  108.8 3.7 copy-start.35
  108.8 3.7 copy-start.41
  126.0 1.0 copy-start.6
  127.0 127.0 %copy-start.18 = (f32[256,32]{1,0:T(8,128)}, f32[256,32]{1,0:T(8,128)S(1)}, u32[]{:S(2)}) copy-start(f32[256,32]{1,0:T(8,128)S(1)} %get-tuple-element.37.dt) | copy-start | bytes 98308
  138.4 21.4 %all-to-all-start.1 = ((bf16[32,2,64,128]{3,2,1,0:T(8,128)(2,1)}), bf16[32,2,64,128]{3,2,1,0:T(8,128)(2,1)S(1)}, u32[]{:S(2)}, u32[]{:S(2)}) async-start(bf16[32,2,64,128]{3,2,1,0:T(8,128)(2,1)} %get-tuple-element.39), calls=%async_computation.1 | async-start | bytes 2097152 | tf_op jit(solution)/shard_map/all_to_all | solution.py:460
  161.9 29.6 %all-to-all-start.2 = ((bf16[32,2,64,128]{3,2,1,0:T(8,128)(2,1)}), bf16[32,2,64,128]{3,2,1,0:T(8,128)(2,1)S(1)}, u32[]{:S(2)}, u32[]{:S(2)}) async-start(bf16[32,2,64,128]{3,2,1,0:T(8,128)(2,1)} %shard_map.281), calls=%async_computation.2 | async-start | bytes 2097152 | tf_op jit(solution)/shard_map/all_to_all | solution.py:460
  180.4 1.3 copy-start.4
  186.5 5.9 copy-start.28
  191.5 1.0 copy-start
  221.5 1.0 copy-start.2
  223.7 24.1 %copy-start.7 = (bf16[256,2048]{1,0:T(8,128)(2,1)}, bf16[256,2048]{1,0:T(8,128)(2,1)S(1)}, u32[]{:S(2)}) copy-start(bf16[256,2048]{1,0:T(8,128)(2,1)S(1)} %get-tuple-element.49) | copy-start | bytes 3145732
  223.7 24.1 %copy-start.9 = (bf16[256,2048]{1,0:T(8,128)(2,1)}, bf16[256,2048]{1,0:T(8,128)(2,1)S(1)}, u32[]{:S(2)}) copy-start(bf16[256,2048]{1,0:T(8,128)(2,1)S(1)} %get-tuple-element.41.d_y) | copy-start | bytes 3145732
  249.9 25.9 %all-to-all-start.4 = ((bf16[32,2,64,128]{3,2,1,0:T(8,128)(2,1)}), bf16[32,2,64,128]{3,2,1,0:T(8,128)(2,1)S(1)}, u32[]{:S(2)}, u32[]{:S(2)}) async-start(bf16[32,2,64,128]{3,2,1,0:T(8,128)(2,1)} %shard_map.284), calls=%async_computation.4 | async-start | bytes 2097152 | tf_op jit(solution)/shard_map/all_to_all | solution.py:460
  253.8 22.0 %copy-start.1 = (bf16[32,2,64,128]{3,2,1,0:T(8,128)(2,1)S(1)}, bf16[32,2,64,128]{3,2,1,0:T(8,128)(2,1)}, u32[]{:S(2)}) copy-start(bf16[32,2,64,128]{3,2,1,0:T(8,128)(2,1)} %copy-done) | copy-start | bytes 3145732
  253.9 96.5 %reduce-scatter.9.cloned.1.call-start = ((), (), s32[]{:S(2)}) async-start(), calls=%async_computation.14 | async-start | bytes 737280 | tf_op jit(solution)/shard_map/reduce_scatter | solution.py:468
  254.1 1.3 copy-start.10
  273.8 1.3 copy-start.5
  275.8 1.2 copy-start.11
  277.0 0.9 copy-start.15
  278.0 0.9 copy-start.17
  278.9 0.9 copy-start.19
  279.8 0.9 copy-start.21
  285.7 33.7 %copy-start.46 = (bf16[272,1024]{1,0:T(8,128)(2,1)S(1)}, bf16[272,1024]{1,0:T(8,128)(2,1)}, u32[]{:S(2)}) copy-start(bf16[272,1024]{1,0:T(8,128)(2,1)} %copy-done.45) | copy-start | bytes 1671172
  318.8 0.9 copy-start.29
  318.8 1.4 copy-start.43
  318.8 2.3 copy-start.8
  318.8 2.3 copy-start.47
  321.1 82.6 %reduce-scatter.5.cloned.1.call-start = ((), (), s32[]{:S(2)}) async-start(), calls=%async_computation.12 | async-start | bytes 5242880 | tf_op jit(solution)/shard_map/reduce_scatter | solution.py:468
  324.4 1.2 copy-start.3
  324.4 132.8 %reduce-scatter.11.cloned.1.call-start = ((), (), s32[]{:S(2)}) async-start(), calls=%async_computation.15 | async-start | bytes 5242880 | tf_op jit(solution)/shard_map/reduce_scatter | solution.py:468
  330.0 180.8 %reduce-scatter.7.cloned.1.call-start = ((), (), s32[]{:S(2)}) async-start(), calls=%async_computation.13 | async-start | bytes 5242880 | tf_op jit(solution)/shard_map/reduce_scatter | solution.py:468
  335.7 1.2 copy-start.50
  335.7 497.9 %all-reduce.5.cloned.1.call-start = ((), (), s32[]{:S(2)}) async-start(), calls=%async_computation.16 | async-start | bytes 6586368 | tf_op jit(solution)/shard_map/psum | solution.py:469
  510.7 4.1 copy-start.48
  510.8 8.0 copy-start.64
  514.8 3.9 copy-start.52
  517.0 3.8 copy-start.27
  517.0 3.8 copy-start.30
  517.0 3.9 copy-start.44
  517.0 6.1 copy-start.58
  517.1 5.9 collective-permute-start.1
  523.1 5.2 copy-start.32
  523.1 77.8 %copy-start.53 = (bf16[2,128,1024]{2,1,0:T(8,128)(2,1)S(1)}, bf16[2,128,1024]{2,1,0:T(8,128)(2,1)}, u32[]{:S(2)}) copy-start(bf16[2,128,1024]{2,1,0:T(8,128)(2,1)} %param.16) | copy-start | bytes 1572868
  835.0 4.6 copy-start.55
  839.7 1.6 copy-start.54
  (14 other events, 10.0 us)
Sparse Core Ops, SparseCore 0:
  9.7 41.3 all-gather.5
  52.8 38.2 all-gather.7
  92.8 41.2 all-gather.9
  321.2 29.0 reduce-scatter.8
  352.8 50.8 reduce-scatter.4
  406.3 50.8 reduce-scatter.10
  459.8 50.8 reduce-scatter.6
  513.7 319.9 all-reduce.4

commit v2 on v1

--- a/solution.py
+++ b/solution.py
@@ -456,6 +456,230 @@
     )(d_stepped, xc, d_y, x_raw, start, end, bcc, dt, r, bc_raw, dt_raw, d_bc_in, row_dot, taps_x, bias_x, taps_bc, bias_bc, dt_bias, a_log, d_skip)
 
 
+REDUCE = (("x", "y", "z"), ("y", "z", "x"), ("z", "x", "y"))
+GATHER = (("l", "z", "x"), ("l", "x", "z"), ("x", "z", "l"))
+PIECE = 128
+EXTRA = 32
+PIECE_ROWS = (PIECE, PIECE + EXTRA, PIECE)
+SMALL = 3 * 128
+
+
+def position():
+    seq, shard = lax.axis_index("seq"), lax.axis_index("wshard")
+    high, core = shard // 2, shard % 2
+    low = seq % 2
+    return {"z": seq // 8, "x": (seq // 2) % 4, "y": high * 2 + low, "l": low, "core": core}
+
+
+def device(at):
+    return {"seq": at["z"] * 8 + at["x"] * 2 + at["y"] % 2, "wshard": (at["y"] // 2) * 2 + at["core"]}
+
+
+def moved(at, axis, to):
+    new = dict(at)
+    if axis == "l":
+        new["y"] = (at["y"] // 2) * 2 + to
+        new["l"] = to
+    else:
+        new[axis] = to
+        if axis == "y":
+            new["l"] = to % 2
+    return new
+
+
+def peers(at, axis):
+    size = 2 if axis in ("l", "core") else 4
+    return [moved(at, axis, lax.rem(at[axis] + d, size)) for d in range(1, size)]
+
+
+def greet(everyone):
+    barrier = pltpu.get_barrier_semaphore()
+    for other in everyone:
+        pl.semaphore_signal(barrier, inc=1, device_id=device(other), device_id_type=pl.DeviceIdType.MESH)
+    pl.semaphore_wait(barrier, len(everyone))
+
+
+def reduce_kernel(
+    keep_n, give_n, d_gate, d_wide, d_small, keep_m, give_m, cot, vector,
+    out_z, out_x, out_out,
+    sib_n, sib_gate, sib_wide, sib_small, sib_m, sib_cot, sib_vector,
+    parts_z, parts_x, parts_out,
+    got_z1, got_x1, got_out1, sum_z1, sum_x1, sum_out1,
+    got_z2, got_x2, got_out2, sum_z2, sum_x2, sum_out2,
+    got_z3, got_x3, got_out3,
+    sib_send, sib_recv, red_send, red_recv, all_send, all_recv,
+):
+    at = position()
+    sibling = peers(at, "core")[0]
+    everyone = [sibling] + [p for axis in ("x", "y", "z") for p in peers(at, axis)]
+    greet(everyone)
+    started = []
+
+    def copy(src, dst, send, recv, to):
+        one = pltpu.make_async_remote_copy(
+            src_ref=src, dst_ref=dst, send_sem=send, recv_sem=recv,
+            device_id=device(to), device_id_type=pl.DeviceIdType.MESH,
+        )
+        one.start()
+        started.append(one)
+        return one
+
+    given = (give_n, d_gate, give_m, cot, d_wide, d_small, vector)
+    taken = (sib_n, sib_gate, sib_m, sib_cot, sib_wide, sib_small, sib_vector)
+    from_sibling = [
+        copy(a, b, sib_send.at[i], sib_recv.at[i], sibling) for i, (a, b) in enumerate(zip(given, taken))
+    ]
+
+    parts = (parts_z, parts_x, parts_out)
+    got = ((got_z1, got_x1, got_out1), (got_z2, got_x2, got_out2), (got_z3, got_x3, got_out3))
+    sums = ((sum_z1, sum_x1, sum_out1), (sum_z2, sum_x2, sum_out2))
+    outs = (out_z, out_x, out_out)
+
+    def send_stage(stage, which, src):
+        axis = REDUCE[which][stage]
+        return [
+            copy(
+                src.at[to[axis]], got[stage][which].at[d],
+                red_send.at[which, stage, d], red_recv.at[which, stage, d], to,
+            )
+            for d, to in enumerate(peers(at, axis))
+        ]
+
+    from_sibling[0].wait_recv()
+    from_sibling[1].wait_recv()
+
+    def tile_z(n, _):
+        cols = pl.ds(pl.multiple_of(n * 256, 256), 256)
+        res = mm(keep_n[:, 0:ROWS], d_gate[:, cols], NN) + mm(sib_n[:, 0:ROWS], sib_gate[:, cols], NN)
+        for y in range(4):
+            for k in range(2):
+                parts_z[n // 2, y, (n % 2) * 2 + k] = res[128 * y : 128 * y + 128, 128 * k : 128 * k + 128].astype(BF16)
+        return 0
+
+    lax.fori_loop(0, 8, tile_z, 0)
+    arriving = [send_stage(0, 0, parts_z), None, None]
+
+    from_sibling[2].wait_recv()
+    from_sibling[3].wait_recv()
+
+    def tile_out(n, _):
+        cols = pl.ds(pl.multiple_of(n * 256, 256), 256)
+        res = mm(keep_m[...], cot[:, cols], NN) + mm(sib_m[...], sib_cot[:, cols], NN)
+        for y in range(4):
+            for half in range(2):
+                for k in range(2):
+                    row = 256 * y + 128 * half
+                    parts_out[(n % 2) * 2 + k, half * 2 + n // 2, y] = res[row : row + 128, 128 * k : 128 * k + 128].astype(BF16)
+        return 0
+
+    lax.fori_loop(0, 4, tile_out, 0)
+    arriving[2] = send_stage(0, 2, parts_out)
+
+    for i in (4, 5, 6):
+        from_sibling[i].wait_recv()
+
+    def tile_x(n, _):
+        cols = pl.ds(pl.multiple_of(n * 256, 256), 256)
+        res = mm(keep_n[...], d_wide[:, cols], NN) + mm(sib_n[...], sib_wide[:, cols], NN)
+        for y in range(4):
+            for k in range(2):
+                parts_x[y, (n % 2) * 2 + k, n // 2, 0:PIECE] = res[128 * y : 128 * y + 128, 128 * k : 128 * k + 128].astype(BF16)
+        return 0
+
+    lax.fori_loop(0, 8, tile_x, 0)
+    res = mm(keep_n[...], d_small[...], NN) + mm(sib_n[...], sib_small[...], NN)
+    total = (vector[...] + sib_vector[...]).astype(BF16)
+    for y in range(4):
+        for z in range(4):
+            row = 128 * y + EXTRA * z
+            for k in range(3):
+                parts_x[y, z, k, PIECE:] = res[row : row + EXTRA, 128 * k : 128 * k + 128].astype(BF16)
+            parts_x[y, z, 3, PIECE:] = total[EXTRA * z : EXTRA * z + EXTRA, :]
+    arriving[1] = send_stage(0, 1, parts_x)
+
+    order = (0, 2, 1)
+    for stage in range(2):
+        for which in order:
+            for one in arriving[which]:
+                one.wait_recv()
+            src = parts[which] if stage == 0 else sums[0][which]
+            dst, arrived = sums[stage][which], got[stage][which]
+            mine = at[REDUCE[which][stage]]
+
+            def add(i, _, src=src, dst=dst, arrived=arrived, mine=mine, stage=stage):
+                if stage == 0:
+                    for j in range(4):
+                        value = src[mine, i, j].astype(F32)
+                        for d in range(3):
+                            value = value + arrived[d, i, j].astype(F32)
+                        dst[i, j] = value.astype(BF16)
+                else:
+                    value = src[mine, i].astype(F32)
+                    for d in range(3):
+                        value = value + arrived[d, i].astype(F32)
+                    dst[i] = value.astype(BF16)
+                return 0
+
+            lax.fori_loop(0, 4, add, 0)
+            arriving[which] = send_stage(stage + 1, which, dst)
+
+    def gather_stage(stage, which):
+        first, second, third = GATHER[which]
+        index = (at[third], at[second], at[first])[: 3 - stage]
+        ref = outs[which].at[index]
+        return [
+            copy(ref, ref, all_send.at[which, stage, d], all_recv.at[which, stage, d], to)
+            for d, to in enumerate(peers(at, (first, second, third)[stage]))
+        ]
+
+    for which in order:
+        for one in arriving[which]:
+            one.wait_recv()
+        first, second, third = GATHER[which]
+        value = sums[1][which][at[REDUCE[which][2]]].astype(F32)
+        for d in range(3):
+            value = value + got[2][which][d].astype(F32)
+        outs[which][at[third], at[second], at[first]] = value.astype(BF16)
+        arriving[which] = gather_stage(0, which)
+    for stage in (1, 2):
+        for which in order:
+            for one in arriving[which]:
+                one.wait_recv()
+            arriving[which] = gather_stage(stage, which)
+    for which in order:
+        for one in arriving[which]:
+            one.wait_recv()
+    for one in started:
+        one.wait_send()
+
+
+def reduce_grads(keep_n, give_n, d_gate, d_wide, d_small, keep_m, give_m, cot, vector):
+    vmem = pl.BlockSpec(memory_space=pltpu.VMEM)
+    dims = {"x": 4, "z": 4, "l": 2}
+    out_shape = [
+        jax.ShapeDtypeStruct((*(dims[a] for a in reversed(GATHER[i])), PIECE_ROWS[i], 128), BF16) for i in range(3)
+    ]
+    like = [pltpu.VMEM(a.shape, a.dtype) for a in (give_n, d_gate, d_wide, d_small, give_m, cot, vector)]
+
+    def bufs(*lead):
+        return [pltpu.VMEM((*lead, PIECE_ROWS[i], 128), BF16) for i in range(3)]
+
+    sems = [pltpu.SemaphoreType.DMA((7,))] * 2 + [pltpu.SemaphoreType.DMA((3, 3, 3))] * 4
+    return pl.pallas_call(
+        reduce_kernel,
+        out_shape=out_shape,
+        in_specs=[vmem] * 9,
+        out_specs=[vmem] * 3,
+        scratch_shapes=[
+            *like, *bufs(4, 4, 4), *bufs(3, 4, 4), *bufs(4, 4), *bufs(3, 4), *bufs(4), *bufs(3), *sems,
+        ],
+        compiler_params=pltpu.CompilerParams(
+            vmem_limit_bytes=VMEM_LIMIT, collective_id=1, has_side_effects=True
+        ),
+        cost_estimate=pl.CostEstimate(flops=int(4e9), bytes_accessed=int(4e7), transcendentals=0),
+    )(keep_n, give_n, d_gate, d_wide, d_small, keep_m, give_m, cot, vector)
+
+
 def swap(values):
     return lax.all_to_all(values, "seq", split_axis=0, concat_axis=0, tiled=True)
 
@@ -464,9 +688,11 @@
     return lax.all_gather(shard, "wshard", axis=0, tiled=True)
 
 
-def reduce_rows(term):
-    part = lax.psum_scatter(term.astype(BF16), "wshard", scatter_dimension=0, tiled=True)
-    return lax.psum(part, "seq").astype(F32)
+def by_core(rows, core):
+    cut = rows.reshape(2, 2, rows.shape[0] // 4, rows.shape[1])
+    keep = lax.dynamic_index_in_dim(cut, core, 1, keepdims=False)
+    give = lax.dynamic_index_in_dim(cut, 1 - core, 1, keepdims=False)
+    return keep.reshape(-1, rows.shape[1]), give.reshape(-1, rows.shape[1])
 
 
 def shards(
@@ -512,8 +738,6 @@
     )
     v_all = swap(v)
     layer_out = (hidden + mm(mixed, full_out, NN)).astype(BF16).reshape(SEQS, TOK, width)
-    grad_w_out = reduce_rows(mm(mixed, upstream, TN))
-    grad_w_z = reduce_rows(mm(normed[:ROWS], d_gate, TN))
     d_stepped, d_bc_in = inside_back(xc, d_y, bcc, dt, r)
     d_normed_z = mm(d_gate, full_z, NT)
     end = swap(states(decay, v_all, True))
@@ -521,8 +745,6 @@
         d_stepped, xc, d_y, x_raw, start, end, bcc, dt, r, bc_raw, dt_raw, d_bc_in, row_dot,
         taps_x, bias_x, conv_bc_weight, bias_bc, bias_dt, log_a, skip,
     )
-    grad_w_x = reduce_rows(mm(normed, d_x_raw, TN))
-    grad_small = reduce_rows(jnp.concatenate([mm(normed, d_bc_raw, TN), mm(normed, d_dt_raw, TN)], axis=1))
     d_normed = mm(d_x_raw, full_x, NT) + mm(d_bc_raw, full_bc, NT) + mm(d_dt_raw, full_dt, NT)
     back_tail = d_normed[ROWS:].reshape(SEQS, HALO, width)[:, HALO - (TAPS - 1) :]
     back_tail = lax.ppermute(back_tail, "seq", [(i + 1, i) for i in range(chunks - 1)])
@@ -536,14 +758,30 @@
 
     pieces = (g_x[: TAPS + 1], g_bc[: TAPS + 1], g_heads[:3], g_in, g_norm)
     sizes = [p.size for p in pieces]
-    total = lax.psum(jnp.concatenate([p.reshape(-1) for p in pieces]), ("seq", "wshard"))
+    vector = jnp.concatenate([*(p.reshape(-1) for p in pieces), jnp.zeros((PIECE * 128 - sum(sizes),), F32)])
+    core = lax.axis_index("wshard") % 2
+    keep_n, give_n = by_core(normed.T, core)
+    keep_m, give_m = by_core(mixed.T, core)
+    d_small = jnp.concatenate([d_bc_raw, d_dt_raw, jnp.zeros((ALL, SMALL - 2 * STATE - HEADS), BF16)], axis=1)
+    sum_z, sum_x, sum_out = reduce_grads(
+        keep_n, give_n, d_gate, d_x_raw, d_small, keep_m, give_m, upstream, vector.reshape(PIECE, 128)
+    )
+    grad_w_z = sum_z.transpose(2, 3, 0, 1, 4).reshape(2 * PIECE, INNER).astype(F32)
+    grad_w_x = sum_x[:, :, :, :PIECE].transpose(2, 3, 1, 0, 4).reshape(2 * PIECE, INNER).astype(F32)
+    extra = sum_x[:, :, :, PIECE:].transpose(1, 2, 0, 3, 4).reshape(4, 2 * PIECE, 128).astype(F32)
+    grad_w_bc = jnp.concatenate([extra[0], extra[1]], axis=1)
+    grad_w_dt = extra[2][:, :HEADS]
+    total = extra[3][:PIECE].reshape(-1)[: sum(sizes)]
+    grad_w_out = (
+        sum_out.reshape(2, 4, 2, 2, PIECE, 128).transpose(0, 2, 4, 3, 1, 5).reshape(4 * PIECE, width).astype(F32)
+    )
     ends = [sum(sizes[: i + 1]) for i in range(len(sizes) - 1)]
     s_x, s_bc, s_heads, s_in, s_norm = jnp.split(total, ends)
     s_x = lax.dynamic_slice(s_x.reshape(TAPS + 1, INNER), (0, place * HEAD), (TAPS + 1, HEAD))
     s_bc = s_bc.reshape(TAPS + 1, 2 * STATE)
     s_heads = lax.dynamic_slice(s_heads.reshape(3, HEADS), (0, place), (3, 1))
     return (
-        layer_out, input_grad, s_in, grad_w_z, grad_w_x, grad_small[:, : 2 * STATE], grad_small[:, 2 * STATE :],
+        layer_out, input_grad, s_in, grad_w_z, grad_w_x, grad_w_bc, grad_w_dt,
         s_x[:TAPS], s_x[TAPS], s_bc[:TAPS], s_bc[TAPS], s_heads[0], s_heads[1], s_heads[2], s_norm, grad_w_out,
     )
 

time: 852 us -> 501 us (0.59)
  waiting for transfers between devices: 424 us -> 22.8 us
  Pallas kernels: 113 us -> 205 us
  blocking collectives: 195 us -> 127 us
  local copies, waits for them, and re-layouts: 31.4 us -> 72.9 us
  matrix products: 41.8 us -> 26.9 us
    psum x1 -> x0, waiting for transfers between devices: 230 us -> none  [reduce_rows(): return lax.psum(part, 'seq').astype(F32)]
    reduce_scatter x4 -> x0, waiting for transfers between devices: 173 us -> none  [reduce_rows(): lax.psum_scatter(term.astype(BF16), 'wshard', scatter_dimension=0, tiled=...]
    pallas_call x0 -> x1, Pallas kernels: none -> 92.1 us  [reduce_grads(): pl.pallas_call(reduce_kernel, out_shape=out_shape, in_specs=[vmem] * 9, o...]
    psum x1 -> x0, blocking collectives: 68.2 us -> none  [shards(): lax.psum(jnp.concatenate([p.reshape(-1) for p in pieces]), ('seq', 'wshar...]
    convert_element_type x0 -> x7, local copies, waits for them, and re-layouts: none -> 16.2 us  [the longest x2 7.28 us: shards(): sum_x[:, :, :, :PIECE].transpose(2, 3, 1, 0, 4).reshape(2 * PIECE, INNER)]
    dot_general x15 -> x10, matrix products: 41.8 us -> 26.9 us  [mm(): lax.dot_general(a, b, ((dims[0], dims[1]), ((), ())), precision=precision...]
    dynamic_slice x0 -> x4, local copies, waits for them, and re-layouts: none -> 12.9 us  [the longest x3 10.9 us: by_core(): give = lax.dynamic_index_in_dim(cut, 1 - core, 1, keepdims=False)]
    unnamed x134 -> x148, local copies, waits for them, and re-layouts: 22.6 us -> 30.5 us
  transfers between devices with their start and end apart: 13 -> 8, of which waited for: 7 -> 2; matrix products, arithmetic and copies ran while one was open for 6% -> 9% of each run, Pallas kernels for 6% -> 10%
where the time goes in v2:
time: 501 us; the launch traced here: 497 us
  Pallas kernels  205 us (41%)
  blocking collectives  127 us (25%)
  local copies, waits for them, and re-layouts  72.9 us (15%)
  matrix products  26.9 us (5%)
  waiting for transfers between devices  22.8 us (5%)
  starting transfers between devices  17.3 us (3%)
  between operations  16.6 us (3%)
  other arithmetic  8.97 us (2%)
    pallas_call x1, Pallas kernels, reduce_grads(): pl.pallas_call(reduce_kernel, out_shape=out_shape, in_specs=[vmem] * 9, o...  92.1 us
    all_gather x1, blocking collectives, shards(): params = lax.all_gather(own, 'seq', axis=0, tiled=False)  81.5 us
    all_to_all x2, blocking collectives, swap(): lax.all_to_all(values, 'seq', split_axis=0, concat_axis=0, tiled=True)  35.3 us
    pallas_call x1, Pallas kernels, back(): call(back_kernel, [((ALL, INNER), BF16), ((ALL, 2 * STATE), BF16), ((ALL,...  33.2 us
    unnamed x148, local copies, waits for them, and re-layouts  30.5 us
    pallas_call x1, Pallas kernels, middle(): call(middle_kernel, [((ROWS, INNER), BF16), ((ROWS, INNER), BF16), ((ROWS...  29 us
    dot_general x10, matrix products, mm(): lax.dot_general(a, b, ((dims[0], dims[1]), ((), ())), precision=precision...  26.9 us
    pallas_call x1, Pallas kernels, inside_back(): call(inside_back_kernel, [((ROWS, INNER), F32), ((ROWS, 2 * STATE), F32)]...  18.4 us
  transfers between devices with their start and end apart: 8, of which 2 were waited for; matrix products, arithmetic and copies ran while one was open for 9% of the time, Pallas kernels for 10%

profile of v2, /device:TPU:0, one launch (start us, length us, event | category | flops | bytes accessed | tf_op | source)
XLA Modules:
  0.0 497.4 jit_solution(3536352563613058460)
XLA Ops:
  9.5 3.6 collective-permute-start
  15.3 81.5 %all-gather.1 = f32[32,1,384]{2,1,0:T(1,128)S(1)} all-gather(f32[1,1,384]{2,1,0:T(1,128)S(1)} %reshape.218), channel_id=2, replica_groups=mesh['seq'=32,'wshard'=4] {'seq'}, dimensions={0}, use_global_device_ids=true | all-gather | bytes 50688 | tf_op jit(solution)/shard_map/all_gather | solution.py:712
  96.9 10.1 %all_gather.19 = bf16[1024,288]{1,0:T(8,128)(2,1)S(1)} all-gather(bf16[256,288]{1,0:T(8,128)(2,1)S(1)} %pad_maximum_fusion.2), channel_id=1, replica_groups=mesh['seq'=32,'wshard'=4] {'wshard'}, dimensions={0}, use_global_device_ids=true | all-gather | bytes 737280 | tf_op jit(solution)/shard_map/all_gather | solution.py:688
  108.8 3.5 convolution_convert_fusion.x_raw
  112.4 13.6 %shard_map.279 = (bf16[256,2048]{1,0:T(8,128)(2,1)S(1)}, bf16[256,256]{1,0:T(8,128)(2,1)S(1)}, f32[256,32]{1,0:T(8,128)S(1)}, f32[256,32]{1,0:T(8,128)S(1)}, bf16[32,2,64,128]{3,2,1,0:T(8,128)(2,1)}) custom-call(bf16[272,2048]{1,0:T(8,128)(2,1)S(1)} %convolution_convert_fusion.x_raw, bf16[272,256]{1,0:T(8,128)(2,1)S(1)} %convolution_convert_fusion.1.bc_raw, ...), custom_call_target="tpu_custom_call" | custom-call | flops 1000000000 | bytes 10000000 | tf_op jit(solution)/shard_map/pallas_call | solution.py:162
  126.0 1.0 copy-done.4
  127.1 11.2 %all_to_all.29 = f32[32,1,2]{2,1,0:T(1,128)S(1)} all-to-all(f32[32,1,2]{2,1,0:T(1,128)S(1)} %copy.99), channel_id=1, replica_groups=mesh['seq'=32,'wshard'=4] {'seq'}, dimensions={0} | all-to-all | bytes 512 | tf_op jit(solution)/shard_map/all_to_all | solution.py:684
  138.3 3.9 all-to-all-start.1
  142.4 17.3 %all-to-all-done.1.own = bf16[32,2,64,128]{3,2,1,0:T(8,128)(2,1)S(1)} async-done(((bf16[32,2,64,128]{3,2,1,0:T(8,128)(2,1)}), bf16[32,2,64,128]{3,2,1,0:T(8,128)(2,1)S(1)}, u32[]{:S(2)}, u32[]{:S(2)}) %all-to-all-start.1) | async-done | bytes 1048608 | tf_op jit(solution)/shard_map/all_to_all | solution.py:684
  159.7 2.1 shard_map.281
  161.8 3.9 all-to-all-start.2
  165.8 14.6 %shard_map.280.y_in = f32[256,2048]{1,0:T(8,128)S(1)} custom-call(bf16[256,2048]{1,0:T(8,128)(2,1)S(1)} %get-tuple-element.38.xc, bf16[256,256]{1,0:T(8,128)(2,1)S(1)} %get-tuple-element.39.bcc, f32[256,32]{1,0:T(8,128)S(1)} %get-tuple-element.40.dt, f32[256,32]{1,0:T(8,128)S(1)} %get-tuple-element.41.r), custom_call_target="tpu_custom_call" | custom-call | flops 1000000000 | bytes 10000000 | tf_op jit(solution)/shard_map/pallas_call | solution.py:221
  180.4 1.3 copy-done.2
  181.7 5.0 %fusion.2.gate = f32[256,2048]{1,0:T(8,128)} fusion(bf16[1024,2048]{1,0:T(8,128)(2,1)} %all-gather.8.cloned.1.call-done, bf16[272,1024]{1,0:T(8,128)(2,1)} %copy-done.55), kind=kOutput, calls=%fused_computation.18 | convolution fusion | flops 1073741824 | bytes 6815744 | tf_op jit(solution)/shard_map/dot_general | solution.py:28
  186.7 4.9 fusion.12.d_mixed
  191.6 1.0 copy-done
  192.6 29.0 %shard_map.282 = (bf16[256,2048]{1,0:T(8,128)(2,1)S(1)}, bf16[256,2048]{1,0:T(8,128)(2,1)S(1)}, bf16[256,2048]{1,0:T(8,128)(2,1)S(1)}, bf16[32,2,64,128]{3,2,1,0...) custom-call(f32[256,2048]{1,0:T(8,128)} %copy-done.2, bf16[256,2048]{1,0:T(8,128)(2,1)S(1)} %get-tuple-element.38.xc, ...), custom_call_target="tpu_custom_call" | custom-call | flops 1000000000 | bytes 10000000 | tf_op jit(solution)/shard_map/pallas_call | solution.py:301
  221.6 1.0 copy-done.5
  223.8 24.1 %all_to_all.30.own = bf16[32,2,64,128]{3,2,1,0:T(8,128)(2,1)S(1)} all-to-all(bf16[32,2,64,128]{3,2,1,0:T(8,128)(2,1)S(1)} %get-tuple-element.46), channel_id=1, replica_groups=mesh['seq'=32,'wshard'=4] {'seq'}, dimensions={0} | all-to-all | bytes 2097152 | tf_op jit(solution)/shard_map/all_to_all | solution.py:684
  247.9 2.1 shard_map.284
  250.0 4.1 all-to-all-start.4
  255.3 1.2 reshape.198
  256.5 3.6 constant_dynamic-slice_fusion.4
  260.2 2.0 copy.103
  262.2 2.0 copy.104
  264.1 1.6 reshape.201
  265.7 5.3 %constant_dynamic-slice_fusion.2 = (bf16[2,1,512,256]{2,1,0,3:T(2,128)(2,1)}, bf16[2,1,512,256]{2,1,0,3:T(2,128)(2,1)}) fusion(bf16[2,2,512,256]{2,1,0,3:T(2,128)(2,1)} %reshape.201, s32[]{:T(128)S(6)} %select_n.25, s32[]{:T(128)S(6)} %select_n.24), kind=kLoop, calls=%fused_computation.39 | loop fusion | bytes 2097160 | tf_op jit(solution)/shard_map/jit(dynamic_index_in_dim)/dynamic_slice | solution.py:694
  271.0 3.5 copy.117
  274.5 3.5 copy.118
  278.0 1.0 copy-done.21
  279.0 18.4 %shard_map.283 = (f32[256,2048]{1,0:T(8,128)S(1)}, f32[256,256]{1,0:T(8,128)S(1)}) custom-call(bf16[256,2048]{1,0:T(8,128)(2,1)S(1)} %get-tuple-element.38.xc, bf16[256,2048]{1,0:T(8,128)(2,1)S(1)} %copy-done.9, bf16[256,256]{1,0:T(8,128)(2,1)S(1)} %get-tuple-element.39.bcc, f32[256,32]{1,0:T(8,128)S(1)} %copy-done.21, f32[256,32]{1,0:T(8,128)S(1)} %get-tuple-element.41.r), custom_call_target="tpu_custom_call" | custom-call | flops 1000000000 | bytes 10000000 | tf_op jit(solution)/shard_map/pallas_call | solution.py:346
  297.3 1.3 copy-done.3
  299.4 4.3 fusion.1
  303.7 1.2 copy-done.10
  304.9 0.9 copy-done.18
  305.9 0.9 copy-done.22
  306.8 0.9 copy-done.24
  307.7 0.8 copy-done.26
  308.4 0.9 copy-done.28
  312.6 33.2 %shard_map.285 = (bf16[272,2048]{1,0:T(8,128)(2,1)}, bf16[272,256]{1,0:T(8,128)(2,1)S(1)}, bf16[272,32]{1,0:T(8,128)(2,1)S(1)}, f32[8,2048]{1,0:T(8,128)S(1)}, f...) custom-call(f32[256,2048]{1,0:T(8,128)} %copy-done.3, bf16[256,2048]{1,0:T(8,128)(2,1)S(1)} %get-tuple-element.38.xc, ...), custom_call_target="tpu_custom_call" | custom-call | flops 1000000000 | bytes 10000000 | tf_op jit(solution)/shard_map/pallas_call | solution.py:441
  346.2 2.6 fusion.13
  349.3 1.6 collective-permute-start.1
  351.0 0.7 maximum_maximum_fusion.d_small
  351.8 3.4 collective-permute-done.1
  355.5 5.3 %multiply_reduce_fusion.1 = (f32[1024]{0:T(1024)S(1)}, f32[256]{0:T(256)S(1)}, f32[256,1024]{1,0:T(8,128)}) fusion(f32[256]{0:T(256)S(1)} %copy-done.66, bf16[2,128,1024]{2,1,0:T(8,128)(2,1)S(1)} %copy-done.59, f32[2,128,1024]{2,1,0:T(8,128)S(1)} %pad.9, f32[1024]{0:T(1024)S(1)} %copy-done.64, bf16[256,2048]{1,0:T(8,128)(2,1)S(1)} %copy-done.50, ...), kind=kOutput, calls=%fused_computation.15 | convolution fusion | flops 1076099840 | bytes 8923136 | tf_op jit(solution)/shard_map/dot_general | solution.py:28
  360.8 0.7 concatenate.22
  361.5 1.0 copy-done.14
  362.5 1.0 copy-done.16
  363.5 0.9 copy-done.19
  364.5 0.8 copy-done.29
  365.3 1.2 copy-done.51
  366.5 92.1 %shard_map.286 = (bf16[4,4,2,128,128]{4,3,2,1,0:T(8,128)(2,1)S(1)}, bf16[4,4,2,160,128]{4,3,2,1,0:T(8,128)(2,1)}, bf16[2,4,4,128,128]{4,3,2,1,0:T(8,128)(2,1)S(1)}) custom-call(bf16[512,272]{1,0:T(8,128)(2,1)S(1)} %bitcast.97, bf16[512,272]{1,0:T(8,128)(2,1)S(1)} %bitcast.98, bf16[256,2048]{1,0:T(8,128)(2,1)S(1)} %copy-done.51, ...), custom_call_target="tpu_custom_call" | custom-call | flops 4000000000 | bytes 40000000 | tf_op jit(solution)/shard_map/pallas_call | solution.py:668
  458.7 1.0 convert_bitcast_fusion.3
  464.1 0.9 copy.111
  465.1 2.9 convert_bitcast_fusion.1
  467.9 2.7 copy.108
  470.6 3.0 reshape.213
  473.6 4.2 copy.109
  477.9 3.0 reshape.214
  481.2 1.4 copy.113
  482.5 1.8 reshape.215
  484.4 0.9 split.20
  487.2 0.7 pad_maximum_fusion.1
  488.0 2.9 multiply_add_fusion
  (198 shorter events, 18.6 us)
Async XLA Ops:
  7.2 2.3 copy-start.57
  7.2 5.9 %copy-start.65 = (bf16[256,32]{0,1:T(8,128)(2,1)S(1)}, bf16[256,32]{0,1:T(8,128)(2,1)}, u32[]{:S(2)}) copy-start(bf16[256,32]{0,1:T(8,128)(2,1)} %param.21) | copy-start | bytes 49156
  7.2 6.0 %copy-start.68 = (f32[4,64]{1,0:T(4,128)S(1)}, f32[4,64]{1,0:T(4,128)}, u32[]{:S(2)}) copy-start(f32[4,64]{1,0:T(4,128)} %param.22) | copy-start | bytes 3076
  7.2 8.0 %copy-start.69 = (f32[64]{0:T(128)S(1)}, f32[64]{0:T(128)}, u32[]{:S(2)}) copy-start(f32[64]{0:T(128)} %param.23) | copy-start | bytes 772
  7.2 89.6 %copy-start.62 = (bf16[256,256]{1,0:T(8,128)(2,1)S(1)}, bf16[256,256]{1,0:T(8,128)(2,1)}, u32[]{:S(2)}) copy-start(bf16[256,256]{1,0:T(8,128)(2,1)} %param.20) | copy-start | bytes 393220
  7.2 101.6 %all-gather.6.cloned.1.call-start = ((), (), s32[]{:S(2)}) async-start(), calls=%async_computation.5 | async-start | bytes 5242880 | tf_op jit(solution)/shard_map/all_gather | solution.py:688
  8.0 173.8 %all-gather.8.cloned.1.call-start = ((), (), s32[]{:S(2)}) async-start(), calls=%async_computation.6 | async-start | bytes 5242880 | tf_op jit(solution)/shard_map/all_gather | solution.py:688
  8.7 178.0 %all-gather.10.cloned.1.call-start = ((), (), s32[]{:S(2)}) async-start(), calls=%async_computation.7 | async-start | bytes 5242880 | tf_op jit(solution)/shard_map/all_gather | solution.py:688
  9.5 98.2 %collective-permute-start = (bf16[2,3,1024]{2,1,0:T(4,128)(2,1)S(1)}, bf16[2,3,1024]{2,1,0:T(4,128)(2,1)S(1)}, u32[]{:S(2)}, u32[]{:S(2)}) collective-permute-start(bf16[2,3,1024]{2,1,0:T(4,128)(2,1)S(1)} %slice.126), channel_id=1, source_target_pairs={{0,4},{4,8},{8,12},{12,16},{16,20},{20,24},{24,28},{28,32},{32,36}... | collective-permute-start | bytes 36872 | tf_op jit(solution)/shard_map/ppermute | solution.py:705
  96.9 11.0 %copy-start.63 = (f32[1024]{0:T(1024)S(1)}, f32[1024]{0:T(1024)}, u32[]{:S(2)}) copy-start(f32[1024]{0:T(1024)} %param.17) | copy-start | bytes 12292
  107.0 1.4 copy-start.53
  107.2 5.1 %copy-start.41 = (f32[32]{0:T(128)}, f32[32]{0:T(128)S(1)}, u32[]{:S(2)}) copy-start(f32[32]{0:T(128)S(1)} %get-tuple-element.127) | copy-start | bytes 388
  107.2 5.1 %copy-start.43 = (f32[32]{0:T(128)}, f32[32]{0:T(128)S(1)}, u32[]{:S(2)}) copy-start(f32[32]{0:T(128)S(1)} %get-tuple-element.128) | copy-start | bytes 388
  107.3 84.3 %copy-start.37 = (f32[32]{0:T(128)}, f32[32]{0:T(128)S(1)}, u32[]{:S(2)}) copy-start(f32[32]{0:T(128)S(1)} %get-tuple-element.126) | copy-start | bytes 388
  107.6 4.7 copy-start.25
  108.1 4.2 copy-start.55
  108.4 3.9 copy-start.27
  108.8 3.6 copy-start.39
  108.8 3.6 copy-start.45
  126.0 1.0 copy-start.4
  127.0 38.8 %copy-start.20 = (f32[256,32]{1,0:T(8,128)}, f32[256,32]{1,0:T(8,128)S(1)}, u32[]{:S(2)}) copy-start(f32[256,32]{1,0:T(8,128)S(1)} %get-tuple-element.40.dt) | copy-start | bytes 98308
  138.3 21.4 %all-to-all-start.1 = ((bf16[32,2,64,128]{3,2,1,0:T(8,128)(2,1)}), bf16[32,2,64,128]{3,2,1,0:T(8,128)(2,1)S(1)}, u32[]{:S(2)}, u32[]{:S(2)}) async-start(bf16[32,2,64,128]{3,2,1,0:T(8,128)(2,1)} %get-tuple-element.42), calls=%async_computation.1 | async-start | bytes 2097152 | tf_op jit(solution)/shard_map/all_to_all | solution.py:684
  161.8 29.8 %all-to-all-start.2 = ((bf16[32,2,64,128]{3,2,1,0:T(8,128)(2,1)}), bf16[32,2,64,128]{3,2,1,0:T(8,128)(2,1)S(1)}, u32[]{:S(2)}, u32[]{:S(2)}) async-start(bf16[32,2,64,128]{3,2,1,0:T(8,128)(2,1)} %shard_map.281), calls=%async_computation.2 | async-start | bytes 2097152 | tf_op jit(solution)/shard_map/all_to_all | solution.py:684
  180.4 1.3 copy-start.2
  181.7 5.0 %copy-start.11 = (bf16[2,128,1024]{2,1,0:T(8,128)(2,1)S(1)}, bf16[2,128,1024]{2,1,0:T(8,128)(2,1)}, u32[]{:S(2)}) copy-start(bf16[2,128,1024]{2,1,0:T(8,128)(2,1)} %param.31) | copy-start | bytes 1572868
  186.7 5.8 %copy-start.32 = (f32[2048]{0:T(1024)S(1)}, f32[2048]{0:T(1024)}, u32[]{:S(2)}) copy-start(f32[2048]{0:T(1024)} %param.29) | copy-start | bytes 24580
  191.6 1.0 copy-start
  221.6 1.0 copy-start.5
  223.8 24.1 %copy-start.8 = (bf16[256,2048]{1,0:T(8,128)(2,1)}, bf16[256,2048]{1,0:T(8,128)(2,1)S(1)}, u32[]{:S(2)}) copy-start(bf16[256,2048]{1,0:T(8,128)(2,1)S(1)} %get-tuple-element.44.d_y) | copy-start | bytes 3145732
  223.8 24.1 %copy-start.49 = (bf16[256,2048]{1,0:T(8,128)(2,1)}, bf16[256,2048]{1,0:T(8,128)(2,1)S(1)}, u32[]{:S(2)}) copy-start(bf16[256,2048]{1,0:T(8,128)(2,1)S(1)} %get-tuple-element.52.d_gate) | copy-start | bytes 3145732
  247.9 7.4 %copy-start.56 = (bf16[272,1024]{1,0:T(8,128)(2,1)S(1)}, bf16[272,1024]{1,0:T(8,128)(2,1)}, u32[]{:S(2)}) copy-start(bf16[272,1024]{1,0:T(8,128)(2,1)} %copy-done.55) | copy-start | bytes 1671172
  250.0 53.7 %all-to-all-start.4 = ((bf16[32,2,64,128]{3,2,1,0:T(8,128)(2,1)}), bf16[32,2,64,128]{3,2,1,0:T(8,128)(2,1)S(1)}, u32[]{:S(2)}, u32[]{:S(2)}) async-start(bf16[32,2,64,128]{3,2,1,0:T(8,128)(2,1)} %shard_map.284), calls=%async_computation.4 | async-start | bytes 2097152 | tf_op jit(solution)/shard_map/all_to_all | solution.py:684
  256.5 7.6 %copy-start.6 = (bf16[256,2048]{1,0:T(8,128)(2,1)S(1)}, bf16[256,2048]{1,0:T(8,128)(2,1)}, u32[]{:S(2)}) copy-start(bf16[256,2048]{1,0:T(8,128)(2,1)} %copy-done.5) | copy-start | bytes 3145732
  271.0 7.0 %copy-start.9 = (bf16[256,2048]{1,0:T(8,128)(2,1)S(1)}, bf16[256,2048]{1,0:T(8,128)(2,1)}, u32[]{:S(2)}) copy-start(bf16[256,2048]{1,0:T(8,128)(2,1)} %copy-done.8) | copy-start | bytes 3145732
  277.9 21.4 %copy-start.7 = (bf16[256,2048]{1,0:T(8,128)(2,1)S(1)}, bf16[256,2048]{1,0:T(8,128)(2,1)}, u32[]{:S(2)}) copy-start(bf16[256,2048]{1,0:T(8,128)(2,1)} %copy-done.5) | copy-start | bytes 3145732
  278.0 1.0 copy-start.21
  278.9 20.4 %copy-start.58 = (bf16[2,128,1024]{2,1,0:T(8,128)(2,1)S(1)}, bf16[2,128,1024]{2,1,0:T(8,128)(2,1)}, u32[]{:S(2)}) copy-start(bf16[2,128,1024]{2,1,0:T(8,128)(2,1)} %param.16) | copy-start | bytes 1572868
  297.3 1.3 copy-start.3
  299.4 4.3 copy-start.1
  303.7 1.2 copy-start.10
  312.6 33.2 %copy-start.54 = (bf16[1024,288]{1,0:T(8,128)(2,1)S(1)}, bf16[1024,288]{1,0:T(8,128)(2,1)}, u32[]{:S(2)}) copy-start(bf16[1024,288]{1,0:T(8,128)(2,1)} %copy-done.53) | copy-start | bytes 1769476
  312.6 33.5 %copy-start.70 = (bf16[1024,2048]{1,0:T(8,128)(2,1)S(1)}, bf16[1024,2048]{1,0:T(8,128)(2,1)}, u32[]{:S(2)}) copy-start(bf16[1024,2048]{1,0:T(8,128)(2,1)} %all-gather.6.cloned.1.call-done) | copy-start | bytes 12582916
  345.8 3.0 copy-start.30
  345.8 3.0 copy-start.35
  345.8 3.0 copy-start.47
  348.8 2.2 copy-start.67
  348.8 2.9 copy-start.31
  348.8 2.9 copy-start.36
  348.8 2.9 copy-start.48
  348.8 6.5 %copy-start.50 = (bf16[256,2048]{1,0:T(8,128)(2,1)S(1)}, bf16[256,2048]{1,0:T(8,128)(2,1)}, u32[]{:S(2)}) copy-start(bf16[256,2048]{1,0:T(8,128)(2,1)} %copy-done.49) | copy-start | bytes 3145732
  348.9 6.5 %copy-start.59 = (bf16[2,128,1024]{2,1,0:T(8,128)(2,1)S(1)}, bf16[2,128,1024]{2,1,0:T(8,128)(2,1)}, u32[]{:S(2)}) copy-start(bf16[2,128,1024]{2,1,0:T(8,128)(2,1)} %param.16) | copy-start | bytes 1572868
  348.9 6.5 %copy-start.64 = (f32[1024]{0:T(1024)S(1)}, f32[1024]{0:T(1024)}, u32[]{:S(2)}) copy-start(f32[1024]{0:T(1024)} %param.17) | copy-start | bytes 12292
  348.9 6.5 %copy-start.66 = (f32[256]{0:T(256)S(1)}, f32[256]{0:T(256)}, u32[]{:S(2)}) copy-start(f32[256]{0:T(256)} %slice.136) | copy-start | bytes 3076
  349.3 2.4 copy-start.61
  349.3 5.9 %collective-permute-start.1 = (f32[2,3,1024]{2,1,0:T(4,128)S(1)}, f32[2,3,1024]{2,1,0:T(4,128)S(1)}, u32[]{:S(2)}, u32[]{:S(2)}) collective-permute-start(f32[2,3,1024]{2,1,0:T(4,128)S(1)} %slice.169), channel_id=1, source_target_pairs={{4,0},{8,4},{12,8},{16,12},{20,16},{24,20},{28,24},{32,28},{36,32}... | collective-permute-start | bytes 73736 | tf_op jit(solution)/shard_map/ppermute | solution.py:750
  355.4 5.4 %copy-start.52 = (f32[2,128,1024]{2,1,0:T(8,128)}, f32[2,128,1024]{2,1,0:T(8,128)S(1)}, u32[]{:S(2)}) copy-start(f32[2,128,1024]{2,1,0:T(8,128)S(1)} %pad.9) | copy-start | bytes 3145732
  355.4 5.4 %copy-start.34 = (f32[1,2048]{1,0:T(1,128)S(1)}, f32[1,2048]{1,0:T(1,128)}, u32[]{:S(2)}) copy-start(f32[1,2048]{1,0:T(1,128)} %copy-done.33) | copy-start | bytes 24580
  355.4 6.1 %copy-start.12 = (bf16[2,128,1024]{2,1,0:T(8,128)(2,1)S(1)}, bf16[2,128,1024]{2,1,0:T(8,128)(2,1)}, u32[]{:S(2)}) copy-start(bf16[2,128,1024]{2,1,0:T(8,128)(2,1)} %param.31) | copy-start | bytes 1572868
  355.4 6.0 %copy-start.13 = (bf16[2,1,512,256]{3,2,0,1:T(8,128)(2,1)S(1)}, bf16[2,1,512,256]{3,2,0,1:T(8,128)(2,1)}, u32[]{:S(2)}) copy-start(bf16[2,1,512,256]{3,2,0,1:T(8,128)(2,1)} %copy.117) | copy-start | bytes 1572868
  355.4 6.0 %copy-start.15 = (bf16[2,1,256,272]{3,2,0,1:T(8,128)(2,1)S(1)}, bf16[2,1,256,272]{3,2,0,1:T(8,128)(2,1)}, u32[]{:S(2)}) copy-start(bf16[2,1,256,272]{3,2,0,1:T(8,128)(2,1)} %copy.103) | copy-start | bytes 835588
  361.5 1.0 copy-start.14
  362.5 1.0 copy-start.16
  365.3 1.2 copy-start.51
  482.5 5.4 %copy-start.60 = (bf16[2,128,1024]{2,1,0:T(8,128)(2,1)S(1)}, bf16[2,128,1024]{2,1,0:T(8,128)(2,1)}, u32[]{:S(2)}) copy-start(bf16[2,128,1024]{2,1,0:T(8,128)(2,1)} %param.16) | copy-start | bytes 1572868
  (15 other events, 11.4 us)
Sparse Core Ops, SparseCore 0:
  9.7 41.3 all-gather.5
  52.8 38.2 all-gather.7
  92.8 41.2 all-gather.9

commit v3 on v2

--- a/solution.py
+++ b/solution.py
@@ -46,6 +46,19 @@
     return (iota((8, HEADS), 1) == 2 * pair + iota((8, HEADS), 0)).astype(F32)
 
 
+def head_sums(values, ex):
+    high = values.astype(BF16)
+    low = (values - high.astype(F32)).astype(BF16)
+    ex = ex.astype(BF16)
+    return mm(jnp.concatenate([high, low], axis=1), jnp.concatenate([ex, ex], axis=1), NT)
+
+
+def lane_sums(values):
+    high = values.astype(BF16)
+    low = (values - high.astype(F32)).astype(BF16)
+    return mm(jnp.ones((8, 256), BF16), jnp.concatenate([high, low], axis=1), NT)[0:1, :]
+
+
 def causal_mask():
     return iota((TOK, TOK), 0) >= iota((TOK, TOK), 1)
 
@@ -99,7 +112,7 @@
     return out
 
 
-def front_kernel(x_raw, bc_raw, dt_raw, taps_x, bias_x, taps_bc, bias_bc, dt_bias, a_log, xc, bcc, dt, r, u):
+def front_kernel(x_raw, bc_raw, dt_raw, taps_x, bias_x, taps_bc, bias_bc, dt_bias, a_log, xc, bcc, dt, r, u, dt_wide, r_wide, r_rows):
     pair = pl.program_id(0)
 
     @pl.when(pair == 0)
@@ -116,13 +129,17 @@
 
     raw = x_raw[...].astype(F32)
     ex = pair_matrix(pair)
+    both = mm(jnp.concatenate([r[...], dt[...]], axis=0), ex, NN, HIGHEST)
+    r_wide[...] = both[0:ROWS, :]
+    dt_wide[...] = both[ROWS:, :]
+    r_rows[0] = mm(pair_rows(pair), r[...], NT, HIGHEST)
     for b in range(SEQS):
         span = slice(TOK * b, TOK * (b + 1))
         pre = conv_pre(padded_of(raw, b), taps_x[...], bias_x[...])
         low = (pre * jax.nn.sigmoid(pre)).astype(BF16)
         xc[span, :] = low
-        r_lanes = mm(r[span, :], ex, NN, HIGHEST)
-        dt_lanes = mm(dt[span, :], ex, NN, HIGHEST)
+        r_lanes = both[span, :]
+        dt_lanes = both[ROWS + TOK * b : ROWS + TOK * (b + 1), :]
         to_end = jnp.exp(r_lanes[TOK - 1 : TOK, :] - r_lanes)
         scaled = (to_end * (dt_lanes * low.astype(F32))).astype(BF16)
         state = mm(scaled, bcc[span, 0:STATE], TN).astype(BF16)
@@ -139,6 +156,7 @@
 
 
 STATES = pl.BlockSpec((2, SEQS, HEAD, STATE), lambda j: (j, 0, 0, 0))
+PAIR_ROWS = pl.BlockSpec((1, 8, ROWS), lambda j: (j, 0, 0))
 STATES_SHAPE = (HEADS, SEQS, HEAD, STATE)
 VMEM_LIMIT = 48 * 1024 * 1024
 
@@ -161,8 +179,8 @@
 def front(x_raw, bc_raw, dt_raw, taps_x, bias_x, taps_bc, bias_bc, dt_bias, a_log):
     return call(
         front_kernel,
-        [((ROWS, INNER), BF16), ((ROWS, 2 * STATE), BF16), ((ROWS, HEADS), F32), ((ROWS, HEADS), F32), (STATES_SHAPE, BF16)],
-        [lanes(ROWS), whole((ROWS, 2 * STATE)), whole((ROWS, HEADS)), whole((ROWS, HEADS)), STATES],
+        [((ROWS, INNER), BF16), ((ROWS, 2 * STATE), BF16), ((ROWS, HEADS), F32), ((ROWS, HEADS), F32), (STATES_SHAPE, BF16), ((ROWS, INNER), F32), ((ROWS, INNER), F32), ((PAIRS, 8, ROWS), F32)],
+        [lanes(ROWS), whole((ROWS, 2 * STATE)), whole((ROWS, HEADS)), whole((ROWS, HEADS)), STATES, lanes(ROWS), lanes(ROWS), PAIR_ROWS],
         [
             lanes(ALL), whole((ALL, 2 * STATE)), whole((ALL, HEADS)), lanes(TAPS), lanes(1),
             whole((TAPS, 2 * STATE)), whole((1, 2 * STATE)), whole((1, HEADS)), whole((1, HEADS)),
@@ -195,7 +213,7 @@
     )(decay, own)
 
 
-def inside_kernel(xc, bcc, dt, r, y, scores):
+def inside_kernel(xc, bcc, dt_wide, r_wide, r_rows, y, scores):
     pair = pl.program_id(0)
 
     @pl.when(pair == 0)
@@ -204,27 +222,23 @@
             span = slice(TOK * b, TOK * (b + 1))
             scores[b] = mm(bcc[span, STATE:], bcc[span, 0:STATE], NT)
 
-    ex = pair_matrix(pair)
-    rows = pair_rows(pair)
     for b in range(SEQS):
         span = slice(TOK * b, TOK * (b + 1))
-        r_lanes = mm(r[span, :], ex, NN, HIGHEST)
-        dt_lanes = mm(dt[span, :], ex, NN, HIGHEST)
-        r_rows = mm(rows, r[span, :], NT, HIGHEST)
-        first, second = decay_pair(r_lanes, r_rows)
+        dt_lanes = dt_wide[span, :]
+        first, second = decay_pair(r_wide[span, :], r_rows[0, :, span])
         both = jnp.concatenate([scores[b] * first, scores[b] * second], axis=1).astype(BF16)
         stepped = (dt_lanes * xc[span, :].astype(F32)).astype(BF16)
         y[span, :] = mm(both, block_diagonal(stepped), NN)
 
 
-def inside(xc, bcc, dt, r):
+def inside(xc, bcc, dt_wide, r_wide, r_rows):
     return call(
         inside_kernel,
         [((ROWS, INNER), F32)],
         [lanes(ROWS)],
-        [lanes(ROWS), whole((ROWS, 2 * STATE)), whole((ROWS, HEADS)), whole((ROWS, HEADS))],
+        [lanes(ROWS), whole((ROWS, 2 * STATE)), lanes(ROWS), lanes(ROWS), PAIR_ROWS],
         scratch=[pltpu.VMEM((SEQS, TOK, TOK), F32)],
-    )(xc, bcc, dt, r)[0]
+    )(xc, bcc, dt_wide, r_wide, r_rows)[0]
 
 
 def middle_kernel(
@@ -235,7 +249,7 @@
     phase = pl.program_id(0)
     pair = pl.program_id(1)
     ex = pair_matrix(pair)
-    skip = mm(jnp.broadcast_to(d_skip[...], (8, HEADS)), ex, NN, HIGHEST)[0:1, :]
+    skip = d_skip[...]
     z = gate[...]
     sig = jax.nn.sigmoid(z)
     pulled = d_mixed[...] * gain[...]
@@ -250,7 +264,7 @@
         for b in range(SEQS):
             span = slice(TOK * b, TOK * (b + 1))
             before = jnp.concatenate([start[0, b], start[1, b]], axis=0)
-            grown = jnp.exp(mm(r[span, :], ex, NN, HIGHEST))
+            grown = jnp.exp(r[span, :])
             y_all[pair, span, :] = y_in[span, :] + grown * mm(bcc[span, STATE:], before, NT)
         y = (y_all[pair] + skip * xc[...].astype(F32)).astype(BF16).astype(F32)
         gated = y * (z * sig)
@@ -277,10 +291,10 @@
         low = (d_gated * silu).astype(BF16)
         d_y[...] = low
         d_gate[...] = (d_gated * y * (sig * (1.0 + z * (1.0 - sig)))).astype(BF16)
-        row_dot[...] += mm(low.astype(F32) * y_all[pair], ex, NT, HIGHEST)
+        row_dot[...] += head_sums(low.astype(F32) * y_all[pair], ex)
         for b in range(SEQS):
             span = slice(TOK * b, TOK * (b + 1))
-            grown = jnp.exp(mm(r[span, :], ex, NN, HIGHEST))
+            grown = jnp.exp(r[span, :])
             state = mm((grown * low[span, :].astype(F32)).astype(BF16), bcc[span, STATE:], TN).astype(BF16)
             own[0, b] = state[0:HEAD, :]
             own[1, b] = state[HEAD:, :]
@@ -302,13 +316,13 @@
         middle_kernel,
         [((ROWS, INNER), BF16), ((ROWS, INNER), BF16), ((ROWS, INNER), BF16), (STATES_SHAPE, BF16), ((1, INNER), F32), ((ROWS, HEADS), F32)],
         [second(ROWS), second(ROWS), second(ROWS), states_out, second(1), whole((ROWS, HEADS))],
-        [first(ROWS), cols(ROWS), whole((ROWS, 2 * STATE)), whole((ROWS, HEADS)), states_in, whole((1, HEADS)), cols(ROWS), cols(ROWS), cols(1)],
+        [first(ROWS), cols(ROWS), whole((ROWS, 2 * STATE)), cols(ROWS), states_in, cols(1), cols(ROWS), cols(ROWS), cols(1)],
         grid=(2, PAIRS),
         scratch=[pltpu.VMEM((PAIRS, ROWS, 128), F32)] + [pltpu.VMEM((ROWS, 128), F32)] * 4,
     )(y_in, xc, bcc, r, start, d_skip, gate, d_mixed, gain)
 
 
-def inside_back_kernel(xc, d_y, bcc, dt, r, d_stepped, d_bc, scores, d_scores):
+def inside_back_kernel(xc, d_y, bcc, dt_wide, r_wide, r_rows, d_stepped, d_bc, scores, d_scores):
     pair = pl.program_id(0)
 
     @pl.when(pair == 0)
@@ -318,14 +332,10 @@
             span = slice(TOK * b, TOK * (b + 1))
             scores[b] = mm(bcc[span, STATE:], bcc[span, 0:STATE], NT)
 
-    ex = pair_matrix(pair)
-    rows = pair_rows(pair)
     for b in range(SEQS):
         span = slice(TOK * b, TOK * (b + 1))
-        r_lanes = mm(r[span, :], ex, NN, HIGHEST)
-        dt_lanes = mm(dt[span, :], ex, NN, HIGHEST)
-        r_rows = mm(rows, r[span, :], NT, HIGHEST)
-        first, second = decay_pair(r_lanes, r_rows)
+        dt_lanes = dt_wide[span, :]
+        first, second = decay_pair(r_wide[span, :], r_rows[0, :, span])
         both = jnp.concatenate([scores[b] * first, scores[b] * second], axis=0).astype(BF16)
         stepped = (dt_lanes * xc[span, :].astype(F32)).astype(BF16)
         wide = block_diagonal(d_y[span, :])
@@ -342,42 +352,39 @@
             d_bc[span, STATE:] = mm(low, bcc[span, 0:STATE], NN)
 
 
-def inside_back(xc, d_y, bcc, dt, r):
+def inside_back(xc, d_y, bcc, dt_wide, r_wide, r_rows):
     return call(
         inside_back_kernel,
         [((ROWS, INNER), F32), ((ROWS, 2 * STATE), F32)],
         [lanes(ROWS), whole((ROWS, 2 * STATE))],
-        [lanes(ROWS), lanes(ROWS), whole((ROWS, 2 * STATE)), whole((ROWS, HEADS)), whole((ROWS, HEADS))],
+        [lanes(ROWS), lanes(ROWS), whole((ROWS, 2 * STATE)), lanes(ROWS), lanes(ROWS), PAIR_ROWS],
         scratch=[pltpu.VMEM((SEQS, TOK, TOK), F32)] * 2,
-    )(xc, d_y, bcc, dt, r)
+    )(xc, d_y, bcc, dt_wide, r_wide, r_rows)
 
 
 def back_kernel(
-    d_stepped, xc, d_y, x_raw, start, end, bcc, dt, r, bc_raw, dt_raw, d_bc_in, row_dot,
+    d_stepped, xc, d_y, x_raw, start, end, bcc, dt, dt_wide, r_wide, bc_raw, dt_raw, d_bc_in, row_dot,
     taps_x, bias_x, taps_bc, bias_bc, dt_bias, a_log, d_skip,
     d_x_raw, d_bc_raw, d_dt_raw, g_x, g_bc, g_heads,
-    d_bc, d_dt, col_dot, ends, skips,
+    d_bc, sums,
 ):
     pair = pl.program_id(0)
 
     @pl.when(pair == 0)
     def _():
         d_bc[...] = d_bc_in[...]
-        d_dt[...] = jnp.zeros_like(d_dt)
-        col_dot[...] = jnp.zeros_like(col_dot)
-        ends[...] = jnp.zeros_like(ends)
-        skips[...] = jnp.zeros_like(skips)
+        sums[...] = jnp.zeros_like(sums)
 
     ex = pair_matrix(pair)
-    skip = mm(jnp.broadcast_to(d_skip[...], (8, HEADS)), ex, NN, HIGHEST)[0:1, :]
+    skip = d_skip[...]
     raw = x_raw[...].astype(F32)
-    ones = jnp.ones((8, STATE), F32)
     halos, grads = [], None
+    d_steps, cols, end_rows = [], [], []
     skip_sum = jnp.zeros((1, 128), F32)
     for b in range(SEQS):
         span = slice(TOK * b, TOK * (b + 1))
-        r_lanes = mm(r[span, :], ex, NN, HIGHEST)
-        dt_lanes = mm(dt[span, :], ex, NN, HIGHEST)
+        r_lanes = r_wide[span, :]
+        dt_lanes = dt_wide[span, :]
         last = r_lanes[TOK - 1 : TOK, :]
         grown = jnp.exp(r_lanes)
         to_end = jnp.exp(last - r_lanes)
@@ -388,12 +395,11 @@
         stepped = (dt_lanes * x).astype(BF16).astype(F32)
         carried = to_end * mm(bcc[span, 0:STATE], after, NT)
         d_step = d_stepped[span, :] + carried
-        col_dot[span, :] += mm(stepped * d_step, ex, NT, HIGHEST)
+        cols.append(stepped * d_step)
         d_x = dt_lanes * d_step + skip * dy
-        d_dt[span, :] += mm(x * d_step, ex, NT, HIGHEST)
-        inner = mm(ones, before.astype(F32) * after.astype(F32), NT, HIGHEST)[0:1, :]
-        end_row = jnp.sum(stepped * carried, axis=0, keepdims=True) + jnp.exp(last) * inner
-        ends[b] += mm(jnp.broadcast_to(end_row, (8, 128)), ex, NT, HIGHEST)
+        d_steps.append(x * d_step)
+        inner = lane_sums(before.astype(F32) * after.astype(F32))
+        end_rows.append(jnp.sum(stepped * carried, axis=0, keepdims=True) + jnp.exp(last) * inner)
         d_bc[span, STATE:] += mm((grown * dy).astype(BF16), before, NN)
         d_bc[span, 0:STATE] += mm((to_end * stepped).astype(BF16), after, NN)
         skip_sum = skip_sum + jnp.sum(dy * x, axis=0, keepdims=True)
@@ -404,7 +410,8 @@
         grads = parts if grads is None else [g + p for g, p in zip(grads, parts)]
     d_x_raw[ROWS:, :] = jnp.concatenate(halos, axis=0).astype(BF16)
     g_x[...] = jnp.concatenate([*grads, jnp.zeros((8 - TAPS - 1, 128), F32)], axis=0)
-    skips[...] += mm(jnp.broadcast_to(skip_sum, (8, 128)), ex, NT, HIGHEST)
+    few = jnp.concatenate([*end_rows, skip_sum, jnp.zeros((5, 128), F32)], axis=0)
+    sums[...] += head_sums(jnp.concatenate([*d_steps, *cols, few], axis=0), ex)
 
     @pl.when(pair == PAIRS - 1)
     def _():
@@ -427,33 +434,34 @@
         for b in range(SEQS):
             span = slice(TOK * b, TOK * (b + 1))
             step = dt[span, :]
-            d_r = row_dot[span, :] - col_dot[span, :] + jnp.where(is_last, ends[b][0:1, :], 0.0)
+            d_dt = sums[span, :]
+            d_r = row_dot[span, :] - sums[ROWS + TOK * b : ROWS + TOK * (b + 1), :]
+            d_r = d_r + jnp.where(is_last, sums[2 * ROWS + b : 2 * ROWS + b + 1, :], 0.0)
             d_log = mm(tri, d_r, TN, HIGHEST)
-            d_pre = (d_dt[span, :] + rate * d_log) * jax.nn.sigmoid(dt_raw[span, :].astype(F32) + dt_bias[...])
+            d_pre = (d_dt + rate * d_log) * jax.nn.sigmoid(dt_raw[span, :].astype(F32) + dt_bias[...])
             d_dt_raw[span, :] = d_pre.astype(BF16)
             bias_sum = bias_sum + jnp.sum(d_pre, axis=0, keepdims=True)
             log_sum = log_sum + jnp.sum(d_log * step, axis=0, keepdims=True) * rate
         d_dt_raw[ROWS:, :] = jnp.zeros((ALL - ROWS, HEADS), BF16)
-        g_heads[...] = jnp.concatenate([bias_sum, log_sum, skips[0:1, :], jnp.zeros((5, HEADS), F32)], axis=0)
-
-
-def back(d_stepped, xc, d_y, x_raw, start, end, bcc, dt, r, bc_raw, dt_raw, d_bc_in, row_dot, taps_x, bias_x, taps_bc, bias_bc, dt_bias, a_log, d_skip):
+        g_heads[...] = jnp.concatenate([bias_sum, log_sum, sums[2 * ROWS + 2 : 2 * ROWS + 3, :], jnp.zeros((5, HEADS), F32)], axis=0)
+
+
+def back(d_stepped, xc, d_y, x_raw, start, end, bcc, dt, dt_wide, r_wide, bc_raw, dt_raw, d_bc_in, row_dot, taps_x, bias_x, taps_bc, bias_bc, dt_bias, a_log, d_skip):
     return call(
         back_kernel,
         [((ALL, INNER), BF16), ((ALL, 2 * STATE), BF16), ((ALL, HEADS), BF16), ((8, INNER), F32), ((8, 2 * STATE), F32), ((8, HEADS), F32)],
         [lanes(ALL), whole((ALL, 2 * STATE)), whole((ALL, HEADS)), lanes(8), whole((8, 2 * STATE)), whole((8, HEADS))],
         [
             lanes(ROWS), lanes(ROWS), lanes(ROWS), lanes(ALL), STATES, STATES,
-            whole((ROWS, 2 * STATE)), whole((ROWS, HEADS)), whole((ROWS, HEADS)), whole((ALL, 2 * STATE)),
+            whole((ROWS, 2 * STATE)), whole((ROWS, HEADS)), lanes(ROWS), lanes(ROWS), whole((ALL, 2 * STATE)),
             whole((ALL, HEADS)), whole((ROWS, 2 * STATE)), whole((ROWS, HEADS)),
             lanes(TAPS), lanes(1), whole((TAPS, 2 * STATE)), whole((1, 2 * STATE)),
-            whole((1, HEADS)), whole((1, HEADS)), whole((1, HEADS)),
+            whole((1, HEADS)), whole((1, HEADS)), lanes(1),
         ],
         scratch=[
-            pltpu.VMEM((ROWS, 2 * STATE), F32), pltpu.VMEM((ROWS, HEADS), F32), pltpu.VMEM((ROWS, HEADS), F32),
-            pltpu.VMEM((SEQS, 8, HEADS), F32), pltpu.VMEM((8, HEADS), F32),
+            pltpu.VMEM((ROWS, 2 * STATE), F32), pltpu.VMEM((2 * ROWS + 8, HEADS), F32),
         ],
-    )(d_stepped, xc, d_y, x_raw, start, end, bcc, dt, r, bc_raw, dt_raw, d_bc_in, row_dot, taps_x, bias_x, taps_bc, bias_bc, dt_bias, a_log, d_skip)
+    )(d_stepped, xc, d_y, x_raw, start, end, bcc, dt, dt_wide, r_wide, bc_raw, dt_raw, d_bc_in, row_dot, taps_x, bias_x, taps_bc, bias_bc, dt_bias, a_log, d_skip)
 
 
 REDUCE = (("x", "y", "z"), ("y", "z", "x"), ("z", "x", "y"))
@@ -500,9 +508,9 @@
 
 
 def reduce_kernel(
-    keep_n, give_n, d_gate, d_wide, d_small, keep_m, give_m, cot, vector,
+    normed, d_gate, d_wide, d_small, mixed, cot, vector,
     out_z, out_x, out_out,
-    sib_n, sib_gate, sib_wide, sib_small, sib_m, sib_cot, sib_vector,
+    keep_n, keep_m, next_n, next_m, sib_n, sib_gate, sib_wide, sib_small, sib_m, sib_cot, sib_vector,
     parts_z, parts_x, parts_out,
     got_z1, got_x1, got_out1, sum_z1, sum_x1, sum_out1,
     got_z2, got_x2, got_out2, sum_z2, sum_x2, sum_out2,
@@ -524,11 +532,21 @@
         started.append(one)
         return one
 
-    given = (give_n, d_gate, give_m, cot, d_wide, d_small, vector)
-    taken = (sib_n, sib_gate, sib_m, sib_cot, sib_wide, sib_small, sib_vector)
-    from_sibling = [
-        copy(a, b, sib_send.at[i], sib_recv.at[i], sibling) for i, (a, b) in enumerate(zip(given, taken))
-    ]
+    def columns(ref, high, core, size):
+        return ref.at[:, pl.ds(pl.multiple_of((2 * high + core) * size, size), size)]
+
+    def transposed(ref, high, core, size):
+        return ref[:, pl.ds(pl.multiple_of((2 * high + core) * size, size), size)].astype(F32).T.astype(BF16)
+
+    core = at["core"]
+    pairs = [(columns(normed, h, 1 - core, 256), sib_n.at[h]) for h in range(2)] + [(d_gate, sib_gate)]
+    pairs += [(columns(mixed, h, 1 - core, 512), sib_m.at[h]) for h in range(2)]
+    pairs += [(cot, sib_cot), (d_wide, sib_wide), (d_small, sib_small), (vector, sib_vector)]
+    from_sibling = [copy(a, b, sib_send.at[i], sib_recv.at[i], sibling) for i, (a, b) in enumerate(pairs)]
+    for h in range(2):
+        keep_n[256 * h : 256 * (h + 1), :] = transposed(normed, h, core, 256)
+    for h in range(2):
+        keep_m[512 * h : 512 * (h + 1), :] = transposed(mixed, h, core, 512)
 
     parts = (parts_z, parts_x, parts_out)
     got = ((got_z1, got_x1, got_out1), (got_z2, got_x2, got_out2), (got_z3, got_x3, got_out3))
@@ -545,12 +563,14 @@
             for d, to in enumerate(peers(at, axis))
         ]
 
-    from_sibling[0].wait_recv()
-    from_sibling[1].wait_recv()
+    for i in (0, 1, 2):
+        from_sibling[i].wait_recv()
+    for h in range(2):
+        next_n[256 * h : 256 * (h + 1), :] = sib_n[h].astype(F32).T.astype(BF16)
 
     def tile_z(n, _):
         cols = pl.ds(pl.multiple_of(n * 256, 256), 256)
-        res = mm(keep_n[:, 0:ROWS], d_gate[:, cols], NN) + mm(sib_n[:, 0:ROWS], sib_gate[:, cols], NN)
+        res = mm(keep_n[:, 0:ROWS], d_gate[:, cols], NN) + mm(next_n[:, 0:ROWS], sib_gate[:, cols], NN)
         for y in range(4):
             for k in range(2):
                 parts_z[n // 2, y, (n % 2) * 2 + k] = res[128 * y : 128 * y + 128, 128 * k : 128 * k + 128].astype(BF16)
@@ -559,12 +579,14 @@
     lax.fori_loop(0, 8, tile_z, 0)
     arriving = [send_stage(0, 0, parts_z), None, None]
 
-    from_sibling[2].wait_recv()
-    from_sibling[3].wait_recv()
+    for i in (3, 4, 5):
+        from_sibling[i].wait_recv()
+    for h in range(2):
+        next_m[512 * h : 512 * (h + 1), :] = sib_m[h].astype(F32).T.astype(BF16)
 
     def tile_out(n, _):
         cols = pl.ds(pl.multiple_of(n * 256, 256), 256)
-        res = mm(keep_m[...], cot[:, cols], NN) + mm(sib_m[...], sib_cot[:, cols], NN)
+        res = mm(keep_m[...], cot[:, cols], NN) + mm(next_m[...], sib_cot[:, cols], NN)
         for y in range(4):
             for half in range(2):
                 for k in range(2):
@@ -575,19 +597,19 @@
     lax.fori_loop(0, 4, tile_out, 0)
     arriving[2] = send_stage(0, 2, parts_out)
 
-    for i in (4, 5, 6):
+    for i in (6, 7, 8):
         from_sibling[i].wait_recv()
 
     def tile_x(n, _):
         cols = pl.ds(pl.multiple_of(n * 256, 256), 256)
-        res = mm(keep_n[...], d_wide[:, cols], NN) + mm(sib_n[...], sib_wide[:, cols], NN)
+        res = mm(keep_n[...], d_wide[:, cols], NN) + mm(next_n[...], sib_wide[:, cols], NN)
         for y in range(4):
             for k in range(2):
                 parts_x[y, (n % 2) * 2 + k, n // 2, 0:PIECE] = res[128 * y : 128 * y + 128, 128 * k : 128 * k + 128].astype(BF16)
         return 0
 
     lax.fori_loop(0, 8, tile_x, 0)
-    res = mm(keep_n[...], d_small[...], NN) + mm(sib_n[...], sib_small[...], NN)
+    res = mm(keep_n[...], d_small[...], NN) + mm(next_n[...], sib_small[...], NN)
     total = (vector[...] + sib_vector[...]).astype(BF16)
     for y in range(4):
         for z in range(4):
@@ -653,31 +675,167 @@
         one.wait_send()
 
 
-def reduce_grads(keep_n, give_n, d_gate, d_wide, d_small, keep_m, give_m, cot, vector):
+def reduce_grads(normed, d_gate, d_wide, d_small, mixed, cot, vector):
     vmem = pl.BlockSpec(memory_space=pltpu.VMEM)
     dims = {"x": 4, "z": 4, "l": 2}
     out_shape = [
         jax.ShapeDtypeStruct((*(dims[a] for a in reversed(GATHER[i])), PIECE_ROWS[i], 128), BF16) for i in range(3)
     ]
-    like = [pltpu.VMEM(a.shape, a.dtype) for a in (give_n, d_gate, d_wide, d_small, give_m, cot, vector)]
+    turned = [pltpu.VMEM((512, ALL), BF16), pltpu.VMEM((1024, ROWS), BF16)] * 2
+    like = [pltpu.VMEM((2, ALL, 256), BF16)] + [pltpu.VMEM(a.shape, a.dtype) for a in (d_gate, d_wide, d_small)]
+    like += [pltpu.VMEM((2, ROWS, 512), BF16)] + [pltpu.VMEM(a.shape, a.dtype) for a in (cot, vector)]
 
     def bufs(*lead):
         return [pltpu.VMEM((*lead, PIECE_ROWS[i], 128), BF16) for i in range(3)]
 
-    sems = [pltpu.SemaphoreType.DMA((7,))] * 2 + [pltpu.SemaphoreType.DMA((3, 3, 3))] * 4
+    sems = [pltpu.SemaphoreType.DMA((9,))] * 2 + [pltpu.SemaphoreType.DMA((3, 3, 3))] * 4
     return pl.pallas_call(
         reduce_kernel,
         out_shape=out_shape,
-        in_specs=[vmem] * 9,
+        in_specs=[vmem] * 7,
         out_specs=[vmem] * 3,
         scratch_shapes=[
-            *like, *bufs(4, 4, 4), *bufs(3, 4, 4), *bufs(4, 4), *bufs(3, 4), *bufs(4), *bufs(3), *sems,
+            *turned, *like, *bufs(4, 4, 4), *bufs(3, 4, 4), *bufs(4, 4), *bufs(3, 4), *bufs(4), *bufs(3), *sems,
         ],
         compiler_params=pltpu.CompilerParams(
             vmem_limit_bytes=VMEM_LIMIT, collective_id=1, has_side_effects=True
         ),
         cost_estimate=pl.CostEstimate(flops=int(4e9), bytes_accessed=int(4e7), transcendentals=0),
-    )(keep_n, give_n, d_gate, d_wide, d_small, keep_m, give_m, cot, vector)
+    )(normed, d_gate, d_wide, d_small, mixed, cot, vector)
+
+
+def gather_kernel(
+    w_x, w_small, own, full_x, full_small, params, send, recv, here, own_send, own_recv,
+):
+    at = position()
+    sibling = peers(at, "core")[0]
+    partner = moved(at, "y", 3 - at["y"])
+    everyone = [sibling, partner] + [p for axis in ("x", "z", "l") for p in peers(at, axis)]
+    greet(everyone)
+    started = []
+
+    def copy(src, dst, which, to, sems=(send, recv)):
+        one = pltpu.make_async_remote_copy(
+            src_ref=src, dst_ref=dst, send_sem=sems[0].at[which], recv_sem=sems[1].at[which],
+            device_id=device(to), device_id_type=pl.DeviceIdType.MESH,
+        )
+        one.start()
+        started.append(one)
+        return one
+
+    high = at["y"] // 2
+    mine, opposite = high * 2 + at["core"], (1 - high) * 2 + at["core"]
+    half = INNER // 2
+    flows = ((full_x, 0, half, "x", "z"), (full_x, half, half, "z", "x"), (full_small, 0, SMALL, "x", "z"))
+
+    def view(ref, shard, row, count, first, size):
+        row = pl.multiple_of(row, 16)
+        if shard is None:
+            return ref.at[pl.ds(row, count), first : first + size]
+        return ref.at[shard, pl.ds(row, count), first : first + size]
+
+    arriving = []
+    for i, (ref, first, size, a, b) in enumerate(flows):
+        row = (at[b] * 4 + at[a]) * 16
+        src = w_small if i == 2 else w_x
+        arriving.append(copy(view(src, None, row, 16, first, size), view(ref, mine, row, 16, first, size), i, partner))
+    params_here = pltpu.make_async_copy(own, params.at[at["z"], at["x"], at["l"]], here.at[2])
+    local = [
+        pltpu.make_async_copy(w_x, full_x.at[mine], here.at[0]),
+        pltpu.make_async_copy(w_small, full_small.at[mine], here.at[1]),
+        params_here,
+    ]
+    for one in local:
+        one.start()
+    last = [
+        copy(w_x, full_x.at[mine], 24, sibling),
+        copy(w_small, full_small.at[mine], 25, sibling),
+    ]
+    params_here.wait()
+
+    def share(stage):
+        axis = ("l", "x", "z")[stage]
+        ref = params.at[(at["z"], at["x"], at["l"])[: 3 - stage]]
+        return [copy(ref, ref, 3 * stage + d, to, (own_send, own_recv)) for d, to in enumerate(peers(at, axis))]
+
+    shared = share(0)
+    second = []
+    for i, (ref, first, size, a, b) in enumerate(flows):
+        arriving[i].wait_recv()
+        piece = view(ref, opposite, (at[b] * 4 + at[a]) * 16, 16, first, size)
+        second.append([copy(piece, piece, 3 + 3 * i + d, to) for d, to in enumerate(peers(at, a))])
+    for one in shared:
+        one.wait_recv()
+    shared = share(1)
+    third = []
+    for i, (ref, first, size, a, b) in enumerate(flows):
+        for one in second[i]:
+            one.wait_recv()
+        block = view(ref, opposite, at[b] * 64, 64, first, size)
+        third.append([copy(block, block, 12 + 3 * i + d, to) for d, to in enumerate(peers(at, b))])
+        last.append(copy(block, block, 21 + i, sibling))
+    for one in shared:
+        one.wait_recv()
+    shared = share(2)
+    for i, (ref, first, size, a, b) in enumerate(flows):
+        for d in range(3):
+            third[i][d].wait_recv()
+            block = view(ref, opposite, lax.rem(at[b] + 3 - d, 4) * 64, 64, first, size)
+            last.append(copy(block, block, 26 + 3 * i + d, sibling))
+    for one in last + shared:
+        one.wait_recv()
+    for one in local[:2]:
+        one.wait()
+    for one in started:
+        one.wait_send()
+
+
+def gather_weights(w_x, w_small, own):
+    vmem = pl.BlockSpec(memory_space=pltpu.VMEM)
+    return pl.pallas_call(
+        gather_kernel,
+        out_shape=[
+            jax.ShapeDtypeStruct((4, *w_x.shape), BF16),
+            jax.ShapeDtypeStruct((4, *w_small.shape), BF16),
+            jax.ShapeDtypeStruct((4, 4, 2, 8, 128), F32),
+        ],
+        in_specs=[vmem] * 3,
+        out_specs=[vmem] * 3,
+        scratch_shapes=[
+            pltpu.SemaphoreType.DMA((35,)), pltpu.SemaphoreType.DMA((35,)), pltpu.SemaphoreType.DMA((3,)),
+            pltpu.SemaphoreType.DMA((9,)), pltpu.SemaphoreType.DMA((9,)),
+        ],
+        compiler_params=pltpu.CompilerParams(
+            vmem_limit_bytes=VMEM_LIMIT, collective_id=2, has_side_effects=True
+        ),
+        cost_estimate=pl.CostEstimate(flops=int(1e6), bytes_accessed=int(4e7), transcendentals=0),
+    )(w_x, w_small, own)
+
+
+def unpack_kernel(sum_z, sum_x, sum_out, out_z, out_x, out_out, out_extra):
+    for low in range(2):
+        rows = slice(PIECE * low, PIECE * (low + 1))
+        out_z[rows, :] = sum_z[0, 0, low].astype(F32)
+        out_x[rows, :] = sum_x[0, 0, low, 0:PIECE, :].astype(F32)
+        out_out[low, 0] = sum_out[low, 0, 0].astype(F32)
+        out_extra[0, low] = sum_x[0, 0, low, PIECE:, :].astype(F32)
+
+
+def unpack(sum_z, sum_x, sum_out):
+    return call(
+        unpack_kernel,
+        [((2 * PIECE, INNER), F32), ((2 * PIECE, INNER), F32), ((2, 2, PIECE, 8 * 128), F32), ((4, 2, 4 * EXTRA, 128), F32)],
+        [
+            lanes(2 * PIECE), lanes(2 * PIECE),
+            pl.BlockSpec((2, 1, PIECE, 128), lambda i: (0, i // 8, 0, ((i // 4) % 2) * 4 + i % 4)),
+            pl.BlockSpec((1, 2, EXTRA, 128), lambda i: (i // 4, 0, i % 4, 0)),
+        ],
+        [
+            pl.BlockSpec((1, 1, 2, PIECE, 128), lambda i: (i // 4, i % 4, 0, 0, 0)),
+            pl.BlockSpec((1, 1, 2, PIECE + EXTRA, 128), lambda i: (i % 4, i // 4, 0, 0, 0)),
+            pl.BlockSpec((2, 1, 1, PIECE, 128), lambda i: (0, i % 4, i // 4, 0, 0)),
+        ],
+    )(sum_z, sum_x, sum_out)
 
 
 def swap(values):
@@ -686,13 +844,6 @@
 
 def gather_rows(shard):
     return lax.all_gather(shard, "wshard", axis=0, tiled=True)
-
-
-def by_core(rows, core):
-    cut = rows.reshape(2, 2, rows.shape[0] // 4, rows.shape[1])
-    keep = lax.dynamic_index_in_dim(cut, core, 1, keepdims=False)
-    give = lax.dynamic_index_in_dim(cut, 1 - core, 1, keepdims=False)
-    return keep.reshape(-1, rows.shape[1]), give.reshape(-1, rows.shape[1])
 
 
 def shards(
@@ -703,17 +854,19 @@
     chunks = lax.axis_size("seq")
     place = lax.axis_index("seq")
     tail = lax.ppermute(layer_in[:, TOK - (TAPS - 1) :, :], "seq", [(i, i + 1) for i in range(chunks - 1)])
-    full_x = gather_rows(w_x)
-    full_small = gather_rows(jnp.concatenate([w_bc, w_dt], axis=1))
-    full_bc, full_dt = full_small[:, : 2 * STATE], full_small[:, 2 * STATE :]
     full_z = gather_rows(w_z)
     full_out = gather_rows(w_out)
-    own = jnp.concatenate([conv_x_weight.reshape(-1), conv_x_bias, dt_bias, a_log, d_skip, jnp.zeros((61,), F32)])
-    params = lax.all_gather(own, "seq", axis=0, tiled=False)
+    own = jnp.concatenate([conv_x_weight.reshape(-1), conv_x_bias, dt_bias, a_log, d_skip, jnp.zeros((701,), F32)])
+    small = jnp.concatenate([w_bc, w_dt, jnp.zeros((w_bc.shape[0], SMALL - 2 * STATE - HEADS), BF16)], axis=1)
+    full_x, full_small, params = gather_weights(w_x, small, own.reshape(8, 128))
+    full_x = full_x.reshape(width, INNER)
+    full_small = full_small.reshape(width, SMALL)
+    params = params.reshape(HEADS, -1)
     taps_x = params[:, : TAPS * HEAD].reshape(HEADS, TAPS, HEAD).swapaxes(0, 1).reshape(TAPS, INNER)
     bias_x = params[:, TAPS * HEAD : (TAPS + 1) * HEAD].reshape(1, INNER)
     bias_dt, log_a, skip = (params[:, (TAPS + 1) * HEAD + i].reshape(1, HEADS) for i in range(3))
     bias_bc = conv_bc_bias.reshape(1, -1)
+    skip_wide = jnp.repeat(skip, HEAD, axis=1)
 
     hidden = layer_in.astype(F32).reshape(ROWS, width)
     upstream = cotangent.reshape(ROWS, width)
@@ -724,28 +877,29 @@
     inv = inv[:ROWS]
 
     x_raw = mm(normed, full_x, NN).astype(BF16)
-    bc_raw = mm(normed, full_bc, NN).astype(BF16)
-    dt_raw = mm(normed, full_dt, NN).astype(BF16)
-    xc, bcc, dt, r, u = front(x_raw, bc_raw, dt_raw, taps_x, bias_x, conv_bc_weight, bias_bc, bias_dt, log_a)
+    small_raw = mm(normed, full_small, NN).astype(BF16)
+    bc_raw, dt_raw = small_raw[:, : 2 * STATE], small_raw[:, 2 * STATE : 2 * STATE + HEADS]
+    xc, bcc, dt, r, u, dt_wide, r_wide, r_rows = front(x_raw, bc_raw, dt_raw, taps_x, bias_x, conv_bc_weight, bias_bc, bias_dt, log_a)
     decay = jnp.exp(swap(r[TOK - 1 :: TOK].T))
     u_all = swap(u)
-    y_in = inside(xc, bcc, dt, r)
+    y_in = inside(xc, bcc, dt_wide, r_wide, r_rows)
     gate = mm(normed[:ROWS], full_z, NN)
     d_mixed = mm(upstream, full_out, NT)
     start = swap(states(decay, u_all, False))
     mixed, d_y, d_gate, v, g_norm, row_dot = middle(
-        y_in, xc, bcc, r, start, skip, gate, d_mixed, gain_norm.reshape(1, INNER)
+        y_in, xc, bcc, r_wide, start, skip_wide, gate, d_mixed, gain_norm.reshape(1, INNER)
     )
     v_all = swap(v)
     layer_out = (hidden + mm(mixed, full_out, NN)).astype(BF16).reshape(SEQS, TOK, width)
-    d_stepped, d_bc_in = inside_back(xc, d_y, bcc, dt, r)
+    d_stepped, d_bc_in = inside_back(xc, d_y, bcc, dt_wide, r_wide, r_rows)
     d_normed_z = mm(d_gate, full_z, NT)
     end = swap(states(decay, v_all, True))
     d_x_raw, d_bc_raw, d_dt_raw, g_x, g_bc, g_heads = back(
-        d_stepped, xc, d_y, x_raw, start, end, bcc, dt, r, bc_raw, dt_raw, d_bc_in, row_dot,
-        taps_x, bias_x, conv_bc_weight, bias_bc, bias_dt, log_a, skip,
+        d_stepped, xc, d_y, x_raw, start, end, bcc, dt, dt_wide, r_wide, bc_raw, dt_raw, d_bc_in, row_dot,
+        taps_x, bias_x, conv_bc_weight, bias_bc, bias_dt, log_a, skip_wide,
     )
-    d_normed = mm(d_x_raw, full_x, NT) + mm(d_bc_raw, full_bc, NT) + mm(d_dt_raw, full_dt, NT)
+    d_small = jnp.concatenate([d_bc_raw, d_dt_raw, jnp.zeros((ALL, SMALL - 2 * STATE - HEADS), BF16)], axis=1)
+    d_normed = mm(d_x_raw, full_x, NT) + mm(d_small, full_small, NT)
     back_tail = d_normed[ROWS:].reshape(SEQS, HALO, width)[:, HALO - (TAPS - 1) :]
     back_tail = lax.ppermute(back_tail, "seq", [(i + 1, i) for i in range(chunks - 1)])
     d_normed = d_normed[:ROWS] + d_normed_z
@@ -759,22 +913,14 @@
     pieces = (g_x[: TAPS + 1], g_bc[: TAPS + 1], g_heads[:3], g_in, g_norm)
     sizes = [p.size for p in pieces]
     vector = jnp.concatenate([*(p.reshape(-1) for p in pieces), jnp.zeros((PIECE * 128 - sum(sizes),), F32)])
-    core = lax.axis_index("wshard") % 2
-    keep_n, give_n = by_core(normed.T, core)
-    keep_m, give_m = by_core(mixed.T, core)
-    d_small = jnp.concatenate([d_bc_raw, d_dt_raw, jnp.zeros((ALL, SMALL - 2 * STATE - HEADS), BF16)], axis=1)
-    sum_z, sum_x, sum_out = reduce_grads(
-        keep_n, give_n, d_gate, d_x_raw, d_small, keep_m, give_m, upstream, vector.reshape(PIECE, 128)
+    grad_w_z, grad_w_x, grad_w_out, extra = unpack(
+        *reduce_grads(normed, d_gate, d_x_raw, d_small, mixed, upstream, vector.reshape(PIECE, 128))
     )
-    grad_w_z = sum_z.transpose(2, 3, 0, 1, 4).reshape(2 * PIECE, INNER).astype(F32)
-    grad_w_x = sum_x[:, :, :, :PIECE].transpose(2, 3, 1, 0, 4).reshape(2 * PIECE, INNER).astype(F32)
-    extra = sum_x[:, :, :, PIECE:].transpose(1, 2, 0, 3, 4).reshape(4, 2 * PIECE, 128).astype(F32)
+    grad_w_out = grad_w_out.reshape(4 * PIECE, width)
+    extra = extra.reshape(4, 2 * PIECE, 128)
     grad_w_bc = jnp.concatenate([extra[0], extra[1]], axis=1)
     grad_w_dt = extra[2][:, :HEADS]
     total = extra[3][:PIECE].reshape(-1)[: sum(sizes)]
-    grad_w_out = (
-        sum_out.reshape(2, 4, 2, 2, PIECE, 128).transpose(0, 2, 4, 3, 1, 5).reshape(4 * PIECE, width).astype(F32)
-    )
     ends = [sum(sizes[: i + 1]) for i in range(len(sizes) - 1)]
     s_x, s_bc, s_heads, s_in, s_norm = jnp.split(total, ends)
     s_x = lax.dynamic_slice(s_x.reshape(TAPS + 1, INNER), (0, place * HEAD), (TAPS + 1, HEAD))

time: 501 us -> 367 us (0.73)
  blocking collectives: 127 us -> 36.8 us
  local copies, waits for them, and re-layouts: 72.9 us -> 38.7 us
    all_gather x2 -> x0, blocking collectives: 91.6 us -> none  [the longest x1 81.5 us: shards(): params = lax.all_gather(own, 'seq', axis=0, tiled=False)]
    pallas_call x1 -> x3, Pallas kernels: 92.1 us -> 126 us  [the longest x1 93.6 us: reduce_grads(): pl.pallas_call(reduce_kernel, out_shape=out_shape, in_specs=[vmem] * 7, o...]
    pallas_call x1, Pallas kernels: 33.2 us -> 16.1 us  [back(): call(back_kernel, [((ALL, INNER), BF16), ((ALL, 2 * STATE), BF16), ((ALL,...]
    convert_element_type x7 -> x0, local copies, waits for them, and re-layouts: 16.2 us -> none  [the longest x2 7.28 us: shards(): sum_x[:, :, :, :PIECE].transpose(2, 3, 1, 0, 4).reshape(2 * PIECE, INNER)]
    dynamic_slice x4 -> x0, local copies, waits for them, and re-layouts: 12.9 us -> none  [the longest x3 10.9 us: by_core(): give = lax.dynamic_index_in_dim(cut, 1 - core, 1, keepdims=False)]
    pallas_call x1, Pallas kernels: 18.4 us -> 12.3 us  [inside_back(): call(inside_back_kernel, [((ROWS, INNER), F32), ((ROWS, 2 * STATE), F32)]...]
    unnamed x148 -> x134, local copies, waits for them, and re-layouts: 30.5 us -> 25.5 us
    dot_general x10 -> x8, matrix products: 26.9 us -> 22.5 us  [mm(): lax.dot_general(a, b, ((dims[0], dims[1]), ((), ())), precision=precision...]
  transfers between devices with their start and end apart: 8 -> 7, of which waited for: 2 -> 2; matrix products, arithmetic and copies ran while one was open for 9% -> 7% of each run, Pallas kernels for 10% -> 18%
where the time goes in v3:
time: 367 us; the launch traced here: 364 us
  Pallas kernels  206 us (56%)
  local copies, waits for them, and re-layouts  38.7 us (11%)
  blocking collectives  36.8 us (10%)
  matrix products  22.5 us (6%)
  waiting for transfers between devices  19.5 us (5%)
  starting transfers between devices  19 us (5%)
  between operations  16.8 us (5%)
  other arithmetic  4.62 us (1%)
    pallas_call x1, Pallas kernels, reduce_grads(): pl.pallas_call(reduce_kernel, out_shape=out_shape, in_specs=[vmem] * 7, o...  93.6 us
    all_to_all x2, blocking collectives, swap(): lax.all_to_all(values, 'seq', split_axis=0, concat_axis=0, tiled=True)  36.8 us
    pallas_call x1, Pallas kernels, gather_weights(): pl.pallas_call(gather_kernel, out_shape=[jax.ShapeDtypeStruct((4, *w_x.sh...  26.4 us
    unnamed x134, local copies, waits for them, and re-layouts  25.5 us
    pallas_call x1, Pallas kernels, middle(): call(middle_kernel, [((ROWS, INNER), BF16), ((ROWS, INNER), BF16), ((ROWS...  24 us
    dot_general x8, matrix products, mm(): lax.dot_general(a, b, ((dims[0], dims[1]), ((), ())), precision=precision...  22.5 us
    pallas_call x1, Pallas kernels, back(): call(back_kernel, [((ALL, INNER), BF16), ((ALL, 2 * STATE), BF16), ((ALL,...  16.1 us
    all_to_all x3, waiting for transfers between devices, swap(): lax.all_to_all(values, 'seq', split_axis=0, concat_axis=0, tiled=True)  15.9 us
  transfers between devices with their start and end apart: 7, of which 2 were waited for; matrix products, arithmetic and copies ran while one was open for 7% of the time, Pallas kernels for 18%

profile of v3, /device:TPU:0, one launch (start us, length us, event | category | flops | bytes accessed | tf_op | source)
XLA Modules:
  0.0 364.2 jit_solution(15014117963868123859)
XLA Ops:
  7.3 0.7 all-gather.3.cloned.1.call-update
  8.0 0.7 all-gather.5.cloned.1.call-update
  9.4 4.2 %collective-permute-start = (bf16[2,3,1024]{2,1,0:T(4,128)(2,1)}, bf16[2,3,1024]{2,1,0:T(4,128)(2,1)}, u32[]{:S(2)}, u32[]{:S(2)}) collective-permute-start(bf16[2,3,1024]{2,1,0:T(4,128)(2,1)} %slice.121), channel_id=1, source_target_pairs={{0,4},{4,8},{8,12},{12,16},{16,20},{20,24},{24,28},{28,32},{32,36}... | collective-permute-start | bytes 36872 | tf_op jit(solution)/shard_map/ppermute | solution.py:856
  16.3 26.4 %shard_map.279 = (bf16[4,256,2048]{2,1,0:T(8,128)(2,1)}, bf16[4,256,384]{2,1,0:T(8,128)(2,1)S(1)}, f32[4,4,2,8,128]{4,3,2,1,0:T(8,128)S(1)}) custom-call(bf16[256,2048]{1,0:T(8,128)(2,1)S(1)} %copy-done.9, bf16[256,384]{1,0:T(8,128)(2,1)S(1)} %maximum_maximum_fusion.1.w_small, f32[8,128]{1,0:T(8,128)S(1)} %bitcast.89), custom_call_target="tpu_custom_call" | custom-call | flops 1000000 | bytes 40000000 | tf_op jit(solution)/shard_map/pallas_call | solution.py:795
  42.7 0.8 fusion.5
  45.0 0.7 reshape.181.taps_x
  45.8 0.7 bitcast_convert_fusion
  47.4 1.5 copy-done.62
  49.0 1.3 convolution_convert_fusion.x_raw
  50.4 13.3 %shard_map.280 = (bf16[256,2048]{1,0:T(8,128)(2,1)S(1)}, bf16[256,256]{1,0:T(8,128)(2,1)S(1)}, f32[256,32]{1,0:T(8,128)S(1)}, f32[256,32]{1,0:T(8,128)S(1)}, bf1...) custom-call(bf16[272,2048]{1,0:T(8,128)(2,1)S(1)} %convolution_conve, ...), custom_call_target="tpu_custom_call" | custom-call | flops 1000000000 | bytes 10000000 | tf_op jit(solution)/shard_map/pallas_call | solution.py:180
  63.7 1.0 copy-done.8
  64.7 1.0 copy-done.10
  67.0 0.9 slice.128
  67.9 0.7 copy.62
  68.6 12.7 %all_to_all.29 = f32[32,1,2]{2,1,0:T(1,128)} all-to-all(f32[32,1,2]{2,1,0:T(1,128)} %copy.62), channel_id=1, replica_groups=mesh['seq'=32,'wshard'=4] {'seq'}, dimensions={0} | all-to-all | bytes 512 | tf_op jit(solution)/shard_map/all_to_all | solution.py:842
  81.4 4.7 %all-to-all-start.1 = ((bf16[32,2,64,128]{3,2,1,0:T(8,128)(2,1)}), bf16[32,2,64,128]{3,2,1,0:T(8,128)(2,1)}, u32[]{:S(2)}, u32[]{:S(2)}) async-start(bf16[32,2,64,128]{3,2,1,0:T(8,128)(2,1)} %copy-done.10), calls=%async_computation.1 | async-start | bytes 2097152 | tf_op jit(solution)/shard_map/all_to_all | solution.py:842
  86.0 0.8 copy.63
  86.8 0.7 copy.64.decay
  87.6 15.9 %all-to-all-done.1.own = bf16[32,2,64,128]{3,2,1,0:T(8,128)(2,1)} async-done(((bf16[32,2,64,128]{3,2,1,0:T(8,128)(2,1)}), bf16[32,2,64,128]{3,2,1,0:T(8,128)(2,1)}, u32[]{:S(2)}, u32[]{:S(2)}) %all-to-all-start.1) | async-done | bytes 1048608 | tf_op jit(solution)/shard_map/all_to_all | solution.py:842
  103.4 0.7 copy-done.17
  104.1 1.5 shard_map.282
  105.7 1.0 copy-done.2
  106.7 4.7 %all-to-all-start.2 = ((bf16[32,2,64,128]{3,2,1,0:T(8,128)(2,1)}), bf16[32,2,64,128]{3,2,1,0:T(8,128)(2,1)}, u32[]{:S(2)}, u32[]{:S(2)}) async-start(bf16[32,2,64,128]{3,2,1,0:T(8,128)(2,1)} %copy-done.2), calls=%async_computation.2 | async-start | bytes 2097152 | tf_op jit(solution)/shard_map/all_to_all | solution.py:842
  111.3 0.8 copy.70
  112.1 0.7 broadcast_in_dim.23
  112.8 0.8 broadcast_in_dim.24.d_skip
  113.6 10.7 %shard_map.281.y_in = f32[256,2048]{1,0:T(8,128)S(1)} custom-call(bf16[256,2048]{1,0:T(8,128)(2,1)S(1)} %get-tuple-element.51.xc, bf16[256,256]{1,0:T(8,128)(2,1)S(1)} %get-tuple-element.52.bcc, f32[256,2048]{1,0:T(8,128)S(1)} %get-tuple-element.53.dt_wide, f32[256,2048]{1,0:T(8,128)} %get-tuple-element.54.r_wide.r, f32[16,8,256]{2,1,0:T(8,128)S(1)} %get-tuple-element.55.r_rows), custom_call_target="tpu_custom_call" | custom-call | flops 1000000000 | bytes 10000000 | tf_op jit(solution)/shard_map/pallas_call | solution.py:235
  124.3 1.3 copy-done.1
  125.6 5.0 %fusion.1.gate = f32[256,2048]{1,0:T(8,128)} fusion(bf16[1024,2048]{1,0:T(8,128)(2,1)} %all-gather.3.cloned.1.call-done, bf16[272,1024]{1,0:T(8,128)(2,1)} %copy-done.5), kind=kOutput, calls=%fused_computation.13 | convolution fusion | flops 1073741824 | bytes 6815744 | tf_op jit(solution)/shard_map/dot_general | solution.py:28
  130.6 4.8 %fusion.7.d_mixed = f32[256,2048]{1,0:T(8,128)} fusion(bf16[256,1024]{1,0:T(8,128)(2,1)S(1)} %bitcast.84, bf16[2048,1024]{1,0:T(8,128)(2,1)} %all-gather.5.cloned.1.call-done), kind=kOutput, calls=%fused_computation.34 | convolution fusion | flops 1073741824 | bytes 6815744 | tf_op jit(solution)/shard_map/dot_general | solution.py:28
  135.4 24.0 %shard_map.283 = (bf16[256,2048]{1,0:T(8,128)(2,1)S(1)}, bf16[256,2048]{1,0:T(8,128)(2,1)S(1)}, bf16[256,2048]{1,0:T(8,128)(2,1)S(1)}, bf16[32,2,64,128]{3,2,1,0...) custom-call(f32[256,2048]{1,0:T(8,128)} %copy-done.1, bf16[256,2048]{1,0:T(8,128)(2,1)S(1)} %get-tuple-element.51.xc, ...), custom_call_target="tpu_custom_call" | custom-call | flops 1000000000 | bytes 10000000 | tf_op jit(solution)/shard_map/pallas_call | solution.py:315
  159.5 1.0 copy-done.39
  160.4 1.0 copy-done.41
  161.4 24.1 %all_to_all.30.own = bf16[32,2,64,128]{3,2,1,0:T(8,128)(2,1)S(1)} all-to-all(bf16[32,2,64,128]{3,2,1,0:T(8,128)(2,1)S(1)} %get-tuple-element.61), channel_id=1, replica_groups=mesh['seq'=32,'wshard'=4] {'seq'}, dimensions={0} | all-to-all | bytes 2097152 | tf_op jit(solution)/shard_map/all_to_all | solution.py:842
  185.5 2.1 shard_map.285
  187.6 4.1 %all-to-all-start.4 = ((bf16[32,2,64,128]{3,2,1,0:T(8,128)(2,1)}), bf16[32,2,64,128]{3,2,1,0:T(8,128)(2,1)S(1)}, u32[]{:S(2)}, u32[]{:S(2)}) async-start(bf16[32,2,64,128]{3,2,1,0:T(8,128)(2,1)} %shard_map.285), calls=%async_computation.4 | async-start | bytes 2097152 | tf_op jit(solution)/shard_map/all_to_all | solution.py:842
  191.8 1.2 slice.131
  193.0 12.3 %shard_map.284 = (f32[256,2048]{1,0:T(8,128)S(1)}, f32[256,256]{1,0:T(8,128)S(1)}) custom-call(bf16[256,2048]{1,0:T(8,128)(2,1)S(1)} %get-tuple-element.51.xc, bf16[256,2048]{1,0:T(8,128)(2,1)S(1)} %get-tuple-element.59.d_y, bf16[256,256]{1,0:T(8,128)(2,1)S(1)} %get-tuple-element.52.bcc, f32[256,2048]{1,0:T(8,128)} %copy-done, ...), custom_call_target="tpu_custom_call" | custom-call | flops 1000000000 | bytes 10000000 | tf_op jit(solution)/shard_map/pallas_call | solution.py:356
  205.3 1.3 copy-done.7
  206.6 0.7 copy-done.15
  207.3 0.9 copy-done.14
  208.2 0.9 copy-done.16
  209.2 0.8 copy-done.20
  209.9 0.9 copy-done.22
  210.8 0.9 copy-done.24
  211.7 0.7 copy-done.26
  212.4 0.7 copy-done.31
  213.8 0.7 copy-done.35
  214.4 0.7 copy-done.37
  215.1 16.1 %shard_map.286 = (bf16[272,2048]{1,0:T(8,128)(2,1)}, bf16[272,256]{1,0:T(8,128)(2,1)S(1)}, bf16[272,32]{1,0:T(8,128)(2,1)S(1)}, f32[8,2048]{1,0:T(8,128)S(1)}, f...) custom-call(f32[256,2048]{1,0:T(8,128)} %copy-done.7, bf16[256,2048]{1,0:T(8,128)(2,1)S(1)} %get-tuple-element.51.xc, ...), custom_call_target="tpu_custom_call" | custom-call | flops 1000000000 | bytes 10000000 | tf_op jit(solution)/shard_map/pallas_call | solution.py:450
  231.3 2.8 fusion.8
  234.7 1.3 collective-permute-start.1
  236.1 2.1 fusion
  238.3 2.2 collective-permute-done.1
  240.7 5.6 %multiply_reduce_fusion.1 = (f32[1024]{0:T(1024)S(1)}, f32[256]{0:T(256)S(1)}, f32[256,1024]{1,0:T(8,128)}) fusion(f32[256]{0:T(256)S(1)} %copy-done.58, bf16[2,128,1024]{2,1,0:T(8,128)(2,1)S(1)} %copy-done.48, f32[2,128,1024]{2,1,0:T(8,128)S(1)} %pad.9, f32[1024]{0:T(1024)S(1)} %copy-done.53, bf16[256,2048]{1,0:T(8,128)(2,1)} %copy-done.41, ...), kind=kOutput, calls=%fused_computation.10 | convolution fusion | flops 1076099840 | bytes 8923136 | tf_op jit(solution)/shard_map/dot_general | solution.py:28
  246.4 1.2 copy-done.42
  247.6 93.6 %shard_map.287 = (bf16[4,4,2,128,128]{4,3,2,1,0:T(8,128)(2,1)S(1)}, bf16[4,4,2,160,128]{4,3,2,1,0:T(8,128)(2,1)}, bf16[2,4,4,128,128]{4,3,2,1,0:T(8,128)(2,1)S(1)}) custom-call(bf16[272,1024]{1,0:T(8,128)(2,1)S(1)} %copy-done.6, bf16[256,2048]{1,0:T(8,128)(2,1)S(1)} %copy-done.42, bf16[272,2048]{1,0:T(8,128)(2,1)} %get-tuple-element.65.d_wide, ...), custom_call_target="tpu_custom_call" | custom-call | flops 4000000000 | bytes 40000000 | tf_op jit(solution)/shard_map/pallas_call | solution.py:692
  341.2 1.3 copy-done.43
  342.5 6.3 %shard_map.288 = (f32[256,2048]{1,0:T(8,128)}, f32[256,2048]{1,0:T(8,128)}, f32[2,2,128,1024]{3,2,1,0:T(8,128)}, f32[4,2,128,128]{3,2,1,0:T(8,128)S(1)}) custom-call(bf16[4,4,2,128,128]{4,3,2,1,0:T(8,128)(2,1)S(1)} %get-tuple-element.73.sum_z, bf16[4,4,2,160,128]{4,3,2,1,0:T(8,128)(2,1)S(1)} %copy-done.43, ...), custom_call_target="tpu_custom_call" | custom-call | flops 1000000000 | bytes 10000000 | tf_op jit(solution)/shard_map/pallas_call | solution.py:825
  348.9 0.7 split.25
  349.6 0.7 split.23
  352.0 0.7 copy.71
  354.0 0.7 pad_maximum_fusion.1
  354.8 2.6 multiply_add_fusion
  (164 shorter events, 10.0 us)
Async XLA Ops:
  7.2 1.5 copy-start.46
  7.2 6.3 %copy-start.54 = (bf16[256,32]{0,1:T(8,128)(2,1)S(1)}, bf16[256,32]{0,1:T(8,128)(2,1)}, u32[]{:S(2)}) copy-start(bf16[256,32]{0,1:T(8,128)(2,1)} %param.21) | copy-start | bytes 49156
  7.2 6.4 %copy-start.59 = (f32[4,64]{1,0:T(4,128)S(1)}, f32[4,64]{1,0:T(4,128)}, u32[]{:S(2)}) copy-start(f32[4,64]{1,0:T(4,128)} %param.22) | copy-start | bytes 3076
  7.2 8.5 %copy-start.60 = (f32[64]{0:T(128)S(1)}, f32[64]{0:T(128)}, u32[]{:S(2)}) copy-start(f32[64]{0:T(128)} %param.23) | copy-start | bytes 772
  7.2 8.6 %copy-start.51 = (bf16[256,256]{1,0:T(8,128)(2,1)S(1)}, bf16[256,256]{1,0:T(8,128)(2,1)}, u32[]{:S(2)}) copy-start(bf16[256,256]{1,0:T(8,128)(2,1)} %param.20) | copy-start | bytes 393220
  7.2 9.1 %copy-start.9 = (bf16[256,2048]{1,0:T(8,128)(2,1)S(1)}, bf16[256,2048]{1,0:T(8,128)(2,1)}, u32[]{:S(2)}) copy-start(bf16[256,2048]{1,0:T(8,128)(2,1)} %w_x.1) | copy-start | bytes 3145732
  7.2 118.4 %all-gather.3.cloned.1.call-start = ((), (), s32[]{:S(2)}) async-start(), calls=%async_computation.5 | async-start | bytes 5242880 | tf_op jit(solution)/shard_map/all_gather | solution.py:846
  8.0 122.6 %all-gather.5.cloned.1.call-start = ((), (), s32[]{:S(2)}) async-start(), calls=%async_computation.6 | async-start | bytes 5242880 | tf_op jit(solution)/shard_map/all_gather | solution.py:846
  9.4 36.4 %collective-permute-start = (bf16[2,3,1024]{2,1,0:T(4,128)(2,1)}, bf16[2,3,1024]{2,1,0:T(4,128)(2,1)}, u32[]{:S(2)}, u32[]{:S(2)}) collective-permute-start(bf16[2,3,1024]{2,1,0:T(4,128)(2,1)} %slice.121), channel_id=1, source_target_pairs={{0,4},{4,8},{8,12},{12,16},{16,20},{20,24},{24,28},{28,32},{32,36}... | collective-permute-start | bytes 36872 | tf_op jit(solution)/shard_map/ppermute | solution.py:856
  42.7 4.2 %copy-start.3 = (bf16[4,256,384]{2,1,0:T(8,128)(2,1)}, bf16[4,256,384]{2,1,0:T(8,128)(2,1)S(1)}, u32[]{:S(2)}) copy-start(bf16[4,256,384]{2,1,0:T(8,128)(2,1)S(1)} %get-tuple-element.49) | copy-start | bytes 2359300
  42.7 4.0 %copy-start.52 = (f32[1024]{0:T(1024)S(1)}, f32[1024]{0:T(1024)}, u32[]{:S(2)}) copy-start(f32[1024]{0:T(1024)} %param.17) | copy-start | bytes 12292
  45.8 4.5 %copy-start.25 = (f32[1,2048]{1,0:T(1,128)}, f32[1,2048]{1,0:T(1,128)S(1)}, u32[]{:S(2)}) copy-start(f32[1,2048]{1,0:T(1,128)S(1)} %reshape.182.bias_x) | copy-start | bytes 24580
  46.5 2.4 copy-start.62
  46.7 3.6 copy-start.55
  46.9 3.4 copy-start.5
  47.4 2.9 copy-start.13
  48.9 1.4 copy-start.19
  48.9 1.4 copy-start.30
  48.9 1.4 copy-start.32
  48.9 1.4 copy-start.34
  49.0 1.4 copy-start.36
  63.7 1.0 copy-start.8
  64.7 1.0 copy-start.10
  67.0 46.6 %copy-start = (f32[256,2048]{1,0:T(8,128)}, f32[256,2048]{1,0:T(8,128)S(1)}, u32[]{:S(2)}) copy-start(f32[256,2048]{1,0:T(8,128)S(1)} %get-tuple-element.53.dt_wide) | copy-start | bytes 6291460
  81.4 22.1 %all-to-all-start.1 = ((bf16[32,2,64,128]{3,2,1,0:T(8,128)(2,1)}), bf16[32,2,64,128]{3,2,1,0:T(8,128)(2,1)}, u32[]{:S(2)}, u32[]{:S(2)}) async-start(bf16[32,2,64,128]{3,2,1,0:T(8,128)(2,1)} %copy-done.10), calls=%async_computation.1 | async-start | bytes 2097152 | tf_op jit(solution)/shard_map/all_to_all | solution.py:842
  103.4 0.7 copy-start.17
  105.7 1.0 copy-start.2
  106.7 28.7 %all-to-all-start.2 = ((bf16[32,2,64,128]{3,2,1,0:T(8,128)(2,1)}), bf16[32,2,64,128]{3,2,1,0:T(8,128)(2,1)}, u32[]{:S(2)}, u32[]{:S(2)}) async-start(bf16[32,2,64,128]{3,2,1,0:T(8,128)(2,1)} %copy-done.2), calls=%async_computation.2 | async-start | bytes 2097152 | tf_op jit(solution)/shard_map/all_to_all | solution.py:842
  124.3 1.3 copy-start.1
  125.6 5.0 %copy-start.11 = (bf16[2,128,1024]{2,1,0:T(8,128)(2,1)S(1)}, bf16[2,128,1024]{2,1,0:T(8,128)(2,1)}, u32[]{:S(2)}) copy-start(bf16[2,128,1024]{2,1,0:T(8,128)(2,1)} %param.31) | copy-start | bytes 1572868
  130.6 4.8 %copy-start.29 = (f32[2048]{0:T(1024)S(1)}, f32[2048]{0:T(1024)}, u32[]{:S(2)}) copy-start(f32[2048]{0:T(1024)} %param.29) | copy-start | bytes 24580
  159.5 1.0 copy-start.39
  160.4 1.0 copy-start.41
  161.4 24.1 %copy-start.23 = (f32[256,32]{1,0:T(8,128)}, f32[256,32]{1,0:T(8,128)S(1)}, u32[]{:S(2)}) copy-start(f32[256,32]{1,0:T(8,128)S(1)} %get-tuple-element.64.row_dot) | copy-start | bytes 98308
  161.4 24.1 %copy-start.27 = (f32[1,2048]{1,0:T(1,128)}, f32[1,2048]{1,0:T(1,128)S(1)}, u32[]{:S(2)}) copy-start(f32[1,2048]{1,0:T(1,128)S(1)} %get-tuple-element.72) | copy-start | bytes 24580
  161.4 24.1 %copy-start.18 = (f32[32,2]{1,0:T(8,128)S(1)}, f32[32,2]{1,0:T(8,128)}, u32[]{:S(2)}) copy-start(f32[32,2]{1,0:T(8,128)} %copy.64.decay) | copy-start | bytes 772
  187.6 19.7 %all-to-all-start.4 = ((bf16[32,2,64,128]{3,2,1,0:T(8,128)(2,1)}), bf16[32,2,64,128]{3,2,1,0:T(8,128)(2,1)S(1)}, u32[]{:S(2)}, u32[]{:S(2)}) async-start(bf16[32,2,64,128]{3,2,1,0:T(8,128)(2,1)} %shard_map.285), calls=%async_computation.4 | async-start | bytes 2097152 | tf_op jit(solution)/shard_map/all_to_all | solution.py:842
  205.3 1.3 copy-start.7
  206.6 0.7 copy-start.15
  207.3 0.9 copy-start.14
  208.2 0.9 copy-start.16
  209.2 0.8 copy-start.20
  209.9 0.9 copy-start.22
  210.8 0.9 copy-start.24
  211.7 0.7 copy-start.26
  215.1 16.1 %copy-start.63 = (bf16[4,256,2048]{2,1,0:T(8,128)(2,1)S(1)}, bf16[4,256,2048]{2,1,0:T(8,128)(2,1)}, u32[]{:S(2)}) copy-start(bf16[4,256,2048]{2,1,0:T(8,128)(2,1)} %get-tuple-element.48) | copy-start | bytes 12582916
  231.3 2.8 copy-start.57
  231.3 2.9 copy-start.4
  231.3 4.7 %copy-start.61 = (bf16[2048,1024]{1,0:T(8,128)(2,1)S(1)}, bf16[2048,1024]{1,0:T(8,128)(2,1)}, u32[]{:S(2)}) copy-start(bf16[2048,1024]{1,0:T(8,128)(2,1)} %all-gather.5.cloned.1.call-done) | copy-start | bytes 12582916
  234.0 2.0 copy-start.40
  234.1 2.0 copy-start.47
  234.6 1.3 copy-start.50
  234.7 5.8 %collective-permute-start.1 = (f32[2,3,1024]{2,1,0:T(4,128)S(1)}, f32[2,3,1024]{2,1,0:T(4,128)S(1)}, u32[]{:S(2)}, u32[]{:S(2)}) collective-permute-start(f32[2,3,1024]{2,1,0:T(4,128)S(1)} %slice.162), channel_id=1, source_target_pairs={{4,0},{8,4},{12,8},{16,12},{20,16},{24,20},{28,24},{32,28},{36,32}... | collective-permute-start | bytes 73736 | tf_op jit(solution)/shard_map/ppermute | solution.py:904
  236.0 4.6 %copy-start.48 = (bf16[2,128,1024]{2,1,0:T(8,128)(2,1)S(1)}, bf16[2,128,1024]{2,1,0:T(8,128)(2,1)}, u32[]{:S(2)}) copy-start(bf16[2,128,1024]{2,1,0:T(8,128)(2,1)} %param.16) | copy-start | bytes 1572868
  236.0 4.6 %copy-start.53 = (f32[1024]{0:T(1024)S(1)}, f32[1024]{0:T(1024)}, u32[]{:S(2)}) copy-start(f32[1024]{0:T(1024)} %param.17) | copy-start | bytes 12292
  236.0 4.6 %copy-start.58 = (f32[256]{0:T(256)S(1)}, f32[256]{0:T(256)}, u32[]{:S(2)}) copy-start(f32[256]{0:T(256)} %slice.131) | copy-start | bytes 3076
  240.6 5.7 %copy-start.44 = (f32[2,128,1024]{2,1,0:T(8,128)}, f32[2,128,1024]{2,1,0:T(8,128)S(1)}, u32[]{:S(2)}) copy-start(f32[2,128,1024]{2,1,0:T(8,128)S(1)} %pad.9) | copy-start | bytes 3145732
  240.6 5.7 %copy-start.28 = (f32[1,2048]{1,0:T(1,128)S(1)}, f32[1,2048]{1,0:T(1,128)}, u32[]{:S(2)}) copy-start(f32[1,2048]{1,0:T(1,128)} %copy-done.27) | copy-start | bytes 24580
  240.7 5.7 %copy-start.6 = (bf16[272,1024]{1,0:T(8,128)(2,1)S(1)}, bf16[272,1024]{1,0:T(8,128)(2,1)}, u32[]{:S(2)}) copy-start(bf16[272,1024]{1,0:T(8,128)(2,1)} %copy-done.5) | copy-start | bytes 1671172
  240.7 5.7 %copy-start.12 = (bf16[2,128,1024]{2,1,0:T(8,128)(2,1)S(1)}, bf16[2,128,1024]{2,1,0:T(8,128)(2,1)}, u32[]{:S(2)}) copy-start(bf16[2,128,1024]{2,1,0:T(8,128)(2,1)} %param.31) | copy-start | bytes 1572868
  246.4 1.2 copy-start.42
  341.2 1.3 copy-start.43
  342.5 12.2 %copy-start.45 = (f32[2,128,1024]{2,1,0:T(8,128)S(1)}, f32[2,128,1024]{2,1,0:T(8,128)}, u32[]{:S(2)}) copy-start(f32[2,128,1024]{2,1,0:T(8,128)} %copy-done.44) | copy-start | bytes 3145732
  342.5 12.2 %copy-start.49 = (bf16[2,128,1024]{2,1,0:T(8,128)(2,1)S(1)}, bf16[2,128,1024]{2,1,0:T(8,128)(2,1)}, u32[]{:S(2)}) copy-start(bf16[2,128,1024]{2,1,0:T(8,128)(2,1)} %param.16) | copy-start | bytes 1572868
  (7 other events, 4.5 us)
Sparse Core Ops, SparseCore 0:
  9.7 40.9 all-gather.2
  52.4 41.7 all-gather.4

commit v4 on v3

--- a/solution.py
+++ b/solution.py
@@ -322,154 +322,14 @@
     )(y_in, xc, bcc, r, start, d_skip, gate, d_mixed, gain)
 
 
-def inside_back_kernel(xc, d_y, bcc, dt_wide, r_wide, r_rows, d_stepped, d_bc, scores, d_scores):
-    pair = pl.program_id(0)
-
-    @pl.when(pair == 0)
-    def _():
-        d_scores[...] = jnp.zeros_like(d_scores)
-        for b in range(SEQS):
-            span = slice(TOK * b, TOK * (b + 1))
-            scores[b] = mm(bcc[span, STATE:], bcc[span, 0:STATE], NT)
-
-    for b in range(SEQS):
-        span = slice(TOK * b, TOK * (b + 1))
-        dt_lanes = dt_wide[span, :]
-        first, second = decay_pair(r_wide[span, :], r_rows[0, :, span])
-        both = jnp.concatenate([scores[b] * first, scores[b] * second], axis=0).astype(BF16)
-        stepped = (dt_lanes * xc[span, :].astype(F32)).astype(BF16)
-        wide = block_diagonal(d_y[span, :])
-        d_stepped[span, :] = mm(both, wide, TN)
-        d_both = mm(wide, stepped, NT)
-        d_scores[b] += d_both[0:TOK, :] * first + d_both[TOK:, :] * second
-
-    @pl.when(pair == PAIRS - 1)
-    def _():
-        for b in range(SEQS):
-            span = slice(TOK * b, TOK * (b + 1))
-            low = d_scores[b].astype(BF16)
-            d_bc[span, 0:STATE] = mm(low, bcc[span, STATE:], TN)
-            d_bc[span, STATE:] = mm(low, bcc[span, 0:STATE], NN)
-
-
-def inside_back(xc, d_y, bcc, dt_wide, r_wide, r_rows):
-    return call(
-        inside_back_kernel,
-        [((ROWS, INNER), F32), ((ROWS, 2 * STATE), F32)],
-        [lanes(ROWS), whole((ROWS, 2 * STATE))],
-        [lanes(ROWS), lanes(ROWS), whole((ROWS, 2 * STATE)), lanes(ROWS), lanes(ROWS), PAIR_ROWS],
-        scratch=[pltpu.VMEM((SEQS, TOK, TOK), F32)] * 2,
-    )(xc, d_y, bcc, dt_wide, r_wide, r_rows)
-
-
-def back_kernel(
-    d_stepped, xc, d_y, x_raw, start, end, bcc, dt, dt_wide, r_wide, bc_raw, dt_raw, d_bc_in, row_dot,
-    taps_x, bias_x, taps_bc, bias_bc, dt_bias, a_log, d_skip,
-    d_x_raw, d_bc_raw, d_dt_raw, g_x, g_bc, g_heads,
-    d_bc, sums,
-):
-    pair = pl.program_id(0)
-
-    @pl.when(pair == 0)
-    def _():
-        d_bc[...] = d_bc_in[...]
-        sums[...] = jnp.zeros_like(sums)
-
-    ex = pair_matrix(pair)
-    skip = d_skip[...]
-    raw = x_raw[...].astype(F32)
-    halos, grads = [], None
-    d_steps, cols, end_rows = [], [], []
-    skip_sum = jnp.zeros((1, 128), F32)
-    for b in range(SEQS):
-        span = slice(TOK * b, TOK * (b + 1))
-        r_lanes = r_wide[span, :]
-        dt_lanes = dt_wide[span, :]
-        last = r_lanes[TOK - 1 : TOK, :]
-        grown = jnp.exp(r_lanes)
-        to_end = jnp.exp(last - r_lanes)
-        before = jnp.concatenate([start[0, b], start[1, b]], axis=0)
-        after = jnp.concatenate([end[0, b], end[1, b]], axis=0)
-        x = xc[span, :].astype(F32)
-        dy = d_y[span, :].astype(F32)
-        stepped = (dt_lanes * x).astype(BF16).astype(F32)
-        carried = to_end * mm(bcc[span, 0:STATE], after, NT)
-        d_step = d_stepped[span, :] + carried
-        cols.append(stepped * d_step)
-        d_x = dt_lanes * d_step + skip * dy
-        d_steps.append(x * d_step)
-        inner = lane_sums(before.astype(F32) * after.astype(F32))
-        end_rows.append(jnp.sum(stepped * carried, axis=0, keepdims=True) + jnp.exp(last) * inner)
-        d_bc[span, STATE:] += mm((grown * dy).astype(BF16), before, NN)
-        d_bc[span, 0:STATE] += mm((to_end * stepped).astype(BF16), after, NN)
-        skip_sum = skip_sum + jnp.sum(dy * x, axis=0, keepdims=True)
-        d_pad, d_taps, d_bias = conv_back(padded_of(raw, b), taps_x[...], bias_x[...], d_x)
-        d_x_raw[span, :] = d_pad[HALO:, :].astype(BF16)
-        halos.append(d_pad[0:HALO, :])
-        parts = [*d_taps, d_bias]
-        grads = parts if grads is None else [g + p for g, p in zip(grads, parts)]
-    d_x_raw[ROWS:, :] = jnp.concatenate(halos, axis=0).astype(BF16)
-    g_x[...] = jnp.concatenate([*grads, jnp.zeros((8 - TAPS - 1, 128), F32)], axis=0)
-    few = jnp.concatenate([*end_rows, skip_sum, jnp.zeros((5, 128), F32)], axis=0)
-    sums[...] += head_sums(jnp.concatenate([*d_steps, *cols, few], axis=0), ex)
-
-    @pl.when(pair == PAIRS - 1)
-    def _():
-        raw = bc_raw[...].astype(F32)
-        halos, grads = [], None
-        for b in range(SEQS):
-            span = slice(TOK * b, TOK * (b + 1))
-            d_pad, d_taps, d_bias = conv_back(padded_of(raw, b), taps_bc[...], bias_bc[...], d_bc[span, :])
-            d_bc_raw[span, :] = d_pad[HALO:, :].astype(BF16)
-            halos.append(d_pad[0:HALO, :])
-            parts = [*d_taps, d_bias]
-            grads = parts if grads is None else [g + p for g, p in zip(grads, parts)]
-        d_bc_raw[ROWS:, :] = jnp.concatenate(halos, axis=0).astype(BF16)
-        g_bc[...] = jnp.concatenate([*grads, jnp.zeros((8 - TAPS - 1, 2 * STATE), F32)], axis=0)
-        rate = -jnp.exp(a_log[...])
-        tri = causal_mask().astype(F32)
-        is_last = iota((TOK, HEADS), 0) == TOK - 1
-        bias_sum = jnp.zeros((1, HEADS), F32)
-        log_sum = jnp.zeros((1, HEADS), F32)
-        for b in range(SEQS):
-            span = slice(TOK * b, TOK * (b + 1))
-            step = dt[span, :]
-            d_dt = sums[span, :]
-            d_r = row_dot[span, :] - sums[ROWS + TOK * b : ROWS + TOK * (b + 1), :]
-            d_r = d_r + jnp.where(is_last, sums[2 * ROWS + b : 2 * ROWS + b + 1, :], 0.0)
-            d_log = mm(tri, d_r, TN, HIGHEST)
-            d_pre = (d_dt + rate * d_log) * jax.nn.sigmoid(dt_raw[span, :].astype(F32) + dt_bias[...])
-            d_dt_raw[span, :] = d_pre.astype(BF16)
-            bias_sum = bias_sum + jnp.sum(d_pre, axis=0, keepdims=True)
-            log_sum = log_sum + jnp.sum(d_log * step, axis=0, keepdims=True) * rate
-        d_dt_raw[ROWS:, :] = jnp.zeros((ALL - ROWS, HEADS), BF16)
-        g_heads[...] = jnp.concatenate([bias_sum, log_sum, sums[2 * ROWS + 2 : 2 * ROWS + 3, :], jnp.zeros((5, HEADS), F32)], axis=0)
-
-
-def back(d_stepped, xc, d_y, x_raw, start, end, bcc, dt, dt_wide, r_wide, bc_raw, dt_raw, d_bc_in, row_dot, taps_x, bias_x, taps_bc, bias_bc, dt_bias, a_log, d_skip):
-    return call(
-        back_kernel,
-        [((ALL, INNER), BF16), ((ALL, 2 * STATE), BF16), ((ALL, HEADS), BF16), ((8, INNER), F32), ((8, 2 * STATE), F32), ((8, HEADS), F32)],
-        [lanes(ALL), whole((ALL, 2 * STATE)), whole((ALL, HEADS)), lanes(8), whole((8, 2 * STATE)), whole((8, HEADS))],
-        [
-            lanes(ROWS), lanes(ROWS), lanes(ROWS), lanes(ALL), STATES, STATES,
-            whole((ROWS, 2 * STATE)), whole((ROWS, HEADS)), lanes(ROWS), lanes(ROWS), whole((ALL, 2 * STATE)),
-            whole((ALL, HEADS)), whole((ROWS, 2 * STATE)), whole((ROWS, HEADS)),
-            lanes(TAPS), lanes(1), whole((TAPS, 2 * STATE)), whole((1, 2 * STATE)),
-            whole((1, HEADS)), whole((1, HEADS)), lanes(1),
-        ],
-        scratch=[
-            pltpu.VMEM((ROWS, 2 * STATE), F32), pltpu.VMEM((2 * ROWS + 8, HEADS), F32),
-        ],
-    )(d_stepped, xc, d_y, x_raw, start, end, bcc, dt, dt_wide, r_wide, bc_raw, dt_raw, d_bc_in, row_dot, taps_x, bias_x, taps_bc, bias_bc, dt_bias, a_log, d_skip)
-
-
-REDUCE = (("x", "y", "z"), ("y", "z", "x"), ("z", "x", "y"))
-GATHER = (("l", "z", "x"), ("l", "x", "z"), ("x", "z", "l"))
+REDUCE = (("y", "z", "x"), ("x", "y", "z"), ("x", "y", "z"), ("y", "z", "x"), ("z", "x", "y"))
+GATHER = (("l", "z", "x"), ("x", "z", "l"), ("l", "z", "x"), ("l", "x", "z"), ("x", "z", "l"))
 PIECE = 128
 EXTRA = 32
-PIECE_ROWS = (PIECE, PIECE + EXTRA, PIECE)
+PIECE_ROWS = (PIECE, PIECE, 48, 48, 32 + EXTRA)
+SETS = len(PIECE_ROWS)
 SMALL = 3 * 128
+VECTOR = (16, INNER)
 
 
 def position():
@@ -507,20 +367,38 @@
     pl.semaphore_wait(barrier, len(everyone))
 
 
-def reduce_kernel(
-    normed, d_gate, d_wide, d_small, mixed, cot, vector,
-    out_z, out_x, out_out,
-    keep_n, keep_m, next_n, next_m, sib_n, sib_gate, sib_wide, sib_small, sib_m, sib_cot, sib_vector,
-    parts_z, parts_x, parts_out,
-    got_z1, got_x1, got_out1, sum_z1, sum_x1, sum_out1,
-    got_z2, got_x2, got_out2, sum_z2, sum_x2, sum_out2,
-    got_z3, got_x3, got_out3,
-    sib_send, sib_recv, red_send, red_recv, all_send, all_recv,
+def tail_kernel(
+    v, decay, xc, d_y, bcc, dt, dt_wide, r_wide, r_rows, x_raw, start, bc_raw, dt_raw, row_dot,
+    taps_x, bias_x, taps_bc, bias_bc, dt_bias, a_log, d_skip, g_norm,
+    normed, d_gate, mixed, cot, layer_in, gain_in, full_z, full_x, full_small,
+    out_z, out_out, out_xa, out_xb, out_xc, input_grad, vector,
+    weights, v_all, g_own, end, d_stepped, scores, d_scores, d_bc, sums, d_x_raw, d_small, g_x, g_bc, g_heads,
+    d_normed, halo_out, halo_in, few_own, few_got,
+    keep_n, keep_m, next_n, next_m, sib_n, sib_gate, sib_m, sib_cot, sib_wide, sib_small,
+    parts_z, parts_out, parts_xa, parts_xb, parts_xc,
+    got_z1, got_out1, got_xa1, got_xb1, got_xc1, sum_z1, sum_out1, sum_xa1, sum_xb1, sum_xc1,
+    got_z2, got_out2, got_xa2, got_xb2, got_xc2, sum_z2, sum_out2, sum_xa2, sum_xb2, sum_xc2,
+    got_z3, got_out3, got_xa3, got_xb3, got_xc3,
+    v_send, v_recv, g_send, g_recv, sib_send, sib_recv, red_send, red_recv, all_send, all_recv,
+    few_send, few_recv, halo_sem, load_sem,
 ):
     at = position()
+    me = lax.axis_index("seq")
+    core = at["core"]
     sibling = peers(at, "core")[0]
-    everyone = [sibling] + [p for axis in ("x", "y", "z") for p in peers(at, axis)]
-    greet(everyone)
+    barrier = pltpu.get_barrier_semaphore()
+
+    def greet_chunk(d, _):
+        pl.semaphore_signal(
+            barrier, inc=1, device_id={"seq": lax.rem(me + d, HEADS)}, device_id_type=pl.DeviceIdType.MESH
+        )
+        return 0
+
+    lax.fori_loop(1, HEADS, greet_chunk, 0)
+    others = [sibling] + peers(at, "y")
+    for other in others:
+        pl.semaphore_signal(barrier, inc=1, device_id=device(other), device_id_type=pl.DeviceIdType.MESH)
+    pl.semaphore_wait(barrier, HEADS - 1 + len(others))
     started = []
 
     def copy(src, dst, send, recv, to):
@@ -532,30 +410,103 @@
         started.append(one)
         return one
 
-    def columns(ref, high, core, size):
-        return ref.at[:, pl.ds(pl.multiple_of((2 * high + core) * size, size), size)]
-
-    def transposed(ref, high, core, size):
-        return ref[:, pl.ds(pl.multiple_of((2 * high + core) * size, size), size)].astype(F32).T.astype(BF16)
-
-    core = at["core"]
+    def chunk_copy(src, dst, send, recv, to, at_dst):
+        return pltpu.make_async_remote_copy(
+            src_ref=src.at[to], dst_ref=dst.at[at_dst], send_sem=send.at[to], recv_sem=recv.at[at_dst],
+            device_id={"seq": to}, device_id_type=pl.DeviceIdType.MESH,
+        )
+
+    def swap_start(src, dst, send, recv):
+        def go(d, _):
+            chunk_copy(src, dst, send, recv, lax.rem(me + d, HEADS), me).start()
+            return 0
+
+        lax.fori_loop(1, HEADS, go, 0)
+        dst[me] = src[me]
+
+    def swap_wait(src, dst, send, recv):
+        def go(d, _):
+            other = lax.rem(me + d, HEADS)
+            chunk_copy(src, dst, send, recv, other, other).wait_recv()
+            return 0
+
+        lax.fori_loop(1, HEADS, go, 0)
+
+    def swap_sent(src, dst, send, recv):
+        def go(d, _):
+            chunk_copy(src, dst, send, recv, lax.rem(me + d, HEADS), me).wait_send()
+            return 0
+
+        lax.fori_loop(1, HEADS, go, 0)
+
+    def lane_block(j, size=128):
+        return pl.ds(pl.multiple_of(j * size, size), size)
+
+    swap_start(v, v_all, v_send, v_recv)
+
+    def columns(ref, high, which, size):
+        return ref.at[:, lane_block(2 * high + which, size)]
+
+    def transposed(ref, high, which, size):
+        return ref[:, lane_block(2 * high + which, size)].astype(F32).T.astype(BF16)
+
     pairs = [(columns(normed, h, 1 - core, 256), sib_n.at[h]) for h in range(2)] + [(d_gate, sib_gate)]
-    pairs += [(columns(mixed, h, 1 - core, 512), sib_m.at[h]) for h in range(2)]
-    pairs += [(cot, sib_cot), (d_wide, sib_wide), (d_small, sib_small), (vector, sib_vector)]
+    pairs += [(columns(mixed, h, 1 - core, 512), sib_m.at[h]) for h in range(2)] + [(cot, sib_cot)]
     from_sibling = [copy(a, b, sib_send.at[i], sib_recv.at[i], sibling) for i, (a, b) in enumerate(pairs)]
-    for h in range(2):
-        keep_n[256 * h : 256 * (h + 1), :] = transposed(normed, h, core, 256)
-    for h in range(2):
-        keep_m[512 * h : 512 * (h + 1), :] = transposed(mixed, h, core, 512)
-
-    parts = (parts_z, parts_x, parts_out)
-    got = ((got_z1, got_x1, got_out1), (got_z2, got_x2, got_out2), (got_z3, got_x3, got_out3))
-    sums = ((sum_z1, sum_x1, sum_out1), (sum_z2, sum_x2, sum_out2))
-    outs = (out_z, out_x, out_out)
+    loading = pltpu.make_async_copy(full_z, weights, load_sem)
+    loading.start()
+
+    d_scores[...] = jnp.zeros_like(d_scores)
+    for b in range(SEQS):
+        span = slice(TOK * b, TOK * (b + 1))
+        scores[b] = mm(bcc[span, STATE:], bcc[span, 0:STATE], NT)
+
+    def inside_pair(j, _):
+        cols = lane_block(j)
+        for b in range(SEQS):
+            span = slice(TOK * b, TOK * (b + 1))
+            first, second = decay_pair(r_wide[span, cols], r_rows[j, :, span])
+            both = jnp.concatenate([scores[b] * first, scores[b] * second], axis=0).astype(BF16)
+            stepped = (dt_wide[span, cols] * xc[span, cols].astype(F32)).astype(BF16)
+            wide = block_diagonal(d_y[span, cols])
+            d_stepped[span, cols] = mm(both, wide, TN)
+            d_both = mm(wide, stepped, NT)
+            d_scores[b] += d_both[0:TOK, :] * first + d_both[TOK:, :] * second
+        return 0
+
+    lax.fori_loop(0, PAIRS, inside_pair, 0)
+    for b in range(SEQS):
+        span = slice(TOK * b, TOK * (b + 1))
+        low = d_scores[b].astype(BF16)
+        d_bc[span, 0:STATE] = mm(low, bcc[span, STATE:], TN)
+        d_bc[span, STATE:] = mm(low, bcc[span, 0:STATE], NN)
+
+    swap_wait(v, v_all, v_send, v_recv)
+
+    def chunk_step(i, carry):
+        c = HEADS - 1 - i
+        after = []
+        for b in range(SEQS):
+            g_own[c, b] = carry[b].astype(BF16)
+            after.append(decay[c, b] * carry[b] + v_all[c, b].astype(F32))
+        return tuple(after)
+
+    lax.fori_loop(0, HEADS, chunk_step, tuple(jnp.zeros((HEAD, STATE), F32) for _ in range(SEQS)))
+    swap_start(g_own, end, g_send, g_recv)
+
+    parts = (parts_z, parts_out, parts_xa, parts_xb, parts_xc)
+    got = (
+        (got_z1, got_out1, got_xa1, got_xb1, got_xc1),
+        (got_z2, got_out2, got_xa2, got_xb2, got_xc2),
+        (got_z3, got_out3, got_xa3, got_xb3, got_xc3),
+    )
+    partial = ((sum_z1, sum_out1, sum_xa1, sum_xb1, sum_xc1), (sum_z2, sum_out2, sum_xa2, sum_xb2, sum_xc2))
+    outs = (out_z, out_out, out_xa, out_xb, out_xc)
+    arriving = [None] * SETS
 
     def send_stage(stage, which, src):
         axis = REDUCE[which][stage]
-        return [
+        arriving[which] = [
             copy(
                 src.at[to[axis]], got[stage][which].at[d],
                 red_send.at[which, stage, d], red_recv.at[which, stage, d], to,
@@ -563,145 +514,376 @@
             for d, to in enumerate(peers(at, axis))
         ]
 
-    for i in (0, 1, 2):
-        from_sibling[i].wait_recv()
+    def arrived(which):
+        for one in arriving[which]:
+            one.wait_recv()
+
+    def add_stage(stage, which):
+        arrived(which)
+        src = parts[which] if stage == 0 else partial[0][which]
+        dst, came = partial[stage][which], got[stage][which]
+        mine = at[REDUCE[which][stage]]
+
+        def add(i, _):
+            for j in range(4) if stage == 0 else ((),):
+                index = (i, j) if stage == 0 else (i,)
+                value = src[(mine, *index)].astype(F32)
+                for d in range(3):
+                    value = value + came[(d, *index)].astype(F32)
+                dst[index] = value.astype(BF16)
+            return 0
+
+        lax.fori_loop(0, 4, add, 0)
+        send_stage(stage + 1, which, dst)
+
+    def gather_stage(stage, which):
+        first, second, third = GATHER[which]
+        index = (at[third], at[second], at[first])[: 3 - stage]
+        ref = outs[which].at[index]
+        arriving[which] = [
+            copy(ref, ref, all_send.at[which, stage, d], all_recv.at[which, stage, d], to)
+            for d, to in enumerate(peers(at, (first, second, third)[stage]))
+        ]
+
+    def last_add(which):
+        arrived(which)
+        first, second, third = GATHER[which]
+        value = partial[1][which][at[REDUCE[which][2]]].astype(F32)
+        for d in range(3):
+            value = value + got[2][which][d].astype(F32)
+        outs[which][at[third], at[second], at[first]] = value.astype(BF16)
+        gather_stage(0, which)
+
+    def gather_next(stage, which):
+        arrived(which)
+        gather_stage(stage, which)
+
+    for h in range(2):
+        keep_n[256 * h : 256 * (h + 1), :] = transposed(normed, h, core, 256)
+        keep_m[512 * h : 512 * (h + 1), :] = transposed(mixed, h, core, 512)
+    for one in from_sibling[:3]:
+        one.wait_recv()
     for h in range(2):
         next_n[256 * h : 256 * (h + 1), :] = sib_n[h].astype(F32).T.astype(BF16)
 
     def tile_z(n, _):
-        cols = pl.ds(pl.multiple_of(n * 256, 256), 256)
+        cols = lane_block(n, 256)
         res = mm(keep_n[:, 0:ROWS], d_gate[:, cols], NN) + mm(next_n[:, 0:ROWS], sib_gate[:, cols], NN)
         for y in range(4):
             for k in range(2):
-                parts_z[n // 2, y, (n % 2) * 2 + k] = res[128 * y : 128 * y + 128, 128 * k : 128 * k + 128].astype(BF16)
+                parts_z[y, (n % 2) * 2 + k, n // 2] = res[128 * y : 128 * y + 128, 128 * k : 128 * k + 128].astype(BF16)
         return 0
 
     lax.fori_loop(0, 8, tile_z, 0)
-    arriving = [send_stage(0, 0, parts_z), None, None]
-
-    for i in (3, 4, 5):
-        from_sibling[i].wait_recv()
+    send_stage(0, 0, parts_z)
+    for one in from_sibling[3:]:
+        one.wait_recv()
     for h in range(2):
         next_m[512 * h : 512 * (h + 1), :] = sib_m[h].astype(F32).T.astype(BF16)
 
     def tile_out(n, _):
-        cols = pl.ds(pl.multiple_of(n * 256, 256), 256)
+        cols = lane_block(n, 256)
         res = mm(keep_m[...], cot[:, cols], NN) + mm(next_m[...], sib_cot[:, cols], NN)
         for y in range(4):
             for half in range(2):
                 for k in range(2):
                     row = 256 * y + 128 * half
-                    parts_out[(n % 2) * 2 + k, half * 2 + n // 2, y] = res[row : row + 128, 128 * k : 128 * k + 128].astype(BF16)
+                    parts_out[half * 2 + n // 2, y, (n % 2) * 2 + k] = res[row : row + 128, 128 * k : 128 * k + 128].astype(BF16)
         return 0
 
     lax.fori_loop(0, 4, tile_out, 0)
-    arriving[2] = send_stage(0, 2, parts_out)
-
-    for i in (6, 7, 8):
-        from_sibling[i].wait_recv()
+    send_stage(0, 1, parts_out)
+
+    loading.wait()
+    for n in range(4):
+        cols = slice(256 * n, 256 * (n + 1))
+        d_normed[0:ROWS, cols] = mm(d_gate[...], weights[cols, :], NT)
+    loading = pltpu.make_async_copy(full_x, weights, load_sem)
+    loading.start()
+
+    swap_wait(g_own, end, g_send, g_recv)
+    sums[...] = jnp.zeros_like(sums)
+
+    def back_pair(j, _):
+        cols = lane_block(j)
+        ex = pair_matrix(j)
+        skip = d_skip[:, cols]
+        raw = x_raw[:, cols].astype(F32)
+        halos, grads = [], None
+        d_steps, dots, end_rows = [], [], []
+        skip_sum = jnp.zeros((1, 128), F32)
+        for b in range(SEQS):
+            span = slice(TOK * b, TOK * (b + 1))
+            r_lanes = r_wide[span, cols]
+            dt_lanes = dt_wide[span, cols]
+            last = r_lanes[TOK - 1 : TOK, :]
+            grown = jnp.exp(r_lanes)
+            to_end = jnp.exp(last - r_lanes)
+            before = jnp.concatenate([start[2 * j, b], start[2 * j + 1, b]], axis=0)
+            after = jnp.concatenate([end[2 * j, b], end[2 * j + 1, b]], axis=0)
+            x = xc[span, cols].astype(F32)
+            dy = d_y[span, cols].astype(F32)
+            stepped = (dt_lanes * x).astype(BF16).astype(F32)
+            carried = to_end * mm(bcc[span, 0:STATE], after, NT)
+            d_step = d_stepped[span, cols] + carried
+            dots.append(stepped * d_step)
+            d_x = dt_lanes * d_step + skip * dy
+            d_steps.append(x * d_step)
+            inner = lane_sums(before.astype(F32) * after.astype(F32))
+            end_rows.append(jnp.sum(stepped * carried, axis=0, keepdims=True) + jnp.exp(last) * inner)
+            d_bc[span, STATE:] += mm((grown * dy).astype(BF16), before, NN)
+            d_bc[span, 0:STATE] += mm((to_end * stepped).astype(BF16), after, NN)
+            skip_sum = skip_sum + jnp.sum(dy * x, axis=0, keepdims=True)
+            d_pad, d_taps, d_bias = conv_back(padded_of(raw, b), taps_x[:, cols], bias_x[:, cols], d_x)
+            d_x_raw[span, cols] = d_pad[HALO:, :].astype(BF16)
+            halos.append(d_pad[0:HALO, :])
+            found = [*d_taps, d_bias]
+            grads = found if grads is None else [g + p for g, p in zip(grads, found)]
+        d_x_raw[ROWS:, cols] = jnp.concatenate(halos, axis=0).astype(BF16)
+        g_x[:, cols] = jnp.concatenate([*grads, jnp.zeros((8 - TAPS - 1, 128), F32)], axis=0)
+        few = jnp.concatenate([*end_rows, skip_sum, jnp.zeros((5, 128), F32)], axis=0)
+        sums[...] += head_sums(jnp.concatenate([*d_steps, *dots, few], axis=0), ex)
+        return 0
+
+    wide_coming = []
+    for quarter in range(4):
+        lax.fori_loop(4 * quarter, 4 * quarter + 4, back_pair, 0)
+        cols = slice(512 * quarter, 512 * (quarter + 1))
+        wide_coming.append(
+            copy(d_x_raw.at[:, cols], sib_wide.at[:, cols], sib_send.at[6 + quarter], sib_recv.at[6 + quarter], sibling)
+        )
+    raw = bc_raw[...].astype(F32)
+    halos, grads = [], None
+    for b in range(SEQS):
+        span = slice(TOK * b, TOK * (b + 1))
+        d_pad, d_taps, d_bias = conv_back(padded_of(raw, b), taps_bc[...], bias_bc[...], d_bc[span, :])
+        d_small[span, 0 : 2 * STATE] = d_pad[HALO:, :].astype(BF16)
+        halos.append(d_pad[0:HALO, :])
+        found = [*d_taps, d_bias]
+        grads = found if grads is None else [g + p for g, p in zip(grads, found)]
+    d_small[ROWS:, 0 : 2 * STATE] = jnp.concatenate(halos, axis=0).astype(BF16)
+    d_small[ROWS:, 2 * STATE :] = jnp.zeros((ALL - ROWS, SMALL - 2 * STATE), BF16)
+    g_bc[...] = jnp.concatenate([*grads, jnp.zeros((8 - TAPS - 1, 2 * STATE), F32)], axis=0)
+    rate = -jnp.exp(a_log[...])
+    tri = causal_mask().astype(F32)
+    is_last = iota((TOK, HEADS), 0) == TOK - 1
+    bias_sum = jnp.zeros((1, HEADS), F32)
+    log_sum = jnp.zeros((1, HEADS), F32)
+    for b in range(SEQS):
+        span = slice(TOK * b, TOK * (b + 1))
+        step = dt[span, :]
+        d_dt = sums[span, :]
+        d_r = row_dot[span, :] - sums[ROWS + TOK * b : ROWS + TOK * (b + 1), :]
+        d_r = d_r + jnp.where(is_last, sums[2 * ROWS + b : 2 * ROWS + b + 1, :], 0.0)
+        d_log = mm(tri, d_r, TN, HIGHEST)
+        d_pre = (d_dt + rate * d_log) * jax.nn.sigmoid(dt_raw[span, :].astype(F32) + dt_bias[...])
+        d_small[span, 2 * STATE :] = jnp.concatenate(
+            [d_pre, jnp.zeros((TOK, SMALL - 2 * STATE - HEADS), F32)], axis=1
+        ).astype(BF16)
+        bias_sum = bias_sum + jnp.sum(d_pre, axis=0, keepdims=True)
+        log_sum = log_sum + jnp.sum(d_log * step, axis=0, keepdims=True) * rate
+    g_heads[...] = jnp.concatenate(
+        [bias_sum, log_sum, sums[2 * ROWS + 2 : 2 * ROWS + 3, :], jnp.zeros((5, HEADS), F32)], axis=0
+    )
+    small_coming = copy(d_small, sib_small, sib_send.at[10], sib_recv.at[10], sibling)
+
+    add_stage(0, 0)
+    add_stage(0, 1)
 
     def tile_x(n, _):
-        cols = pl.ds(pl.multiple_of(n * 256, 256), 256)
-        res = mm(keep_n[...], d_wide[:, cols], NN) + mm(next_n[...], sib_wide[:, cols], NN)
+        cols = lane_block(n, 256)
+        res = mm(keep_n[...], d_x_raw[:, cols], NN) + mm(next_n[...], sib_wide[:, cols], NN)
         for y in range(4):
             for k in range(2):
-                parts_x[y, (n % 2) * 2 + k, n // 2, 0:PIECE] = res[128 * y : 128 * y + 128, 128 * k : 128 * k + 128].astype(BF16)
+                block = res[128 * y : 128 * y + 128, 128 * k : 128 * k + 128].astype(BF16)
+                x, z = n // 2, (n % 2) * 2 + k
+                parts_xa[x, y, z] = block[0:48]
+                parts_xb[y, z, x] = block[48:96]
+                parts_xc[z, x, y, 0:32] = block[96:128]
         return 0
 
-    lax.fori_loop(0, 8, tile_x, 0)
+    for quarter in range(4):
+        wide_coming[quarter].wait_recv()
+        lax.fori_loop(2 * quarter, 2 * quarter + 2, tile_x, 0)
+    send_stage(0, 2, parts_xa)
+    send_stage(0, 3, parts_xb)
+    small_coming.wait_recv()
     res = mm(keep_n[...], d_small[...], NN) + mm(next_n[...], sib_small[...], NN)
-    total = (vector[...] + sib_vector[...]).astype(BF16)
     for y in range(4):
         for z in range(4):
             row = 128 * y + EXTRA * z
             for k in range(3):
-                parts_x[y, z, k, PIECE:] = res[row : row + EXTRA, 128 * k : 128 * k + 128].astype(BF16)
-            parts_x[y, z, 3, PIECE:] = total[EXTRA * z : EXTRA * z + EXTRA, :]
-    arriving[1] = send_stage(0, 1, parts_x)
-
-    order = (0, 2, 1)
-    for stage in range(2):
-        for which in order:
-            for one in arriving[which]:
-                one.wait_recv()
-            src = parts[which] if stage == 0 else sums[0][which]
-            dst, arrived = sums[stage][which], got[stage][which]
-            mine = at[REDUCE[which][stage]]
-
-            def add(i, _, src=src, dst=dst, arrived=arrived, mine=mine, stage=stage):
-                if stage == 0:
-                    for j in range(4):
-                        value = src[mine, i, j].astype(F32)
-                        for d in range(3):
-                            value = value + arrived[d, i, j].astype(F32)
-                        dst[i, j] = value.astype(BF16)
-                else:
-                    value = src[mine, i].astype(F32)
-                    for d in range(3):
-                        value = value + arrived[d, i].astype(F32)
-                    dst[i] = value.astype(BF16)
-                return 0
-
-            lax.fori_loop(0, 4, add, 0)
-            arriving[which] = send_stage(stage + 1, which, dst)
-
-    def gather_stage(stage, which):
-        first, second, third = GATHER[which]
-        index = (at[third], at[second], at[first])[: 3 - stage]
-        ref = outs[which].at[index]
-        return [
-            copy(ref, ref, all_send.at[which, stage, d], all_recv.at[which, stage, d], to)
-            for d, to in enumerate(peers(at, (first, second, third)[stage]))
+                parts_xc[z, k, y, 32:] = res[row : row + EXTRA, 128 * k : 128 * k + 128].astype(BF16)
+            parts_xc[z, 3, y, 32:] = jnp.zeros((EXTRA, 128), BF16)
+    send_stage(0, 4, parts_xc)
+
+    loading.wait()
+    d_normed[ROWS:, :] = jnp.zeros((ALL - ROWS, d_normed.shape[1]), F32)
+    for n in range(4):
+        cols = slice(256 * n, 256 * (n + 1))
+        d_normed[:, cols] += mm(d_x_raw[...], weights[cols, :], NT) + mm(d_small[...], full_small[cols, :], NT)
+    halo_out[...] = d_normed[ROWS:, :]
+    halo = pltpu.make_async_remote_copy(
+        src_ref=halo_out, dst_ref=halo_in, send_sem=halo_sem.at[0], recv_sem=halo_sem.at[1],
+        device_id={"seq": lax.rem(me + HEADS - 1, HEADS)}, device_id_type=pl.DeviceIdType.MESH,
+    )
+    halo.start()
+    started.append(halo)
+    add_stage(1, 0)
+    add_stage(1, 1)
+    halo.wait_recv()
+    inner = jnp.where(me == HEADS - 1, 0.0, 1.0)
+    for b in range(SEQS):
+        near = slice(TOK * (b + 1) - HALO, TOK * (b + 1))
+        d_normed[near, :] += inner * halo_in[HALO * b : HALO * (b + 1), :]
+    g_in = jnp.zeros((1, d_normed.shape[1]), F32)
+    for n in range(4):
+        span = slice(64 * n, 64 * (n + 1))
+        hidden = layer_in[span, :].astype(F32)
+        inv = lax.rsqrt(jnp.mean(hidden * hidden, axis=1, keepdims=True) + EPS)
+        unit = hidden * inv
+        grad = d_normed[span, :]
+        g_in = g_in + jnp.sum(grad * unit, axis=0, keepdims=True)
+        pulled = grad * gain_in[...]
+        d_hidden = inv * (pulled - unit * jnp.mean(pulled * unit, axis=1, keepdims=True))
+        input_grad[span, :] = cot[span, :].astype(F32) + d_hidden
+
+    few_axes = ("core", "x", "z", "y")
+    rest = jnp.concatenate(
+        [
+            g_bc[...], jnp.concatenate([g_heads[...], jnp.zeros((8, 128 - HEADS), F32)], axis=1),
+            jnp.zeros((8, INNER - 2 * STATE - 128), F32),
+        ],
+        axis=1,
+    )
+    wide_in = jnp.concatenate([g_in, jnp.zeros((1, INNER - g_in.shape[1]), F32)], axis=1)
+    few = jnp.concatenate([g_x[...], g_norm[...], wide_in, rest[0 : TAPS + 1], jnp.zeros((1, INNER), F32)], axis=0)
+
+    few_coming = [None]
+
+    def few_start(stage, value):
+        few_own[stage] = value.astype(BF16)
+        axis = few_axes[stage]
+        few_got[stage, at[axis]] = few_own[stage]
+        few_coming[0] = [
+            copy(
+                few_own.at[stage], few_got.at[stage, at[axis]],
+                few_send.at[stage, d], few_recv.at[stage, d], to,
+            )
+            for d, to in enumerate(peers(at, axis))
         ]
 
-    for which in order:
-        for one in arriving[which]:
+    def few_sum(stage):
+        for one in few_coming[0]:
             one.wait_recv()
-        first, second, third = GATHER[which]
-        value = sums[1][which][at[REDUCE[which][2]]].astype(F32)
-        for d in range(3):
-            value = value + got[2][which][d].astype(F32)
-        outs[which][at[third], at[second], at[first]] = value.astype(BF16)
-        arriving[which] = gather_stage(0, which)
+        value = few_got[stage, 0].astype(F32)
+        for i in range(1, 2 if stage == 0 else 4):
+            value = value + few_got[stage, i].astype(F32)
+        return value
+
+    few_start(0, few)
+    last_add(0)
+    last_add(1)
+    few_start(1, few_sum(0))
+    for which in (2, 3, 4):
+        add_stage(0, which)
+    gather_next(1, 0)
+    gather_next(1, 1)
+    few_start(2, few_sum(1))
+    for which in (2, 3, 4):
+        add_stage(1, which)
+    gather_next(2, 0)
+    gather_next(2, 1)
+    few_start(3, few_sum(2))
+    for which in (2, 3, 4):
+        last_add(which)
+    vector[...] = few_sum(3)
     for stage in (1, 2):
-        for which in order:
-            for one in arriving[which]:
-                one.wait_recv()
-            arriving[which] = gather_stage(stage, which)
-    for which in order:
-        for one in arriving[which]:
-            one.wait_recv()
+        for which in (2, 3, 4):
+            gather_next(stage, which)
+    for which in range(SETS):
+        arrived(which)
     for one in started:
         one.wait_send()
-
-
-def reduce_grads(normed, d_gate, d_wide, d_small, mixed, cot, vector):
+    swap_sent(v, v_all, v_send, v_recv)
+    swap_sent(g_own, end, g_send, g_recv)
+
+
+def tail(*args):
     vmem = pl.BlockSpec(memory_space=pltpu.VMEM)
+    hbm = pl.BlockSpec(memory_space=pl.ANY)
+    specs = [vmem] * len(args)
+    specs[1] = pl.BlockSpec(memory_space=pltpu.SMEM)
+    specs[-3] = specs[-2] = hbm
+    width = args[-2].shape[0]
     dims = {"x": 4, "z": 4, "l": 2}
     out_shape = [
-        jax.ShapeDtypeStruct((*(dims[a] for a in reversed(GATHER[i])), PIECE_ROWS[i], 128), BF16) for i in range(3)
+        jax.ShapeDtypeStruct((*(dims[a] for a in reversed(GATHER[i])), PIECE_ROWS[i], 128), BF16) for i in range(SETS)
     ]
-    turned = [pltpu.VMEM((512, ALL), BF16), pltpu.VMEM((1024, ROWS), BF16)] * 2
-    like = [pltpu.VMEM((2, ALL, 256), BF16)] + [pltpu.VMEM(a.shape, a.dtype) for a in (d_gate, d_wide, d_small)]
-    like += [pltpu.VMEM((2, ROWS, 512), BF16)] + [pltpu.VMEM(a.shape, a.dtype) for a in (cot, vector)]
+    out_shape += [jax.ShapeDtypeStruct((ROWS, width), F32), jax.ShapeDtypeStruct(VECTOR, F32)]
 
     def bufs(*lead):
-        return [pltpu.VMEM((*lead, PIECE_ROWS[i], 128), BF16) for i in range(3)]
-
-    sems = [pltpu.SemaphoreType.DMA((9,))] * 2 + [pltpu.SemaphoreType.DMA((3, 3, 3))] * 4
+        return [pltpu.VMEM((*lead, PIECE_ROWS[i], 128), BF16) for i in range(SETS)]
+
+    def sems(*shape):
+        return [pltpu.SemaphoreType.DMA(shape)] * 2
+
+    scratch = [
+        pltpu.VMEM((width, INNER), BF16), *[pltpu.VMEM(STATES_SHAPE, BF16)] * 3, pltpu.VMEM((ROWS, INNER), F32),
+        *[pltpu.VMEM((SEQS, TOK, TOK), F32)] * 2, pltpu.VMEM((ROWS, 2 * STATE), F32),
+        pltpu.VMEM((2 * ROWS + 8, HEADS), F32), pltpu.VMEM((ALL, INNER), BF16), pltpu.VMEM((ALL, SMALL), BF16),
+        pltpu.VMEM((8, INNER), F32), pltpu.VMEM((8, 2 * STATE), F32), pltpu.VMEM((8, HEADS), F32),
+        pltpu.VMEM((ALL, width), F32), *[pltpu.VMEM((SEQS * HALO, width), F32)] * 2,
+        pltpu.VMEM((4, *VECTOR), BF16), pltpu.VMEM((4, 4, *VECTOR), BF16),
+        *[pltpu.VMEM((512, ALL), BF16), pltpu.VMEM((1024, ROWS), BF16)] * 2,
+        pltpu.VMEM((2, ALL, 256), BF16), pltpu.VMEM((ROWS, INNER), BF16), pltpu.VMEM((2, ROWS, 512), BF16),
+        pltpu.VMEM((ROWS, width), BF16), pltpu.VMEM((ALL, INNER), BF16), pltpu.VMEM((ALL, SMALL), BF16),
+        *bufs(4, 4, 4), *bufs(3, 4, 4), *bufs(4, 4), *bufs(3, 4), *bufs(4), *bufs(3),
+        *sems(HEADS), *sems(HEADS), *sems(11), *sems(SETS, 3, 3), *sems(SETS, 3, 3), *sems(4, 3),
+        pltpu.SemaphoreType.DMA((2,)), pltpu.SemaphoreType.DMA,
+    ]
     return pl.pallas_call(
-        reduce_kernel,
+        tail_kernel,
         out_shape=out_shape,
-        in_specs=[vmem] * 7,
-        out_specs=[vmem] * 3,
-        scratch_shapes=[
-            *turned, *like, *bufs(4, 4, 4), *bufs(3, 4, 4), *bufs(4, 4), *bufs(3, 4), *bufs(4), *bufs(3), *sems,
+        in_specs=specs,
+        out_specs=[vmem] * len(out_shape),
+        scratch_shapes=scratch,
+        compiler_params=pltpu.CompilerParams(
+            vmem_limit_bytes=62 * 1024 * 1024, collective_id=1, has_side_effects=True
+        ),
+        cost_estimate=pl.CostEstimate(flops=int(8e9), bytes_accessed=int(4e7), transcendentals=0),
+    )(*args)
+
+
+def unpack_kernel(sum_z, sum_out, sum_xa, sum_xb, sum_xc, out_z, out_x, out_out, out_extra):
+    for low in range(2):
+        base = PIECE * low
+        out_z[base : base + PIECE, :] = sum_z[0, 0, low].astype(F32)
+        out_x[base : base + 48, :] = sum_xa[0, 0, low].astype(F32)
+        out_x[base + 48 : base + 96, :] = sum_xb[0, 0, low].astype(F32)
+        out_x[base + 96 : base + 128, :] = sum_xc[low, 0, 0, 0:32, :].astype(F32)
+        out_out[low, 0] = sum_out[low, 0, 0].astype(F32)
+        out_extra[0, low] = sum_xc[low, 0, 0, 32:, :].astype(F32)
+
+
+def unpack(*gathered):
+    specs = []
+    for i in range(SETS):
+        def where(n, order=GATHER[i]):
+            return tuple({"x": n // 4, "z": n % 4, "l": 0}[a] for a in reversed(order)) + (0, 0)
+
+        block = tuple(2 if a == "l" else 1 for a in reversed(GATHER[i])) + (PIECE_ROWS[i], 128)
+        specs.append(pl.BlockSpec(block, where))
+    return call(
+        unpack_kernel,
+        [((2 * PIECE, INNER), F32), ((2 * PIECE, INNER), F32), ((2, 2, PIECE, 8 * 128), F32), ((4, 2, 4 * EXTRA, 128), F32)],
+        [
+            lanes(2 * PIECE), lanes(2 * PIECE),
+            pl.BlockSpec((2, 1, PIECE, 128), lambda i: (0, i // 8, 0, ((i // 4) % 2) * 4 + i % 4)),
+            pl.BlockSpec((1, 2, EXTRA, 128), lambda i: (i // 4, 0, i % 4, 0)),
         ],
-        compiler_params=pltpu.CompilerParams(
-            vmem_limit_bytes=VMEM_LIMIT, collective_id=1, has_side_effects=True
-        ),
-        cost_estimate=pl.CostEstimate(flops=int(4e9), bytes_accessed=int(4e7), transcendentals=0),
-    )(normed, d_gate, d_wide, d_small, mixed, cot, vector)
+        specs,
+    )(*gathered)
 
 
 def gather_kernel(
@@ -812,32 +994,6 @@
     )(w_x, w_small, own)
 
 
-def unpack_kernel(sum_z, sum_x, sum_out, out_z, out_x, out_out, out_extra):
-    for low in range(2):
-        rows = slice(PIECE * low, PIECE * (low + 1))
-        out_z[rows, :] = sum_z[0, 0, low].astype(F32)
-        out_x[rows, :] = sum_x[0, 0, low, 0:PIECE, :].astype(F32)
-        out_out[low, 0] = sum_out[low, 0, 0].astype(F32)
-        out_extra[0, low] = sum_x[0, 0, low, PIECE:, :].astype(F32)
-
-
-def unpack(sum_z, sum_x, sum_out):
-    return call(
-        unpack_kernel,
-        [((2 * PIECE, INNER), F32), ((2 * PIECE, INNER), F32), ((2, 2, PIECE, 8 * 128), F32), ((4, 2, 4 * EXTRA, 128), F32)],
-        [
-            lanes(2 * PIECE), lanes(2 * PIECE),
-            pl.BlockSpec((2, 1, PIECE, 128), lambda i: (0, i // 8, 0, ((i // 4) % 2) * 4 + i % 4)),
-            pl.BlockSpec((1, 2, EXTRA, 128), lambda i: (i // 4, 0, i % 4, 0)),
-        ],
-        [
-            pl.BlockSpec((1, 1, 2, PIECE, 128), lambda i: (i // 4, i % 4, 0, 0, 0)),
-            pl.BlockSpec((1, 1, 2, PIECE + EXTRA, 128), lambda i: (i % 4, i // 4, 0, 0, 0)),
-            pl.BlockSpec((2, 1, 1, PIECE, 128), lambda i: (0, i % 4, i // 4, 0, 0)),
-        ],
-    )(sum_z, sum_x, sum_out)
-
-
 def swap(values):
     return lax.all_to_all(values, "seq", split_axis=0, concat_axis=0, tiled=True)
 
@@ -853,7 +1009,7 @@
     width = layer_in.shape[2]
     chunks = lax.axis_size("seq")
     place = lax.axis_index("seq")
-    tail = lax.ppermute(layer_in[:, TOK - (TAPS - 1) :, :], "seq", [(i, i + 1) for i in range(chunks - 1)])
+    earlier = lax.ppermute(layer_in[:, TOK - (TAPS - 1) :, :], "seq", [(i, i + 1) for i in range(chunks - 1)])
     full_z = gather_rows(w_z)
     full_out = gather_rows(w_out)
     own = jnp.concatenate([conv_x_weight.reshape(-1), conv_x_bias, dt_bias, a_log, d_skip, jnp.zeros((701,), F32)])
@@ -870,11 +1026,10 @@
 
     hidden = layer_in.astype(F32).reshape(ROWS, width)
     upstream = cotangent.reshape(ROWS, width)
-    halo = jnp.pad(tail, ((0, 0), (HALO - (TAPS - 1), 0), (0, 0))).reshape(SEQS * HALO, width).astype(F32)
+    halo = jnp.pad(earlier, ((0, 0), (HALO - (TAPS - 1), 0), (0, 0))).reshape(SEQS * HALO, width).astype(F32)
     tokens = jnp.concatenate([hidden, halo], axis=0)
     inv = lax.rsqrt(jnp.mean(tokens * tokens, axis=-1, keepdims=True) + EPS)
     normed = (tokens * inv * gain_in[None, :]).astype(BF16)
-    inv = inv[:ROWS]
 
     x_raw = mm(normed, full_x, NN).astype(BF16)
     small_raw = mm(normed, full_small, NN).astype(BF16)
@@ -889,43 +1044,23 @@
     mixed, d_y, d_gate, v, g_norm, row_dot = middle(
         y_in, xc, bcc, r_wide, start, skip_wide, gate, d_mixed, gain_norm.reshape(1, INNER)
     )
-    v_all = swap(v)
     layer_out = (hidden + mm(mixed, full_out, NN)).astype(BF16).reshape(SEQS, TOK, width)
-    d_stepped, d_bc_in = inside_back(xc, d_y, bcc, dt_wide, r_wide, r_rows)
-    d_normed_z = mm(d_gate, full_z, NT)
-    end = swap(states(decay, v_all, True))
-    d_x_raw, d_bc_raw, d_dt_raw, g_x, g_bc, g_heads = back(
-        d_stepped, xc, d_y, x_raw, start, end, bcc, dt, dt_wide, r_wide, bc_raw, dt_raw, d_bc_in, row_dot,
-        taps_x, bias_x, conv_bc_weight, bias_bc, bias_dt, log_a, skip_wide,
+    *gathered, input_grad, total = tail(
+        v, decay, xc, d_y, bcc, dt, dt_wide, r_wide, r_rows, x_raw, start, bc_raw, dt_raw, row_dot,
+        taps_x, bias_x, conv_bc_weight, bias_bc, bias_dt, log_a, skip_wide, g_norm,
+        normed, d_gate, mixed, upstream, layer_in.reshape(ROWS, width), gain_in.reshape(1, width),
+        full_z, full_x, full_small,
     )
-    d_small = jnp.concatenate([d_bc_raw, d_dt_raw, jnp.zeros((ALL, SMALL - 2 * STATE - HEADS), BF16)], axis=1)
-    d_normed = mm(d_x_raw, full_x, NT) + mm(d_small, full_small, NT)
-    back_tail = d_normed[ROWS:].reshape(SEQS, HALO, width)[:, HALO - (TAPS - 1) :]
-    back_tail = lax.ppermute(back_tail, "seq", [(i + 1, i) for i in range(chunks - 1)])
-    d_normed = d_normed[:ROWS] + d_normed_z
-    d_normed = d_normed + jnp.pad(back_tail, ((0, 0), (TOK - (TAPS - 1), 0), (0, 0))).reshape(ROWS, width)
-    unit = hidden * inv
-    g_in = jnp.sum(d_normed * unit, axis=0)
-    pulled = d_normed * gain_in[None, :]
-    d_hidden = inv * (pulled - unit * jnp.mean(pulled * unit, axis=-1, keepdims=True))
-    input_grad = (upstream.astype(F32) + d_hidden).reshape(SEQS, TOK, width)
-
-    pieces = (g_x[: TAPS + 1], g_bc[: TAPS + 1], g_heads[:3], g_in, g_norm)
-    sizes = [p.size for p in pieces]
-    vector = jnp.concatenate([*(p.reshape(-1) for p in pieces), jnp.zeros((PIECE * 128 - sum(sizes),), F32)])
-    grad_w_z, grad_w_x, grad_w_out, extra = unpack(
-        *reduce_grads(normed, d_gate, d_x_raw, d_small, mixed, upstream, vector.reshape(PIECE, 128))
-    )
+    input_grad = input_grad.reshape(SEQS, TOK, width)
+    grad_w_z, grad_w_x, grad_w_out, extra = unpack(*gathered)
     grad_w_out = grad_w_out.reshape(4 * PIECE, width)
     extra = extra.reshape(4, 2 * PIECE, 128)
     grad_w_bc = jnp.concatenate([extra[0], extra[1]], axis=1)
     grad_w_dt = extra[2][:, :HEADS]
-    total = extra[3][:PIECE].reshape(-1)[: sum(sizes)]
-    ends = [sum(sizes[: i + 1]) for i in range(len(sizes) - 1)]
-    s_x, s_bc, s_heads, s_in, s_norm = jnp.split(total, ends)
-    s_x = lax.dynamic_slice(s_x.reshape(TAPS + 1, INNER), (0, place * HEAD), (TAPS + 1, HEAD))
-    s_bc = s_bc.reshape(TAPS + 1, 2 * STATE)
-    s_heads = lax.dynamic_slice(s_heads.reshape(3, HEADS), (0, place), (3, 1))
+    s_x = lax.dynamic_slice(total[: TAPS + 1], (0, place * HEAD), (TAPS + 1, HEAD))
+    s_norm, s_in = total[8], total[9, :width]
+    s_bc = total[10 : 10 + TAPS + 1, : 2 * STATE]
+    s_heads = lax.dynamic_slice(total[10:13], (0, 2 * STATE + place), (3, 1))
     return (
         layer_out, input_grad, s_in, grad_w_z, grad_w_x, grad_w_bc, grad_w_dt,
         s_x[:TAPS], s_x[TAPS], s_bc[:TAPS], s_bc[TAPS], s_heads[0], s_heads[1], s_heads[2], s_norm, grad_w_out,

time: 367 us -> 323 us (0.88)
  blocking collectives: 36.8 us -> 12.7 us
  local copies, waits for them, and re-layouts: 38.7 us -> 30.3 us
  matrix products: 22.5 us -> 15.8 us
  Pallas kernels: 206 us -> 212 us
  starting transfers between devices: 19 us -> 13.9 us
    all_to_all x2 -> x1, blocking collectives: 36.8 us -> 12.7 us  [swap(): lax.all_to_all(values, 'seq', split_axis=0, concat_axis=0, tiled=True)]
    pallas_call x3 -> x1, Pallas kernels: 122 us -> 129 us  [tail(): pl.pallas_call(tail_kernel, out_shape=out_shape, in_specs=specs, out_spec...]
    dot_general x8 -> x5, matrix products: 22.5 us -> 15.8 us  [mm(): lax.dot_general(a, b, ((dims[0], dims[1]), ((), ())), precision=precision...]
    unnamed x134 -> x99, local copies, waits for them, and re-layouts: 25.5 us -> 19.6 us
    all_to_all x3 -> x2, starting transfers between devices: 13.4 us -> 10.3 us  [swap(): lax.all_to_all(values, 'seq', split_axis=0, concat_axis=0, tiled=True)]
    all_to_all x3 -> x2, waiting for transfers between devices: 15.9 us -> 17.2 us  [swap(): lax.all_to_all(values, 'seq', split_axis=0, concat_axis=0, tiled=True)]
  transfers between devices with their start and end apart: 7 -> 5, of which waited for: 2 -> 1; matrix products, arithmetic and copies ran while one was open for 7% -> 4% of each run, Pallas kernels for 18% -> 16%
where the time goes in v4:
time: 323 us; the launch traced here: 321 us
  Pallas kernels  212 us (66%)
  local copies, waits for them, and re-layouts  30.3 us (9%)
  waiting for transfers between devices  18.6 us (6%)
  between operations  16.5 us (5%)
  matrix products  15.8 us (5%)
  starting transfers between devices  13.9 us (4%)
  blocking collectives  12.7 us (4%)
    pallas_call x1, Pallas kernels, tail(): pl.pallas_call(tail_kernel, out_shape=out_shape, in_specs=specs, out_spec...  129 us
    pallas_call x1, Pallas kernels, gather_weights(): pl.pallas_call(gather_kernel, out_shape=[jax.ShapeDtypeStruct((4, *w_x.sh...  26.8 us
    pallas_call x1, Pallas kernels, middle(): call(middle_kernel, [((ROWS, INNER), BF16), ((ROWS, INNER), BF16), ((ROWS...  24 us
    unnamed x99, local copies, waits for them, and re-layouts  19.6 us
    all_to_all x2, waiting for transfers between devices, swap(): lax.all_to_all(values, 'seq', split_axis=0, concat_axis=0, tiled=True)  17.2 us
    dot_general x5, matrix products, mm(): lax.dot_general(a, b, ((dims[0], dims[1]), ((), ())), precision=precision...  15.8 us
    pallas_call x1, Pallas kernels, front(): call(front_kernel, [((ROWS, INNER), BF16), ((ROWS, 2 * STATE), BF16), ((R...  13.2 us
    all_to_all x1, blocking collectives, swap(): lax.all_to_all(values, 'seq', split_axis=0, concat_axis=0, tiled=True)  12.7 us
  transfers between devices with their start and end apart: 5, of which 1 were waited for; matrix products, arithmetic and copies ran while one was open for 4% of the time, Pallas kernels for 16%

profile of v4, /device:TPU:0, one launch (start us, length us, event | category | flops | bytes accessed | tf_op | source)
XLA Modules:
  0.0 321.3 jit_solution(5311451926455945192)
XLA Ops:
  7.3 0.7 all-gather.3.cloned.1.call-update
  8.0 0.7 all-gather.5.cloned.1.call-update
  8.8 3.6 %collective-permute-start = (bf16[2,3,1024]{2,1,0:T(4,128)(2,1)S(1)}, bf16[2,3,1024]{2,1,0:T(4,128)(2,1)S(1)}, u32[]{:S(2)}, u32[]{:S(2)}) collective-permute-start(bf16[2,3,1024]{2,1,0:T(4,128)(2,1)S(1)} %slice.81), channel_id=1, source_target_pairs={{0,4},{4,8},{8,12},{12,16},{16,20},{20,24},{24,28},{28,32},{32,36}... | collective-permute-start | bytes 36872 | tf_op jit(solution)/shard_map/ppermute | solution.py:1012
  12.3 0.1 copy.50
  12.5 0.1 reshape.112
  14.6 0.1 concatenate.14
  14.7 26.8 %shard_map.279 = (bf16[4,256,2048]{2,1,0:T(8,128)(2,1)}, bf16[4,256,384]{2,1,0:T(8,128)(2,1)S(1)}, f32[4,4,2,8,128]{4,3,2,1,0:T(8,128)S(1)}) custom-call(bf16[256,2048]{1,0:T(8,128)(2,1)S(1)} %copy-done.4, bf16[256,384]{1,0:T(8,128)(2,1)S(1)} %maximum_maximum_fusion.w_small, f32[8,128]{1,0:T(8,128)S(1)} %bitcast.54), custom_call_target="tpu_custom_call" | custom-call | flops 1000000 | bytes 40000000 | tf_op jit(solution)/shard_map/pallas_call | solution.py:977
  41.6 0.8 fusion.4
  42.4 0.1 reshape.111
  42.5 0.1 copy.60
  42.6 0.1 copy.61
  42.7 0.1 reshape.117
  42.8 0.1 reshape.118.taps_x
  42.9 0.1 reshape.119.bias_x
  43.0 0.2 multiply_reduce_fusion
  43.2 0.2 multiply_convert_fusion.normed
  43.4 0.5 convolution_convert_fusion.1
  43.9 1.6 copy-done.45
  45.5 1.3 convolution_convert_fusion.x_raw
  47.0 13.2 %shard_map.280 = (bf16[256,2048]{1,0:T(8,128)(2,1)S(1)}, bf16[256,256]{1,0:T(8,128)(2,1)S(1)}, f32[256,32]{1,0:T(8,128)S(1)}, f32[256,32]{1,0:T(8,128)S(1)}, bf1...) custom-call(bf16[272,2048]{1,0:T(8,128)(2,1)S(1)} %convolution_convert, ...), custom_call_target="tpu_custom_call" | custom-call | flops 1000000000 | bytes 10000000 | tf_op jit(solution)/shard_map/pallas_call | solution.py:180
  60.1 1.3 copy-done.2
  61.5 0.1 copy.54
  61.6 12.7 %all_to_all.19 = f32[32,1,2]{2,1,0:T(1,128)S(1)} all-to-all(f32[32,1,2]{2,1,0:T(1,128)S(1)} %copy.54), channel_id=1, replica_groups=mesh['seq'=32,'wshard'=4] {'seq'}, dimensions={0} | all-to-all | bytes 512 | tf_op jit(solution)/shard_map/all_to_all | solution.py:998
  74.2 3.9 %all-to-all-start.1 = ((bf16[32,2,64,128]{3,2,1,0:T(8,128)(2,1)}), bf16[32,2,64,128]{3,2,1,0:T(8,128)(2,1)S(1)}, u32[]{:S(2)}, u32[]{:S(2)}) async-start(bf16[32,2,64,128]{3,2,1,0:T(8,128)(2,1)} %get-tuple-element.53), calls=%async_computation.1 | async-start | bytes 2097152 | tf_op jit(solution)/shard_map/all_to_all | solution.py:998
  78.2 0.1 copy.55
  78.3 0.1 copy.56.decay
  78.4 17.2 %all-to-all-done.1.own = bf16[32,2,64,128]{3,2,1,0:T(8,128)(2,1)S(1)} async-done(((bf16[32,2,64,128]{3,2,1,0:T(8,128)(2,1)}), bf16[32,2,64,128]{3,2,1,0:T(8,128)(2,1)S(1)}, u32[]{:S(2)}, u32[]{:S(2)}) %all-to-all-start.1) | async-done | bytes 1048608 | tf_op jit(solution)/shard_map/all_to_all | solution.py:998
  95.6 2.1 shard_map.282
  97.6 6.3 %all-to-all-start.2 = ((bf16[32,2,64,128]{3,2,1,0:T(8,128)(2,1)}), bf16[32,2,64,128]{3,2,1,0:T(8,128)(2,1)S(1)}, u32[]{:S(2)}, u32[]{:S(2)}) async-start(bf16[32,2,64,128]{3,2,1,0:T(8,128)(2,1)} %shard_map.282), calls=%async_computation.2 | async-start | bytes 2097152 | tf_op jit(solution)/shard_map/all_to_all | solution.py:998
  104.0 0.1 copy.62
  104.2 0.1 broadcast_in_dim.18.d_skip
  104.3 1.6 copy-done.3
  105.9 10.7 %shard_map.281.y_in = f32[256,2048]{1,0:T(8,128)S(1)} custom-call(bf16[256,2048]{1,0:T(8,128)(2,1)S(1)} %get-tuple-element.47.xc, bf16[256,256]{1,0:T(8,128)(2,1)S(1)} %get-tuple-element.48.bcc, f32[256,2048]{1,0:T(8,128)S(1)} %copy-done.3, f32[256,2048]{1,0:T(8,128)} %get-tuple-element.50.r_wide.r, f32[16,8,256]{2,1,0:T(8,128)S(1)} %get-tuple-element.51.r_rows), custom_call_target="tpu_custom_call" | custom-call | flops 1000000000 | bytes 10000000 | tf_op jit(solution)/shard_map/pallas_call | solution.py:235
  116.6 1.3 copy-done
  117.9 4.7 %fusion.1.gate = f32[256,2048]{1,0:T(8,128)} fusion(bf16[1024,2048]{1,0:T(8,128)(2,1)} %all-gather.3.cloned.1.call-done.full_z, bf16[272,1024]{1,0:T(8,128)(2,1)S(1)} %copy-done.35), kind=kOutput, calls=%fused_computation.7 | convolution fusion | flops 1073741824 | bytes 6815744 | tf_op jit(solution)/shard_map/dot_general | solution.py:28
  122.6 5.0 %fusion.6.d_mixed = f32[256,2048]{1,0:T(8,128)} fusion(bf16[256,1024]{1,0:T(8,128)(2,1)} %bitcast.81, bf16[2048,1024]{1,0:T(8,128)(2,1)} %all-gather.5.cloned.1.call-done), kind=kOutput, calls=%fused_computation.22 | convolution fusion | flops 1073741824 | bytes 6815744 | tf_op jit(solution)/shard_map/dot_general | solution.py:28
  127.6 0.9 copy-done.33
  128.6 24.0 %shard_map.283 = (bf16[256,2048]{1,0:T(8,128)(2,1)S(1)}, bf16[256,2048]{1,0:T(8,128)(2,1)S(1)}, bf16[256,2048]{1,0:T(8,128)(2,1)S(1)}, bf16[32,2,64,128]{3,2,1,0...) custom-call(f32[256,2048]{1,0:T(8,128)} %copy-done, bf16[256,2048]{1,0:T(8,128)(2,1)S(1)} %get-tuple-element.47.xc, ...), custom_call_target="tpu_custom_call" | custom-call | flops 1000000000 | bytes 10000000 | tf_op jit(solution)/shard_map/pallas_call | solution.py:315
  152.6 1.0 copy-done.17
  153.6 1.0 copy-done.19
  154.6 1.0 copy-done.20
  155.6 1.0 copy-done.21
  156.6 0.7 copy-done.22
  157.2 0.6 copy-done.23
  157.8 129.2 %shard_map.284 = (bf16[4,4,2,128,128]{4,3,2,1,0:T(8,128)(2,1)}, bf16[2,4,4,128,128]{4,3,2,1,0:T(8,128)(2,1)}, bf16[4,4,2,48,128]{4,3,2,1,0:T(8,128)(2,1)}, bf16[...) custom-call(bf16[32,2,64,128]{3,2,1,0:T(8,128)(2,1)} %copy-done.21, ...), custom_call_target="tpu_custom_call" | custom-call | flops 8000000000 | bytes 40000000 | tf_op jit(solution)/shard_map/pallas_call | solution.py:845
  287.0 0.8 slice.96
  287.9 0.6 slice.97
  288.5 0.5 slice_bitcast_fusion
  289.0 0.8 slice.101
  289.9 1.4 slice.105
  291.3 1.4 slice.91
  292.7 1.3 slice.99
  293.9 1.3 slice.100
  295.2 1.2 copy-done.26
  296.4 1.2 copy-done.27
  297.7 1.0 copy-done.28
  298.7 1.0 copy-done.29
  299.7 1.0 copy-done.30
  300.7 6.4 %shard_map.285 = (f32[256,2048]{1,0:T(8,128)}, f32[256,2048]{1,0:T(8,128)}, f32[2,2,128,1024]{3,2,1,0:T(8,128)}, f32[4,2,128,128]{3,2,1,0:T(8,128)S(1)}) custom-call(bf16[4,4,2,128,128]{4,3,2,1,0:T(8,128)(2,1)S(1)} %copy-done.26, bf16[2,4,4,128,128]{4,3,2,1,0:T(8,128)(2,1)S(1)} %copy-done.27, bf16[4,4,2,48,128]{4,3,2,1,0:T(8,128)(2,1)S(1)} %copy-done.29, ...), custom_call_target="tpu_custom_call" | custom-call | flops 1000000000 | bytes 10000000 | tf_op jit(solution)/shard_map/pallas_call | solution.py:877
  307.1 0.7 copy.63
  307.9 0.5 fusion.5
  308.4 0.7 pad_maximum_fusion.1
  309.1 4.3 %fusion = bf16[256,1024]{1,0:T(8,128)(2,1)} fusion(bf16[256,2048]{1,0:T(8,128)(2,1)S(1)} %copy-done.18, bf16[2048,1024]{1,0:T(8,128)(2,1)} %all-gather.5.cloned.1.call-done, bf16[256,1024]{1,0:T(8,128)(2,1)S(1)} %bitcast.65), kind=kOutput, calls=%fused_computation.2 | convolution fusion | flops 1074528256 | bytes 6291456 | tf_op jit(solution)/shard_map/dot_general | solution.py:28
  313.5 1.0 copy.73
  (101 shorter events, 0.7 us)
Async XLA Ops:
  7.2 1.5 copy-start.37
  7.2 5.1 %copy-start.41 = (bf16[256,32]{0,1:T(8,128)(2,1)S(1)}, bf16[256,32]{0,1:T(8,128)(2,1)}, u32[]{:S(2)}) copy-start(bf16[256,32]{0,1:T(8,128)(2,1)} %param.21) | copy-start | bytes 49156
  7.2 5.3 %copy-start.43 = (f32[4,64]{1,0:T(4,128)S(1)}, f32[4,64]{1,0:T(4,128)}, u32[]{:S(2)}) copy-start(f32[4,64]{1,0:T(4,128)} %param.22) | copy-start | bytes 3076
  7.2 7.4 %copy-start.44 = (f32[64]{0:T(128)S(1)}, f32[64]{0:T(128)}, u32[]{:S(2)}) copy-start(f32[64]{0:T(128)} %param.23) | copy-start | bytes 772
  7.2 7.5 %copy-start.39 = (bf16[256,256]{1,0:T(8,128)(2,1)S(1)}, bf16[256,256]{1,0:T(8,128)(2,1)}, u32[]{:S(2)}) copy-start(bf16[256,256]{1,0:T(8,128)(2,1)} %param.20) | copy-start | bytes 393220
  7.2 7.5 %copy-start.4 = (bf16[256,2048]{1,0:T(8,128)(2,1)S(1)}, bf16[256,2048]{1,0:T(8,128)(2,1)}, u32[]{:S(2)}) copy-start(bf16[256,2048]{1,0:T(8,128)(2,1)} %w_x.1) | copy-start | bytes 3145732
  7.2 110.7 %all-gather.3.cloned.1.call-start = ((), (), s32[]{:S(2)}) async-start(), calls=%async_computation.3 | async-start | bytes 5242880 | tf_op jit(solution)/shard_map/all_gather | solution.py:1002
  8.0 114.7 %all-gather.5.cloned.1.call-start = ((), (), s32[]{:S(2)}) async-start(), calls=%async_computation.4 | async-start | bytes 5242880 | tf_op jit(solution)/shard_map/all_gather | solution.py:1002
  8.8 34.2 %collective-permute-start = (bf16[2,3,1024]{2,1,0:T(4,128)(2,1)S(1)}, bf16[2,3,1024]{2,1,0:T(4,128)(2,1)S(1)}, u32[]{:S(2)}, u32[]{:S(2)}) collective-permute-start(bf16[2,3,1024]{2,1,0:T(4,128)(2,1)S(1)} %slice.81), channel_id=1, source_target_pairs={{0,4},{4,8},{8,12},{12,16},{16,20},{20,24},{24,28},{28,32},{32,36}... | collective-permute-start | bytes 36872 | tf_op jit(solution)/shard_map/ppermute | solution.py:1012
  41.5 1.9 copy-start.5
  41.5 1.7 copy-start.42
  42.6 4.3 %copy-start.15 = (f32[32,1]{0,1:T(1,128)}, f32[32,1]{0,1:T(1,128)S(1)}, u32[]{:S(2)}) copy-start(f32[32,1]{0,1:T(1,128)S(1)} %copy.60) | copy-start | bytes 388
  42.7 4.2 %copy-start.16 = (f32[32,1]{0,1:T(1,128)}, f32[32,1]{0,1:T(1,128)S(1)}, u32[]{:S(2)}) copy-start(f32[32,1]{0,1:T(1,128)S(1)} %copy.61) | copy-start | bytes 388
  42.9 4.0 %copy-start.11 = (f32[4,2048]{1,0:T(4,128)}, f32[4,2048]{1,0:T(4,128)S(1)}, u32[]{:S(2)}) copy-start(f32[4,2048]{1,0:T(4,128)S(1)} %reshape.118.taps_x) | copy-start | bytes 98308
  43.0 3.9 %copy-start.13 = (f32[1,2048]{1,0:T(1,128)}, f32[1,2048]{1,0:T(1,128)S(1)}, u32[]{:S(2)}) copy-start(f32[1,2048]{1,0:T(1,128)S(1)} %reshape.119.bias_x) | copy-start | bytes 24580
  43.0 2.5 copy-start.45
  43.4 3.5 %copy-start.34 = (bf16[272,1024]{1,0:T(8,128)(2,1)}, bf16[272,1024]{1,0:T(8,128)(2,1)S(1)}, u32[]{:S(2)}) copy-start(bf16[272,1024]{1,0:T(8,128)(2,1)S(1)} %multiply_convert_fusion.normed) | copy-start | bytes 1671172
  43.9 3.0 copy-start.7
  43.9 3.0 copy-start.9
  45.5 1.4 copy-start.24
  45.5 1.4 copy-start.25
  46.9 13.3 %copy-start.31 = (bf16[272,2048]{1,0:T(8,128)(2,1)}, bf16[272,2048]{1,0:T(8,128)(2,1)S(1)}, u32[]{:S(2)}) copy-start(bf16[272,2048]{1,0:T(8,128)(2,1)S(1)} %convolution_convert_fusion.x_raw) | copy-start | bytes 3342340
  60.1 1.3 copy-start.2
  61.5 36.2 %copy-start.32 = (f32[256,32]{1,0:T(8,128)}, f32[256,32]{1,0:T(8,128)S(1)}, u32[]{:S(2)}) copy-start(f32[256,32]{1,0:T(8,128)S(1)} %get-tuple-element.57.dt) | copy-start | bytes 98308
  61.5 42.8 %copy-start.8 = (f32[16,8,256]{2,1,0:T(8,128)}, f32[16,8,256]{2,1,0:T(8,128)S(1)}, u32[]{:S(2)}) copy-start(f32[16,8,256]{2,1,0:T(8,128)S(1)} %get-tuple-element.51.r_rows) | copy-start | bytes 393220
  61.5 66.2 %copy-start.1 = (bf16[256,2048]{1,0:T(8,128)(2,1)}, bf16[256,2048]{1,0:T(8,128)(2,1)S(1)}, u32[]{:S(2)}) copy-start(bf16[256,2048]{1,0:T(8,128)(2,1)S(1)} %get-tuple-element.47.xc) | copy-start | bytes 3145732
  61.5 66.2 %copy-start.6 = (bf16[256,256]{1,0:T(8,128)(2,1)}, bf16[256,256]{1,0:T(8,128)(2,1)S(1)}, u32[]{:S(2)}) copy-start(bf16[256,256]{1,0:T(8,128)(2,1)S(1)} %get-tuple-element.48.bcc) | copy-start | bytes 393220
  74.2 21.3 %all-to-all-start.1 = ((bf16[32,2,64,128]{3,2,1,0:T(8,128)(2,1)}), bf16[32,2,64,128]{3,2,1,0:T(8,128)(2,1)S(1)}, u32[]{:S(2)}, u32[]{:S(2)}) async-start(bf16[32,2,64,128]{3,2,1,0:T(8,128)(2,1)} %get-tuple-element.53), calls=%async_computation.1 | async-start | bytes 2097152 | tf_op jit(solution)/shard_map/all_to_all | solution.py:998
  78.3 19.3 %copy-start.10 = (f32[32,2]{1,0:T(8,128)}, f32[32,2]{1,0:T(8,128)S(1)}, u32[]{:S(2)}) copy-start(f32[32,2]{1,0:T(8,128)S(1)} %copy.56.decay) | copy-start | bytes 772
  78.3 25.6 %copy-start.40 = (f32[32,1]{1,0:T(8,128)S(1)}, f32[32,1]{1,0:T(8,128)}, u32[]{:S(2)}) copy-start(f32[32,1]{1,0:T(8,128)} %get-tuple-element.75) | copy-start | bytes 388
  97.6 30.0 %all-to-all-start.2 = ((bf16[32,2,64,128]{3,2,1,0:T(8,128)(2,1)}), bf16[32,2,64,128]{3,2,1,0:T(8,128)(2,1)S(1)}, u32[]{:S(2)}, u32[]{:S(2)}) async-start(bf16[32,2,64,128]{3,2,1,0:T(8,128)(2,1)} %shard_map.282), calls=%async_computation.2 | async-start | bytes 2097152 | tf_op jit(solution)/shard_map/all_to_all | solution.py:998
  104.2 23.4 %copy-start.12 = (f32[1,2048]{1,0:T(1,128)}, f32[1,2048]{1,0:T(1,128)S(1)}, u32[]{:S(2)}) copy-start(f32[1,2048]{1,0:T(1,128)S(1)} %broadcast_in_dim.18.d_skip) | copy-start | bytes 24580
  104.3 1.6 copy-start.3
  105.9 12.0 %copy-start.35 = (bf16[272,1024]{1,0:T(8,128)(2,1)S(1)}, bf16[272,1024]{1,0:T(8,128)(2,1)}, u32[]{:S(2)}) copy-start(bf16[272,1024]{1,0:T(8,128)(2,1)} %copy-done.34) | copy-start | bytes 1671172
  116.6 1.3 copy-start
  122.6 5.9 %copy-start.14 = (f32[2048]{0:T(1024)S(1)}, f32[2048]{0:T(1024)}, u32[]{:S(2)}) copy-start(f32[2048]{0:T(1024)} %param.29) | copy-start | bytes 24580
  127.6 1.0 copy-start.33
  152.6 1.0 copy-start.17
  153.6 1.0 copy-start.19
  154.6 1.0 copy-start.20
  155.6 1.0 copy-start.21
  156.6 0.7 copy-start.22
  157.2 0.6 copy-start.23
  295.2 1.2 copy-start.26
  296.4 1.2 copy-start.27
  297.7 1.0 copy-start.28
  298.7 1.0 copy-start.29
  299.7 1.0 copy-start.30
  300.7 8.4 %copy-start.18 = (bf16[256,2048]{1,0:T(8,128)(2,1)S(1)}, bf16[256,2048]{1,0:T(8,128)(2,1)}, u32[]{:S(2)}) copy-start(bf16[256,2048]{1,0:T(8,128)(2,1)} %copy-done.17) | copy-start | bytes 3145732
  300.7 8.4 %copy-start.38 = (bf16[2,128,1024]{2,1,0:T(8,128)(2,1)S(1)}, bf16[2,128,1024]{2,1,0:T(8,128)(2,1)}, u32[]{:S(2)}) copy-start(bf16[2,128,1024]{2,1,0:T(8,128)(2,1)} %param.16) | copy-start | bytes 1572868
  309.1 4.3 %copy-start.36 = (f32[256,1024]{1,0:T(8,128)S(1)}, f32[256,1024]{1,0:T(8,128)}, u32[]{:S(2)}) copy-start(f32[256,1024]{1,0:T(8,128)} %get-tuple-element.61) | copy-start | bytes 3145732
Sparse Core Ops, SparseCore 0:
  9.7 40.9 all-gather.2
  52.4 49.3 all-gather.4

commit v5 on v4

--- a/solution.py
+++ b/solution.py
@@ -112,41 +112,6 @@
     return out
 
 
-def front_kernel(x_raw, bc_raw, dt_raw, taps_x, bias_x, taps_bc, bias_bc, dt_bias, a_log, xc, bcc, dt, r, u, dt_wide, r_wide, r_rows):
-    pair = pl.program_id(0)
-
-    @pl.when(pair == 0)
-    def _():
-        raw = bc_raw[...].astype(F32)
-        steps = dt_raw[0:ROWS, :].astype(F32) + dt_bias[...]
-        dt[...] = jax.nn.softplus(steps)
-        tri = causal_mask().astype(F32)
-        decay = dt[...] * (-jnp.exp(a_log[...]))
-        for b in range(SEQS):
-            pre = conv_pre(padded_of(raw, b), taps_bc[...], bias_bc[...])
-            bcc[TOK * b : TOK * (b + 1), :] = (pre * jax.nn.sigmoid(pre)).astype(BF16)
-            r[TOK * b : TOK * (b + 1), :] = mm(tri, decay[TOK * b : TOK * (b + 1), :], NN, HIGHEST)
-
-    raw = x_raw[...].astype(F32)
-    ex = pair_matrix(pair)
-    both = mm(jnp.concatenate([r[...], dt[...]], axis=0), ex, NN, HIGHEST)
-    r_wide[...] = both[0:ROWS, :]
-    dt_wide[...] = both[ROWS:, :]
-    r_rows[0] = mm(pair_rows(pair), r[...], NT, HIGHEST)
-    for b in range(SEQS):
-        span = slice(TOK * b, TOK * (b + 1))
-        pre = conv_pre(padded_of(raw, b), taps_x[...], bias_x[...])
-        low = (pre * jax.nn.sigmoid(pre)).astype(BF16)
-        xc[span, :] = low
-        r_lanes = both[span, :]
-        dt_lanes = both[ROWS + TOK * b : ROWS + TOK * (b + 1), :]
-        to_end = jnp.exp(r_lanes[TOK - 1 : TOK, :] - r_lanes)
-        scaled = (to_end * (dt_lanes * low.astype(F32))).astype(BF16)
-        state = mm(scaled, bcc[span, 0:STATE], TN).astype(BF16)
-        u[0, b] = state[0:HEAD, :]
-        u[1, b] = state[HEAD:, :]
-
-
 def whole(shape):
     return pl.BlockSpec(shape, lambda *_: (0,) * len(shape))
 
@@ -155,8 +120,6 @@
     return pl.BlockSpec((rows, 128), lambda j: (0, j))
 
 
-STATES = pl.BlockSpec((2, SEQS, HEAD, STATE), lambda j: (j, 0, 0, 0))
-PAIR_ROWS = pl.BlockSpec((1, 8, ROWS), lambda j: (j, 0, 0))
 STATES_SHAPE = (HEADS, SEQS, HEAD, STATE)
 VMEM_LIMIT = 48 * 1024 * 1024
 
@@ -176,69 +139,156 @@
     )
 
 
-def front(x_raw, bc_raw, dt_raw, taps_x, bias_x, taps_bc, bias_bc, dt_bias, a_log):
-    return call(
-        front_kernel,
-        [((ROWS, INNER), BF16), ((ROWS, 2 * STATE), BF16), ((ROWS, HEADS), F32), ((ROWS, HEADS), F32), (STATES_SHAPE, BF16), ((ROWS, INNER), F32), ((ROWS, INNER), F32), ((PAIRS, 8, ROWS), F32)],
-        [lanes(ROWS), whole((ROWS, 2 * STATE)), whole((ROWS, HEADS)), whole((ROWS, HEADS)), STATES, lanes(ROWS), lanes(ROWS), PAIR_ROWS],
-        [
-            lanes(ALL), whole((ALL, 2 * STATE)), whole((ALL, HEADS)), lanes(TAPS), lanes(1),
-            whole((TAPS, 2 * STATE)), whole((1, 2 * STATE)), whole((1, HEADS)), whole((1, HEADS)),
-        ],
-    )(x_raw, bc_raw, dt_raw, taps_x, bias_x, taps_bc, bias_bc, dt_bias, a_log)
-
-
-def states_kernel(reverse, decay, own, before):
-    chunks = own.shape[0]
-
-    def step(i, carry):
-        c = chunks - 1 - i if reverse else i
+def chunk_copy(src, dst, send, recv, to, slot):
+    return pltpu.make_async_remote_copy(
+        src_ref=src.at[to], dst_ref=dst.at[slot], send_sem=send.at[to], recv_sem=recv.at[slot],
+        device_id={"seq": to}, device_id_type=pl.DeviceIdType.MESH,
+    )
+
+
+def each_other(me, step):
+    def go(d, _):
+        step(lax.rem(me + d, HEADS))
+        return 0
+
+    lax.fori_loop(1, HEADS, go, 0)
+
+
+def greet_chunks(me):
+    barrier = pltpu.get_barrier_semaphore()
+    each_other(
+        me,
+        lambda other: pl.semaphore_signal(
+            barrier, inc=1, device_id={"seq": other}, device_id_type=pl.DeviceIdType.MESH
+        ),
+    )
+    return barrier
+
+
+def lane_block(j, size=128):
+    return pl.ds(pl.multiple_of(j * size, size), size)
+
+
+def head_kernel(
+    x_raw, bc_raw, dt_raw, taps_x, bias_x, taps_bc, bias_bc, dt_bias, a_log,
+    xc, bcc, dt, dt_wide, r_wide, r_rows, y_in, start, decay,
+    r, scores, u, u_all, own_decay, s_own, u_send, u_recv, e_send, e_recv, s_send, s_recv,
+):
+    me = lax.axis_index("seq")
+    barrier = greet_chunks(me)
+    raw = bc_raw[...].astype(F32)
+    dt[...] = jax.nn.softplus(dt_raw[0:ROWS, :].astype(F32) + dt_bias[...])
+    tri = causal_mask().astype(F32)
+    rates = dt[...] * (-jnp.exp(a_log[...]))
+    for b in range(SEQS):
+        span = slice(TOK * b, TOK * (b + 1))
+        pre = conv_pre(padded_of(raw, b), taps_bc[...], bias_bc[...])
+        bcc[span, :] = (pre * jax.nn.sigmoid(pre)).astype(BF16)
+        r[span, :] = mm(tri, rates[span, :], NN, HIGHEST)
+        scores[b] = mm(bcc[span, STATE:], bcc[span, 0:STATE], NT)
+    first = iota((8, 128), 1) < HEAD
+    pl.semaphore_wait(barrier, HEADS - 1)
+
+    def front_pair(i, _):
+        j = lax.rem(me // 2 + i, PAIRS)
+        cols = lane_block(j)
+        raw = x_raw[:, cols].astype(F32)
+        both = mm(jnp.concatenate([r[...], dt[...]], axis=0), pair_matrix(j), NN, HIGHEST)
+        r_wide[:, cols] = both[0:ROWS, :]
+        dt_wide[:, cols] = both[ROWS:, :]
+        r_rows[j] = mm(pair_rows(j), r[...], NT, HIGHEST)
+        ends = []
+        for b in range(SEQS):
+            span = slice(TOK * b, TOK * (b + 1))
+            pre = conv_pre(padded_of(raw, b), taps_x[:, cols], bias_x[:, cols])
+            low = (pre * jax.nn.sigmoid(pre)).astype(BF16)
+            xc[span, cols] = low
+            r_lanes = both[span, :]
+            dt_lanes = both[ROWS + TOK * b : ROWS + TOK * (b + 1), :]
+            last = r_lanes[TOK - 1 : TOK, :]
+            ends.append(last)
+            scaled = (jnp.exp(last - r_lanes) * (dt_lanes * low.astype(F32))).astype(BF16)
+            state = mm(scaled, bcc[span, 0:STATE], TN).astype(BF16)
+            u[2 * j, b] = state[0:HEAD, :]
+            u[2 * j + 1, b] = state[HEAD:, :]
+        shrink = jnp.exp(jnp.concatenate([*ends, jnp.zeros((8 - SEQS, 128), F32)], axis=0))
+        turned = pltpu.roll(shrink, HEAD, 1)
+        own_decay[2 * j] = jnp.where(first, shrink, turned)
+        own_decay[2 * j + 1] = jnp.where(first, turned, shrink)
+        for q in range(2):
+            to = 2 * j + q
+
+            @pl.when(to != me)
+            def _():
+                chunk_copy(u, u_all, u_send, u_recv, to, me).start()
+                chunk_copy(own_decay, decay, e_send, e_recv, to, me).start()
+
+        return 0
+
+    lax.fori_loop(0, PAIRS, front_pair, 0)
+    u_all[me] = u[me]
+    decay[me] = own_decay[me]
+
+    def inside_pair(j, _):
+        cols = lane_block(j)
+        for b in range(SEQS):
+            span = slice(TOK * b, TOK * (b + 1))
+            one, two = decay_pair(r_wide[span, cols], r_rows[j, :, span])
+            both = jnp.concatenate([scores[b] * one, scores[b] * two], axis=1).astype(BF16)
+            stepped = (dt_wide[span, cols] * xc[span, cols].astype(F32)).astype(BF16)
+            y_in[span, cols] = mm(both, block_diagonal(stepped), NN)
+        return 0
+
+    lax.fori_loop(0, 6, inside_pair, 0)
+    each_other(me, lambda other: chunk_copy(u, u_all, u_send, u_recv, other, other).wait_recv())
+    each_other(me, lambda other: chunk_copy(own_decay, decay, e_send, e_recv, other, other).wait_recv())
+
+    def chunk_step(c, carry):
         after = []
         for b in range(SEQS):
-            before[c, b] = carry[b].astype(BF16)
-            after.append(decay[c, b] * carry[b] + own[c, b].astype(F32))
+            s_own[c, b] = carry[b].astype(BF16)
+            after.append(decay[c, b : b + 1, :] * carry[b] + u_all[c, b].astype(F32))
         return tuple(after)
 
-    lax.fori_loop(0, chunks, step, tuple(jnp.zeros((HEAD, STATE), F32) for _ in range(SEQS)))
-
-
-def states(decay, own, reverse):
+    lax.fori_loop(0, HEADS, chunk_step, tuple(jnp.zeros((HEAD, STATE), F32) for _ in range(SEQS)))
+    each_other(me, lambda other: chunk_copy(s_own, start, s_send, s_recv, other, me).start())
+    start[me] = s_own[me]
+    lax.fori_loop(6, PAIRS, inside_pair, 0)
+    each_other(me, lambda other: chunk_copy(s_own, start, s_send, s_recv, other, other).wait_recv())
+    each_other(me, lambda other: chunk_copy(u, u_all, u_send, u_recv, other, me).wait_send())
+    each_other(me, lambda other: chunk_copy(own_decay, decay, e_send, e_recv, other, me).wait_send())
+    each_other(me, lambda other: chunk_copy(s_own, start, s_send, s_recv, other, me).wait_send())
+
+
+def head(*args):
+    vmem = pl.BlockSpec(memory_space=pltpu.VMEM)
+    outs = [
+        ((ROWS, INNER), BF16), ((ROWS, 2 * STATE), BF16), ((ROWS, HEADS), F32), ((ROWS, INNER), F32), ((ROWS, INNER), F32),
+        ((PAIRS, 8, ROWS), F32), ((ROWS, INNER), F32), (STATES_SHAPE, BF16), ((HEADS, 8, 128), F32),
+    ]
     return pl.pallas_call(
-        functools.partial(states_kernel, reverse),
-        out_shape=jax.ShapeDtypeStruct(own.shape, BF16),
-        in_specs=[pl.BlockSpec(memory_space=pltpu.SMEM), pl.BlockSpec(memory_space=pltpu.VMEM)],
-        out_specs=pl.BlockSpec(memory_space=pltpu.VMEM),
-        compiler_params=pltpu.CompilerParams(vmem_limit_bytes=VMEM_LIMIT),
-        cost_estimate=pl.CostEstimate(flops=int(1e6), bytes_accessed=int(2e6), transcendentals=0),
-    )(decay, own)
-
-
-def inside_kernel(xc, bcc, dt_wide, r_wide, r_rows, y, scores):
-    pair = pl.program_id(0)
-
-    @pl.when(pair == 0)
-    def _():
-        for b in range(SEQS):
-            span = slice(TOK * b, TOK * (b + 1))
-            scores[b] = mm(bcc[span, STATE:], bcc[span, 0:STATE], NT)
-
-    for b in range(SEQS):
-        span = slice(TOK * b, TOK * (b + 1))
-        dt_lanes = dt_wide[span, :]
-        first, second = decay_pair(r_wide[span, :], r_rows[0, :, span])
-        both = jnp.concatenate([scores[b] * first, scores[b] * second], axis=1).astype(BF16)
-        stepped = (dt_lanes * xc[span, :].astype(F32)).astype(BF16)
-        y[span, :] = mm(both, block_diagonal(stepped), NN)
-
-
-def inside(xc, bcc, dt_wide, r_wide, r_rows):
-    return call(
-        inside_kernel,
-        [((ROWS, INNER), F32)],
-        [lanes(ROWS)],
-        [lanes(ROWS), whole((ROWS, 2 * STATE)), lanes(ROWS), lanes(ROWS), PAIR_ROWS],
-        scratch=[pltpu.VMEM((SEQS, TOK, TOK), F32)],
-    )(xc, bcc, dt_wide, r_wide, r_rows)[0]
+        head_kernel,
+        out_shape=[jax.ShapeDtypeStruct(s, d) for s, d in outs],
+        in_specs=[vmem] * len(args),
+        out_specs=[vmem] * len(outs),
+        scratch_shapes=[
+            pltpu.VMEM((ROWS, HEADS), F32), pltpu.VMEM((SEQS, TOK, TOK), F32), *[pltpu.VMEM(STATES_SHAPE, BF16)] * 2,
+            pltpu.VMEM((HEADS, 8, 128), F32), pltpu.VMEM(STATES_SHAPE, BF16),
+            *[pltpu.SemaphoreType.DMA((HEADS,))] * 6,
+        ],
+        compiler_params=pltpu.CompilerParams(
+            vmem_limit_bytes=VMEM_LIMIT, collective_id=3, has_side_effects=True
+        ),
+        cost_estimate=pl.CostEstimate(flops=int(2e9), bytes_accessed=int(2e7), transcendentals=0),
+    )(*args)
+
+
+WIDE = 512
+QUADS = INNER // WIDE
+
+
+def fold(values):
+    return sum((values[:, 128 * i : 128 * (i + 1)] for i in range(1, WIDE // 128)), values[:, 0:128])
 
 
 def middle_kernel(
@@ -247,8 +297,8 @@
     y_all, square, cross, scale, slope,
 ):
     phase = pl.program_id(0)
-    pair = pl.program_id(1)
-    ex = pair_matrix(pair)
+    quad = pl.program_id(1)
+    ex = (iota((HEADS, WIDE), 0) == 8 * quad + (iota((HEADS, WIDE), 1) >> 6)).astype(F32)
     skip = d_skip[...]
     z = gate[...]
     sig = jax.nn.sigmoid(z)
@@ -256,24 +306,24 @@
 
     @pl.when(phase == 0)
     def _():
-        @pl.when(pair == 0)
+        @pl.when(quad == 0)
         def _():
             square[...] = jnp.zeros_like(square)
             cross[...] = jnp.zeros_like(cross)
 
         for b in range(SEQS):
             span = slice(TOK * b, TOK * (b + 1))
-            before = jnp.concatenate([start[0, b], start[1, b]], axis=0)
+            before = jnp.concatenate([start[h, b] for h in range(8)], axis=0)
             grown = jnp.exp(r[span, :])
-            y_all[pair, span, :] = y_in[span, :] + grown * mm(bcc[span, STATE:], before, NT)
-        y = (y_all[pair] + skip * xc[...].astype(F32)).astype(BF16).astype(F32)
+            y_all[quad, span, :] = y_in[span, :] + grown * mm(bcc[span, STATE:], before, NT)
+        y = (y_all[quad] + skip * xc[...].astype(F32)).astype(BF16).astype(F32)
         gated = y * (z * sig)
-        square[...] += gated * gated
-        cross[...] += pulled * gated
+        square[...] += fold(gated * gated)
+        cross[...] += fold(pulled * gated)
 
     @pl.when(phase == 1)
     def _():
-        @pl.when(pair == 0)
+        @pl.when(quad == 0)
         def _():
             inv = lax.rsqrt(jnp.sum(square[...], axis=1, keepdims=True) * (1.0 / INNER) + EPS)
             mean = jnp.sum(cross[...], axis=1, keepdims=True) * (1.0 / INNER)
@@ -281,52 +331,54 @@
             slope[...] = jnp.broadcast_to(inv * inv * inv * mean, slope.shape)
             row_dot[...] = jnp.zeros_like(row_dot)
 
-        y = (y_all[pair] + skip * xc[...].astype(F32)).astype(BF16).astype(F32)
+        y = (y_all[quad] + skip * xc[...].astype(F32)).astype(BF16).astype(F32)
         silu = z * sig
         gated = y * silu
-        unit = gated * scale[...]
+        inv = jnp.concatenate([scale[...]] * 4, axis=1)
+        unit = gated * inv
         mixed[...] = (unit * gain[...]).astype(BF16)
         d_gain[...] = jnp.sum(d_mixed[...] * unit, axis=0, keepdims=True)
-        d_gated = scale[...] * pulled - gated * slope[...]
+        d_gated = inv * pulled - gated * jnp.concatenate([slope[...]] * 4, axis=1)
         low = (d_gated * silu).astype(BF16)
         d_y[...] = low
         d_gate[...] = (d_gated * y * (sig * (1.0 + z * (1.0 - sig)))).astype(BF16)
-        row_dot[...] += head_sums(low.astype(F32) * y_all[pair], ex)
+        row_dot[...] += head_sums(low.astype(F32) * y_all[quad], ex)
         for b in range(SEQS):
             span = slice(TOK * b, TOK * (b + 1))
             grown = jnp.exp(r[span, :])
             state = mm((grown * low[span, :].astype(F32)).astype(BF16), bcc[span, STATE:], TN).astype(BF16)
-            own[0, b] = state[0:HEAD, :]
-            own[1, b] = state[HEAD:, :]
+            for h in range(8):
+                own[h, b] = state[HEAD * h : HEAD * (h + 1), :]
 
 
 def middle(y_in, xc, bcc, r, start, d_skip, gate, d_mixed, gain):
     def cols(rows):
-        return pl.BlockSpec((rows, 128), lambda p, j: (0, j))
+        return pl.BlockSpec((rows, WIDE), lambda p, j: (0, j))
 
     def first(rows):
-        return pl.BlockSpec((rows, 128), lambda p, j: (0, jnp.where(p == 0, j, PAIRS - 1)))
+        return pl.BlockSpec((rows, WIDE), lambda p, j: (0, jnp.where(p == 0, j, QUADS - 1)))
 
     def second(rows):
-        return pl.BlockSpec((rows, 128), lambda p, j: (0, jnp.where(p == 1, j, 0)))
-
-    states_in = pl.BlockSpec((2, SEQS, HEAD, STATE), lambda p, j: (jnp.where(p == 0, j, PAIRS - 1), 0, 0, 0))
-    states_out = pl.BlockSpec((2, SEQS, HEAD, STATE), lambda p, j: (jnp.where(p == 1, j, 0), 0, 0, 0))
+        return pl.BlockSpec((rows, WIDE), lambda p, j: (0, jnp.where(p == 1, j, 0)))
+
+    states_in = pl.BlockSpec((8, SEQS, HEAD, STATE), lambda p, j: (jnp.where(p == 0, j, QUADS - 1), 0, 0, 0))
+    states_out = pl.BlockSpec((8, SEQS, HEAD, STATE), lambda p, j: (jnp.where(p == 1, j, 0), 0, 0, 0))
     return call(
         middle_kernel,
         [((ROWS, INNER), BF16), ((ROWS, INNER), BF16), ((ROWS, INNER), BF16), (STATES_SHAPE, BF16), ((1, INNER), F32), ((ROWS, HEADS), F32)],
         [second(ROWS), second(ROWS), second(ROWS), states_out, second(1), whole((ROWS, HEADS))],
         [first(ROWS), cols(ROWS), whole((ROWS, 2 * STATE)), cols(ROWS), states_in, cols(1), cols(ROWS), cols(ROWS), cols(1)],
-        grid=(2, PAIRS),
-        scratch=[pltpu.VMEM((PAIRS, ROWS, 128), F32)] + [pltpu.VMEM((ROWS, 128), F32)] * 4,
+        grid=(2, QUADS),
+        scratch=[pltpu.VMEM((QUADS, ROWS, WIDE), F32)] + [pltpu.VMEM((ROWS, 128), F32)] * 4,
     )(y_in, xc, bcc, r, start, d_skip, gate, d_mixed, gain)
 
 
-REDUCE = (("y", "z", "x"), ("x", "y", "z"), ("x", "y", "z"), ("y", "z", "x"), ("z", "x", "y"))
-GATHER = (("l", "z", "x"), ("x", "z", "l"), ("l", "z", "x"), ("l", "x", "z"), ("x", "z", "l"))
+REDUCE = (("y", "z", "x"), ("z", "x", "y"), ("x", "y", "z")) + (("x", "y", "z"), ("y", "z", "x"), ("z", "x", "y"))
+GATHER = (("l", "z", "x"), ("l", "x", "z"), ("x", "z", "l")) * 2
 PIECE = 128
 EXTRA = 32
-PIECE_ROWS = (PIECE, PIECE, 48, 48, 32 + EXTRA)
+PIECE_ROWS = (80, 48 + 32, 96, 48, 48, 32 + EXTRA)
+EARLY, LATE = (0, 1, 2), (3, 4, 5)
 SETS = len(PIECE_ROWS)
 SMALL = 3 * 128
 VECTOR = (16, INNER)
@@ -371,14 +423,14 @@
     v, decay, xc, d_y, bcc, dt, dt_wide, r_wide, r_rows, x_raw, start, bc_raw, dt_raw, row_dot,
     taps_x, bias_x, taps_bc, bias_bc, dt_bias, a_log, d_skip, g_norm,
     normed, d_gate, mixed, cot, layer_in, gain_in, full_z, full_x, full_small,
-    out_z, out_out, out_xa, out_xb, out_xc, input_grad, vector,
+    out_za, out_zb, out_zc, out_xa, out_xb, out_xc, input_grad, vector,
     weights, v_all, g_own, end, d_stepped, scores, d_scores, d_bc, sums, d_x_raw, d_small, g_x, g_bc, g_heads,
     d_normed, halo_out, halo_in, few_own, few_got,
     keep_n, keep_m, next_n, next_m, sib_n, sib_gate, sib_m, sib_cot, sib_wide, sib_small,
-    parts_z, parts_out, parts_xa, parts_xb, parts_xc,
-    got_z1, got_out1, got_xa1, got_xb1, got_xc1, sum_z1, sum_out1, sum_xa1, sum_xb1, sum_xc1,
-    got_z2, got_out2, got_xa2, got_xb2, got_xc2, sum_z2, sum_out2, sum_xa2, sum_xb2, sum_xc2,
-    got_z3, got_out3, got_xa3, got_xb3, got_xc3,
+    parts_za, parts_zb, parts_zc, parts_xa, parts_xb, parts_xc,
+    got_za1, got_zb1, got_zc1, got_xa1, got_xb1, got_xc1, sum_za1, sum_zb1, sum_zc1, sum_xa1, sum_xb1, sum_xc1,
+    got_za2, got_zb2, got_zc2, got_xa2, got_xb2, got_xc2, sum_za2, sum_zb2, sum_zc2, sum_xa2, sum_xb2, sum_xc2,
+    got_za3, got_zb3, got_zc3, got_xa3, got_xb3, got_xc3,
     v_send, v_recv, g_send, g_recv, sib_send, sib_recv, red_send, red_recv, all_send, all_recv,
     few_send, few_recv, halo_sem, load_sem,
 ):
@@ -386,15 +438,7 @@
     me = lax.axis_index("seq")
     core = at["core"]
     sibling = peers(at, "core")[0]
-    barrier = pltpu.get_barrier_semaphore()
-
-    def greet_chunk(d, _):
-        pl.semaphore_signal(
-            barrier, inc=1, device_id={"seq": lax.rem(me + d, HEADS)}, device_id_type=pl.DeviceIdType.MESH
-        )
-        return 0
-
-    lax.fori_loop(1, HEADS, greet_chunk, 0)
+    barrier = greet_chunks(me)
     others = [sibling] + peers(at, "y")
     for other in others:
         pl.semaphore_signal(barrier, inc=1, device_id=device(other), device_id_type=pl.DeviceIdType.MESH)
@@ -410,37 +454,15 @@
         started.append(one)
         return one
 
-    def chunk_copy(src, dst, send, recv, to, at_dst):
-        return pltpu.make_async_remote_copy(
-            src_ref=src.at[to], dst_ref=dst.at[at_dst], send_sem=send.at[to], recv_sem=recv.at[at_dst],
-            device_id={"seq": to}, device_id_type=pl.DeviceIdType.MESH,
-        )
-
     def swap_start(src, dst, send, recv):
-        def go(d, _):
-            chunk_copy(src, dst, send, recv, lax.rem(me + d, HEADS), me).start()
-            return 0
-
-        lax.fori_loop(1, HEADS, go, 0)
+        each_other(me, lambda other: chunk_copy(src, dst, send, recv, other, me).start())
         dst[me] = src[me]
 
     def swap_wait(src, dst, send, recv):
-        def go(d, _):
-            other = lax.rem(me + d, HEADS)
-            chunk_copy(src, dst, send, recv, other, other).wait_recv()
-            return 0
-
-        lax.fori_loop(1, HEADS, go, 0)
+        each_other(me, lambda other: chunk_copy(src, dst, send, recv, other, other).wait_recv())
 
     def swap_sent(src, dst, send, recv):
-        def go(d, _):
-            chunk_copy(src, dst, send, recv, lax.rem(me + d, HEADS), me).wait_send()
-            return 0
-
-        lax.fori_loop(1, HEADS, go, 0)
-
-    def lane_block(j, size=128):
-        return pl.ds(pl.multiple_of(j * size, size), size)
+        each_other(me, lambda other: chunk_copy(src, dst, send, recv, other, me).wait_send())
 
     swap_start(v, v_all, v_send, v_recv)
 
@@ -488,20 +510,23 @@
         after = []
         for b in range(SEQS):
             g_own[c, b] = carry[b].astype(BF16)
-            after.append(decay[c, b] * carry[b] + v_all[c, b].astype(F32))
+            after.append(decay[c, b : b + 1, :] * carry[b] + v_all[c, b].astype(F32))
         return tuple(after)
 
     lax.fori_loop(0, HEADS, chunk_step, tuple(jnp.zeros((HEAD, STATE), F32) for _ in range(SEQS)))
     swap_start(g_own, end, g_send, g_recv)
 
-    parts = (parts_z, parts_out, parts_xa, parts_xb, parts_xc)
+    parts = (parts_za, parts_zb, parts_zc, parts_xa, parts_xb, parts_xc)
     got = (
-        (got_z1, got_out1, got_xa1, got_xb1, got_xc1),
-        (got_z2, got_out2, got_xa2, got_xb2, got_xc2),
-        (got_z3, got_out3, got_xa3, got_xb3, got_xc3),
-    )
-    partial = ((sum_z1, sum_out1, sum_xa1, sum_xb1, sum_xc1), (sum_z2, sum_out2, sum_xa2, sum_xb2, sum_xc2))
-    outs = (out_z, out_out, out_xa, out_xb, out_xc)
+        (got_za1, got_zb1, got_zc1, got_xa1, got_xb1, got_xc1),
+        (got_za2, got_zb2, got_zc2, got_xa2, got_xb2, got_xc2),
+        (got_za3, got_zb3, got_zc3, got_xa3, got_xb3, got_xc3),
+    )
+    partial = (
+        (sum_za1, sum_zb1, sum_zc1, sum_xa1, sum_xb1, sum_xc1),
+        (sum_za2, sum_zb2, sum_zc2, sum_xa2, sum_xb2, sum_xc2),
+    )
+    outs = (out_za, out_zb, out_zc, out_xa, out_xb, out_xc)
     arriving = [None] * SETS
 
     def send_stage(stage, which, src):
@@ -571,11 +596,14 @@
         res = mm(keep_n[:, 0:ROWS], d_gate[:, cols], NN) + mm(next_n[:, 0:ROWS], sib_gate[:, cols], NN)
         for y in range(4):
             for k in range(2):
-                parts_z[y, (n % 2) * 2 + k, n // 2] = res[128 * y : 128 * y + 128, 128 * k : 128 * k + 128].astype(BF16)
+                block = res[128 * y : 128 * y + 128, 128 * k : 128 * k + 128].astype(BF16)
+                x, z = n // 2, (n % 2) * 2 + k
+                parts_za[y, z, x] = block[0:80]
+                parts_zb[z, x, y, 0:48] = block[80:128]
         return 0
 
     lax.fori_loop(0, 8, tile_z, 0)
-    send_stage(0, 0, parts_z)
+    send_stage(0, 0, parts_za)
     for one in from_sibling[3:]:
         one.wait_recv()
     for h in range(2):
@@ -588,11 +616,15 @@
             for half in range(2):
                 for k in range(2):
                     row = 256 * y + 128 * half
-                    parts_out[half * 2 + n // 2, y, (n % 2) * 2 + k] = res[row : row + 128, 128 * k : 128 * k + 128].astype(BF16)
+                    block = res[row : row + 128, 128 * k : 128 * k + 128].astype(BF16)
+                    x, z = half * 2 + n // 2, (n % 2) * 2 + k
+                    parts_zb[z, x, y, 48:80] = block[0:32]
+                    parts_zc[x, y, z] = block[32:128]
         return 0
 
     lax.fori_loop(0, 4, tile_out, 0)
-    send_stage(0, 1, parts_out)
+    send_stage(0, 1, parts_zb)
+    send_stage(0, 2, parts_zc)
 
     loading.wait()
     for n in range(4):
@@ -687,8 +719,8 @@
     )
     small_coming = copy(d_small, sib_small, sib_send.at[10], sib_recv.at[10], sibling)
 
-    add_stage(0, 0)
-    add_stage(0, 1)
+    for which in EARLY:
+        add_stage(0, which)
 
     def tile_x(n, _):
         cols = lane_block(n, 256)
@@ -705,8 +737,8 @@
     for quarter in range(4):
         wide_coming[quarter].wait_recv()
         lax.fori_loop(2 * quarter, 2 * quarter + 2, tile_x, 0)
-    send_stage(0, 2, parts_xa)
-    send_stage(0, 3, parts_xb)
+    send_stage(0, 3, parts_xa)
+    send_stage(0, 4, parts_xb)
     small_coming.wait_recv()
     res = mm(keep_n[...], d_small[...], NN) + mm(next_n[...], sib_small[...], NN)
     for y in range(4):
@@ -715,7 +747,9 @@
             for k in range(3):
                 parts_xc[z, k, y, 32:] = res[row : row + EXTRA, 128 * k : 128 * k + 128].astype(BF16)
             parts_xc[z, 3, y, 32:] = jnp.zeros((EXTRA, 128), BF16)
-    send_stage(0, 4, parts_xc)
+    send_stage(0, 5, parts_xc)
+    for which in EARLY:
+        add_stage(1, which)
 
     loading.wait()
     d_normed[ROWS:, :] = jnp.zeros((ALL - ROWS, d_normed.shape[1]), F32)
@@ -729,8 +763,8 @@
     )
     halo.start()
     started.append(halo)
-    add_stage(1, 0)
-    add_stage(1, 1)
+    for which in EARLY:
+        last_add(which)
     halo.wait_recv()
     inner = jnp.where(me == HEADS - 1, 0.0, 1.0)
     for b in range(SEQS):
@@ -782,25 +816,24 @@
         return value
 
     few_start(0, few)
-    last_add(0)
-    last_add(1)
+    for which in EARLY:
+        gather_next(1, which)
+    for which in LATE:
+        add_stage(0, which)
     few_start(1, few_sum(0))
-    for which in (2, 3, 4):
-        add_stage(0, which)
-    gather_next(1, 0)
-    gather_next(1, 1)
+    for which in LATE:
+        add_stage(1, which)
     few_start(2, few_sum(1))
-    for which in (2, 3, 4):
-        add_stage(1, which)
-    gather_next(2, 0)
-    gather_next(2, 1)
+    for which in EARLY:
+        gather_next(2, which)
+    for which in LATE:
+        last_add(which)
     few_start(3, few_sum(2))
-    for which in (2, 3, 4):
-        last_add(which)
+    for which in LATE:
+        gather_next(1, which)
     vector[...] = few_sum(3)
-    for stage in (1, 2):
-        for which in (2, 3, 4):
-            gather_next(stage, which)
+    for which in LATE:
+        gather_next(2, which)
     for which in range(SETS):
         arrived(which)
     for one in started:
@@ -813,7 +846,6 @@
     vmem = pl.BlockSpec(memory_space=pltpu.VMEM)
     hbm = pl.BlockSpec(memory_space=pl.ANY)
     specs = [vmem] * len(args)
-    specs[1] = pl.BlockSpec(memory_space=pltpu.SMEM)
     specs[-3] = specs[-2] = hbm
     width = args[-2].shape[0]
     dims = {"x": 4, "z": 4, "l": 2}
@@ -855,14 +887,16 @@
     )(*args)
 
 
-def unpack_kernel(sum_z, sum_out, sum_xa, sum_xb, sum_xc, out_z, out_x, out_out, out_extra):
+def unpack_kernel(sum_za, sum_zb, sum_zc, sum_xa, sum_xb, sum_xc, out_z, out_x, out_out, out_extra):
     for low in range(2):
         base = PIECE * low
-        out_z[base : base + PIECE, :] = sum_z[0, 0, low].astype(F32)
+        out_z[base : base + 80, :] = sum_za[0, 0, low].astype(F32)
+        out_z[base + 80 : base + 128, :] = sum_zb[0, 0, low, 0:48, :].astype(F32)
+        out_out[low, 0, 0:32, :] = sum_zb[0, 0, low, 48:80, :].astype(F32)
+        out_out[low, 0, 32:128, :] = sum_zc[low, 0, 0].astype(F32)
         out_x[base : base + 48, :] = sum_xa[0, 0, low].astype(F32)
         out_x[base + 48 : base + 96, :] = sum_xb[0, 0, low].astype(F32)
         out_x[base + 96 : base + 128, :] = sum_xc[low, 0, 0, 0:32, :].astype(F32)
-        out_out[low, 0] = sum_out[low, 0, 0].astype(F32)
         out_extra[0, low] = sum_xc[low, 0, 0, 32:, :].astype(F32)
 
 
@@ -994,10 +1028,6 @@
     )(w_x, w_small, own)
 
 
-def swap(values):
-    return lax.all_to_all(values, "seq", split_axis=0, concat_axis=0, tiled=True)
-
-
 def gather_rows(shard):
     return lax.all_gather(shard, "wshard", axis=0, tiled=True)
 
@@ -1034,13 +1064,11 @@
     x_raw = mm(normed, full_x, NN).astype(BF16)
     small_raw = mm(normed, full_small, NN).astype(BF16)
     bc_raw, dt_raw = small_raw[:, : 2 * STATE], small_raw[:, 2 * STATE : 2 * STATE + HEADS]
-    xc, bcc, dt, r, u, dt_wide, r_wide, r_rows = front(x_raw, bc_raw, dt_raw, taps_x, bias_x, conv_bc_weight, bias_bc, bias_dt, log_a)
-    decay = jnp.exp(swap(r[TOK - 1 :: TOK].T))
-    u_all = swap(u)
-    y_in = inside(xc, bcc, dt_wide, r_wide, r_rows)
+    xc, bcc, dt, dt_wide, r_wide, r_rows, y_in, start, decay = head(
+        x_raw, bc_raw, dt_raw, taps_x, bias_x, conv_bc_weight, bias_bc, bias_dt, log_a
+    )
     gate = mm(normed[:ROWS], full_z, NN)
     d_mixed = mm(upstream, full_out, NT)
-    start = swap(states(decay, u_all, False))
     mixed, d_y, d_gate, v, g_norm, row_dot = middle(
         y_in, xc, bcc, r_wide, start, skip_wide, gate, d_mixed, gain_norm.reshape(1, INNER)
     )

time: 323 us -> 283 us (0.88)
  waiting for transfers between devices: 18.6 us -> 3.35 us
  blocking collectives: 12.7 us -> 0 us
  starting transfers between devices: 13.9 us -> 3.64 us
    pallas_call x3 -> x1, Pallas kernels: 26 us -> 50.8 us  [head(): pl.pallas_call(head_kernel, out_shape=[jax.ShapeDtypeStruct(s, d) for s,...]
    all_to_all x2 -> x0, waiting for transfers between devices: 17.2 us -> none  [swap(): lax.all_to_all(values, 'seq', split_axis=0, concat_axis=0, tiled=True)]
    pallas_call x1, Pallas kernels: 24 us -> 10.5 us  [middle(): call(middle_kernel, [((ROWS, INNER), BF16), ((ROWS, INNER), BF16), ((ROWS...]
    pallas_call x1, Pallas kernels: 129 us -> 116 us  [tail(): pl.pallas_call(tail_kernel, out_shape=out_shape, in_specs=specs, out_spec...]
    all_to_all x1 -> x0, blocking collectives: 12.7 us -> none  [swap(): lax.all_to_all(values, 'seq', split_axis=0, concat_axis=0, tiled=True)]
    all_to_all x2 -> x0, starting transfers between devices: 10.3 us -> none  [swap(): lax.all_to_all(values, 'seq', split_axis=0, concat_axis=0, tiled=True)]
    unnamed x99 -> x97, local copies, waits for them, and re-layouts: 19.6 us -> 20.5 us
  transfers between devices with their start and end apart: 5 -> 3, of which waited for: 1 -> 1; matrix products, arithmetic and copies ran while one was open for 4% -> 3% of each run, Pallas kernels for 16% -> 28%
where the time goes in v5:
time: 283 us; the launch traced here: 282 us
  Pallas kernels  211 us (75%)
  local copies, waits for them, and re-layouts  30.1 us (11%)
  between operations  16.5 us (6%)
  matrix products  16.2 us (6%)
  starting transfers between devices  3.64 us (1%)
  waiting for transfers between devices  3.35 us (1%)
    pallas_call x1, Pallas kernels, tail(): pl.pallas_call(tail_kernel, out_shape=out_shape, in_specs=specs, out_spec...  116 us
    pallas_call x1, Pallas kernels, head(): pl.pallas_call(head_kernel, out_shape=[jax.ShapeDtypeStruct(s, d) for s,...  50.8 us
    pallas_call x1, Pallas kernels, gather_weights(): pl.pallas_call(gather_kernel, out_shape=[jax.ShapeDtypeStruct((4, *w_x.sh...  26.8 us
    unnamed x97, local copies, waits for them, and re-layouts  20.5 us
    dot_general x5, matrix products, mm(): lax.dot_general(a, b, ((dims[0], dims[1]), ((), ())), precision=precision...  16.2 us
    pallas_call x1, Pallas kernels, middle(): call(middle_kernel, [((ROWS, INNER), BF16), ((ROWS, INNER), BF16), ((ROWS...  10.5 us
    pallas_call x1, Pallas kernels, unpack(): call(unpack_kernel, [((2 * PIECE, INNER), F32), ((2 * PIECE, INNER), F32)...  6.36 us
  transfers between devices with their start and end apart: 3, of which 1 were waited for; matrix products, arithmetic and copies ran while one was open for 3% of the time, Pallas kernels for 28%

profile of v5, /device:TPU:0, one launch (start us, length us, event | category | flops | bytes accessed | tf_op | source)
XLA Modules:
  0.0 281.9 jit_solution(11937322403349448804)
XLA Ops:
  7.3 0.7 all-gather.3.cloned.1.call-update
  8.0 0.0 all-gather.5.cloned.1.call-start
  8.0 0.7 all-gather.5.cloned.1.call-update
  8.8 3.6 %collective-permute-start = (bf16[2,3,1024]{2,1,0:T(4,128)(2,1)S(1)}, bf16[2,3,1024]{2,1,0:T(4,128)(2,1)S(1)}, u32[]{:S(2)}, u32[]{:S(2)}) collective-permute-start(bf16[2,3,1024]{2,1,0:T(4,128)(2,1)S(1)} %slice.78), channel_id=1, source_target_pairs={{0,4},{4,8},{8,12},{12,16},{16,20},{20,24},{24,28},{28,32},{32,36}... | collective-permute-start | bytes 36872 | tf_op jit(solution)/shard_map/ppermute | solution.py:1042
  12.3 0.1 copy.32
  12.5 0.1 reshape.109
  14.5 0.1 pad.9.clone
  14.6 0.1 concatenate.14
  14.7 26.8 %shard_map.279 = (bf16[4,256,2048]{2,1,0:T(8,128)(2,1)}, bf16[4,256,384]{2,1,0:T(8,128)(2,1)S(1)}, f32[4,4,2,8,128]{4,3,2,1,0:T(8,128)S(1)}) custom-call(bf16[256,2048]{1,0:T(8,128)(2,1)S(1)} %copy-done, bf16[256,384]{1,0:T(8,128)(2,1)S(1)} %maximum_maximum_fusion.w_small, f32[8,128]{1,0:T(8,128)S(1)} %bitcast.49), custom_call_target="tpu_custom_call" | custom-call | flops 1000000 | bytes 40000000 | tf_op jit(solution)/shard_map/pallas_call | solution.py:1011
  41.6 0.1 fusion.4
  41.7 0.1 reshape.108
  41.8 0.1 copy.38
  41.9 0.1 copy.39
  41.9 0.1 reshape.114
  42.1 0.1 reshape.115.taps_x
  42.2 0.1 reshape.116.bias_x
  42.2 0.1 copy.40
  42.3 0.1 broadcast_in_dim.17
  42.4 0.1 broadcast_in_dim.18.d_skip
  42.5 0.2 multiply_reduce_fusion
  42.7 0.2 multiply_convert_fusion.normed
  42.9 0.5 convolution_convert_fusion.1
  43.5 1.5 copy-done.43
  45.0 1.3 convolution_convert_fusion.x_raw
  46.5 50.8 %shard_map.280 = (bf16[256,2048]{1,0:T(8,128)(2,1)S(1)}, bf16[256,256]{1,0:T(8,128)(2,1)S(1)}, f32[256,32]{1,0:T(8,128)S(1)}, f32[256,2048]{1,0:T(8,128)S(1)}, f...) custom-call(bf16[272,2048]{1,0:T(8,128)(2,1)S(1)} %convolution_conve, ...), custom_call_target="tpu_custom_call" | custom-call | flops 2000000000 | bytes 20000000 | tf_op jit(solution)/shard_map/pallas_call | solution.py:269
  97.3 1.0 copy-done.2
  98.2 1.0 copy-done.28
  99.3 1.3 copy-done.29
  100.6 0.6 copy-done.30
  101.2 0.7 copy-done.31
  101.9 0.7 copy-done.32
  102.6 5.2 %fusion.1.gate = f32[256,2048]{1,0:T(8,128)} fusion(bf16[1024,2048]{1,0:T(8,128)(2,1)} %all-gather.3.cloned.1.call-done.full_z, bf16[272,1024]{1,0:T(8,128)(2,1)S(1)} %copy-done.34), kind=kOutput, calls=%fused_computation.7 | convolution fusion | flops 1073741824 | bytes 6815744 | tf_op jit(solution)/shard_map/dot_general | solution.py:28
  107.8 2.0 all-gather.5.cloned.1.call-done
  109.8 4.8 %fusion.6.d_mixed = f32[256,2048]{1,0:T(8,128)} fusion(bf16[256,1024]{1,0:T(8,128)(2,1)S(1)} %bitcast.76, bf16[2048,1024]{1,0:T(8,128)(2,1)} %all-gather.5.cloned.1.call-done), kind=kOutput, calls=%fused_computation.21 | convolution fusion | flops 1073741824 | bytes 6815744 | tf_op jit(solution)/shard_map/dot_general | solution.py:28
  114.6 10.5 %shard_map.281 = (bf16[256,2048]{1,0:T(8,128)(2,1)S(1)}, bf16[256,2048]{1,0:T(8,128)(2,1)S(1)}, bf16[256,2048]{1,0:T(8,128)(2,1)S(1)}, bf16[32,2,64,128]{3,2,1,0...) custom-call(f32[256,2048]{1,0:T(8,128)} %get-tuple-element.49.y_in, ...), custom_call_target="tpu_custom_call" | custom-call | flops 1000000000 | bytes 10000000 | tf_op jit(solution)/shard_map/pallas_call | solution.py:366
  125.1 1.0 copy-done.13
  126.1 1.0 copy-done.15
  127.1 1.0 copy-done.16
  128.1 1.0 copy-done.17
  129.0 0.6 copy-done.18
  129.7 0.6 copy-done.19
  130.3 116.5 %shard_map.282 = (bf16[4,4,2,80,128]{4,3,2,1,0:T(8,128)(2,1)}, bf16[4,4,2,80,128]{4,3,2,1,0:T(8,128)(2,1)}, bf16[2,4,4,96,128]{4,3,2,1,0:T(8,128)(2,1)}, bf16[4,...) custom-call(bf16[32,2,64,128]{3,2,1,0:T(8,128)(2,1)} %copy-done.17, ...), custom_call_target="tpu_custom_call" | custom-call | flops 8000000000 | bytes 40000000 | tf_op jit(solution)/shard_map/pallas_call | solution.py:877
  246.8 0.8 slice.92
  247.6 0.1 constant_dynamic-slice_fusion.1
  247.7 0.6 slice.93
  248.3 0.5 slice_bitcast_fusion
  248.8 0.8 slice.97
  249.6 1.4 slice.101
  251.1 1.4 slice.87
  252.4 1.3 slice.95
  253.7 1.3 slice.96
  255.0 1.1 copy-done.22
  256.1 1.1 copy-done.23
  257.2 1.1 copy-done.24
  258.3 1.0 copy-done.25
  259.3 1.0 copy-done.26
  260.3 1.0 copy-done.27
  261.3 6.4 %shard_map.283 = (f32[256,2048]{1,0:T(8,128)}, f32[256,2048]{1,0:T(8,128)}, f32[2,2,128,1024]{3,2,1,0:T(8,128)}, f32[4,2,128,128]{3,2,1,0:T(8,128)S(1)}) custom-call(bf16[4,4,2,80,128]{4,3,2,1,0:T(8,128)(2,1)S(1)} %copy-done.23, bf16[4,4,2,80,128]{4,3,2,1,0:T(8,128)(2,1)S(1)} %copy-done.24, bf16[2,4,4,96,128]{4,3,2,1,0:T(8,128)(2,1)S(1)} %copy-done.22, ...), custom_call_target="tpu_custom_call" | custom-call | flops 1000000000 | bytes 10000000 | tf_op jit(solution)/shard_map/pallas_call | solution.py:911
  267.7 0.7 copy.41
  268.4 0.1 constant_dynamic-slice_fusion
  268.5 0.5 fusion.5
  269.0 0.7 pad_maximum_fusion.1
  269.7 4.3 %fusion = bf16[256,1024]{1,0:T(8,128)(2,1)} fusion(bf16[256,2048]{1,0:T(8,128)(2,1)S(1)} %copy-done.14, bf16[2048,1024]{1,0:T(8,128)(2,1)} %all-gather.5.cloned.1.call-done, bf16[256,1024]{1,0:T(8,128)(2,1)S(1)} %bitcast.60), kind=kOutput, calls=%fused_computation.2 | convolution fusion | flops 1074528256 | bytes 6291456 | tf_op jit(solution)/shard_map/dot_general | solution.py:28
  274.1 1.0 copy.51
  (87 shorter events, 0.4 us)
Async XLA Ops:
  7.2 1.5 copy-start.36
  7.2 5.1 %copy-start.39 = (bf16[256,32]{0,1:T(8,128)(2,1)S(1)}, bf16[256,32]{0,1:T(8,128)(2,1)}, u32[]{:S(2)}) copy-start(bf16[256,32]{0,1:T(8,128)(2,1)} %param.21) | copy-start | bytes 49156
  7.2 5.3 %copy-start.41 = (f32[4,64]{1,0:T(4,128)S(1)}, f32[4,64]{1,0:T(4,128)}, u32[]{:S(2)}) copy-start(f32[4,64]{1,0:T(4,128)} %param.22) | copy-start | bytes 3076
  7.2 7.4 %copy-start.42 = (f32[64]{0:T(128)S(1)}, f32[64]{0:T(128)}, u32[]{:S(2)}) copy-start(f32[64]{0:T(128)} %param.23) | copy-start | bytes 772
  7.2 7.5 %copy-start.38 = (bf16[256,256]{1,0:T(8,128)(2,1)S(1)}, bf16[256,256]{1,0:T(8,128)(2,1)}, u32[]{:S(2)}) copy-start(bf16[256,256]{1,0:T(8,128)(2,1)} %param.20) | copy-start | bytes 393220
  7.2 7.5 %copy-start = (bf16[256,2048]{1,0:T(8,128)(2,1)S(1)}, bf16[256,2048]{1,0:T(8,128)(2,1)}, u32[]{:S(2)}) copy-start(bf16[256,2048]{1,0:T(8,128)(2,1)} %w_x.1) | copy-start | bytes 3145732
  7.2 95.3 %all-gather.3.cloned.1.call-start = ((), (), s32[]{:S(2)}) async-start(), calls=%async_computation | async-start | bytes 5242880 | tf_op jit(solution)/shard_map/all_gather | solution.py:1032
  8.0 101.8 %all-gather.5.cloned.1.call-start = ((), (), s32[]{:S(2)}) async-start(), calls=%async_computation.1 | async-start | bytes 5242880 | tf_op jit(solution)/shard_map/all_gather | solution.py:1032
  8.8 33.7 %collective-permute-start = (bf16[2,3,1024]{2,1,0:T(4,128)(2,1)S(1)}, bf16[2,3,1024]{2,1,0:T(4,128)(2,1)S(1)}, u32[]{:S(2)}, u32[]{:S(2)}) collective-permute-start(bf16[2,3,1024]{2,1,0:T(4,128)(2,1)S(1)} %slice.78), channel_id=1, source_target_pairs={{0,4},{4,8},{8,12},{12,16},{16,20},{20,24},{24,28},{28,32},{32,36}... | collective-permute-start | bytes 36872 | tf_op jit(solution)/shard_map/ppermute | solution.py:1042
  41.5 1.4 copy-start.3
  41.5 1.2 copy-start.40
  41.9 4.5 %copy-start.11 = (f32[32,1]{0,1:T(1,128)}, f32[32,1]{0,1:T(1,128)S(1)}, u32[]{:S(2)}) copy-start(f32[32,1]{0,1:T(1,128)S(1)} %copy.38) | copy-start | bytes 388
  41.9 4.4 %copy-start.12 = (f32[32,1]{0,1:T(1,128)}, f32[32,1]{0,1:T(1,128)S(1)}, u32[]{:S(2)}) copy-start(f32[32,1]{0,1:T(1,128)S(1)} %copy.39) | copy-start | bytes 388
  42.2 4.2 %copy-start.7 = (f32[4,2048]{1,0:T(4,128)}, f32[4,2048]{1,0:T(4,128)S(1)}, u32[]{:S(2)}) copy-start(f32[4,2048]{1,0:T(4,128)S(1)} %reshape.115.taps_x) | copy-start | bytes 98308
  42.2 4.1 %copy-start.9 = (f32[1,2048]{1,0:T(1,128)}, f32[1,2048]{1,0:T(1,128)S(1)}, u32[]{:S(2)}) copy-start(f32[1,2048]{1,0:T(1,128)S(1)} %reshape.116.bias_x) | copy-start | bytes 24580
  42.5 72.1 %copy-start.8 = (f32[1,2048]{1,0:T(1,128)}, f32[1,2048]{1,0:T(1,128)S(1)}, u32[]{:S(2)}) copy-start(f32[1,2048]{1,0:T(1,128)S(1)} %broadcast_in_dim.18.d_skip) | copy-start | bytes 24580
  42.5 2.5 copy-start.43
  42.9 3.5 %copy-start.33 = (bf16[272,1024]{1,0:T(8,128)(2,1)}, bf16[272,1024]{1,0:T(8,128)(2,1)S(1)}, u32[]{:S(2)}) copy-start(bf16[272,1024]{1,0:T(8,128)(2,1)S(1)} %multiply_convert_fusion.normed) | copy-start | bytes 1671172
  43.4 3.0 %copy-start.4 = (bf16[272,256]{1,0:T(8,128)(2,1)}, bf16[272,256]{1,0:T(8,128)(2,1)S(1)}, u32[]{:S(2)}) copy-start(bf16[272,256]{1,0:T(8,128)(2,1)S(1)} %slice.102.bc_raw) | copy-start | bytes 417796
  43.4 3.0 %copy-start.6 = (bf16[272,32]{1,0:T(8,128)(2,1)}, bf16[272,32]{1,0:T(8,128)(2,1)S(1)}, u32[]{:S(2)}) copy-start(bf16[272,32]{1,0:T(8,128)(2,1)S(1)} %slice.103.dt_raw) | copy-start | bytes 52228
  45.0 1.4 copy-start.20
  45.0 1.4 copy-start.21
  46.4 56.1 %copy-start.34 = (bf16[272,1024]{1,0:T(8,128)(2,1)S(1)}, bf16[272,1024]{1,0:T(8,128)(2,1)}, u32[]{:S(2)}) copy-start(bf16[272,1024]{1,0:T(8,128)(2,1)} %copy-done.33) | copy-start | bytes 1671172
  97.2 1.0 copy-start.2
  98.2 1.0 copy-start.28
  99.3 1.3 copy-start.29
  100.6 0.7 copy-start.30
  101.2 0.7 copy-start.31
  101.9 0.7 copy-start.32
  102.5 12.0 %copy-start.1 = (bf16[256,2048]{1,0:T(8,128)(2,1)}, bf16[256,2048]{1,0:T(8,128)(2,1)S(1)}, u32[]{:S(2)}) copy-start(bf16[256,2048]{1,0:T(8,128)(2,1)S(1)} %get-tuple-element.50.xc) | copy-start | bytes 3145732
  102.6 12.0 %copy-start.5 = (bf16[256,256]{1,0:T(8,128)(2,1)}, bf16[256,256]{1,0:T(8,128)(2,1)S(1)}, u32[]{:S(2)}) copy-start(bf16[256,256]{1,0:T(8,128)(2,1)S(1)} %get-tuple-element.51.bcc) | copy-start | bytes 393220
  102.6 7.2 %copy-start.44 = (bf16[2,128,1024]{2,1,0:T(8,128)(2,1)S(1)}, bf16[2,128,1024]{2,1,0:T(8,128)(2,1)}, u32[]{:S(2)}) copy-start(bf16[2,128,1024]{2,1,0:T(8,128)(2,1)} %param.31) | copy-start | bytes 1572868
  109.8 4.8 %copy-start.10 = (f32[2048]{0:T(1024)S(1)}, f32[2048]{0:T(1024)}, u32[]{:S(2)}) copy-start(f32[2048]{0:T(1024)} %param.29) | copy-start | bytes 24580
  125.1 1.0 copy-start.13
  126.1 1.0 copy-start.15
  127.1 1.0 copy-start.16
  128.1 1.0 copy-start.17
  129.0 0.7 copy-start.18
  129.7 0.6 copy-start.19
  255.0 1.1 copy-start.22
  256.1 1.1 copy-start.23
  257.2 1.1 copy-start.24
  258.3 1.0 copy-start.25
  259.3 1.0 copy-start.26
  260.3 1.0 copy-start.27
  261.3 8.4 %copy-start.14 = (bf16[256,2048]{1,0:T(8,128)(2,1)S(1)}, bf16[256,2048]{1,0:T(8,128)(2,1)}, u32[]{:S(2)}) copy-start(bf16[256,2048]{1,0:T(8,128)(2,1)} %copy-done.13) | copy-start | bytes 3145732
  261.3 8.4 %copy-start.37 = (bf16[2,128,1024]{2,1,0:T(8,128)(2,1)S(1)}, bf16[2,128,1024]{2,1,0:T(8,128)(2,1)}, u32[]{:S(2)}) copy-start(bf16[2,128,1024]{2,1,0:T(8,128)(2,1)} %param.16) | copy-start | bytes 1572868
  269.7 4.3 %copy-start.35 = (f32[256,1024]{1,0:T(8,128)S(1)}, f32[256,1024]{1,0:T(8,128)}, u32[]{:S(2)}) copy-start(f32[256,1024]{1,0:T(8,128)} %get-tuple-element.64) | copy-start | bytes 3145732
Sparse Core Ops, SparseCore 0:
  9.7 40.9 all-gather.2
  52.4 57.2 all-gather.4

commit v6 on v5

--- a/solution.py
+++ b/solution.py
@@ -121,7 +121,7 @@
 
 
 STATES_SHAPE = (HEADS, SEQS, HEAD, STATE)
-VMEM_LIMIT = 48 * 1024 * 1024
+VMEM_LIMIT = 62 * 1024 * 1024
 
 
 def call(kernel, outs, out_specs, in_specs, grid=(PAIRS,), scratch=(), cost=None):
@@ -139,6 +139,100 @@
     )
 
 
+def position():
+    seq, shard = lax.axis_index("seq"), lax.axis_index("wshard")
+    high, core = shard // 2, shard % 2
+    low = seq % 2
+    return {"z": seq // 8, "x": (seq // 2) % 4, "y": high * 2 + low, "l": low, "core": core}
+
+
+def device(at):
+    return {"seq": at["z"] * 8 + at["x"] * 2 + at["y"] % 2, "wshard": (at["y"] // 2) * 2 + at["core"]}
+
+
+def moved(at, axis, to):
+    new = dict(at)
+    if axis == "l":
+        new["y"] = (at["y"] // 2) * 2 + to
+        new["l"] = to
+    else:
+        new[axis] = to
+        if axis == "y":
+            new["l"] = to % 2
+    return new
+
+
+def peers(at, axis):
+    size = 2 if axis in ("l", "core") else 4
+    return [moved(at, axis, lax.rem(at[axis] + d, size)) for d in range(1, size)]
+
+
+def greet(everyone, more=0):
+    barrier = pltpu.get_barrier_semaphore()
+    for other in everyone:
+        pl.semaphore_signal(barrier, inc=1, device_id=device(other), device_id_type=pl.DeviceIdType.MESH)
+    pl.semaphore_wait(barrier, len(everyone) + more)
+
+
+class Flows:
+    def __init__(self, at, flows, copy):
+        self.at, self.flows, self.copy = at, flows, copy
+        high = at["y"] // 2
+        self.mine, self.opposite = high * 2 + at["core"], (1 - high) * 2 + at["core"]
+        self.sibling = peers(at, "core")[0]
+        self.partner = moved(at, "y", 3 - at["y"])
+        self.last = []
+
+    def view(self, ref, shard, row, count, first, size):
+        row = pl.multiple_of(row, 16)
+        if shard is None:
+            return ref.at[pl.ds(row, count), first : first + size]
+        return ref.at[shard, pl.ds(row, count), first : first + size]
+
+    def begin(self):
+        self.arriving = []
+        for i, (src, ref, first, size, a, b, rows) in enumerate(self.flows):
+            row = (self.at[b] * 4 + self.at[a]) * rows
+            here = self.view(src, None, row, rows, first, size)
+            there = self.view(ref, self.mine, row, rows, first, size)
+            self.arriving.append(self.copy(here, there, i, self.partner))
+
+    def spread(self):
+        n = len(self.flows)
+        self.second = []
+        for i, (src, ref, first, size, a, b, rows) in enumerate(self.flows):
+            self.arriving[i].wait_recv()
+            piece = self.view(ref, self.opposite, (self.at[b] * 4 + self.at[a]) * rows, rows, first, size)
+            self.second.append([self.copy(piece, piece, n + 3 * i + d, to) for d, to in enumerate(peers(self.at, a))])
+
+    def spread_more(self):
+        n = len(self.flows)
+        self.third = []
+        for i, (src, ref, first, size, a, b, rows) in enumerate(self.flows):
+            for one in self.second[i]:
+                one.wait_recv()
+            block = self.view(ref, self.opposite, self.at[b] * 4 * rows, 4 * rows, first, size)
+            self.third.append([self.copy(block, block, 4 * n + 3 * i + d, to) for d, to in enumerate(peers(self.at, b))])
+            self.last.append(self.copy(block, block, 7 * n + i, self.sibling))
+
+    def forward(self):
+        n = len(self.flows)
+        for i, (src, ref, first, size, a, b, rows) in enumerate(self.flows):
+            for d in range(3):
+                self.third[i][d].wait_recv()
+                block = self.view(ref, self.opposite, lax.rem(self.at[b] + 3 - d, 4) * 4 * rows, 4 * rows, first, size)
+                self.last.append(self.copy(block, block, 8 * n + 3 * i + d, self.sibling))
+
+    def own(self, pairs):
+        n = len(self.flows)
+        for j, (src, ref) in enumerate(pairs):
+            self.last.append(self.copy(src, ref.at[self.mine], 11 * n + j, self.sibling))
+
+    def finish(self):
+        for one in self.last:
+            one.wait_recv()
+
+
 def chunk_copy(src, dst, send, recv, to, slot):
     return pltpu.make_async_remote_copy(
         src_ref=src.at[to], dst_ref=dst.at[slot], send_sem=send.at[to], recv_sem=recv.at[slot],
@@ -167,6 +261,15 @@
 
 def lane_block(j, size=128):
     return pl.ds(pl.multiple_of(j * size, size), size)
+
+
+def pairs_loop(first, last, body):
+    def two(i, _):
+        body(2 * i, 0)
+        body(2 * i + 1, 0)
+        return 0
+
+    lax.fori_loop(first // 2, last // 2, two, 0)
 
 
 def head_kernel(
@@ -225,7 +328,7 @@
 
         return 0
 
-    lax.fori_loop(0, PAIRS, front_pair, 0)
+    pairs_loop(0, PAIRS, front_pair)
     u_all[me] = u[me]
     decay[me] = own_decay[me]
 
@@ -239,7 +342,7 @@
             y_in[span, cols] = mm(both, block_diagonal(stepped), NN)
         return 0
 
-    lax.fori_loop(0, 6, inside_pair, 0)
+    pairs_loop(0, 6, inside_pair)
     each_other(me, lambda other: chunk_copy(u, u_all, u_send, u_recv, other, other).wait_recv())
     each_other(me, lambda other: chunk_copy(own_decay, decay, e_send, e_recv, other, other).wait_recv())
 
@@ -253,7 +356,7 @@
     lax.fori_loop(0, HEADS, chunk_step, tuple(jnp.zeros((HEAD, STATE), F32) for _ in range(SEQS)))
     each_other(me, lambda other: chunk_copy(s_own, start, s_send, s_recv, other, me).start())
     start[me] = s_own[me]
-    lax.fori_loop(6, PAIRS, inside_pair, 0)
+    pairs_loop(6, PAIRS, inside_pair)
     each_other(me, lambda other: chunk_copy(s_own, start, s_send, s_recv, other, other).wait_recv())
     each_other(me, lambda other: chunk_copy(u, u_all, u_send, u_recv, other, me).wait_send())
     each_other(me, lambda other: chunk_copy(own_decay, decay, e_send, e_recv, other, me).wait_send())
@@ -292,17 +395,23 @@
 
 
 def middle_kernel(
-    y_in, xc, bcc, r, start, d_skip, gate, d_mixed, gain,
+    y_in, xc, bcc, r, start, d_skip, normed, cot, w_z, w_out, gain,
     mixed, d_y, d_gate, own, d_gain, row_dot,
-    y_all, square, cross, scale, slope,
+    y_all, gate, d_mixed, square, cross, scale, slope,
 ):
     phase = pl.program_id(0)
     quad = pl.program_id(1)
     ex = (iota((HEADS, WIDE), 0) == 8 * quad + (iota((HEADS, WIDE), 1) >> 6)).astype(F32)
     skip = d_skip[...]
-    z = gate[...]
+
+    @pl.when(phase == 0)
+    def _():
+        gate[quad] = mm(normed[0:ROWS, :], w_z[...], NN)
+        d_mixed[quad] = mm(cot[...], w_out[...], NT)
+
+    z = gate[quad]
     sig = jax.nn.sigmoid(z)
-    pulled = d_mixed[...] * gain[...]
+    pulled = d_mixed[quad] * gain[...]
 
     @pl.when(phase == 0)
     def _():
@@ -337,7 +446,7 @@
         inv = jnp.concatenate([scale[...]] * 4, axis=1)
         unit = gated * inv
         mixed[...] = (unit * gain[...]).astype(BF16)
-        d_gain[...] = jnp.sum(d_mixed[...] * unit, axis=0, keepdims=True)
+        d_gain[...] = jnp.sum(d_mixed[quad] * unit, axis=0, keepdims=True)
         d_gated = inv * pulled - gated * jnp.concatenate([slope[...]] * 4, axis=1)
         low = (d_gated * silu).astype(BF16)
         d_y[...] = low
@@ -351,7 +460,7 @@
                 own[h, b] = state[HEAD * h : HEAD * (h + 1), :]
 
 
-def middle(y_in, xc, bcc, r, start, d_skip, gate, d_mixed, gain):
+def middle(y_in, xc, bcc, r, start, d_skip, normed, cot, w_z, w_out, gain):
     def cols(rows):
         return pl.BlockSpec((rows, WIDE), lambda p, j: (0, j))
 
@@ -361,16 +470,17 @@
     def second(rows):
         return pl.BlockSpec((rows, WIDE), lambda p, j: (0, jnp.where(p == 1, j, 0)))
 
+    out_rows = pl.BlockSpec((WIDE, w_out.shape[1]), lambda p, j: (jnp.where(p == 0, j, QUADS - 1), 0))
     states_in = pl.BlockSpec((8, SEQS, HEAD, STATE), lambda p, j: (jnp.where(p == 0, j, QUADS - 1), 0, 0, 0))
     states_out = pl.BlockSpec((8, SEQS, HEAD, STATE), lambda p, j: (jnp.where(p == 1, j, 0), 0, 0, 0))
     return call(
         middle_kernel,
         [((ROWS, INNER), BF16), ((ROWS, INNER), BF16), ((ROWS, INNER), BF16), (STATES_SHAPE, BF16), ((1, INNER), F32), ((ROWS, HEADS), F32)],
         [second(ROWS), second(ROWS), second(ROWS), states_out, second(1), whole((ROWS, HEADS))],
-        [first(ROWS), cols(ROWS), whole((ROWS, 2 * STATE)), cols(ROWS), states_in, cols(1), cols(ROWS), cols(ROWS), cols(1)],
+        [first(ROWS), cols(ROWS), whole((ROWS, 2 * STATE)), cols(ROWS), states_in, cols(1), whole(normed.shape), whole(cot.shape), first(w_z.shape[0]), out_rows, cols(1)],
         grid=(2, QUADS),
-        scratch=[pltpu.VMEM((QUADS, ROWS, WIDE), F32)] + [pltpu.VMEM((ROWS, 128), F32)] * 4,
-    )(y_in, xc, bcc, r, start, d_skip, gate, d_mixed, gain)
+        scratch=[pltpu.VMEM((QUADS, ROWS, WIDE), F32)] * 3 + [pltpu.VMEM((ROWS, 128), F32)] * 4,
+    )(y_in, xc, bcc, r, start, d_skip, normed, cot, w_z, w_out, gain)
 
 
 REDUCE = (("y", "z", "x"), ("z", "x", "y"), ("x", "y", "z")) + (("x", "y", "z"), ("y", "z", "x"), ("z", "x", "y"))
@@ -384,46 +494,11 @@
 VECTOR = (16, INNER)
 
 
-def position():
-    seq, shard = lax.axis_index("seq"), lax.axis_index("wshard")
-    high, core = shard // 2, shard % 2
-    low = seq % 2
-    return {"z": seq // 8, "x": (seq // 2) % 4, "y": high * 2 + low, "l": low, "core": core}
-
-
-def device(at):
-    return {"seq": at["z"] * 8 + at["x"] * 2 + at["y"] % 2, "wshard": (at["y"] // 2) * 2 + at["core"]}
-
-
-def moved(at, axis, to):
-    new = dict(at)
-    if axis == "l":
-        new["y"] = (at["y"] // 2) * 2 + to
-        new["l"] = to
-    else:
-        new[axis] = to
-        if axis == "y":
-            new["l"] = to % 2
-    return new
-
-
-def peers(at, axis):
-    size = 2 if axis in ("l", "core") else 4
-    return [moved(at, axis, lax.rem(at[axis] + d, size)) for d in range(1, size)]
-
-
-def greet(everyone):
-    barrier = pltpu.get_barrier_semaphore()
-    for other in everyone:
-        pl.semaphore_signal(barrier, inc=1, device_id=device(other), device_id_type=pl.DeviceIdType.MESH)
-    pl.semaphore_wait(barrier, len(everyone))
-
-
 def tail_kernel(
     v, decay, xc, d_y, bcc, dt, dt_wide, r_wide, r_rows, x_raw, start, bc_raw, dt_raw, row_dot,
     taps_x, bias_x, taps_bc, bias_bc, dt_bias, a_log, d_skip, g_norm,
-    normed, d_gate, mixed, cot, layer_in, gain_in, full_z, full_x, full_small,
-    out_za, out_zb, out_zc, out_xa, out_xb, out_xc, input_grad, vector,
+    normed, d_gate, mixed, cot, layer_in, gain_in, full_z, full_x, full_out, full_small,
+    out_za, out_zb, out_zc, out_xa, out_xb, out_xc, input_grad, layer_out, vector,
     weights, v_all, g_own, end, d_stepped, scores, d_scores, d_bc, sums, d_x_raw, d_small, g_x, g_bc, g_heads,
     d_normed, halo_out, halo_in, few_own, few_got,
     keep_n, keep_m, next_n, next_m, sib_n, sib_gate, sib_m, sib_cot, sib_wide, sib_small,
@@ -475,8 +550,17 @@
     pairs = [(columns(normed, h, 1 - core, 256), sib_n.at[h]) for h in range(2)] + [(d_gate, sib_gate)]
     pairs += [(columns(mixed, h, 1 - core, 512), sib_m.at[h]) for h in range(2)] + [(cot, sib_cot)]
     from_sibling = [copy(a, b, sib_send.at[i], sib_recv.at[i], sibling) for i, (a, b) in enumerate(pairs)]
-    loading = pltpu.make_async_copy(full_z, weights, load_sem)
-    loading.start()
+
+    half = weights.shape[2]
+    halves = (slice(0, half), slice(half, 2 * half))
+
+    def load(views):
+        going = [pltpu.make_async_copy(views[h], weights.at[h], load_sem.at[h]) for h in range(2)]
+        for one in going:
+            one.start()
+        return going
+
+    loading = load([full_z.at[:, h] for h in halves])
 
     d_scores[...] = jnp.zeros_like(d_scores)
     for b in range(SEQS):
@@ -496,7 +580,7 @@
             d_scores[b] += d_both[0:TOK, :] * first + d_both[TOK:, :] * second
         return 0
 
-    lax.fori_loop(0, PAIRS, inside_pair, 0)
+    pairs_loop(0, PAIRS, inside_pair)
     for b in range(SEQS):
         span = slice(TOK * b, TOK * (b + 1))
         low = d_scores[b].astype(BF16)
@@ -626,12 +710,12 @@
     send_stage(0, 1, parts_zb)
     send_stage(0, 2, parts_zc)
 
-    loading.wait()
+    for one in loading:
+        one.wait()
     for n in range(4):
         cols = slice(256 * n, 256 * (n + 1))
-        d_normed[0:ROWS, cols] = mm(d_gate[...], weights[cols, :], NT)
-    loading = pltpu.make_async_copy(full_x, weights, load_sem)
-    loading.start()
+        d_normed[0:ROWS, cols] = sum(mm(d_gate[:, h], weights[i, cols, :], NT) for i, h in enumerate(halves))
+    loading = load([full_x.at[:, h] for h in halves])
 
     swap_wait(g_own, end, g_send, g_recv)
     sums[...] = jnp.zeros_like(sums)
@@ -679,7 +763,7 @@
 
     wide_coming = []
     for quarter in range(4):
-        lax.fori_loop(4 * quarter, 4 * quarter + 4, back_pair, 0)
+        pairs_loop(4 * quarter, 4 * quarter + 4, back_pair)
         cols = slice(512 * quarter, 512 * (quarter + 1))
         wide_coming.append(
             copy(d_x_raw.at[:, cols], sib_wide.at[:, cols], sib_send.at[6 + quarter], sib_recv.at[6 + quarter], sibling)
@@ -751,11 +835,15 @@
     for which in EARLY:
         add_stage(1, which)
 
-    loading.wait()
+    for one in loading:
+        one.wait()
     d_normed[ROWS:, :] = jnp.zeros((ALL - ROWS, d_normed.shape[1]), F32)
     for n in range(4):
         cols = slice(256 * n, 256 * (n + 1))
-        d_normed[:, cols] += mm(d_x_raw[...], weights[cols, :], NT) + mm(d_small[...], full_small[cols, :], NT)
+        d_normed[:, cols] += mm(d_small[...], full_small[cols, :], NT) + sum(
+            mm(d_x_raw[:, h], weights[i, cols, :], NT) for i, h in enumerate(halves)
+        )
+    loading = load([full_out.at[h, :] for h in halves])
     halo_out[...] = d_normed[ROWS:, :]
     halo = pltpu.make_async_remote_copy(
         src_ref=halo_out, dst_ref=halo_in, send_sem=halo_sem.at[0], recv_sem=halo_sem.at[1],
@@ -826,6 +914,12 @@
     few_start(2, few_sum(1))
     for which in EARLY:
         gather_next(2, which)
+    for one in loading:
+        one.wait()
+    for n in range(4):
+        cols = slice(256 * n, 256 * (n + 1))
+        product = sum(mm(mixed[:, h], weights[i, :, cols], NN) for i, h in enumerate(halves))
+        layer_out[:, cols] = (layer_in[:, cols].astype(F32) + product).astype(BF16)
     for which in LATE:
         last_add(which)
     few_start(3, few_sum(2))
@@ -846,13 +940,13 @@
     vmem = pl.BlockSpec(memory_space=pltpu.VMEM)
     hbm = pl.BlockSpec(memory_space=pl.ANY)
     specs = [vmem] * len(args)
-    specs[-3] = specs[-2] = hbm
-    width = args[-2].shape[0]
+    specs[-4] = specs[-3] = specs[-2] = hbm
+    width = args[-1].shape[0]
     dims = {"x": 4, "z": 4, "l": 2}
     out_shape = [
         jax.ShapeDtypeStruct((*(dims[a] for a in reversed(GATHER[i])), PIECE_ROWS[i], 128), BF16) for i in range(SETS)
     ]
-    out_shape += [jax.ShapeDtypeStruct((ROWS, width), F32), jax.ShapeDtypeStruct(VECTOR, F32)]
+    out_shape += [jax.ShapeDtypeStruct((ROWS, width), d) for d in (F32, BF16)] + [jax.ShapeDtypeStruct(VECTOR, F32)]
 
     def bufs(*lead):
         return [pltpu.VMEM((*lead, PIECE_ROWS[i], 128), BF16) for i in range(SETS)]
@@ -861,7 +955,7 @@
         return [pltpu.SemaphoreType.DMA(shape)] * 2
 
     scratch = [
-        pltpu.VMEM((width, INNER), BF16), *[pltpu.VMEM(STATES_SHAPE, BF16)] * 3, pltpu.VMEM((ROWS, INNER), F32),
+        pltpu.VMEM((2, width, INNER // 2), BF16), *[pltpu.VMEM(STATES_SHAPE, BF16)] * 3, pltpu.VMEM((ROWS, INNER), F32),
         *[pltpu.VMEM((SEQS, TOK, TOK), F32)] * 2, pltpu.VMEM((ROWS, 2 * STATE), F32),
         pltpu.VMEM((2 * ROWS + 8, HEADS), F32), pltpu.VMEM((ALL, INNER), BF16), pltpu.VMEM((ALL, SMALL), BF16),
         pltpu.VMEM((8, INNER), F32), pltpu.VMEM((8, 2 * STATE), F32), pltpu.VMEM((8, HEADS), F32),
@@ -872,7 +966,7 @@
         pltpu.VMEM((ROWS, width), BF16), pltpu.VMEM((ALL, INNER), BF16), pltpu.VMEM((ALL, SMALL), BF16),
         *bufs(4, 4, 4), *bufs(3, 4, 4), *bufs(4, 4), *bufs(3, 4), *bufs(4), *bufs(3),
         *sems(HEADS), *sems(HEADS), *sems(11), *sems(SETS, 3, 3), *sems(SETS, 3, 3), *sems(4, 3),
-        pltpu.SemaphoreType.DMA((2,)), pltpu.SemaphoreType.DMA,
+        pltpu.SemaphoreType.DMA((2,)), pltpu.SemaphoreType.DMA((2,)),
     ]
     return pl.pallas_call(
         tail_kernel,
@@ -881,54 +975,86 @@
         out_specs=[vmem] * len(out_shape),
         scratch_shapes=scratch,
         compiler_params=pltpu.CompilerParams(
-            vmem_limit_bytes=62 * 1024 * 1024, collective_id=1, has_side_effects=True
+            vmem_limit_bytes=VMEM_LIMIT, collective_id=1, has_side_effects=True
         ),
         cost_estimate=pl.CostEstimate(flops=int(8e9), bytes_accessed=int(4e7), transcendentals=0),
     )(*args)
 
 
-def unpack_kernel(sum_za, sum_zb, sum_zc, sum_xa, sum_xb, sum_xc, out_z, out_x, out_out, out_extra):
+def unpack_kernel(
+    sum_za, sum_zb, sum_zc, sum_xa, sum_xb, sum_xc, total,
+    out_z, out_x, out_out, out_extra, g_x, g_norm, g_in, g_bc, g_heads,
+):
     for low in range(2):
         base = PIECE * low
-        out_z[base : base + 80, :] = sum_za[0, 0, low].astype(F32)
-        out_z[base + 80 : base + 128, :] = sum_zb[0, 0, low, 0:48, :].astype(F32)
-        out_out[low, 0, 0:32, :] = sum_zb[0, 0, low, 48:80, :].astype(F32)
-        out_out[low, 0, 32:128, :] = sum_zc[low, 0, 0].astype(F32)
-        out_x[base : base + 48, :] = sum_xa[0, 0, low].astype(F32)
-        out_x[base + 48 : base + 96, :] = sum_xb[0, 0, low].astype(F32)
-        out_x[base + 96 : base + 128, :] = sum_xc[low, 0, 0, 0:32, :].astype(F32)
-        out_extra[0, low] = sum_xc[low, 0, 0, 32:, :].astype(F32)
-
-
-def unpack(*gathered):
+        for z in range(4):
+            cols = slice(128 * z, 128 * (z + 1))
+            out_z[base : base + 80, cols] = sum_za[0, z, low].astype(F32)
+            out_z[base + 80 : base + 128, cols] = sum_zb[z, 0, low, 0:48, :].astype(F32)
+            out_out[low, 0, 0:32, cols] = sum_zb[z, 0, low, 48:80, :].astype(F32)
+            out_out[low, 0, 32:128, cols] = sum_zc[low, z, 0].astype(F32)
+            out_x[base : base + 48, cols] = sum_xa[0, z, low].astype(F32)
+            out_x[base + 48 : base + 96, cols] = sum_xb[z, 0, low].astype(F32)
+            out_x[base + 96 : base + 128, cols] = sum_xc[low, z, 0, 0:32, :].astype(F32)
+            out_extra[0, low, EXTRA * z : EXTRA * (z + 1), :] = sum_xc[low, z, 0, 32:, :].astype(F32)
+
+    @pl.when(pl.program_id(0) == 0)
+    def _():
+        g_x[...] = total[0:8, :]
+        rest = total[8:16, :]
+        g_norm[...] = rest[0:1, :]
+        g_in[...] = rest[1:2, 0 : g_in.shape[1]]
+        g_bc[...] = rest[2 : 2 + TAPS + 1, 0 : 2 * STATE]
+        g_heads[...] = rest[2:5, 2 * STATE : 2 * STATE + 128]
+
+
+def unpack(width, *gathered):
+    few = ((8, INNER), (1, INNER), (1, width), (TAPS + 1, 2 * STATE), (3, 128))
     specs = []
     for i in range(SETS):
         def where(n, order=GATHER[i]):
-            return tuple({"x": n // 4, "z": n % 4, "l": 0}[a] for a in reversed(order)) + (0, 0)
-
-        block = tuple(2 if a == "l" else 1 for a in reversed(GATHER[i])) + (PIECE_ROWS[i], 128)
+            return tuple({"x": n, "z": 0, "l": 0}[a] for a in reversed(order)) + (0, 0)
+
+        block = tuple({"x": 1, "z": 4, "l": 2}[a] for a in reversed(GATHER[i])) + (PIECE_ROWS[i], 128)
         specs.append(pl.BlockSpec(block, where))
+    wide = pl.BlockSpec((2 * PIECE, WIDE), lambda i: (0, i))
     return call(
         unpack_kernel,
-        [((2 * PIECE, INNER), F32), ((2 * PIECE, INNER), F32), ((2, 2, PIECE, 8 * 128), F32), ((4, 2, 4 * EXTRA, 128), F32)],
+        [((2 * PIECE, INNER), F32), ((2 * PIECE, INNER), F32), ((2, 2, PIECE, 8 * 128), F32), ((4, 2, 4 * EXTRA, 128), F32)]
+        + [(d, F32) for d in few],
         [
-            lanes(2 * PIECE), lanes(2 * PIECE),
-            pl.BlockSpec((2, 1, PIECE, 128), lambda i: (0, i // 8, 0, ((i // 4) % 2) * 4 + i % 4)),
-            pl.BlockSpec((1, 2, EXTRA, 128), lambda i: (i // 4, 0, i % 4, 0)),
+            wide, wide,
+            pl.BlockSpec((2, 1, PIECE, WIDE), lambda i: (0, i // 2, 0, i % 2)),
+            pl.BlockSpec((1, 2, 4 * EXTRA, 128), lambda i: (i, 0, 0, 0)), *[whole(d) for d in few],
         ],
-        specs,
+        [*specs, whole(VECTOR)],
+        grid=(4,),
     )(*gathered)
 
 
 def gather_kernel(
-    w_x, w_small, own, full_x, full_small, params, send, recv, here, own_send, own_recv,
+    w_x, w_small, own, tokens, w_z, w_out, full_x, full_small, params, earlier, full_z, full_out, send, recv, here, own_send, own_recv, near_send, near_recv,
 ):
     at = position()
     sibling = peers(at, "core")[0]
     partner = moved(at, "y", 3 - at["y"])
     everyone = [sibling, partner] + [p for axis in ("x", "z", "l") for p in peers(at, axis)]
-    greet(everyone)
+    me = lax.axis_index("seq")
+    after, before = lax.rem(me + 1, HEADS), lax.rem(me + HEADS - 1, HEADS)
+    barrier = pltpu.get_barrier_semaphore()
+    for chunk in (after, before):
+        pl.semaphore_signal(barrier, inc=1, device_id={"seq": chunk}, device_id_type=pl.DeviceIdType.MESH)
+    greet(everyone, 2)
     started = []
+    near = []
+    for b in range(SEQS):
+        one = pltpu.make_async_remote_copy(
+            src_ref=tokens.at[b, TOK - 16 :], dst_ref=earlier.at[b], send_sem=near_send.at[b], recv_sem=near_recv.at[b],
+            device_id={"seq": after}, device_id_type=pl.DeviceIdType.MESH,
+        )
+        one.start()
+        started.append(one)
+        near.append(one)
 
     def copy(src, dst, which, to, sems=(send, recv)):
         one = pltpu.make_async_remote_copy(
@@ -939,34 +1065,29 @@
         started.append(one)
         return one
 
-    high = at["y"] // 2
-    mine, opposite = high * 2 + at["core"], (1 - high) * 2 + at["core"]
-    half = INNER // 2
-    flows = ((full_x, 0, half, "x", "z"), (full_x, half, half, "z", "x"), (full_small, 0, SMALL, "x", "z"))
-
-    def view(ref, shard, row, count, first, size):
-        row = pl.multiple_of(row, 16)
-        if shard is None:
-            return ref.at[pl.ds(row, count), first : first + size]
-        return ref.at[shard, pl.ds(row, count), first : first + size]
-
-    arriving = []
-    for i, (ref, first, size, a, b) in enumerate(flows):
-        row = (at[b] * 4 + at[a]) * 16
-        src = w_small if i == 2 else w_x
-        arriving.append(copy(view(src, None, row, 16, first, size), view(ref, mine, row, 16, first, size), i, partner))
+    half, quarter = INNER // 2, w_out.shape[1] // 2
+    flows = Flows(
+        at,
+        (
+            (w_x, full_x, 0, half, "x", "z", 16), (w_x, full_x, half, half, "z", "x", 16),
+            (w_small, full_small, 0, SMALL, "x", "z", 16),
+            (w_z, full_z, 0, half, "x", "z", 16), (w_z, full_z, half, half, "z", "x", 16),
+            (w_out, full_out, 0, quarter, "x", "z", 32), (w_out, full_out, quarter, quarter, "z", "x", 32),
+        ),
+        copy,
+    )
+    flows.begin()
     params_here = pltpu.make_async_copy(own, params.at[at["z"], at["x"], at["l"]], here.at[2])
     local = [
-        pltpu.make_async_copy(w_x, full_x.at[mine], here.at[0]),
-        pltpu.make_async_copy(w_small, full_small.at[mine], here.at[1]),
+        pltpu.make_async_copy(w_x, full_x.at[flows.mine], here.at[0]),
+        pltpu.make_async_copy(w_small, full_small.at[flows.mine], here.at[1]),
         params_here,
+        pltpu.make_async_copy(w_z, full_z.at[flows.mine], here.at[3]),
+        pltpu.make_async_copy(w_out, full_out.at[flows.mine], here.at[4]),
     ]
     for one in local:
         one.start()
-    last = [
-        copy(w_x, full_x.at[mine], 24, sibling),
-        copy(w_small, full_small.at[mine], 25, sibling),
-    ]
+    flows.own([(w_x, full_x), (w_small, full_small), (w_z, full_z), (w_out, full_out)])
     params_here.wait()
 
     def share(stage):
@@ -975,61 +1096,48 @@
         return [copy(ref, ref, 3 * stage + d, to, (own_send, own_recv)) for d, to in enumerate(peers(at, axis))]
 
     shared = share(0)
-    second = []
-    for i, (ref, first, size, a, b) in enumerate(flows):
-        arriving[i].wait_recv()
-        piece = view(ref, opposite, (at[b] * 4 + at[a]) * 16, 16, first, size)
-        second.append([copy(piece, piece, 3 + 3 * i + d, to) for d, to in enumerate(peers(at, a))])
+    flows.spread()
     for one in shared:
         one.wait_recv()
     shared = share(1)
-    third = []
-    for i, (ref, first, size, a, b) in enumerate(flows):
-        for one in second[i]:
-            one.wait_recv()
-        block = view(ref, opposite, at[b] * 64, 64, first, size)
-        third.append([copy(block, block, 12 + 3 * i + d, to) for d, to in enumerate(peers(at, b))])
-        last.append(copy(block, block, 21 + i, sibling))
+    flows.spread_more()
     for one in shared:
         one.wait_recv()
     shared = share(2)
-    for i, (ref, first, size, a, b) in enumerate(flows):
-        for d in range(3):
-            third[i][d].wait_recv()
-            block = view(ref, opposite, lax.rem(at[b] + 3 - d, 4) * 64, 64, first, size)
-            last.append(copy(block, block, 26 + 3 * i + d, sibling))
-    for one in last + shared:
+    flows.forward()
+    flows.finish()
+    for one in shared + near:
         one.wait_recv()
-    for one in local[:2]:
+    for one in (*local[:2], *local[3:]):
         one.wait()
     for one in started:
         one.wait_send()
 
 
-def gather_weights(w_x, w_small, own):
+def gather_weights(w_x, w_small, own, tokens, w_z, w_out):
     vmem = pl.BlockSpec(memory_space=pltpu.VMEM)
+    hbm = pl.BlockSpec(memory_space=pl.ANY)
     return pl.pallas_call(
         gather_kernel,
         out_shape=[
             jax.ShapeDtypeStruct((4, *w_x.shape), BF16),
             jax.ShapeDtypeStruct((4, *w_small.shape), BF16),
             jax.ShapeDtypeStruct((4, 4, 2, 8, 128), F32),
+            jax.ShapeDtypeStruct((SEQS, 16, tokens.shape[2]), BF16),
+            jax.ShapeDtypeStruct((4, *w_z.shape), BF16),
+            jax.ShapeDtypeStruct((4, *w_out.shape), BF16),
         ],
-        in_specs=[vmem] * 3,
-        out_specs=[vmem] * 3,
+        in_specs=[vmem] * 4 + [hbm] * 2,
+        out_specs=[vmem] * 4 + [hbm] * 2,
         scratch_shapes=[
-            pltpu.SemaphoreType.DMA((35,)), pltpu.SemaphoreType.DMA((35,)), pltpu.SemaphoreType.DMA((3,)),
-            pltpu.SemaphoreType.DMA((9,)), pltpu.SemaphoreType.DMA((9,)),
+            pltpu.SemaphoreType.DMA((81,)), pltpu.SemaphoreType.DMA((81,)), pltpu.SemaphoreType.DMA((5,)),
+            pltpu.SemaphoreType.DMA((9,)), pltpu.SemaphoreType.DMA((9,)), pltpu.SemaphoreType.DMA((2,)), pltpu.SemaphoreType.DMA((2,)),
         ],
         compiler_params=pltpu.CompilerParams(
-            vmem_limit_bytes=VMEM_LIMIT, collective_id=2, has_side_effects=True
+            vmem_limit_bytes=48 * 1024 * 1024, collective_id=2, has_side_effects=True
         ),
         cost_estimate=pl.CostEstimate(flops=int(1e6), bytes_accessed=int(4e7), transcendentals=0),
-    )(w_x, w_small, own)
-
-
-def gather_rows(shard):
-    return lax.all_gather(shard, "wshard", axis=0, tiled=True)
+    )(w_x, w_small, own, tokens, w_z, w_out)
 
 
 def shards(
@@ -1037,14 +1145,12 @@
     dt_bias, a_log, d_skip, gain_norm, w_out, cotangent,
 ):
     width = layer_in.shape[2]
-    chunks = lax.axis_size("seq")
     place = lax.axis_index("seq")
-    earlier = lax.ppermute(layer_in[:, TOK - (TAPS - 1) :, :], "seq", [(i, i + 1) for i in range(chunks - 1)])
-    full_z = gather_rows(w_z)
-    full_out = gather_rows(w_out)
     own = jnp.concatenate([conv_x_weight.reshape(-1), conv_x_bias, dt_bias, a_log, d_skip, jnp.zeros((701,), F32)])
     small = jnp.concatenate([w_bc, w_dt, jnp.zeros((w_bc.shape[0], SMALL - 2 * STATE - HEADS), BF16)], axis=1)
-    full_x, full_small, params = gather_weights(w_x, small, own.reshape(8, 128))
+    full_x, full_small, params, earlier, full_z, full_out = gather_weights(
+        w_x, small, own.reshape(8, 128), layer_in, w_z, w_out
+    )
     full_x = full_x.reshape(width, INNER)
     full_small = full_small.reshape(width, SMALL)
     params = params.reshape(HEADS, -1)
@@ -1056,7 +1162,9 @@
 
     hidden = layer_in.astype(F32).reshape(ROWS, width)
     upstream = cotangent.reshape(ROWS, width)
-    halo = jnp.pad(earlier, ((0, 0), (HALO - (TAPS - 1), 0), (0, 0))).reshape(SEQS * HALO, width).astype(F32)
+    halo = earlier[:, HALO:].astype(F32)
+    kept = (lax.broadcasted_iota(jnp.int32, halo.shape, 1) >= HALO - (TAPS - 1)) & (place > 0)
+    halo = jnp.where(kept, halo, 0.0).reshape(SEQS * HALO, width)
     tokens = jnp.concatenate([hidden, halo], axis=0)
     inv = lax.rsqrt(jnp.mean(tokens * tokens, axis=-1, keepdims=True) + EPS)
     normed = (tokens * inv * gain_in[None, :]).astype(BF16)
@@ -1067,28 +1175,27 @@
     xc, bcc, dt, dt_wide, r_wide, r_rows, y_in, start, decay = head(
         x_raw, bc_raw, dt_raw, taps_x, bias_x, conv_bc_weight, bias_bc, bias_dt, log_a
     )
-    gate = mm(normed[:ROWS], full_z, NN)
-    d_mixed = mm(upstream, full_out, NT)
+    full_z = full_z.reshape(width, INNER)
+    full_out = full_out.reshape(INNER, width)
     mixed, d_y, d_gate, v, g_norm, row_dot = middle(
-        y_in, xc, bcc, r_wide, start, skip_wide, gate, d_mixed, gain_norm.reshape(1, INNER)
-    )
-    layer_out = (hidden + mm(mixed, full_out, NN)).astype(BF16).reshape(SEQS, TOK, width)
-    *gathered, input_grad, total = tail(
+        y_in, xc, bcc, r_wide, start, skip_wide, normed, upstream, full_z, full_out, gain_norm.reshape(1, INNER)
+    )
+    *gathered, input_grad, layer_out, total = tail(
         v, decay, xc, d_y, bcc, dt, dt_wide, r_wide, r_rows, x_raw, start, bc_raw, dt_raw, row_dot,
         taps_x, bias_x, conv_bc_weight, bias_bc, bias_dt, log_a, skip_wide, g_norm,
         normed, d_gate, mixed, upstream, layer_in.reshape(ROWS, width), gain_in.reshape(1, width),
-        full_z, full_x, full_small,
-    )
+        full_z, full_x, full_out, full_small,
+    )
+    layer_out = layer_out.reshape(SEQS, TOK, width)
     input_grad = input_grad.reshape(SEQS, TOK, width)
-    grad_w_z, grad_w_x, grad_w_out, extra = unpack(*gathered)
+    grad_w_z, grad_w_x, grad_w_out, extra, s_x, s_norm, s_in, s_bc, s_heads = unpack(width, *gathered, total)
     grad_w_out = grad_w_out.reshape(4 * PIECE, width)
     extra = extra.reshape(4, 2 * PIECE, 128)
     grad_w_bc = jnp.concatenate([extra[0], extra[1]], axis=1)
     grad_w_dt = extra[2][:, :HEADS]
-    s_x = lax.dynamic_slice(total[: TAPS + 1], (0, place * HEAD), (TAPS + 1, HEAD))
-    s_norm, s_in = total[8], total[9, :width]
-    s_bc = total[10 : 10 + TAPS + 1, : 2 * STATE]
-    s_heads = lax.dynamic_slice(total[10:13], (0, 2 * STATE + place), (3, 1))
+    s_x = lax.dynamic_slice(s_x, (0, place * HEAD), (TAPS + 1, HEAD))
+    s_norm, s_in = s_norm.reshape(INNER), s_in.reshape(width)
+    s_heads = lax.dynamic_slice(s_heads, (0, place), (3, 1))
     return (
         layer_out, input_grad, s_in, grad_w_z, grad_w_x, grad_w_bc, grad_w_dt,
         s_x[:TAPS], s_x[TAPS], s_bc[:TAPS], s_bc[TAPS], s_heads[0], s_heads[1], s_heads[2], s_norm, grad_w_out,

time: 283 us -> 261 us (0.922)
  Pallas kernels: 211 us -> 230 us
  between operations: 16.5 us -> 2.78 us
  matrix products: 16.2 us -> 2.8 us
  local copies, waits for them, and re-layouts: 30.1 us -> 21.7 us
  starting transfers between devices: 3.64 us -> 0 us
  waiting for transfers between devices: 3.35 us -> 0 us
    pallas_call x1, Pallas kernels: 26.8 us -> 43.1 us  [gather_weights(): pl.pallas_call(gather_kernel, out_shape=[jax.ShapeDtypeStruct((4, *w_x.sh...]
    dot_general x5 -> x2, matrix products: 16.2 us -> 2.8 us  [mm(): lax.dot_general(a, b, ((dims[0], dims[1]), ((), ())), precision=precision...]
    unnamed x97 -> x30, local copies, waits for them, and re-layouts: 20.5 us -> 9.68 us
    slice x5 -> x0, local copies, waits for them, and re-layouts: 4.5 us -> none  [the longest x2 2.8 us: shards(): s_norm, s_in = (total[8], total[9, :width])]
    pallas_call x1, Pallas kernels: 10.5 us -> 14.6 us  [middle(): call(middle_kernel, [((ROWS, INNER), BF16), ((ROWS, INNER), BF16), ((ROWS...]
    ppermute x1 -> x0, starting transfers between devices: 3.56 us -> none  [shards(): lax.ppermute(layer_in[:, TOK - (TAPS - 1):, :], 'seq', [(i, i + 1) for i...]
  transfers between devices with their start and end apart: 3 -> 0, of which waited for: 1 -> 0; matrix products, arithmetic and copies ran while one was open for 3% -> 0% of each run, Pallas kernels for 28% -> 0%
where the time goes in v6:
time: 261 us; the launch traced here: 259 us
  Pallas kernels  230 us (88%)
  local copies, waits for them, and re-layouts  21.7 us (8%)
  matrix products  2.8 us (1%)
  between operations  2.78 us (1%)
    pallas_call x1, Pallas kernels, tail(): pl.pallas_call(tail_kernel, out_shape=out_shape, in_specs=specs, out_spec...  115 us
    pallas_call x1, Pallas kernels, head(): pl.pallas_call(head_kernel, out_shape=[jax.ShapeDtypeStruct(s, d) for s,...  51.3 us
    pallas_call x1, Pallas kernels, gather_weights(): pl.pallas_call(gather_kernel, out_shape=[jax.ShapeDtypeStruct((4, *w_x.sh...  43.1 us
    pallas_call x1, Pallas kernels, middle(): call(middle_kernel, [((ROWS, INNER), BF16), ((ROWS, INNER), BF16), ((ROWS...  14.6 us
    unnamed x30, local copies, waits for them, and re-layouts  9.68 us
    pallas_call x1, Pallas kernels, unpack(): call(unpack_kernel, [((2 * PIECE, INNER), F32), ((2 * PIECE, INNER), F32)...  5.79 us

profile of v6, /device:TPU:0, one launch (start us, length us, event | category | flops | bytes accessed | tf_op | source)
XLA Modules:
  0.0 259.3 jit_solution(16240721620489338455)
XLA Ops:
  0.6 0.8 copy.32
  1.5 0.1 pad.6.clone
  1.6 0.9 maximum_maximum_fusion.w_small
  2.5 0.8 reshape.121
  5.2 0.7 concatenate.13
  6.0 0.0 copy-start
  6.0 1.0 copy-done
  7.0 0.0 copy-start.2
  7.0 1.2 copy-done.2
  8.2 0.0 copy-start.3
  8.2 1.2 copy-done.3
  9.5 0.0 copy-start.4
  9.5 1.2 copy-done.4
  10.7 0.0 copy-start.1
  10.7 43.1 %shard_map.279 = (bf16[4,256,2048]{2,1,0:T(8,128)(2,1)}, bf16[4,256,384]{2,1,0:T(8,128)(2,1)S(1)}, f32[4,4,2,8,128]{4,3,2,1,0:T(8,128)S(1)}, bf16[2,16,1024]{2,1...) custom-call(bf16[256,2048]{1,0:T(8,128)(2,1)S(1)} %copy-done.2, ...), custom_call_target="tpu_custom_call" | custom-call | flops 1000000 | bytes 40000000 | tf_op jit(solution)/shard_map/pallas_call | solution.py:1120
  53.8 0.0 copy-start.5
  53.9 0.0 copy-start.9
  53.9 0.1 select_bitcast_fusion
  54.0 0.0 copy-done.1
  54.0 0.1 reshape.120
  54.1 0.0 copy-start.10
  54.1 0.2 multiply_reduce_fusion
  54.3 0.3 copy-done.9
  54.6 0.2 multiply_convert_fusion.normed
  54.7 0.0 copy-start.6
  54.7 0.0 copy-done.5
  54.8 0.5 convolution_convert_fusion.1
  55.2 0.7 slice.79.bc_raw
  55.9 0.6 slice.80.dt_raw
  56.5 0.1 copy-done.10
  56.6 2.3 convolution_convert_fusion.x_raw
  58.9 0.0 copy-done.6
  59.0 0.1 fusion.1
  59.0 0.6 copy.38
  59.6 0.6 copy.39
  60.2 0.1 reshape.127
  60.3 0.7 reshape.128.taps_x
  61.0 0.7 reshape.129.bias_x
  61.7 51.3 %shard_map.280 = (bf16[256,2048]{1,0:T(8,128)(2,1)}, bf16[256,256]{1,0:T(8,128)(2,1)}, f32[256,32]{1,0:T(8,128)}, f32[256,2048]{1,0:T(8,128)}, f32[256,2048]{1,0...) custom-call(bf16[272,2048]{1,0:T(8,128)(2,1)} %convolution_convert_f, ...), custom_call_target="tpu_custom_call" | custom-call | flops 2000000000 | bytes 20000000 | tf_op jit(solution)/shard_map/pallas_call | solution.py:372
  113.0 0.1 copy.40
  113.1 0.1 broadcast_in_dim.22
  113.1 0.7 broadcast_in_dim.23.d_skip
  113.8 14.6 %shard_map.281 = (bf16[256,2048]{1,0:T(8,128)(2,1)}, bf16[256,2048]{1,0:T(8,128)(2,1)}, bf16[256,2048]{1,0:T(8,128)(2,1)}, bf16[32,2,64,128]{3,2,1,0:T(8,128)(2,...) custom-call(f32[256,2048]{1,0:T(8,128)} %get-tuple-element.59.y_in, bf16[256,2048]{1,0:T(8,128)(2,1)} %get-tuple-element.60.xc, ...), custom_call_target="tpu_custom_call" | custom-call | flops 1000000000 | bytes 10000000 | tf_op jit(solution)/shard_map/pallas_call | solution.py:476
  128.5 115.0 %shard_map.282 = (bf16[4,4,2,80,128]{4,3,2,1,0:T(8,128)(2,1)}, bf16[4,4,2,80,128]{4,3,2,1,0:T(8,128)(2,1)}, bf16[2,4,4,96,128]{4,3,2,1,0:T(8,128)(2,1)}, bf16[4,...) custom-call(bf16[32,2,64,128]{3,2,1,0:T(8,128)(2,1)} %get-tuple-elem, ...), custom_call_target="tpu_custom_call" | custom-call | flops 8000000000 | bytes 40000000 | tf_op jit(solution)/shard_map/pallas_call | solution.py:971
  243.5 0.0 copy-start.8
  243.5 5.8 %shard_map.283 = (f32[256,2048]{1,0:T(8,128)}, f32[256,2048]{1,0:T(8,128)}, f32[2,2,128,1024]{3,2,1,0:T(8,128)}, f32[4,2,128,128]{3,2,1,0:T(8,128)}, f32[8,2048]...) custom-call(bf16[4,4,2,80,128]{4,3,2,1,0:T(8,128)(2,1)} %get-tuple-element.78.sum_za, ...), custom_call_target="tpu_custom_call" | custom-call | flops 1000000000 | bytes 10000000 | tf_op jit(solution)/shard_map/pallas_call | solution.py:1021
  249.3 0.0 copy-start.7
  249.3 1.1 fusion
  250.4 0.7 pad_maximum_fusion.1
  251.2 0.7 copy.41
  251.8 0.8 constant_dynamic-slice_fusion.1
  252.6 0.6 slice.72
  253.2 0.5 slice_bitcast_fusion
  253.7 0.8 constant_dynamic-slice_fusion
  254.4 0.5 fusion.2
  255.0 1.3 slice.74
  256.3 1.3 slice.75
  257.5 0.0 copy-done.8
  257.5 0.8 copy.52
  258.3 0.0 copy-done.7
  258.3 1.0 copy.53
  (8 shorter events, 0.1 us)
Async XLA Ops:
  6.0 1.0 copy-start
  7.0 1.2 copy-start.2
  8.2 1.2 copy-start.3
  9.5 1.2 copy-start.4
  10.7 43.3 %copy-start.1 = (bf16[2,128,1024]{2,1,0:T(8,128)(2,1)S(1)}, bf16[2,128,1024]{2,1,0:T(8,128)(2,1)}, u32[]{:S(2)}) copy-start(bf16[2,128,1024]{2,1,0:T(8,128)(2,1)} %tokens.1) | copy-start | bytes 1572868
  53.8 0.9 copy-start.5
  53.9 0.7 copy-start.9
  54.1 2.5 copy-start.10
  54.7 4.2 %copy-start.6 = (bf16[272,1024]{1,0:T(8,128)(2,1)}, bf16[272,1024]{1,0:T(8,128)(2,1)S(1)}, u32[]{:S(2)}) copy-start(bf16[272,1024]{1,0:T(8,128)(2,1)S(1)} %multiply_convert_fusion.normed) | copy-start | bytes 1671172
  243.5 14.1 %copy-start.8 = (bf16[256,1024]{1,0:T(8,128)(2,1)S(1)}, bf16[256,1024]{1,0:T(8,128)(2,1)}, u32[]{:S(2)}) copy-start(bf16[256,1024]{1,0:T(8,128)(2,1)} %get-tuple-element.76) | copy-start | bytes 1572868
  249.3 9.1 %copy-start.7 = (f32[256,1024]{1,0:T(8,128)S(1)}, f32[256,1024]{1,0:T(8,128)}, u32[]{:S(2)}) copy-start(f32[256,1024]{1,0:T(8,128)} %get-tuple-element.77) | copy-start | bytes 3145732

commit v7 on v6

--- a/solution.py
+++ b/solution.py
@@ -53,6 +53,14 @@
     return mm(jnp.concatenate([high, low], axis=1), jnp.concatenate([ex, ex], axis=1), NT)
 
 
+def three_terms(values):
+    high = values.astype(BF16)
+    rest = values - high.astype(F32)
+    middle = rest.astype(BF16)
+    low = (rest - middle.astype(F32)).astype(BF16)
+    return jnp.concatenate([high, middle, low], axis=1)
+
+
 def lane_sums(values):
     high = values.astype(BF16)
     low = (values - high.astype(F32)).astype(BF16)
@@ -235,9 +243,14 @@
 
 def chunk_copy(src, dst, send, recv, to, slot):
     return pltpu.make_async_remote_copy(
-        src_ref=src.at[to], dst_ref=dst.at[slot], send_sem=send.at[to], recv_sem=recv.at[slot],
+        src_ref=src.at[to], dst_ref=dst.at[slot], send_sem=send, recv_sem=recv,
         device_id={"seq": to}, device_id_type=pl.DeviceIdType.MESH,
     )
+
+
+def wait_others(ref, sem):
+    rest = ref.at[pl.ds(0, HEADS - 1)]
+    pltpu.make_async_copy(rest, rest, sem).wait()
 
 
 def each_other(me, step):
@@ -275,7 +288,7 @@
 def head_kernel(
     x_raw, bc_raw, dt_raw, taps_x, bias_x, taps_bc, bias_bc, dt_bias, a_log,
     xc, bcc, dt, dt_wide, r_wide, r_rows, y_in, start, decay,
-    r, scores, u, u_all, own_decay, s_own, u_send, u_recv, e_send, e_recv, s_send, s_recv,
+    r, terms, scores, u, u_all, own_decay, s_own, u_send, u_recv, e_send, e_recv, s_send, s_recv,
 ):
     me = lax.axis_index("seq")
     barrier = greet_chunks(me)
@@ -289,6 +302,7 @@
         bcc[span, :] = (pre * jax.nn.sigmoid(pre)).astype(BF16)
         r[span, :] = mm(tri, rates[span, :], NN, HIGHEST)
         scores[b] = mm(bcc[span, STATE:], bcc[span, 0:STATE], NT)
+    terms[...] = three_terms(jnp.concatenate([r[...], dt[...]], axis=0))
     first = iota((8, 128), 1) < HEAD
     pl.semaphore_wait(barrier, HEADS - 1)
 
@@ -296,10 +310,12 @@
         j = lax.rem(me // 2 + i, PAIRS)
         cols = lane_block(j)
         raw = x_raw[:, cols].astype(F32)
-        both = mm(jnp.concatenate([r[...], dt[...]], axis=0), pair_matrix(j), NN, HIGHEST)
+        ex = pair_matrix(j).astype(BF16)
+        both = mm(terms[...], jnp.concatenate([ex] * 3, axis=0), NN)
         r_wide[:, cols] = both[0:ROWS, :]
         dt_wide[:, cols] = both[ROWS:, :]
-        r_rows[j] = mm(pair_rows(j), r[...], NT, HIGHEST)
+        rows = pair_rows(j).astype(BF16)
+        r_rows[j] = mm(jnp.concatenate([rows] * 3, axis=1), terms[0:ROWS, :], NT)
         ends = []
         for b in range(SEQS):
             span = slice(TOK * b, TOK * (b + 1))
@@ -343,8 +359,8 @@
         return 0
 
     pairs_loop(0, 6, inside_pair)
-    each_other(me, lambda other: chunk_copy(u, u_all, u_send, u_recv, other, other).wait_recv())
-    each_other(me, lambda other: chunk_copy(own_decay, decay, e_send, e_recv, other, other).wait_recv())
+    wait_others(u_all, u_recv)
+    wait_others(decay, e_recv)
 
     def chunk_step(c, carry):
         after = []
@@ -357,10 +373,10 @@
     each_other(me, lambda other: chunk_copy(s_own, start, s_send, s_recv, other, me).start())
     start[me] = s_own[me]
     pairs_loop(6, PAIRS, inside_pair)
-    each_other(me, lambda other: chunk_copy(s_own, start, s_send, s_recv, other, other).wait_recv())
-    each_other(me, lambda other: chunk_copy(u, u_all, u_send, u_recv, other, me).wait_send())
-    each_other(me, lambda other: chunk_copy(own_decay, decay, e_send, e_recv, other, me).wait_send())
-    each_other(me, lambda other: chunk_copy(s_own, start, s_send, s_recv, other, me).wait_send())
+    wait_others(start, s_recv)
+    wait_others(u, u_send)
+    wait_others(own_decay, e_send)
+    wait_others(s_own, s_send)
 
 
 def head(*args):
@@ -375,9 +391,10 @@
         in_specs=[vmem] * len(args),
         out_specs=[vmem] * len(outs),
         scratch_shapes=[
-            pltpu.VMEM((ROWS, HEADS), F32), pltpu.VMEM((SEQS, TOK, TOK), F32), *[pltpu.VMEM(STATES_SHAPE, BF16)] * 2,
+            pltpu.VMEM((ROWS, HEADS), F32), pltpu.VMEM((2 * ROWS, 3 * HEADS), BF16), pltpu.VMEM((SEQS, TOK, TOK), F32),
+            *[pltpu.VMEM(STATES_SHAPE, BF16)] * 2,
             pltpu.VMEM((HEADS, 8, 128), F32), pltpu.VMEM(STATES_SHAPE, BF16),
-            *[pltpu.SemaphoreType.DMA((HEADS,))] * 6,
+            *[pltpu.SemaphoreType.DMA] * 6,
         ],
         compiler_params=pltpu.CompilerParams(
             vmem_limit_bytes=VMEM_LIMIT, collective_id=3, has_side_effects=True
@@ -533,12 +550,6 @@
         each_other(me, lambda other: chunk_copy(src, dst, send, recv, other, me).start())
         dst[me] = src[me]
 
-    def swap_wait(src, dst, send, recv):
-        each_other(me, lambda other: chunk_copy(src, dst, send, recv, other, other).wait_recv())
-
-    def swap_sent(src, dst, send, recv):
-        each_other(me, lambda other: chunk_copy(src, dst, send, recv, other, me).wait_send())
-
     swap_start(v, v_all, v_send, v_recv)
 
     def columns(ref, high, which, size):
@@ -587,7 +598,7 @@
         d_bc[span, 0:STATE] = mm(low, bcc[span, STATE:], TN)
         d_bc[span, STATE:] = mm(low, bcc[span, 0:STATE], NN)
 
-    swap_wait(v, v_all, v_send, v_recv)
+    wait_others(v_all, v_recv)
 
     def chunk_step(i, carry):
         c = HEADS - 1 - i
@@ -717,7 +728,7 @@
         d_normed[0:ROWS, cols] = sum(mm(d_gate[:, h], weights[i, cols, :], NT) for i, h in enumerate(halves))
     loading = load([full_x.at[:, h] for h in halves])
 
-    swap_wait(g_own, end, g_send, g_recv)
+    wait_others(end, g_recv)
     sums[...] = jnp.zeros_like(sums)
 
     def back_pair(j, _):
@@ -932,8 +943,8 @@
         arrived(which)
     for one in started:
         one.wait_send()
-    swap_sent(v, v_all, v_send, v_recv)
-    swap_sent(g_own, end, g_send, g_recv)
+    wait_others(v, v_send)
+    wait_others(g_own, g_send)
 
 
 def tail(*args):
@@ -965,7 +976,7 @@
         pltpu.VMEM((2, ALL, 256), BF16), pltpu.VMEM((ROWS, INNER), BF16), pltpu.VMEM((2, ROWS, 512), BF16),
         pltpu.VMEM((ROWS, width), BF16), pltpu.VMEM((ALL, INNER), BF16), pltpu.VMEM((ALL, SMALL), BF16),
         *bufs(4, 4, 4), *bufs(3, 4, 4), *bufs(4, 4), *bufs(3, 4), *bufs(4), *bufs(3),
-        *sems(HEADS), *sems(HEADS), *sems(11), *sems(SETS, 3, 3), *sems(SETS, 3, 3), *sems(4, 3),
+        *[pltpu.SemaphoreType.DMA] * 4, *sems(11), *sems(SETS, 3, 3), *sems(SETS, 3, 3), *sems(4, 3),
         pltpu.SemaphoreType.DMA((2,)), pltpu.SemaphoreType.DMA((2,)),
     ]
     return pl.pallas_call(

time: 261 us -> 252 us (0.966)
  Pallas kernels: 230 us -> 221 us
    pallas_call x1, Pallas kernels: 115 us -> 111 us  [tail(): pl.pallas_call(tail_kernel, out_shape=out_shape, in_specs=specs, out_spec...]
    pallas_call x1, Pallas kernels: 51.3 us -> 47.2 us  [head(): pl.pallas_call(head_kernel, out_shape=[jax.ShapeDtypeStruct(s, d) for s,...]
where the time goes in v7:
time: 252 us; the launch traced here: 251 us
  Pallas kernels  221 us (88%)
  local copies, waits for them, and re-layouts  21.7 us (9%)
  matrix products  2.8 us (1%)
  between operations  2.78 us (1%)
    pallas_call x1, Pallas kernels, tail(): pl.pallas_call(tail_kernel, out_shape=out_shape, in_specs=specs, out_spec...  111 us
    pallas_call x1, Pallas kernels, head(): pl.pallas_call(head_kernel, out_shape=[jax.ShapeDtypeStruct(s, d) for s,...  47.2 us
    pallas_call x1, Pallas kernels, gather_weights(): pl.pallas_call(gather_kernel, out_shape=[jax.ShapeDtypeStruct((4, *w_x.sh...  43.1 us
    pallas_call x1, Pallas kernels, middle(): call(middle_kernel, [((ROWS, INNER), BF16), ((ROWS, INNER), BF16), ((ROWS...  14.6 us
    unnamed x30, local copies, waits for them, and re-layouts  9.68 us
    pallas_call x1, Pallas kernels, unpack(): call(unpack_kernel, [((2 * PIECE, INNER), F32), ((2 * PIECE, INNER), F32)...  5.79 us

profile of v7, /device:TPU:0, one launch (start us, length us, event | category | flops | bytes accessed | tf_op | source)
XLA Modules:
  0.0 250.9 jit_solution(9767304674502077343)
XLA Ops:
  0.6 0.8 copy.32
  1.5 0.1 pad.6.clone
  1.6 0.9 maximum_maximum_fusion.w_small
  2.5 0.8 reshape.121
  5.2 0.7 concatenate.13
  6.0 0.0 copy-start
  6.0 1.0 copy-done
  7.0 0.0 copy-start.2
  7.0 1.2 copy-done.2
  8.2 0.0 copy-start.3
  8.2 1.2 copy-done.3
  9.5 0.0 copy-start.4
  9.5 1.2 copy-done.4
  10.7 0.0 copy-start.1
  10.7 43.1 %shard_map.279 = (bf16[4,256,2048]{2,1,0:T(8,128)(2,1)}, bf16[4,256,384]{2,1,0:T(8,128)(2,1)S(1)}, f32[4,4,2,8,128]{4,3,2,1,0:T(8,128)S(1)}, bf16[2,16,1024]{2,1...) custom-call(bf16[256,2048]{1,0:T(8,128)(2,1)S(1)} %copy-done.2, ...), custom_call_target="tpu_custom_call" | custom-call | flops 1000000 | bytes 40000000 | tf_op jit(solution)/shard_map/pallas_call | solution.py:1131
  53.8 0.0 copy-start.5
  53.9 0.0 copy-start.9
  53.9 0.1 select_bitcast_fusion
  54.0 0.0 copy-done.1
  54.0 0.1 reshape.120
  54.1 0.0 copy-start.10
  54.1 0.2 multiply_reduce_fusion
  54.3 0.3 copy-done.9
  54.6 0.2 multiply_convert_fusion.normed
  54.7 0.0 copy-start.6
  54.7 0.0 copy-done.5
  54.8 0.5 convolution_convert_fusion.1
  55.2 0.7 slice.79.bc_raw
  55.9 0.6 slice.80.dt_raw
  56.5 0.1 copy-done.10
  56.6 2.3 convolution_convert_fusion.x_raw
  58.9 0.0 copy-done.6
  59.0 0.1 fusion.1
  59.0 0.6 copy.38
  59.6 0.6 copy.39
  60.2 0.1 reshape.127
  60.3 0.7 reshape.128.taps_x
  61.0 0.7 reshape.129.bias_x
  61.7 47.2 %shard_map.280 = (bf16[256,2048]{1,0:T(8,128)(2,1)}, bf16[256,256]{1,0:T(8,128)(2,1)}, f32[256,32]{1,0:T(8,128)}, f32[256,2048]{1,0:T(8,128)}, f32[256,2048]{1,0...) custom-call(bf16[272,2048]{1,0:T(8,128)(2,1)} %convolution_convert_f, ...), custom_call_target="tpu_custom_call" | custom-call | flops 2000000000 | bytes 20000000 | tf_op jit(solution)/shard_map/pallas_call | solution.py:388
  108.9 0.1 copy.40
  109.0 0.1 broadcast_in_dim.22
  109.1 0.7 broadcast_in_dim.23.d_skip
  109.7 14.6 %shard_map.281 = (bf16[256,2048]{1,0:T(8,128)(2,1)}, bf16[256,2048]{1,0:T(8,128)(2,1)}, bf16[256,2048]{1,0:T(8,128)(2,1)}, bf16[32,2,64,128]{3,2,1,0:T(8,128)(2,...) custom-call(f32[256,2048]{1,0:T(8,128)} %get-tuple-element.59.y_in, bf16[256,2048]{1,0:T(8,128)(2,1)} %get-tuple-element.60.xc, ...), custom_call_target="tpu_custom_call" | custom-call | flops 1000000000 | bytes 10000000 | tf_op jit(solution)/shard_map/pallas_call | solution.py:493
  124.4 110.7 %shard_map.282 = (bf16[4,4,2,80,128]{4,3,2,1,0:T(8,128)(2,1)}, bf16[4,4,2,80,128]{4,3,2,1,0:T(8,128)(2,1)}, bf16[2,4,4,96,128]{4,3,2,1,0:T(8,128)(2,1)}, bf16[4,...) custom-call(bf16[32,2,64,128]{3,2,1,0:T(8,128)(2,1)} %get-tuple-elem, ...), custom_call_target="tpu_custom_call" | custom-call | flops 8000000000 | bytes 40000000 | tf_op jit(solution)/shard_map/pallas_call | solution.py:982
  235.1 0.0 copy-start.8
  235.1 5.8 %shard_map.283 = (f32[256,2048]{1,0:T(8,128)}, f32[256,2048]{1,0:T(8,128)}, f32[2,2,128,1024]{3,2,1,0:T(8,128)}, f32[4,2,128,128]{3,2,1,0:T(8,128)}, f32[8,2048]...) custom-call(bf16[4,4,2,80,128]{4,3,2,1,0:T(8,128)(2,1)} %get-tuple-element.78.sum_za, ...), custom_call_target="tpu_custom_call" | custom-call | flops 1000000000 | bytes 10000000 | tf_op jit(solution)/shard_map/pallas_call | solution.py:1032
  240.9 0.0 copy-start.7
  240.9 1.1 fusion
  242.1 0.7 pad_maximum_fusion.1
  242.8 0.7 copy.41
  243.5 0.8 constant_dynamic-slice_fusion.1
  244.3 0.6 slice.72
  244.8 0.5 slice_bitcast_fusion
  245.3 0.8 constant_dynamic-slice_fusion
  246.1 0.5 fusion.2
  246.6 1.3 slice.74
  247.9 1.3 slice.75
  249.2 0.0 copy-done.8
  249.2 0.8 copy.52
  250.0 0.0 copy-done.7
  250.0 1.0 copy.53
  (8 shorter events, 0.1 us)
Async XLA Ops:
  6.0 1.0 copy-start
  7.0 1.2 copy-start.2
  8.2 1.2 copy-start.3
  9.5 1.2 copy-start.4
  10.7 43.3 %copy-start.1 = (bf16[2,128,1024]{2,1,0:T(8,128)(2,1)S(1)}, bf16[2,128,1024]{2,1,0:T(8,128)(2,1)}, u32[]{:S(2)}) copy-start(bf16[2,128,1024]{2,1,0:T(8,128)(2,1)} %tokens.1) | copy-start | bytes 1572868
  53.8 0.9 copy-start.5
  53.9 0.7 copy-start.9
  54.1 2.5 copy-start.10
  54.7 4.2 %copy-start.6 = (bf16[272,1024]{1,0:T(8,128)(2,1)}, bf16[272,1024]{1,0:T(8,128)(2,1)S(1)}, u32[]{:S(2)}) copy-start(bf16[272,1024]{1,0:T(8,128)(2,1)S(1)} %multiply_convert_fusion.normed) | copy-start | bytes 1671172
  235.1 14.1 %copy-start.8 = (bf16[256,1024]{1,0:T(8,128)(2,1)S(1)}, bf16[256,1024]{1,0:T(8,128)(2,1)}, u32[]{:S(2)}) copy-start(bf16[256,1024]{1,0:T(8,128)(2,1)} %get-tuple-element.76) | copy-start | bytes 1572868
  240.9 9.1 %copy-start.7 = (f32[256,1024]{1,0:T(8,128)S(1)}, f32[256,1024]{1,0:T(8,128)}, u32[]{:S(2)}) copy-start(f32[256,1024]{1,0:T(8,128)} %get-tuple-element.77) | copy-start | bytes 3145732
